TPU v7x, 32 devices: a whole 2x2x4 slice. The times are simulated.
32 devices in a mesh: cls: 8 (over y, x, core), prt: 4 (over z).
Axes of the slice: x: 2, y: 2, z: 4, core: 2. Of those that a mesh axis runs over, the one named last changes fastest.
Arguments:
- particles: bfloat16 [512, 128, 512], P(('cls', 'prt')), may hold values from -20100 to 20100
- references: bfloat16 [512, 128, 512], P('cls'), may hold values from -6 to 6
- owner_groups: int32 [512, 4], P(('cls', 'prt')), may hold values from 0 to 7, all different within a row; in each aligned block of 16 rows (0 to 15, 16 to 31, ...) at most 16 rows name the same one
- class_order: int32 [512, 4, 64], P(('cls', 'prt')), may hold values from 0 to 63, each once within a row
Outputs:
- class_sums: float32 [512, 128, 512], P('cls', 'prt')
- class_weights: float32 [512], P('cls')
- log_norm: float32 [512], P(('cls', 'prt'))
Inputs may be any that keep to these rules, and one draw needn't show every extreme that they name: `owner_groups`: each row names 4 different groups. Among the 16 particles of one device, no group is named by more than 16 rows, a bound that some block reaches. `class_order`: each row along the last dimension is a permutation.
All inputs are finite; a program needn't handle non-finite values.
Results may differ from a plain program's by a relative error of at most 0.0029.
Values may be sent and summed in bfloat16 or wider, within the bound.
No kernel may reach another device: no remote copies, remote signals or barrier semaphores. Data moves between devices by JAX's collectives and lax.ppermute only.
A program may use at most 128 MiB of HBM per device.

v0:
```python
import math

import jax
import jax.numpy as jnp
from jax import lax
from jax.sharding import PartitionSpec as P

CYCLES = 128
HARM = 256
ROTS = 36
OWN_TOP = 4
CAND_OWN = 4


lowest = -1e30


def spectral_tables():
    harmonic = jnp.arange(HARM, dtype=jnp.float32)
    angles = 2.0 * math.pi * jnp.arange(ROTS, dtype=jnp.float32) / ROTS
    phase = harmonic[:, None] * angles[None, :]
    forward = jnp.concatenate([jnp.cos(phase), jnp.sin(phase)], 0)
    backward = jnp.concatenate([jnp.cos(phase), -jnp.sin(phase)], 0).T
    return (forward, backward)


def class_accumulate(lanes, mixed):
    l_re = lanes[..., :HARM]
    l_im = lanes[..., HARM:]
    y_re = mixed[..., :HARM]
    y_im = mixed[..., HARM:]
    s_re = jnp.einsum("lrm,lcm->crm", l_re, y_re, preferred_element_type=jnp.float32) - jnp.einsum(
        "lrm,lcm->crm", l_im, y_im, preferred_element_type=jnp.float32
    )
    s_im = jnp.einsum("lrm,lcm->crm", l_re, y_im, preferred_element_type=jnp.float32) + jnp.einsum(
        "lrm,lcm->crm", l_im, y_re, preferred_element_type=jnp.float32
    )
    return jnp.concatenate([s_re, s_im], -1)


def per_device(particles, references, owner_groups, class_order):
    n_cls = lax.axis_size("cls")
    count = particles.shape[0]
    groups = references.shape[0]
    cap = max(2, 2 * count * OWN_TOP // n_cls)
    slots = n_cls * cap
    width = 2 * HARM
    flat_owner = owner_groups.reshape(-1)
    owner_hot = (flat_owner[:, None] == jnp.arange(n_cls, dtype=jnp.int32)[None, :]).astype(
        jnp.int32
    )
    before = jnp.cumsum(owner_hot, axis=0) - owner_hot
    rank = jnp.sum(before * owner_hot, axis=1)
    slot_of = flat_owner * cap + rank
    match = slot_of[None, :] == jnp.arange(slots, dtype=jnp.int32)[:, None]
    member = jnp.any(match.reshape(slots, count, OWN_TOP), axis=2)
    filled = jnp.any(member, axis=1)
    dispatch = member.astype(jnp.bfloat16)
    outgoing = jnp.dot(
        dispatch, particles.reshape(count, CYCLES * width), preferred_element_type=jnp.float32
    )
    outgoing = outgoing.astype(jnp.bfloat16).reshape(n_cls, cap, CYCLES, width)
    match_int = match.astype(jnp.int32)
    picks = class_order[:, :, :CAND_OWN].reshape(count * OWN_TOP, CAND_OWN)
    slot_cand = jnp.where(filled[:, None], jnp.dot(match_int, picks), -1)
    owner_rows = jnp.repeat(jnp.arange(count, dtype=jnp.int32), OWN_TOP)
    slot_pid = jnp.where(filled, jnp.dot(match_int, owner_rows), -1)
    labels_out = jnp.concatenate([slot_cand, slot_pid[:, None]], 1).reshape(
        n_cls, cap, CAND_OWN + 1
    )
    arrived, labels = (
        lax.all_to_all(outgoing, "cls", split_axis=0, concat_axis=0, tiled=True),
        lax.all_to_all(labels_out, "cls", split_axis=0, concat_axis=0, tiled=True),
    )
    lanes = arrived.reshape(slots, CYCLES, width)
    labels = labels.reshape(slots, CAND_OWN + 1)
    forward, backward = spectral_tables()
    scale = 2.0 / math.sqrt(CYCLES * width)
    norms = jnp.sum(jnp.square(references.astype(jnp.float32)), axis=(1, 2))
    l_re = lanes[..., :HARM]
    l_im = lanes[..., HARM:]
    r_re = references[..., :HARM]
    r_im = references[..., HARM:]
    x_re = jnp.einsum("lrm,crm->lcm", l_re, r_re, preferred_element_type=jnp.float32) + jnp.einsum(
        "lrm,crm->lcm", l_im, r_im, preferred_element_type=jnp.float32
    )
    x_im = jnp.einsum("lrm,crm->lcm", l_im, r_re, preferred_element_type=jnp.float32) - jnp.einsum(
        "lrm,crm->lcm", l_re, r_im, preferred_element_type=jnp.float32
    )
    cross = jnp.concatenate([x_re, x_im], -1)
    corr = jnp.dot(
        cross.reshape(slots * groups, width), forward, precision=lax.Precision.HIGHEST
    ).reshape(slots, groups, ROTS)
    score = (corr - 0.5 * norms[None, :, None]) * scale
    candidate = jnp.any(
        labels[:, :CAND_OWN, None] == jnp.arange(groups, dtype=jnp.int32)[None, None, :], axis=1
    )
    part_max = jnp.max(jnp.where(candidate[:, :, None], score, lowest), axis=(1, 2))
    part_sum = jnp.sum(
        jnp.where(candidate[:, :, None], jnp.exp(score - part_max[:, None, None]), 0.0), axis=(1, 2)
    )
    sender_ids = labels[:, CAND_OWN].astype(jnp.float32)
    table_max, table_sum, table_ids = (
        lax.all_gather(part_max.reshape(1, n_cls, cap), "cls", axis=0, tiled=True),
        lax.all_gather(part_sum.reshape(1, n_cls, cap), "cls", axis=0, tiled=True),
        lax.all_gather(sender_ids.reshape(1, n_cls, cap), "cls", axis=0, tiled=True),
    )
    local_ids = jnp.arange(count, dtype=jnp.float32)
    hit = table_ids[..., None] == local_ids
    top = jnp.max(jnp.where(hit, table_max[..., None], lowest), axis=(0, 2))
    total = jnp.sum(
        jnp.where(
            hit, table_sum[..., None] * jnp.exp(table_max[..., None] - top[None, :, None, :]), 0.0
        ),
        axis=(0, 2),
    )
    table_norm = top + jnp.log(total)
    slot_ids = labels[:, CAND_OWN].reshape(n_cls, cap)
    slot_norm = jnp.sum(
        jnp.where(
            slot_ids[..., None] == jnp.arange(count, dtype=jnp.int32), table_norm[:, None, :], 0.0
        ),
        axis=2,
    ).reshape(slots)
    own_norm = lax.dynamic_index_in_dim(table_norm, lax.axis_index("cls"), 0, keepdims=False)
    weight = jnp.where(candidate[:, :, None], jnp.exp(score - slot_norm[:, None, None]), 0.0)
    mixed = (
        jnp.dot(weight.reshape(slots * groups, ROTS), backward, precision=lax.Precision.HIGHEST)
        .astype(jnp.bfloat16)
        .reshape(slots, groups, width)
    )
    class_weights = lax.psum(jnp.sum(weight, axis=(0, 2)), "prt")
    partial_sums = class_accumulate(lanes, mixed)
    class_sums = lax.psum_scatter(partial_sums, "prt", scatter_dimension=1, tiled=True)
    return (class_sums, class_weights, own_norm)


def solution(mesh):
    in_specs = (
        P(("cls", "prt"), None, None),
        P("cls", None, None),
        P(("cls", "prt"), None),
        P(("cls", "prt"), None, None),
    )
    out_specs = (P("cls", "prt", None), P("cls"), P(("cls", "prt")))
    return jax.shard_map(
        per_device, mesh=mesh, in_specs=in_specs, out_specs=out_specs, check_vma=False
    )
```

profile of v0, /device:TPU:0, one launch (start us, length us, event | category | flops | bytes accessed | tf_op | source)
XLA Modules:
  0.0 770.4 jit_solution(4132569098849755410)
XLA Ops:
  19.3 8.1 %convolution_convert_fusion = bf16[128,65536]{1,0:T(8,128)(2,1)} fusion(pred[128,16]{0,1:T(8,128)(4,1)S(1)} %get-tuple-element.22, bf16[16,65536]{1,0:T(8,128)(2,1)S(1)} %bitcast.63), kind=kOutput, calls=%fused_computation | convolution fusion | flops 276824064 | bytes 18876416 | tf_op jit(solution)/shard_map/dot_general | solution.py:59
  27.4 16.6 %copy.85 = bf16[16,8,128,512]{3,2,1,0:T(8,128)(2,1)} copy(bf16[16,8,128,512]{3,1,2,0:T(8,128)(2,1)} %bitcast.61) | data formatting | bytes 33554432
  76.9 160.8 %all_gather.9 = f32[8,8,16]{2,1,0:T(8,128)} all-gather(f32[1,8,16]{2,1,0:T(8,128)S(1)} %convert_element_type.31), channel_id=1, replica_groups=mesh['cls'=8,'prt'=4] {'cls'}, dimensions={0}, use_global_device_ids=true | all-gather | bytes 4608 | tf_op jit(solution)/shard_map/all_gather | solution.py:106
  238.3 23.6 %copy.71 = bf16[8,16,128,512]{2,1,0,3:T(8,128)(2,1)} copy(bf16[8,16,128,512]{3,2,1,0:T(8,128)(2,1)} %all-to-all-done.1) | data formatting | bytes 33554432 | tf_op jit(solution)/shard_map/all_to_all | solution.py:72
  261.9 13.4 %fusion.39 = f32[256,128,64]{1,2,0:T(8,128)} fusion(bf16[128,128,512]{1,0,2:T(8,128)(2,1)} %bitcast.52, bf16[64,128,256]{1,0,2:T(8,128)(2,1)} %copy.80), kind=kOutput, calls=%fused_computation.66 | convolution fusion | flops 536870912 | bytes 29360128 | tf_op jit(solution)/shard_map/lrm,crm->lcm/dot_general | solution.py:84
  275.3 12.1 %fusion.40 = f32[256,128,64]{1,2,0:T(8,128)} fusion(bf16[128,128,512]{1,0,2:T(8,128)(2,1)} %bitcast.53, bf16[64,128,256]{1,0,2:T(8,128)(2,1)S(1)} %copy-done), kind=kOutput, calls=%fused_computation.67 | convolution fusion | flops 536870912 | bytes 29360128 | tf_op jit(solution)/shard_map/lrm,crm->lcm/dot_general | solution.py:87
  287.4 15.7 %add_bitcast_fusion.1 = f32[128,64,256]{0,1,2:T(8,128)} fusion(f32[256,128,64]{1,2,0:T(8,128)} %fusion.39, bf16[128,128,512]{1,0,2:T(8,128)(2,1)} %bitcast.54, bf16[64,128,256]{1,0,2:T(8,128)(2,1)} %copy.81), kind=kOutput, calls=%fused_computation.10 | convolution fusion | flops 538968064 | bytes 37748736 | tf_op jit(solution)/shard_map/lrm,crm->lcm/dot_general | solution.py:84
  303.1 16.1 %subtract_bitcast_fusion.1 = f32[128,64,256]{0,1,2:T(8,128)} fusion(f32[256,128,64]{1,2,0:T(8,128)} %fusion.40, bf16[128,128,512]{1,0,2:T(8,128)(2,1)} %bitcast.55, bf16[64,128,256]{1,0,2:T(8,128)(2,1)} %copy.81), kind=kOutput, calls=%fused_computation.9 | convolution fusion | flops 538968064 | bytes 37748736 | tf_op jit(solution)/shard_map/lrm,crm->lcm/dot_general | solution.py:87
  319.3 7.2 pad_maximum_fusion
  326.5 19.9 %select_reduce_fusion.1 = (f32[128]{0:T(128)S(1)}, f32[128,64,36]{0,2,1:T(8,128)S(1)}) fusion(pred[128,64]{0,1:T(8,128)(4,1)S(1)} %copy-done.8, f32[64]{0:T(128)S(1)} %copy-done.10, f32[256,36]{0,1:T(8,128)S(1)} %copy-done.4, f32[256,36]{0,1:T(8,128)S(1)} %copy-done.6, f32[128,64,512]{0,1,2:T(8,128)S(1)} %pad_maximum_fusion), kind=kOutput, calls=%fused_computation.23 | convolution fusion | flops 1813137280 | bytes 18039552 | tf_op jit(solution)/shard_map/dot_general | solution.py:91
  347.0 8.1 %all_gather.11 = f32[8,8,16]{2,1,0:T(8,128)S(1)} all-gather(f32[1,8,16]{2,1,0:T(8,128)S(1)} %reshape.107), channel_id=1, replica_groups=mesh['cls'=8,'prt'=4] {'cls'}, dimensions={0}, use_global_device_ids=true | all-gather | bytes 4608 | tf_op jit(solution)/shard_map/all_gather | solution.py:105
  355.1 9.0 %all_gather.10 = f32[8,8,16]{2,1,0:T(8,128)S(1)} all-gather(f32[1,8,16]{2,1,0:T(8,128)S(1)} %reshape.106), channel_id=1, replica_groups=mesh['cls'=8,'prt'=4] {'cls'}, dimensions={0}, use_global_device_ids=true | all-gather | bytes 4608 | tf_op jit(solution)/shard_map/all_gather | solution.py:104
  371.0 15.0 %convolution_convert_fusion.1 = bf16[8192,512]{1,0:T(8,128)(2,1)S(1)} fusion(f32[8192,36]{0,1:T(8,128)} %reshape.108, f32[256,36]{0,1:T(8,128)S(1)} %copy-done.4, f32[256,36]{0,1:T(8,128)S(1)} %copy-done.7), kind=kOutput, calls=%fused_computation.6 | convolution fusion | flops 1816152064 | bytes 9641984 | tf_op jit(solution)/shard_map/dot_general | solution.py:128
  389.6 7.4 copy.83
  397.0 10.2 %fusion.2 = f32[256,64,128]{2,1,0:T(8,128)} fusion(bf16[128,64,256]{0,1,2:T(8,128)(2,1)} %copy.83, bf16[128,128,512]{1,0,2:T(8,128)(2,1)} %bitcast.56), kind=kOutput, calls=%fused_computation.11 | convolution fusion | flops 536870912 | bytes 20971520 | tf_op jit(solution)/shard_map/lrm,lcm->crm/dot_general | solution.py:32
  407.2 7.5 copy.82
  414.7 10.3 %fusion.4 = f32[256,64,128]{2,1,0:T(8,128)} fusion(bf16[128,64,256]{0,1,2:T(8,128)(2,1)} %copy.82, bf16[128,128,512]{1,0,2:T(8,128)(2,1)} %bitcast.57), kind=kOutput, calls=%fused_computation.13 | convolution fusion | flops 536870912 | bytes 20971520 | tf_op jit(solution)/shard_map/lrm,lcm->crm/dot_general | solution.py:35
  425.1 11.4 %subtract_bitcast_fusion = f32[64,128,256]{1,0,2:T(8,128)} fusion(f32[256,64,128]{2,1,0:T(8,128)} %fusion.2, bf16[128,64,256]{0,1,2:T(8,128)(2,1)S(1)} %copy-done.2, bf16[128,128,512]{1,0,2:T(8,128)(2,1)} %bitcast.58), kind=kOutput, calls=%fused_computation.8 | convolution fusion | flops 538968064 | bytes 29360128 | tf_op jit(solution)/shard_map/lrm,lcm->crm/dot_general | solution.py:32
  436.5 11.5 %add_bitcast_fusion = f32[64,128,256]{1,0,2:T(8,128)} fusion(f32[256,64,128]{2,1,0:T(8,128)} %fusion.4, bf16[128,64,256]{0,1,2:T(8,128)(2,1)S(1)} %copy-done.1, bf16[128,128,512]{1,0,2:T(8,128)(2,1)} %bitcast.59), kind=kOutput, calls=%fused_computation.7 | convolution fusion | flops 538968064 | bytes 29360128 | tf_op jit(solution)/shard_map/lrm,lcm->crm/dot_general | solution.py:35
  448.0 10.2 %pad_maximum_fusion.1 = f32[64,128,512]{1,0,2:T(8,128)} fusion(f32[64,128,256]{1,0,2:T(8,128)} %add_bitcast_fusion, f32[64,128,256]{1,0,2:T(8,128)S(1)} %copy-done.3), kind=kLoop, calls=%fused_computation.2 | loop fusion | flops 4194304 | bytes 33554432 | tf_op jit(solution)/shard_map/concatenate | solution.py:38
  458.2 17.5 %copy.78 = f32[64,128,512]{2,0,1:T(8,128)} copy(f32[64,128,512]{1,0,2:T(8,128)} %pad_maximum_fusion.1) | data formatting | bytes 33554432 | tf_op jit(solution)/shard_map/concatenate | solution.py:38
  475.7 12.6 %psum.7 = f32[64]{0:T(128)} all-reduce(f32[64]{0:T(128)S(1)} %get-tuple-element.23), channel_id=1, replica_groups=mesh['cls'=8,'prt'=4] {'prt'}, use_global_device_ids=true, to_apply=%region_13.14 | all-reduce | flops 64 | bytes 512 | tf_op jit(solution)/shard_map/psum | solution.py:132
  488.8 267.7 %reduce-scatter.2.cloned.1.call-done = f32[64,32,512]{2,0,1:T(8,128)} async-done(((f32[64,128,512]{2,0,1:T(8,128)}), f32[64,32,512]{2,0,1:T(8,128)}) %reduce-scatter.2.cloned.1.call-update) | async-done | bytes 4194320 | tf_op jit(solution)/shard_map/reduce_scatter | solution.py:134
  756.4 6.6 copy.79
  (75 shorter events, 57.2 us)
Async XLA Ops:
  11.4 32.6 %all-to-all-start = ((s32[8,16,5]{1,2,0:T(8,128)}), s32[8,16,5]{1,2,0:T(8,128)S(1)}, u32[]{:S(2)}, u32[]{:S(2)}) async-start(s32[8,16,5]{1,2,0:T(8,128)} %pad_add_fusion), calls=%async_computation | async-start | bytes 65536 | tf_op jit(solution)/shard_map/all_to_all | solution.py:73
  44.1 194.2 %all-to-all-start.1 = ((bf16[8,16,128,512]{3,2,1,0:T(8,128)(2,1)}), bf16[8,16,128,512]{3,2,1,0:T(8,128)(2,1)}, u32[]{:S(2)}, u32[]{:S(2)}) async-start(bf16[8,16,128,512]{3,2,1,0:T(8,128)(2,1)} %bitcast.60), calls=%async_computation.1 | async-start | bytes 33554432 | tf_op jit(solution)/shard_map/all_to_all | solution.py:72
  49.8 706.6 %reduce-scatter.2.cloned.1.call-start = ((), (), s32[]{:S(2)}) async-start(), calls=%async_computation.3 | async-start | bytes 20971520 | tf_op jit(solution)/shard_map/reduce_scatter | solution.py:134
  261.9 13.4 %copy-start = (bf16[64,128,256]{1,0,2:T(8,128)(2,1)S(1)}, bf16[64,128,256]{1,0,2:T(8,128)(2,1)}, u32[]{:S(2)}) copy-start(bf16[64,128,256]{1,0,2:T(8,128)(2,1)} %copy.80) | copy-start | bytes 12582916
  319.3 7.2 copy-start.4
  319.3 7.2 copy-start.6
  319.3 7.2 copy-start.8
  319.3 7.2 copy-start.10
  326.5 37.6 %copy-start.5 = (f32[8,8,16]{2,1,0:T(8,128)S(1)}, f32[8,8,16]{2,1,0:T(8,128)}, u32[]{:S(2)}) copy-start(f32[8,8,16]{2,1,0:T(8,128)} %all_gather.9) | copy-start | bytes 12292
  326.5 38.4 %copy-start.9 = (s32[8,16]{1,0:T(8,128)S(1)}, s32[8,16]{1,0:T(8,128)}, u32[]{:S(2)}) copy-start(s32[8,16]{1,0:T(8,128)} %eq.89) | copy-start | bytes 1540
  346.5 24.5 %copy-start.7 = (f32[256,36]{0,1:T(8,128)S(1)}, f32[256,36]{0,1:T(8,128)}, u32[]{:S(2)}) copy-start(f32[256,36]{0,1:T(8,128)} %get-tuple-element.29) | copy-start | bytes 110596
  414.7 10.3 %copy-start.2 = (bf16[128,64,256]{0,1,2:T(8,128)(2,1)S(1)}, bf16[128,64,256]{0,1,2:T(8,128)(2,1)}, u32[]{:S(2)}) copy-start(bf16[128,64,256]{0,1,2:T(8,128)(2,1)} %copy.82) | copy-start | bytes 12582916
  425.1 11.4 %copy-start.1 = (bf16[128,64,256]{0,1,2:T(8,128)(2,1)S(1)}, bf16[128,64,256]{0,1,2:T(8,128)(2,1)}, u32[]{:S(2)}) copy-start(bf16[128,64,256]{0,1,2:T(8,128)(2,1)} %copy.83) | copy-start | bytes 12582916
  436.5 11.5 %copy-start.3 = (f32[64,128,256]{1,0,2:T(8,128)S(1)}, f32[64,128,256]{1,0,2:T(8,128)}, u32[]{:S(2)}) copy-start(f32[64,128,256]{1,0,2:T(8,128)} %subtract_bitcast_fusion) | copy-start | bytes 25165828
Sparse Core Ops, SparseCore 0:
  475.8 280.5 reduce-scatter.1
where the time goes:
time: 780 us; the launch traced here: 770 us
  waiting for transfers between devices  268 us (34%)
  blocking collectives  190 us (24%)
  matrix products  145 us (19%)
  local copies, waits for them, and re-layouts  112 us (14%)
  other arithmetic  29.5 us (4%)
  between operations  14.7 us (2%)
  starting transfers between devices  11 us (1%)
    reduce_scatter x1, waiting for transfers between devices, per_device(): lax.psum_scatter(partial_sums, 'prt', scatter_dimension=1, tiled=True)  268 us
    all_gather x1, blocking collectives, per_device(): lax.all_gather(sender_ids.reshape(1, n_cls, cap), 'cls', axis=0, tiled=True)  161 us
    unnamed x30, local copies, waits for them, and re-layouts  54.8 us
    all_to_all x1, local copies, waits for them, and re-layouts, per_device(): lax.all_to_all(outgoing, 'cls', split_axis=0, concat_axis=0, tiled=True)  23.6 us
    dot_general x1, matrix products, per_device(): jnp.dot(cross.reshape(slots * groups, width), forward, precision=lax.Prec...  19.9 us
    concatenate x1, local copies, waits for them, and re-layouts, class_accumulate(): return jnp.concatenate([s_re, s_im], -1)  17.5 us
    dot_general x1, matrix products, per_device(): jnp.einsum('lrm,crm->lcm', l_re, r_im, preferred_element_type=jnp.float32)  16.1 us
    dot_general x1, matrix products, per_device(): jnp.einsum('lrm,crm->lcm', l_im, r_im, preferred_element_type=jnp.float32)  15.7 us
  transfers between devices with their start and end apart: 3, of which 1 were waited for; matrix products, arithmetic and copies ran while one was open for 7% of the time, Pallas kernels for 0%

commit v1 on v0

--- a/solution.py
+++ b/solution.py
@@ -1,8 +1,12 @@
+import functools
 import math
 
 import jax
 import jax.numpy as jnp
+import numpy as np
 from jax import lax
+from jax.experimental import pallas as pl
+from jax.experimental.pallas import tpu as pltpu
 from jax.sharding import PartitionSpec as P
 
 CYCLES = 128
@@ -38,7 +42,7 @@
     return jnp.concatenate([s_re, s_im], -1)
 
 
-def per_device(particles, references, owner_groups, class_order):
+def dispatch_device(particles, references, owner_groups, class_order):
     n_cls = lax.axis_size("cls")
     count = particles.shape[0]
     groups = references.shape[0]
@@ -135,6 +139,520 @@
     return (class_sums, class_weights, own_norm)
 
 
+LANES = 128
+
+
+def harmonic_plan():
+    half = ROTS // 2
+    turns = HARM // ROTS
+    tail = HARM - turns * ROTS
+    chunk_of = np.zeros(HARM, np.int32)
+    side_of = np.zeros(HARM, np.int32)
+    for m in range(HARM):
+        turn, rest = divmod(m, ROTS)
+        if turn == turns:
+            chunk_of[m] = half * turns + rest // 2
+            side_of[m] = rest % 2
+        elif rest < half:
+            chunk_of[m] = rest * turns + turn
+        else:
+            chunk_of[m] = ((ROTS - rest) % half) * turns + turn
+            side_of[m] = 1
+    return half, turns, tail, chunk_of, side_of
+
+
+HALF, TURNS, TAIL, CHUNK_OF, SIDE_OF = harmonic_plan()
+BODY = HALF * TURNS
+CHUNKS = BODY + TAIL // 2
+EXTRA = TAIL // 2 + 1
+COEF = 2 * HALF * CAND_OWN
+
+
+def selector():
+    return (np.arange(CHUNKS)[:, None] == CHUNK_OF[None, :]).astype(np.float32)
+
+
+def side_masks():
+    return np.stack([SIDE_OF == 0, SIDE_OF == 1]).astype(np.float32)
+
+
+def unselector():
+    sel = selector()
+    return np.concatenate([sel * (SIDE_OF == 0), sel * (SIDE_OF == 1)], 0)
+
+
+def rotation_table():
+    table = np.zeros((HALF, 2, CAND_OWN, ROTS, CAND_OWN))
+    angle = 2.0 * np.pi * np.arange(ROTS) / ROTS
+    for g in range(HALF):
+        first = np.cos(g * angle)
+        second = np.cos(HALF * angle) if g == 0 else np.sin(g * angle)
+        for q in range(CAND_OWN):
+            table[g, 0, q, :, q] = first
+            table[g, 1, q, :, q] = second
+    return table.reshape(COEF, ROTS * CAND_OWN).astype(np.float32)
+
+
+def nt_dot(a, b):
+    return lax.dot_general(a, b, (((1,), (1,)), ((), ())), preferred_element_type=jnp.float32)
+
+
+def masked_stack(piece, masks):
+    parts = []
+    for s in range(2):
+        for b in range(2):
+            parts.append(piece[:, s * HARM : (s + 1) * HARM] * masks[b : b + 1])
+    return jnp.concatenate(parts, 0)
+
+
+def particle_body(x_ref, owner_ref, pick_ref, sel_ref, mask_ref, out_ref, scr):
+    count, cycles, _ = x_ref.shape
+    n_prt = out_ref.shape[0]
+    span = cycles // n_prt
+    masks = mask_ref[...]
+
+    def one(n, carry):
+        x = x_ref[n]
+        w = jnp.concatenate(
+            [masked_stack(x[p * span : (p + 1) * span], masks) for p in range(n_prt)], 0
+        )
+        y = nt_dot(sel_ref[...], w)
+        for p in range(n_prt):
+            scr[p, pl.ds(pl.multiple_of(n * CHUNKS, CHUNKS), CHUNKS), :] = y[
+                :, p * LANES : (p + 1) * LANES
+            ]
+        return carry
+
+    lax.fori_loop(0, count, one, 0)
+
+    def two(c, carry):
+        for p in range(n_prt):
+            out_ref[p, c] = scr[p, pl.ds(c, count, stride=CHUNKS), :].astype(jnp.bfloat16)
+        return carry
+
+    lax.fori_loop(0, CHUNKS, two, 0)
+    lane = lax.broadcasted_iota(jnp.int32, (count, LANES), 1)
+    label = jnp.full((count, LANES), -1, jnp.int32)
+    for t in range(OWN_TOP):
+        mine = (lane // CAND_OWN) == owner_ref[:, t : t + 1]
+        for q in range(CAND_OWN):
+            at = t * CAND_OWN + q
+            label = jnp.where(
+                mine & (lane % CAND_OWN == q), pick_ref[:, at : at + 1], label
+            )
+    label = label.astype(jnp.float32).astype(jnp.bfloat16)
+    for p in range(n_prt):
+        out_ref[p, CHUNKS] = label
+
+
+def arrange_particles(particles, owner, picks, n_prt, sel, masks):
+    count = particles.shape[0]
+    return pl.pallas_call(
+        particle_body,
+        out_shape=jax.ShapeDtypeStruct((n_prt, CHUNKS + 1, count, LANES), jnp.bfloat16),
+        scratch_shapes=[pltpu.VMEM((n_prt, count * CHUNKS, LANES), jnp.float32)],
+        compiler_params=pltpu.CompilerParams(vmem_limit_bytes=32 << 20),
+        cost_estimate=pl.CostEstimate(
+            flops=particles.size * 2 * CHUNKS, bytes_accessed=particles.size * 4, transcendentals=0
+        ),
+        name="arrange_particles",
+    )(particles, owner, picks, sel, masks)
+
+
+def reference_body(at_ref, x_ref, sel_ref, mask_ref, out_ref, scr):
+    rows = x_ref.shape[0]
+    masks = mask_ref[...]
+    step = 4
+
+    def one(n, carry):
+        w = jnp.concatenate([masked_stack(x_ref[n * step + i], masks) for i in range(step)], 0)
+        y = nt_dot(sel_ref[...], w)
+        for i in range(step):
+            scr[pl.ds(pl.multiple_of((n * step + i) * CHUNKS, CHUNKS), CHUNKS), :] = y[
+                :, i * LANES : (i + 1) * LANES
+            ]
+        return carry
+
+    lax.fori_loop(0, rows // step, one, 0)
+
+    def two(c, carry):
+        out_ref[c] = scr[pl.ds(c, rows, stride=CHUNKS), :].astype(jnp.bfloat16)
+        return carry
+
+    lax.fori_loop(0, CHUNKS, two, 0)
+
+
+def arrange_references(references, prt, n_prt, sel, masks):
+    groups, cycles, width = references.shape
+    span = cycles // n_prt
+    block = 16
+    return pl.pallas_call(
+        reference_body,
+        grid_spec=pltpu.PrefetchScalarGridSpec(
+            num_scalar_prefetch=1,
+            grid=(groups // block,),
+            in_specs=[
+                pl.BlockSpec((block, span, width), lambda i, at: (i, at[0], 0)),
+                pl.BlockSpec(sel.shape, lambda i, at: (0, 0)),
+                pl.BlockSpec(masks.shape, lambda i, at: (0, 0)),
+            ],
+            out_specs=pl.BlockSpec((CHUNKS, block, LANES), lambda i, at: (0, i, 0)),
+            scratch_shapes=[pltpu.VMEM((block * CHUNKS, LANES), jnp.float32)],
+        ),
+        out_shape=jax.ShapeDtypeStruct((CHUNKS, groups, LANES), jnp.bfloat16),
+        compiler_params=pltpu.CompilerParams(vmem_limit_bytes=32 << 20),
+        cost_estimate=pl.CostEstimate(
+            flops=groups * span * width * 2 * CHUNKS,
+            bytes_accessed=groups * span * width * 4,
+            transcendentals=0,
+        ),
+        name="arrange_references",
+    )(prt, references, sel, masks)
+
+
+def lane_signs():
+    lane = lax.broadcasted_iota(jnp.int32, (1, LANES), 1)
+    quarter = LANES // 4
+    imag = lane >= 2 * quarter
+    odd = (lane // quarter) % 2 == 1
+    return imag, odd
+
+
+def lanes_of(ref, first, number):
+    parts = []
+    for i in range(first, first + number):
+        part = ref[:, i]
+        parts.append(part.reshape(part.shape[0] * part.shape[1], LANES))
+    return jnp.concatenate(parts, 1) if number > 1 else parts[0]
+
+
+def hot_masks(cand, groups):
+    rows = lax.broadcasted_iota(jnp.int32, (groups, cand.shape[1]), 0).astype(jnp.float32)
+    return [rows == cand[q : q + 1] for q in range(CAND_OWN)]
+
+
+def cross_body(at_ref, p_ref, pt_ref, q_ref, qt_ref, coef_ref, cand_ref, acc, norm):
+    g = pl.program_id(0)
+    groups = q_ref.shape[1]
+    imag, odd = lane_signs()
+    quarter = LANES // 4
+    sign = jnp.where(imag == odd, -1.0, 1.0)
+
+    @pl.when(g == 0)
+    def _():
+        label = lanes_of(pt_ref, TAIL // 2, 1).astype(jnp.float32).T
+        row = lax.broadcasted_iota(jnp.int32, label.shape, 0)
+        base = at_ref[0] * CAND_OWN
+        for q in range(CAND_OWN):
+            cand_ref[q : q + 1, :] = jnp.sum(
+                jnp.where(row == base + q, label, 0.0), axis=0, keepdims=True
+            )
+        cand_ref[CAND_OWN:, :] = jnp.full(
+            (cand_ref.shape[0] - CAND_OWN, cand_ref.shape[1]), -1.0, jnp.float32
+        )
+        total = jnp.zeros((groups, LANES), jnp.float32)
+        for i in range(TAIL // 2):
+            total += jnp.square(qt_ref[i].astype(jnp.float32))
+        norm[...] = total
+
+    first, second = [], []
+    total = norm[...]
+    for i in range(TURNS):
+        q = q_ref[i].astype(jnp.float32)
+        total += jnp.square(q)
+        turned = pltpu.roll(q, LANES // 2, 1) * sign
+        first.append(jnp.where((g == 0) & odd, 0.0, q))
+        second.append(jnp.where(g == 0, jnp.where(odd, q, 0.0), turned))
+    norm[...] = total
+    weights = jnp.concatenate(
+        [jnp.concatenate(first, 1), jnp.concatenate(second, 1)], 0
+    ).astype(jnp.bfloat16)
+    acc[...] = nt_dot(weights, lanes_of(p_ref, 0, TURNS))
+
+    for i in range(TAIL):
+
+        @pl.when(g == i)
+        def _():
+            q = qt_ref[i // 2].astype(jnp.float32)
+            keep = odd if i % 2 else ~odd
+            a = jnp.where(keep, q, 0.0)
+            b = jnp.where(keep, pltpu.roll(q, LANES // 2, 1) * jnp.where(imag, 1.0, -1.0), 0.0)
+            if i == 0:
+                b = jnp.zeros_like(b)
+            w = jnp.concatenate([a, b], 0).astype(jnp.bfloat16)
+            acc[...] += nt_dot(w, lanes_of(pt_ref, i // 2, 1))
+
+    hot = hot_masks(cand_ref[...], groups)
+    rows = []
+    for ab in range(2):
+        part = acc[ab * groups : (ab + 1) * groups, :]
+        for q in range(CAND_OWN):
+            rows.append(jnp.sum(jnp.where(hot[q], part, 0.0), axis=0, keepdims=True))
+    block = 2 * CAND_OWN
+    coef_ref[pl.ds(pl.multiple_of(g * block, block), block), :] = jnp.concatenate(rows, 0)
+
+    @pl.when(g == HALF - 1)
+    def _():
+        half_norm = 0.5 * jnp.sum(norm[...], axis=1, keepdims=True)
+        for q in range(CAND_OWN):
+            coef_ref[q : q + 1, :] -= jnp.sum(
+                jnp.where(hot[q], half_norm, 0.0), axis=0, keepdims=True
+            )
+
+
+def cross_coefficients(gathered, arranged, cls):
+    sources, _, count, _ = gathered.shape
+    groups = arranged.shape[1]
+    total = sources * count
+    half_tail = TAIL // 2
+    return pl.pallas_call(
+        cross_body,
+        grid_spec=pltpu.PrefetchScalarGridSpec(
+            num_scalar_prefetch=1,
+            grid=(HALF,),
+            in_specs=[
+                pl.BlockSpec((sources, TURNS, count, LANES), lambda g, at: (0, g, 0, 0)),
+                pl.BlockSpec(
+                    (sources, EXTRA, count, LANES), lambda g, at: (0, BODY // EXTRA, 0, 0)
+                ),
+                pl.BlockSpec((TURNS, groups, LANES), lambda g, at: (g, 0, 0)),
+                pl.BlockSpec((half_tail, groups, LANES), lambda g, at: (BODY // half_tail, 0, 0)),
+            ],
+            out_specs=[
+                pl.BlockSpec((COEF, total), lambda g, at: (0, 0)),
+                pl.BlockSpec((2 * CAND_OWN, total), lambda g, at: (0, 0)),
+            ],
+            scratch_shapes=[
+                pltpu.VMEM((2 * groups, total), jnp.float32),
+                pltpu.VMEM((groups, LANES), jnp.float32),
+            ],
+        ),
+        out_shape=[
+            jax.ShapeDtypeStruct((COEF, total), jnp.float32),
+            jax.ShapeDtypeStruct((2 * CAND_OWN, total), jnp.float32),
+        ],
+        compiler_params=pltpu.CompilerParams(vmem_limit_bytes=48 << 20),
+        cost_estimate=pl.CostEstimate(
+            flops=4 * gathered.size * groups, bytes_accessed=2 * gathered.size, transcendentals=0
+        ),
+        name="cross_coefficients",
+    )(cls, gathered, gathered, arranged, arranged)
+
+
+def score_body(coef_ref, cand_ref, table_ref, score_ref, stat_ref, *, scale):
+    corr = lax.dot_general(
+        table_ref[...],
+        coef_ref[...],
+        (((0,), (0,)), ((), ())),
+        precision=lax.Precision.HIGHEST,
+        preferred_element_type=jnp.float32,
+    )
+    score = jnp.where(cand_ref[0:1, :] >= 0.0, corr * scale, lowest)
+    top = jnp.max(score, axis=0, keepdims=True)
+    total = jnp.sum(jnp.exp(score - top), axis=0, keepdims=True)
+    score_ref[...] = score
+    stat_ref[0:1, :] = top
+    stat_ref[1:2, :] = jnp.where(cand_ref[0:1, :] >= 0.0, total, 0.0)
+
+
+def scores(coef, cand, table, scale):
+    total = coef.shape[1]
+    return pl.pallas_call(
+        functools.partial(score_body, scale=scale),
+        out_shape=[
+            jax.ShapeDtypeStruct((ROTS * CAND_OWN, total), jnp.float32),
+            jax.ShapeDtypeStruct((2, total), jnp.float32),
+        ],
+        name="scores",
+    )(coef, cand, table)
+
+
+def sums_body(
+    p_ref, pt_ref, score_ref, cand_ref, stat_ref, table_ref, back_ref,
+    out_ref, weight_ref, norm_ref, mix, planes,
+):
+    i = pl.program_id(0)
+    groups = weight_ref.shape[0]
+    total = score_ref.shape[1]
+    imag, odd = lane_signs()
+
+    @pl.when(i == 0)
+    def _():
+        tops = [stat_ref[2 * j : 2 * j + 1, :] for j in range(stat_ref.shape[0] // 2)]
+        top = functools.reduce(jnp.maximum, tops)
+        summed = jnp.zeros_like(top)
+        for j, other in enumerate(tops):
+            summed += stat_ref[2 * j + 1 : 2 * j + 2, :] * jnp.exp(other - top)
+        log_norm = top + jnp.log(summed)
+        norm_ref[...] = log_norm
+        weight = jnp.where(
+            cand_ref[0:1, :] >= 0.0, jnp.exp(score_ref[...] - log_norm), 0.0
+        )
+        mixed = lax.dot_general(
+            table_ref[...],
+            weight,
+            (((1,), (0,)), ((), ())),
+            precision=lax.Precision.HIGHEST,
+            preferred_element_type=jnp.float32,
+        )
+        hot = hot_masks(cand_ref[...], groups)
+        summed = jnp.zeros((groups, total), jnp.float32)
+        for q in range(CAND_OWN):
+            summed += jnp.where(hot[q], mixed[q : q + 1], 0.0)
+        weight_ref[...] = jnp.sum(summed, axis=1, keepdims=True)
+        mix[...] = mixed
+
+    @pl.when(i < HALF)
+    def _():
+        hot = hot_masks(cand_ref[...], groups)
+        block = 2 * CAND_OWN
+        mine = mix[pl.ds(pl.multiple_of(i * block, block), block), :]
+        halves = []
+        for ab in range(2):
+            dense = jnp.zeros((groups, total), jnp.float32)
+            for q in range(CAND_OWN):
+                at = ab * CAND_OWN + q
+                dense = jnp.where(hot[q], mine[at : at + 1], dense)
+            halves.append(dense)
+        weights = jnp.concatenate(halves, 0).astype(jnp.bfloat16)
+        made = jnp.dot(
+            weights, lanes_of(p_ref, 0, TURNS), preferred_element_type=jnp.float32
+        )
+        sign = jnp.where(imag == odd, 1.0, -1.0)
+        for t in range(TURNS):
+            g1 = made[:groups, t * LANES : (t + 1) * LANES]
+            g2 = made[groups:, t * LANES : (t + 1) * LANES]
+            value = jnp.where(
+                i == 0, jnp.where(odd, g2, g1), g1 + sign * pltpu.roll(g2, LANES // 2, 1)
+            )
+            start = pl.multiple_of((i * TURNS + t) * groups, groups)
+            planes[pl.ds(start, groups), :] = value
+
+        for t in range(TAIL):
+
+            @pl.when(i == t)
+            def _():
+                made = jnp.dot(
+                    weights, lanes_of(pt_ref, t // 2, 1), preferred_element_type=jnp.float32
+                )
+                g1, g2 = made[:groups], made[groups:]
+                value = g1
+                if t > 0:
+                    value = g1 + jnp.where(imag, -1.0, 1.0) * pltpu.roll(g2, LANES // 2, 1)
+                rows = pl.ds((BODY + t // 2) * groups, groups)
+                if t % 2:
+                    value = jnp.where(odd, value, planes[rows, :])
+                planes[rows, :] = value
+
+    @pl.when(i >= HALF)
+    def _():
+        block, span, _ = out_ref.shape
+        first = (i - HALF) * block
+        back = back_ref[...]
+        for c in range(block):
+            turned = planes[pl.ds(first + c, CHUNKS, stride=groups), :].T
+            parts = []
+            for s in range(2):
+                at = 2 * s * span
+                parts.append(
+                    jnp.concatenate([turned[at : at + span], turned[at + span : at + 2 * span]], 1)
+                )
+            value = jnp.concatenate(parts, 0)
+            high = value.astype(jnp.bfloat16)
+            low = (value - high.astype(jnp.float32)).astype(jnp.bfloat16)
+            placed = jnp.dot(high, back, preferred_element_type=jnp.float32) + jnp.dot(
+                low, back, preferred_element_type=jnp.float32
+            )
+            out_ref[c, :, :HARM] = placed[:span]
+            out_ref[c, :, HARM:] = placed[span:]
+
+
+def sums(gathered, score, cand, stats, table, back, groups, span):
+    sources, _, count, _ = gathered.shape
+    total = sources * count
+    block = 8
+    whole = lambda i: (0, 0)
+    return pl.pallas_call(
+        sums_body,
+        grid=(HALF + groups // block,),
+        in_specs=[
+            pl.BlockSpec(
+                (sources, TURNS, count, LANES), lambda i: (0, jnp.minimum(i, HALF - 1), 0, 0)
+            ),
+            pl.BlockSpec((sources, EXTRA, count, LANES), lambda i: (0, BODY // EXTRA, 0, 0)),
+            pl.BlockSpec(score.shape, whole),
+            pl.BlockSpec(cand.shape, whole),
+            pl.BlockSpec(stats.shape, whole),
+            pl.BlockSpec(table.shape, whole),
+            pl.BlockSpec(back.shape, whole),
+        ],
+        out_specs=[
+            pl.BlockSpec(
+                (block, span, 2 * HARM), lambda i: (jnp.maximum(i - HALF, 0), 0, 0)
+            ),
+            pl.BlockSpec((groups, 1), whole),
+            pl.BlockSpec((1, total), whole),
+        ],
+        out_shape=[
+            jax.ShapeDtypeStruct((groups, span, 2 * HARM), jnp.float32),
+            jax.ShapeDtypeStruct((groups, 1), jnp.float32),
+            jax.ShapeDtypeStruct((1, total), jnp.float32),
+        ],
+        scratch_shapes=[
+            pltpu.VMEM((COEF, total), jnp.float32),
+            pltpu.VMEM((CHUNKS * groups, LANES), jnp.float32),
+        ],
+        compiler_params=pltpu.CompilerParams(vmem_limit_bytes=48 << 20),
+        cost_estimate=pl.CostEstimate(
+            flops=4 * gathered.size * groups,
+            bytes_accessed=2 * gathered.size + 8 * groups * span * HARM,
+            transcendentals=0,
+        ),
+        name="sums",
+    )(gathered, gathered, score, cand, stats, table, back)
+
+
+def spread(outgoing):
+    arrived = lax.all_to_all(outgoing, "prt", split_axis=0, concat_axis=0, tiled=True)
+    return lax.all_gather(arrived, "cls", axis=0, tiled=True)
+
+
+def gather_device(particles, references, owner_groups, class_order):
+    n_cls, n_prt = lax.axis_size("cls"), lax.axis_size("prt")
+    cls, prt = lax.axis_index("cls"), lax.axis_index("prt")
+    count, cycles, width = particles.shape
+    groups = references.shape[0]
+    span = cycles // n_prt
+    sel = jnp.asarray(selector(), jnp.bfloat16)
+    masks = jnp.asarray(side_masks(), jnp.bfloat16)
+    back = jnp.asarray(unselector(), jnp.bfloat16)
+    table = jnp.asarray(rotation_table())
+    picks = class_order[:, :, :CAND_OWN].reshape(count, OWN_TOP * CAND_OWN)
+    outgoing = arrange_particles(particles, owner_groups, picks, n_prt, sel, masks)
+    gathered = spread(outgoing)
+    arranged = arrange_references(references, prt.reshape(1).astype(jnp.int32), n_prt, sel, masks)
+    coef, cand = cross_coefficients(gathered, arranged, cls.reshape(1).astype(jnp.int32))
+    coef = lax.psum(coef, "prt")
+    scale = 2.0 / math.sqrt(cycles * width)
+    score, stat = scores(coef, cand, table, scale)
+    stats = lax.all_gather(stat, "cls", axis=0, tiled=True)
+    class_sums, class_weights, log_norm = sums(
+        gathered, score, cand, stats, table, back, groups, span
+    )
+    own = lax.dynamic_slice(log_norm[0], ((cls * n_prt + prt) * count,), (count,))
+    return class_sums, class_weights[:, 0], own
+
+
+def per_device(particles, references, owner_groups, class_order):
+    n_cls, n_prt = lax.axis_size("cls"), lax.axis_size("prt")
+    count, cycles, _ = particles.shape
+    groups = references.shape[0]
+    cap = max(2, 2 * count * OWN_TOP // n_cls)
+    fits = 4 * cycles == LANES * n_prt and n_cls * CAND_OWN <= LANES and groups % 16 == 0
+    plan = gather_device if cap >= count and fits else dispatch_device
+    return plan(particles, references, owner_groups, class_order)
+
+
 def solution(mesh):
     in_specs = (
         P(("cls", "prt"), None, None),

time: 780 us -> 267 us (0.34); the launches traced: 770 us -> 266 us
  waiting for transfers between devices: 268 us -> 110 us
  matrix products: 145 us -> 0 us
  blocking collectives: 190 us -> 63.9 us
  local copies, waits for them, and re-layouts: 112 us -> 11.8 us
  Pallas kernels: 0 us -> 64.9 us
  other arithmetic: 29.5 us -> 0.63 us
  starting transfers between devices: 11 us -> 0.08 us
    reduce_scatter x1 -> x0, waiting for transfers between devices: 268 us -> none  [per_device(): lax.psum_scatter(partial_sums, 'prt', scatter_dimension=1, tiled=True)]
    all_gather x3 -> x1, blocking collectives: 178 us -> 9.13 us  [gather_device(): stats = lax.all_gather(stat, 'cls', axis=0, tiled=True)]
    dot_general x13 -> x0, matrix products: 145 us -> none  [the longest x1 19.9 us: per_device(): jnp.dot(cross.reshape(slots * groups, width), forward, precision=lax.Prec...]
    all_gather x0 -> x1, waiting for transfers between devices: none -> 74.4 us  [spread(): return lax.all_gather(arrived, 'cls', axis=0, tiled=True)]
    pallas_call x0 -> x5, Pallas kernels: none -> 64.9 us  [the longest x1 23.5 us: sums(): pl.pallas_call(sums_body, grid=(HALF + groups // block,), in_specs=[pl.Bl...]
    all_to_all x0 -> x1, blocking collectives: none -> 54.8 us  [spread(): lax.all_to_all(outgoing, 'prt', split_axis=0, concat_axis=0, tiled=True)]
    unnamed x30 -> x24, local copies, waits for them, and re-layouts: 54.8 us -> 10.3 us
    psum x0 -> x1, waiting for transfers between devices: none -> 35.9 us  [gather_device(): coef = lax.psum(coef, 'prt')]
  transfers between devices with their start and end apart: 3 -> 2, of which waited for: 1 -> 2; matrix products, arithmetic and copies ran while one was open for 7% -> 0% of each run, Pallas kernels for 0% -> 4%
where the time goes in v1:
time: 267 us; the launch traced here: 266 us
  waiting for transfers between devices  110 us (41%)
  Pallas kernels  64.9 us (24%)
  blocking collectives  63.9 us (24%)
  between operations  14.1 us (5%)
  local copies, waits for them, and re-layouts  11.8 us (4%)
    all_gather x1, waiting for transfers between devices, spread(): return lax.all_gather(arrived, 'cls', axis=0, tiled=True)  74.4 us
    all_to_all x1, blocking collectives, spread(): lax.all_to_all(outgoing, 'prt', split_axis=0, concat_axis=0, tiled=True)  54.8 us
    psum x1, waiting for transfers between devices, gather_device(): coef = lax.psum(coef, 'prt')  35.9 us
    pallas_call x1, Pallas kernels, sums(): pl.pallas_call(sums_body, grid=(HALF + groups // block,), in_specs=[pl.Bl...  23.5 us
    pallas_call x1, Pallas kernels, cross_coefficients(): pl.pallas_call(cross_body, grid_spec=pltpu.PrefetchScalarGridSpec(num_sca...  19.2 us
    pallas_call x1, Pallas kernels, arrange_references(): pl.pallas_call(reference_body, grid_spec=pltpu.PrefetchScalarGridSpec(num...  11.2 us
    unnamed x24, local copies, waits for them, and re-layouts  10.3 us
    all_gather x1, blocking collectives, gather_device(): stats = lax.all_gather(stat, 'cls', axis=0, tiled=True)  9.13 us
  transfers between devices with their start and end apart: 2, of which 2 were waited for; matrix products, arithmetic and copies ran while one was open for 0% of the time, Pallas kernels for 4%

profile of v1, /device:TPU:0, one launch (start us, length us, event | category | flops | bytes accessed | tf_op | source)
XLA Modules:
  0.0 265.7 jit_solution(13956131482891520069)
XLA Ops:
  7.2 0.0 all-gather.3.cloned.1.call-start
  7.2 0.8 copy.16.owner_ref
  8.0 0.9 copy.15
  8.8 0.1 copy.17.pick_ref
  8.9 1.6 copy-done.1
  10.5 0.8 copy-done.4
  11.3 0.7 copy-done.9
  12.0 8.8 %arrange_particles.1 = bf16[4,129,16,128]{3,2,1,0:T(8,128)(2,1)S(1)} custom-call(bf16[16,128,512]{2,1,0:T(8,128)(2,1)S(1)} %copy-done.1, s32[16,4]{1,0:T(8,128)S(1)} %copy.16.owner_ref, s32[16,16]{1,0:T(8,128)S(1)} %copy.17.pick_ref, bf16[128,256]{1,0:T(8,128)(2,1)S(1)} %copy-done.4, bf16[2,256]{1,0:T(2,128)(2,1)S(1)} %copy-done.9), custom_call_target="tpu_custom_call" | custom-call | flops 268435456 | bytes 4194304 | tf_op jit(solution)/shard_map/arrange_particles/pallas_call | solution.py:250
  20.8 54.8 %all_to_all.5 = bf16[4,129,16,128]{3,2,1,0:T(8,128)(2,1)} all-to-all(bf16[4,129,16,128]{3,2,1,0:T(8,128)(2,1)S(1)} %arrange_particles.1), channel_id=1, replica_groups=mesh['cls'=8,'prt'=4] {'prt'}, dimensions={0} | all-to-all | bytes 4227072 | tf_op jit(solution)/shard_map/all_to_all | solution.py:616
  75.6 0.0 all-reduce.2.cloned.1.call-start
  75.7 0.8 copy-done.5
  76.4 3.4 %copy-done = bf16[64,128,512]{2,1,0:T(8,128)(2,1)S(1)} copy-done((bf16[64,128,512]{2,1,0:T(8,128)(2,1)S(1)}, bf16[64,128,512]{2,1,0:T(8,128)(2,1)}, u32[]{:S(2)}) %copy-start) | copy-done | bytes 8388632
  79.8 11.2 %arrange_references.1.q_ref.qt_ref = bf16[128,64,128]{2,1,0:T(8,128)(2,1)S(1)} custom-call(s32[1]{0:T(128)} %bitcast.2.at_ref, bf16[64,128,512]{2,1,0:T(8,128)(2,1)S(1)} %copy-done, bf16[128,256]{1,0:T(8,128)(2,1)S(1)} %copy-done.5, bf16[2,256]{1,0:T(2,128)(2,1)S(1)} %copy-done.10), custom_call_target="tpu_custom_call" | custom-call | flops 268435456 | bytes 4194304 | tf_op jit(solution)/shard_map/arrange_references/pallas_call | solution.py:289
  91.0 74.4 %all-gather.3.cloned.1.call-done.p_ref.pt_ref = bf16[32,129,16,128]{3,2,1,0:T(8,128)(2,1)} async-done(((bf16[4,129,16,128]{3,2,1,0:T(8,128)(2,1)}), bf16[32,129,16,128]{3,2,1,0:T(8,128)(2,1)}) %all-gather.3.cloned.1.call-update) | async-done | bytes 16908304 | tf_op jit(solution)/shard_map/all_gather | solution.py:617
  165.5 19.2 %cross_coefficients.1 = (f32[144,512]{1,0:T(8,128)}, f32[8,512]{1,0:T(8,128)S(1)}) custom-call(s32[1]{0:T(128)} %bitcast.1.at_ref, bf16[32,129,16,128]{3,2,1,0:T(8,128)(2,1)} %all-gather.3.cloned.1.call-done.p_ref.pt_ref, bf16[32,129,16,128]{3,2,1,0:T(8,128)(2,1)} %all-gather.3.cloned.1.call-done.p_ref.pt_ref, ...), custom_call_target="tpu_custom_call" | custom-call | flops 2164260864 | bytes 16908288 | tf_op jit(solution)/shard_map/cross_coefficients/pallas_call | solution.py:408
  184.6 0.6 copy-done.7
  185.3 35.9 %all-reduce.2.cloned.1.call-done.coef_ref = f32[144,512]{1,0:T(8,128)} async-done(((f32[144,512]{1,0:T(8,128)}), f32[144,512]{1,0:T(8,128)}) %all-reduce.2.cloned.1.call-update) | async-done | bytes 294928 | tf_op jit(solution)/shard_map/psum | solution.py:635
  221.2 2.2 scores.1
  223.3 9.1 %all-gather = f32[8,2,512]{2,1,0:T(2,128)S(1)} all-gather(f32[1,2,512]{2,1,0:T(2,128)} %bitcast.9), channel_id=1, replica_groups=mesh['cls'=8,'prt'=4] {'cls'}, dimensions={0}, use_global_device_ids=true | all-gather | bytes 36864 | tf_op jit(solution)/shard_map/all_gather | solution.py:638
  232.5 1.0 copy-done.3
  233.5 0.7 copy-done.8
  234.2 23.5 %sums.1 = (f32[64,32,512]{2,1,0:T(8,128)}, f32[64,1]{1,0:T(8,128)S(1)}, f32[1,512]{1,0:T(1,128)S(1)}) custom-call(bf16[32,129,16,128]{3,2,1,0:T(8,128)(2,1)} %all-gather.3.cloned.1.call-done.p_ref.pt_ref, bf16[32,129,16,128]{3,2,1,0:T(8,128)(2,1)} %all-gather.3.cloned.1.call-done.p_ref.pt_ref, f32[144,512]{1,0:T(8,128)S(1)} %copy-done.3, ...), custom_call_target="tpu_custom_call" | custom-call | flops 2164260864 | bytes 21102592 | tf_op jit(solution)/shard_map/sums/pallas_call | solution.py:575
  257.7 0.6 dynamic-slice_bitcast_fusion
  258.3 0.6 reduce
  (17 shorter events, 0.1 us)
Async XLA Ops:
  7.2 158.3 %all-gather.3.cloned.1.call-start = ((), (), s32[]{:S(2)}) async-start(), calls=%async_computation.1 | async-start | bytes 19021824 | tf_op jit(solution)/shard_map/all_gather | solution.py:617
  8.9 1.6 copy-start.1
  10.5 0.8 copy-start.4
  11.3 0.7 copy-start.9
  75.6 0.8 copy-start.5
  75.6 0.8 copy-start.10
  75.6 145.5 %all-reduce.2.cloned.1.call-start = ((), (), s32[]{:S(2)}) async-start(), calls=%async_computation.2 | async-start | bytes 589824 | tf_op jit(solution)/shard_map/psum | solution.py:635
  76.4 3.4 %copy-start = (bf16[64,128,512]{2,1,0:T(8,128)(2,1)S(1)}, bf16[64,128,512]{2,1,0:T(8,128)(2,1)}, u32[]{:S(2)}) copy-start(bf16[64,128,512]{2,1,0:T(8,128)(2,1)} %x_ref.3) | copy-start | bytes 25165828
  165.5 67.0 %copy-start.2 = (f32[144,144]{1,0:T(8,128)S(1)}, f32[144,144]{1,0:T(8,128)}, u32[]{:S(2)}) copy-start(f32[144,144]{1,0:T(8,128)} %constant.29.clone.table_ref) | copy-start | bytes 248836
  165.5 67.1 %copy-start.6 = (bf16[256,256]{1,0:T(8,128)(2,1)S(1)}, bf16[256,256]{1,0:T(8,128)(2,1)}, u32[]{:S(2)}) copy-start(bf16[256,256]{1,0:T(8,128)(2,1)} %constant.28.clone.back_ref) | copy-start | bytes 393220
  184.6 0.6 copy-start.7
  232.5 1.0 copy-start.3
  233.5 0.7 copy-start.8
Sparse Core Ops, SparseCore 0:
  75.7 89.6 all-gather.2
  185.4 35.7 all-reduce.1

commit v2 on v1

--- a/solution.py
+++ b/solution.py
@@ -166,6 +166,15 @@
 CHUNKS = BODY + TAIL // 2
 EXTRA = TAIL // 2 + 1
 COEF = 2 * HALF * CAND_OWN
+PIECES = ((0, 4), (4, 9), (9, 14), (14, 18))
+
+
+def piece_chunks(piece):
+    first, last = PIECES[piece]
+    chunks = list(range(first * TURNS, last * TURNS))
+    if piece == 0:
+        chunks += list(range(BODY, CHUNKS + 1))
+    return chunks
 
 
 def selector():
@@ -205,9 +214,10 @@
     return jnp.concatenate(parts, 0)
 
 
-def particle_body(x_ref, owner_ref, pick_ref, sel_ref, mask_ref, out_ref, scr):
+def particle_body(x_ref, owner_ref, pick_ref, sel_ref, mask_ref, *refs):
+    outs, scr = refs[:-1], refs[-1]
     count, cycles, _ = x_ref.shape
-    n_prt = out_ref.shape[0]
+    n_prt = outs[0].shape[0]
     span = cycles // n_prt
     masks = mask_ref[...]
 
@@ -225,12 +235,23 @@
 
     lax.fori_loop(0, count, one, 0)
 
-    def two(c, carry):
+    for piece, out_ref in enumerate(outs):
+        chunks = [c for c in piece_chunks(piece) if c < BODY]
+
+        def two(c, carry):
+            for p in range(n_prt):
+                out_ref[p, c] = scr[p, pl.ds(chunks[0] + c, count, stride=CHUNKS), :].astype(
+                    jnp.bfloat16
+                )
+            return carry
+
+        lax.fori_loop(0, len(chunks), two, 0)
+    base = PIECES[0][1] * TURNS
+    for c in range(BODY, CHUNKS):
         for p in range(n_prt):
-            out_ref[p, c] = scr[p, pl.ds(c, count, stride=CHUNKS), :].astype(jnp.bfloat16)
-        return carry
-
-    lax.fori_loop(0, CHUNKS, two, 0)
+            outs[0][p, base + c - BODY] = scr[p, pl.ds(c, count, stride=CHUNKS), :].astype(
+                jnp.bfloat16
+            )
     lane = lax.broadcasted_iota(jnp.int32, (count, LANES), 1)
     label = jnp.full((count, LANES), -1, jnp.int32)
     for t in range(OWN_TOP):
@@ -242,14 +263,17 @@
             )
     label = label.astype(jnp.float32).astype(jnp.bfloat16)
     for p in range(n_prt):
-        out_ref[p, CHUNKS] = label
+        outs[0][p, base + CHUNKS - BODY] = label
 
 
 def arrange_particles(particles, owner, picks, n_prt, sel, masks):
     count = particles.shape[0]
     return pl.pallas_call(
         particle_body,
-        out_shape=jax.ShapeDtypeStruct((n_prt, CHUNKS + 1, count, LANES), jnp.bfloat16),
+        out_shape=[
+            jax.ShapeDtypeStruct((n_prt, len(piece_chunks(i)), count, LANES), jnp.bfloat16)
+            for i in range(len(PIECES))
+        ],
         scratch_shapes=[pltpu.VMEM((n_prt, count * CHUNKS, LANES), jnp.float32)],
         compiler_params=pltpu.CompilerParams(vmem_limit_bytes=32 << 20),
         cost_estimate=pl.CostEstimate(
@@ -259,7 +283,7 @@
     )(particles, owner, picks, sel, masks)
 
 
-def reference_body(at_ref, x_ref, sel_ref, mask_ref, out_ref, scr):
+def reference_body(at_ref, x_ref, sel_ref, mask_ref, out_ref, norm_ref, scr):
     rows = x_ref.shape[0]
     masks = mask_ref[...]
     step = 4
@@ -276,10 +300,11 @@
     lax.fori_loop(0, rows // step, one, 0)
 
     def two(c, carry):
-        out_ref[c] = scr[pl.ds(c, rows, stride=CHUNKS), :].astype(jnp.bfloat16)
-        return carry
-
-    lax.fori_loop(0, CHUNKS, two, 0)
+        value = scr[pl.ds(c, rows, stride=CHUNKS), :]
+        out_ref[c] = value.astype(jnp.bfloat16)
+        return carry + value * value
+
+    norm_ref[...] = lax.fori_loop(0, CHUNKS, two, jnp.zeros((rows, LANES), jnp.float32))
 
 
 def arrange_references(references, prt, n_prt, sel, masks):
@@ -296,10 +321,16 @@
                 pl.BlockSpec(sel.shape, lambda i, at: (0, 0)),
                 pl.BlockSpec(masks.shape, lambda i, at: (0, 0)),
             ],
-            out_specs=pl.BlockSpec((CHUNKS, block, LANES), lambda i, at: (0, i, 0)),
+            out_specs=[
+                pl.BlockSpec((CHUNKS, block, LANES), lambda i, at: (0, i, 0)),
+                pl.BlockSpec((block, LANES), lambda i, at: (i, 0)),
+            ],
             scratch_shapes=[pltpu.VMEM((block * CHUNKS, LANES), jnp.float32)],
         ),
-        out_shape=jax.ShapeDtypeStruct((CHUNKS, groups, LANES), jnp.bfloat16),
+        out_shape=[
+            jax.ShapeDtypeStruct((CHUNKS, groups, LANES), jnp.bfloat16),
+            jax.ShapeDtypeStruct((groups, LANES), jnp.float32),
+        ],
         compiler_params=pltpu.CompilerParams(vmem_limit_bytes=32 << 20),
         cost_estimate=pl.CostEstimate(
             flops=groups * span * width * 2 * CHUNKS,
@@ -331,16 +362,45 @@
     return [rows == cand[q : q + 1] for q in range(CAND_OWN)]
 
 
-def cross_body(at_ref, p_ref, pt_ref, q_ref, qt_ref, coef_ref, cand_ref, acc, norm):
+def residue_weights(q_ref, g, special):
+    imag, odd = lane_signs()
+    sign = jnp.where(imag == odd, -1.0, 1.0)
+    first, second = [], []
+    for i in range(TURNS):
+        q = q_ref[i].astype(jnp.float32)
+        turned = pltpu.roll(q, LANES // 2, 1) * sign
+        if special:
+            first.append(jnp.where((g == 0) & odd, 0.0, q))
+            second.append(jnp.where(g == 0, jnp.where(odd, q, 0.0), turned))
+        else:
+            first.append(q)
+            second.append(turned)
+    return jnp.concatenate(
+        [jnp.concatenate(first, 1), jnp.concatenate(second, 1)], 0
+    ).astype(jnp.bfloat16)
+
+
+def chosen_rows(acc, cand):
+    groups = acc.shape[0] // 2
+    hot = hot_masks(cand, groups)
+    rows = []
+    for ab in range(2):
+        part = acc[ab * groups : (ab + 1) * groups, :]
+        for q in range(CAND_OWN):
+            rows.append(jnp.sum(jnp.where(hot[q], part, 0.0), axis=0, keepdims=True))
+    return jnp.concatenate(rows, 0)
+
+
+def cross_first_body(at_ref, p_ref, *refs):
+    tails, label_ref = refs[: TAIL // 2], refs[TAIL // 2]
+    q_ref, qt_ref, norm_ref, coef_ref, cand_ref, acc = refs[TAIL // 2 + 1 :]
     g = pl.program_id(0)
     groups = q_ref.shape[1]
     imag, odd = lane_signs()
-    quarter = LANES // 4
-    sign = jnp.where(imag == odd, -1.0, 1.0)
 
     @pl.when(g == 0)
     def _():
-        label = lanes_of(pt_ref, TAIL // 2, 1).astype(jnp.float32).T
+        label = lanes_of(label_ref, 0, 1).astype(jnp.float32).T
         row = lax.broadcasted_iota(jnp.int32, label.shape, 0)
         base = at_ref[0] * CAND_OWN
         for q in range(CAND_OWN):
@@ -350,24 +410,8 @@
         cand_ref[CAND_OWN:, :] = jnp.full(
             (cand_ref.shape[0] - CAND_OWN, cand_ref.shape[1]), -1.0, jnp.float32
         )
-        total = jnp.zeros((groups, LANES), jnp.float32)
-        for i in range(TAIL // 2):
-            total += jnp.square(qt_ref[i].astype(jnp.float32))
-        norm[...] = total
-
-    first, second = [], []
-    total = norm[...]
-    for i in range(TURNS):
-        q = q_ref[i].astype(jnp.float32)
-        total += jnp.square(q)
-        turned = pltpu.roll(q, LANES // 2, 1) * sign
-        first.append(jnp.where((g == 0) & odd, 0.0, q))
-        second.append(jnp.where(g == 0, jnp.where(odd, q, 0.0), turned))
-    norm[...] = total
-    weights = jnp.concatenate(
-        [jnp.concatenate(first, 1), jnp.concatenate(second, 1)], 0
-    ).astype(jnp.bfloat16)
-    acc[...] = nt_dot(weights, lanes_of(p_ref, 0, TURNS))
+
+    acc[...] = nt_dot(residue_weights(q_ref, g, True), lanes_of(p_ref, 0, TURNS))
 
     for i in range(TAIL):
 
@@ -380,69 +424,96 @@
             if i == 0:
                 b = jnp.zeros_like(b)
             w = jnp.concatenate([a, b], 0).astype(jnp.bfloat16)
-            acc[...] += nt_dot(w, lanes_of(pt_ref, i // 2, 1))
-
-    hot = hot_masks(cand_ref[...], groups)
-    rows = []
-    for ab in range(2):
-        part = acc[ab * groups : (ab + 1) * groups, :]
-        for q in range(CAND_OWN):
-            rows.append(jnp.sum(jnp.where(hot[q], part, 0.0), axis=0, keepdims=True))
-    block = 2 * CAND_OWN
-    coef_ref[pl.ds(pl.multiple_of(g * block, block), block), :] = jnp.concatenate(rows, 0)
-
-    @pl.when(g == HALF - 1)
+            acc[...] += nt_dot(w, lanes_of(tails[i // 2], 0, 1))
+
+    @pl.when(g == 0)
     def _():
-        half_norm = 0.5 * jnp.sum(norm[...], axis=1, keepdims=True)
-        for q in range(CAND_OWN):
-            coef_ref[q : q + 1, :] -= jnp.sum(
-                jnp.where(hot[q], half_norm, 0.0), axis=0, keepdims=True
-            )
-
-
-def cross_coefficients(gathered, arranged, cls):
+        acc[:groups, :] -= 0.5 * jnp.sum(norm_ref[...], axis=1, keepdims=True)
+
+    coef_ref[...] = chosen_rows(acc[...], cand_ref[...])
+
+
+def cross_body(p_ref, q_ref, cand_ref, coef_ref):
+    acc = nt_dot(residue_weights(q_ref, None, False), lanes_of(p_ref, 0, TURNS))
+    coef_ref[...] = chosen_rows(acc, cand_ref[...])
+
+
+def cross_cost(gathered, groups):
+    return pl.CostEstimate(
+        flops=4 * gathered.size * groups, bytes_accessed=2 * gathered.size, transcendentals=0
+    )
+
+
+def extra_specs(sources, count):
+    base = PIECES[0][1] * TURNS
+    return [
+        pl.BlockSpec((sources, 1, count, LANES), lambda g, *at, k=k: (0, base + k, 0, 0))
+        for k in range(EXTRA)
+    ]
+
+
+def cross_first(gathered, arranged, norms, cls):
     sources, _, count, _ = gathered.shape
     groups = arranged.shape[1]
     total = sources * count
     half_tail = TAIL // 2
+    number = PIECES[0][1]
+    block = 2 * CAND_OWN
+    return pl.pallas_call(
+        cross_first_body,
+        grid_spec=pltpu.PrefetchScalarGridSpec(
+            num_scalar_prefetch=1,
+            grid=(number,),
+            in_specs=[
+                pl.BlockSpec((sources, TURNS, count, LANES), lambda g, at: (0, g, 0, 0)),
+                *extra_specs(sources, count),
+                pl.BlockSpec((TURNS, groups, LANES), lambda g, at: (g, 0, 0)),
+                pl.BlockSpec((half_tail, groups, LANES), lambda g, at: (BODY // half_tail, 0, 0)),
+                pl.BlockSpec((groups, LANES), lambda g, at: (0, 0)),
+            ],
+            out_specs=[
+                pl.BlockSpec((block, total), lambda g, at: (g, 0)),
+                pl.BlockSpec((block, total), lambda g, at: (0, 0)),
+            ],
+            scratch_shapes=[pltpu.VMEM((2 * groups, total), jnp.float32)],
+        ),
+        out_shape=[
+            jax.ShapeDtypeStruct((number * block, total), jnp.float32),
+            jax.ShapeDtypeStruct((block, total), jnp.float32),
+        ],
+        compiler_params=pltpu.CompilerParams(vmem_limit_bytes=48 << 20),
+        cost_estimate=cross_cost(gathered, groups),
+        name="cross_first",
+    )(cls, gathered, *[gathered] * EXTRA, arranged, arranged, norms)
+
+
+def cross_later(gathered, arranged, cand, piece):
+    sources, _, count, _ = gathered.shape
+    groups = arranged.shape[1]
+    total = sources * count
+    first, last = PIECES[piece]
+    block = 2 * CAND_OWN
     return pl.pallas_call(
         cross_body,
-        grid_spec=pltpu.PrefetchScalarGridSpec(
-            num_scalar_prefetch=1,
-            grid=(HALF,),
-            in_specs=[
-                pl.BlockSpec((sources, TURNS, count, LANES), lambda g, at: (0, g, 0, 0)),
-                pl.BlockSpec(
-                    (sources, EXTRA, count, LANES), lambda g, at: (0, BODY // EXTRA, 0, 0)
-                ),
-                pl.BlockSpec((TURNS, groups, LANES), lambda g, at: (g, 0, 0)),
-                pl.BlockSpec((half_tail, groups, LANES), lambda g, at: (BODY // half_tail, 0, 0)),
-            ],
-            out_specs=[
-                pl.BlockSpec((COEF, total), lambda g, at: (0, 0)),
-                pl.BlockSpec((2 * CAND_OWN, total), lambda g, at: (0, 0)),
-            ],
-            scratch_shapes=[
-                pltpu.VMEM((2 * groups, total), jnp.float32),
-                pltpu.VMEM((groups, LANES), jnp.float32),
-            ],
-        ),
-        out_shape=[
-            jax.ShapeDtypeStruct((COEF, total), jnp.float32),
-            jax.ShapeDtypeStruct((2 * CAND_OWN, total), jnp.float32),
-        ],
+        grid=(last - first,),
+        in_specs=[
+            pl.BlockSpec((sources, TURNS, count, LANES), lambda g: (0, g, 0, 0)),
+            pl.BlockSpec((TURNS, groups, LANES), lambda g: (first + g, 0, 0)),
+            pl.BlockSpec((block, total), lambda g: (0, 0)),
+        ],
+        out_specs=pl.BlockSpec((block, total), lambda g: (g, 0)),
+        out_shape=jax.ShapeDtypeStruct(((last - first) * block, total), jnp.float32),
         compiler_params=pltpu.CompilerParams(vmem_limit_bytes=48 << 20),
-        cost_estimate=pl.CostEstimate(
-            flops=4 * gathered.size * groups, bytes_accessed=2 * gathered.size, transcendentals=0
-        ),
-        name="cross_coefficients",
-    )(cls, gathered, gathered, arranged, arranged)
-
-
-def score_body(coef_ref, cand_ref, table_ref, score_ref, stat_ref, *, scale):
+        cost_estimate=cross_cost(gathered, groups),
+        name="cross_later",
+    )(gathered, arranged, cand)
+
+
+def score_body(*refs, scale):
+    *coefs, cand_ref, table_ref, score_ref, stat_ref = refs
     corr = lax.dot_general(
         table_ref[...],
-        coef_ref[...],
+        jnp.concatenate([ref[...] for ref in coefs], 0),
         (((0,), (0,)), ((), ())),
         precision=lax.Precision.HIGHEST,
         preferred_element_type=jnp.float32,
@@ -455,8 +526,8 @@
     stat_ref[1:2, :] = jnp.where(cand_ref[0:1, :] >= 0.0, total, 0.0)
 
 
-def scores(coef, cand, table, scale):
-    total = coef.shape[1]
+def scores(coefs, cand, table, scale):
+    total = cand.shape[1]
     return pl.pallas_call(
         functools.partial(score_body, scale=scale),
         out_shape=[
@@ -464,13 +535,14 @@
             jax.ShapeDtypeStruct((2, total), jnp.float32),
         ],
         name="scores",
-    )(coef, cand, table)
-
-
-def sums_body(
-    p_ref, pt_ref, score_ref, cand_ref, stat_ref, table_ref, back_ref,
-    out_ref, weight_ref, norm_ref, mix, planes,
-):
+    )(*coefs, cand, table)
+
+
+def sums_body(*refs):
+    number = len(PIECES)
+    pieces, tails = refs[:number], refs[number : number + TAIL // 2]
+    score_ref, cand_ref, stat_ref, table_ref, back_ref = refs[number + TAIL // 2 : -5]
+    out_ref, weight_ref, norm_ref, mix, planes = refs[-5:]
     i = pl.program_id(0)
     groups = weight_ref.shape[0]
     total = score_ref.shape[1]
@@ -515,25 +587,31 @@
                 dense = jnp.where(hot[q], mine[at : at + 1], dense)
             halves.append(dense)
         weights = jnp.concatenate(halves, 0).astype(jnp.bfloat16)
-        made = jnp.dot(
-            weights, lanes_of(p_ref, 0, TURNS), preferred_element_type=jnp.float32
-        )
         sign = jnp.where(imag == odd, 1.0, -1.0)
-        for t in range(TURNS):
-            g1 = made[:groups, t * LANES : (t + 1) * LANES]
-            g2 = made[groups:, t * LANES : (t + 1) * LANES]
-            value = jnp.where(
-                i == 0, jnp.where(odd, g2, g1), g1 + sign * pltpu.roll(g2, LANES // 2, 1)
-            )
-            start = pl.multiple_of((i * TURNS + t) * groups, groups)
-            planes[pl.ds(start, groups), :] = value
+        for piece, (first, last) in enumerate(PIECES):
+
+            @pl.when((i >= first) & (i < last))
+            def _():
+                made = jnp.dot(
+                    weights,
+                    lanes_of(pieces[piece], 0, TURNS),
+                    preferred_element_type=jnp.float32,
+                )
+                for t in range(TURNS):
+                    g1 = made[:groups, t * LANES : (t + 1) * LANES]
+                    g2 = made[groups:, t * LANES : (t + 1) * LANES]
+                    value = g1 + sign * pltpu.roll(g2, LANES // 2, 1)
+                    if piece == 0:
+                        value = jnp.where(i == 0, jnp.where(odd, g2, g1), value)
+                    start = pl.multiple_of((i * TURNS + t) * groups, groups)
+                    planes[pl.ds(start, groups), :] = value
 
         for t in range(TAIL):
 
             @pl.when(i == t)
             def _():
                 made = jnp.dot(
-                    weights, lanes_of(pt_ref, t // 2, 1), preferred_element_type=jnp.float32
+                    weights, lanes_of(tails[t // 2], 0, 1), preferred_element_type=jnp.float32
                 )
                 g1, g2 = made[:groups], made[groups:]
                 value = g1
@@ -567,19 +645,26 @@
             out_ref[c, :, HARM:] = placed[span:]
 
 
+def piece_spec(piece, sources, count):
+    first, last = PIECES[piece]
+    return pl.BlockSpec(
+        (sources, TURNS, count, LANES),
+        lambda i: (0, jnp.clip(i, first, last - 1) - first, 0, 0),
+    )
+
+
 def sums(gathered, score, cand, stats, table, back, groups, span):
-    sources, _, count, _ = gathered.shape
+    sources, _, count, _ = gathered[0].shape
     total = sources * count
+    size = sum(piece.size for piece in gathered)
     block = 8
     whole = lambda i: (0, 0)
     return pl.pallas_call(
         sums_body,
         grid=(HALF + groups // block,),
         in_specs=[
-            pl.BlockSpec(
-                (sources, TURNS, count, LANES), lambda i: (0, jnp.minimum(i, HALF - 1), 0, 0)
-            ),
-            pl.BlockSpec((sources, EXTRA, count, LANES), lambda i: (0, BODY // EXTRA, 0, 0)),
+            *[piece_spec(piece, sources, count) for piece in range(len(PIECES))],
+            *extra_specs(sources, count)[: TAIL // 2],
             pl.BlockSpec(score.shape, whole),
             pl.BlockSpec(cand.shape, whole),
             pl.BlockSpec(stats.shape, whole),
@@ -604,12 +689,12 @@
         ],
         compiler_params=pltpu.CompilerParams(vmem_limit_bytes=48 << 20),
         cost_estimate=pl.CostEstimate(
-            flops=4 * gathered.size * groups,
-            bytes_accessed=2 * gathered.size + 8 * groups * span * HARM,
+            flops=4 * size * groups,
+            bytes_accessed=2 * size + 8 * groups * span * HARM,
             transcendentals=0,
         ),
         name="sums",
-    )(gathered, gathered, score, cand, stats, table, back)
+    )(*gathered, *[gathered[0]] * (TAIL // 2), score, cand, stats, table, back)
 
 
 def spread(outgoing):
@@ -629,12 +714,18 @@
     table = jnp.asarray(rotation_table())
     picks = class_order[:, :, :CAND_OWN].reshape(count, OWN_TOP * CAND_OWN)
     outgoing = arrange_particles(particles, owner_groups, picks, n_prt, sel, masks)
-    gathered = spread(outgoing)
-    arranged = arrange_references(references, prt.reshape(1).astype(jnp.int32), n_prt, sel, masks)
-    coef, cand = cross_coefficients(gathered, arranged, cls.reshape(1).astype(jnp.int32))
-    coef = lax.psum(coef, "prt")
+    gathered = [spread(piece) for piece in outgoing]
+    arranged, norms = arrange_references(
+        references, prt.reshape(1).astype(jnp.int32), n_prt, sel, masks
+    )
+    coef, cand = cross_first(gathered[0], arranged, norms, cls.reshape(1).astype(jnp.int32))
+    coefs = [lax.psum(coef, "prt")]
+    for piece in range(1, len(PIECES)):
+        coef = cross_later(gathered[piece], arranged, cand, piece)
+        coef, coefs[-1] = lax.optimization_barrier((coef, coefs[-1]))
+        coefs.append(lax.psum(coef, "prt"))
     scale = 2.0 / math.sqrt(cycles * width)
-    score, stat = scores(coef, cand, table, scale)
+    score, stat = scores(coefs, cand, table, scale)
     stats = lax.all_gather(stat, "cls", axis=0, tiled=True)
     class_sums, class_weights, log_norm = sums(
         gathered, score, cand, stats, table, back, groups, span

time: 267 us -> 389 us (1.46)
  waiting for transfers between devices: 110 us -> 232 us
  blocking collectives: 63.9 us -> 47.3 us
  starting transfers between devices: 0.08 us -> 8.77 us
  local copies, waits for them, and re-layouts: 11.8 us -> 16.1 us
    psum x1 -> x4, waiting for transfers between devices: 35.9 us -> 129 us  [the longest x3 98.7 us: gather_device(): coefs.append(lax.psum(coef, 'prt'))]
    all_gather x1 -> x4, waiting for transfers between devices: 74.4 us -> 103 us  [spread(): return lax.all_gather(arrived, 'cls', axis=0, tiled=True)]
    all_to_all x1 -> x2, blocking collectives: 54.8 us -> 38.1 us  [spread(): lax.all_to_all(outgoing, 'prt', split_axis=0, concat_axis=0, tiled=True)]
    all_to_all x0 -> x2, starting transfers between devices: none -> 8.49 us  [spread(): lax.all_to_all(outgoing, 'prt', split_axis=0, concat_axis=0, tiled=True)]
    unnamed x24 -> x32, local copies, waits for them, and re-layouts: 10.3 us -> 14.6 us
    pallas_call x3 -> x6, Pallas kernels: 51.5 us -> 54.1 us  [the longest x1 24.1 us: sums(): pl.pallas_call(sums_body, grid=(HALF + groups // block,), in_specs=[*[pie...]
  transfers between devices with their start and end apart: 2 -> 10, of which waited for: 2 -> 7; matrix products, arithmetic and copies ran while one was open for 0% -> 0% of each run, Pallas kernels for 4% -> 8%
where the time goes in v2:
time: 389 us; the launch traced here: 388 us
  waiting for transfers between devices  232 us (60%)
  Pallas kernels  68.3 us (18%)
  blocking collectives  47.3 us (12%)
  local copies, waits for them, and re-layouts  16.1 us (4%)
  between operations  14.3 us (4%)
  starting transfers between devices  8.77 us (2%)
    all_gather x4, waiting for transfers between devices, spread(): return lax.all_gather(arrived, 'cls', axis=0, tiled=True)  103 us
    psum x3, waiting for transfers between devices, gather_device(): coefs.append(lax.psum(coef, 'prt'))  98.7 us
    all_to_all x2, blocking collectives, spread(): lax.all_to_all(outgoing, 'prt', split_axis=0, concat_axis=0, tiled=True)  38.1 us
    psum x1, waiting for transfers between devices, gather_device(): coefs = [lax.psum(coef, 'prt')]  30.5 us
    pallas_call x1, Pallas kernels, sums(): pl.pallas_call(sums_body, grid=(HALF + groups // block,), in_specs=[*[pie...  24.1 us
    pallas_call x3, Pallas kernels, cross_later(): pl.pallas_call(cross_body, grid=(last - first,), in_specs=[pl.BlockSpec((...  14.6 us
    unnamed x32, local copies, waits for them, and re-layouts  14.6 us
    pallas_call x1, Pallas kernels, arrange_references(): pl.pallas_call(reference_body, grid_spec=pltpu.PrefetchScalarGridSpec(num...  12 us
  transfers between devices with their start and end apart: 10, of which 7 were waited for; matrix products, arithmetic and copies ran while one was open for 0% of the time, Pallas kernels for 8%

profile of v2, /device:TPU:0, one launch (start us, length us, event | category | flops | bytes accessed | tf_op | source)
XLA Modules:
  0.0 387.8 jit_solution(12803616068696163759)
XLA Ops:
  8.9 1.6 copy-done.3
  12.0 9.5 %arrange_particles.1 = (bf16[4,31,16,128]{3,2,1,0:T(8,128)(2,1)S(1)}, bf16[4,35,16,128]{3,2,1,0:T(8,128)(2,1)S(1)}, bf16[4,35,16,128]{3,2,1,0:T(8,128)(2,1)}, bf16[4,28,16,128]{3,2,1,0:T(8,128)(2,1)}) custom-call(bf16[16,128,512]{2,1,0:T(8,128)(2,1)S(1)} %copy-done.3, s32[16,4]{1,0:T(8,128)S(1)} %copy.16.owner_ref, s32[16,16]{1,0:T(8,128)S(1)} %copy.17.pick_ref, ...), custom_call_target="tpu_custom_call" | custom-call | flops 268435456 | bytes 4194304 | tf_op jit(solution)/shard_map/arrange_particles/pallas_call | solution.py:271
  21.6 20.3 %all_to_all.20 = bf16[4,31,16,128]{3,2,1,0:T(8,128)(2,1)} all-to-all(bf16[4,31,16,128]{3,2,1,0:T(8,128)(2,1)S(1)} %get-tuple-element.22), channel_id=1, replica_groups=mesh['cls'=8,'prt'=4] {'prt'}, dimensions={0} | all-to-all | bytes 1015808 | tf_op jit(solution)/shard_map/all_to_all | solution.py:701
  42.0 17.8 %all_to_all.21 = bf16[4,35,16,128]{3,2,1,0:T(8,128)(2,1)} all-to-all(bf16[4,35,16,128]{3,2,1,0:T(8,128)(2,1)S(1)} %get-tuple-element.23), channel_id=1, replica_groups=mesh['cls'=8,'prt'=4] {'prt'}, dimensions={0} | all-to-all | bytes 1146880 | tf_op jit(solution)/shard_map/all_to_all | solution.py:701
  59.8 3.5 all-to-all-start.2
  63.4 3.4 copy-done.2
  66.8 12.0 %arrange_references.1 = (bf16[128,64,128]{2,1,0:T(8,128)(2,1)S(1)}, f32[64,128]{1,0:T(8,128)S(1)}) custom-call(s32[1]{0:T(128)} %bitcast.1.at_ref, bf16[64,128,512]{2,1,0:T(8,128)(2,1)S(1)} %copy-done.2, bf16[128,256]{1,0:T(8,128)(2,1)S(1)} %copy-done.9, bf16[2,256]{1,0:T(2,128)(2,1)S(1)} %copy-done.12), custom_call_target="tpu_custom_call" | custom-call | flops 268435456 | bytes 4194304 | tf_op jit(solution)/shard_map/arrange_references/pallas_call | solution.py:314
  78.8 5.9 %cross_first.1 = (f32[32,512]{1,0:T(8,128)}, f32[8,512]{1,0:T(8,128)S(1)}) custom-call(s32[1]{0:T(128)} %bitcast.2.at_ref, bf16[32,31,16,128]{3,2,1,0:T(8,128)(2,1)} %all-gather.6.cloned.1.call-done.p_ref.refs_0_.refs_1_.refs_2_.refs_4_.refs_5_, bf16[32,31,16,128]{3,2,1,0:T(8,128)(2,1)} %all-gather.6.cloned.1.call-done.p_ref.refs_0_.refs_1_.refs_2_.refs_4_.refs_5_, ...), custom_call_target="tpu_custom_call" | custom-call | flops 520093696 | bytes 4063232 | tf_op jit(solution)/shard_map/cross_first/pallas_call | solution.py:462
  85.6 5.0 %all-to-all-start.3 = ((bf16[4,28,16,128]{3,2,1,0:T(8,128)(2,1)}), bf16[4,28,16,128]{3,2,1,0:T(8,128)(2,1)S(1)}, u32[]{:S(2)}, u32[]{:S(2)}) async-start(bf16[4,28,16,128]{3,2,1,0:T(8,128)(2,1)} %get-tuple-element.25), calls=%async_computation.3 | async-start | bytes 917504 | tf_op jit(solution)/shard_map/all_to_all | solution.py:701
  90.6 27.1 %all-gather.8.cloned.1.call-done.p_ref.refs_1_ = bf16[32,35,16,128]{3,2,1,0:T(8,128)(2,1)} async-done(((bf16[4,35,16,128]{3,2,1,0:T(8,128)(2,1)}), bf16[32,35,16,128]{3,2,1,0:T(8,128)(2,1)}) %all-gather.8.cloned.1.call-update) | async-done | bytes 4587536 | tf_op jit(solution)/shard_map/all_gather | solution.py:702
  117.7 5.8 %cross_later.3 = f32[40,512]{1,0:T(8,128)} custom-call(bf16[32,35,16,128]{3,2,1,0:T(8,128)(2,1)} %all-gather.8.cloned.1.call-done.p_ref.refs_1_, bf16[128,64,128]{2,1,0:T(8,128)(2,1)S(1)} %get-tuple-element.26.refs_3_.refs_4_.q_ref, f32[8,512]{1,0:T(8,128)S(1)} %get-tuple-element.28.cand_ref.refs_4_.refs_7_), custom_call_target="tpu_custom_call" | custom-call | flops 587202560 | bytes 4587520 | tf_op jit(solution)/shard_map/cross_later/pallas_call | solution.py:496
  123.5 30.5 %all-reduce.5.cloned.1.call-done.refs_0_ = f32[32,512]{1,0:T(8,128)} async-done(((f32[32,512]{1,0:T(8,128)}), f32[32,512]{1,0:T(8,128)}) %all-reduce.5.cloned.1.call-update) | async-done | bytes 65552 | tf_op jit(solution)/shard_map/psum | solution.py:722
  154.9 39.7 %all-gather.10.cloned.1.call-done.p_ref.refs_2_ = bf16[32,35,16,128]{3,2,1,0:T(8,128)(2,1)} async-done(((bf16[4,35,16,128]{3,2,1,0:T(8,128)(2,1)}), bf16[32,35,16,128]{3,2,1,0:T(8,128)(2,1)}) %all-gather.10.cloned.1.call-update) | async-done | bytes 4587536 | tf_op jit(solution)/shard_map/all_gather | solution.py:702
  194.6 5.8 %cross_later.4 = f32[40,512]{1,0:T(8,128)} custom-call(bf16[32,35,16,128]{3,2,1,0:T(8,128)(2,1)} %all-gather.10.cloned.1.call-done.p_ref.refs_2_, bf16[128,64,128]{2,1,0:T(8,128)(2,1)S(1)} %get-tuple-element.26.refs_3_.refs_4_.q_ref, f32[8,512]{1,0:T(8,128)S(1)} %get-tuple-element.28.cand_ref.refs_4_.refs_7_), custom_call_target="tpu_custom_call" | custom-call | flops 587202560 | bytes 4587520 | tf_op jit(solution)/shard_map/cross_later/pallas_call | solution.py:496
  200.4 30.5 %all-reduce.7.cloned.1.call-done.refs_1_ = f32[40,512]{1,0:T(8,128)} async-done(((f32[40,512]{1,0:T(8,128)}), f32[40,512]{1,0:T(8,128)}) %all-reduce.7.cloned.1.call-update) | async-done | bytes 81936 | tf_op jit(solution)/shard_map/psum | solution.py:726
  231.0 36.2 %all-gather.12.cloned.1.call-done.p_ref.refs_3_ = bf16[32,28,16,128]{3,2,1,0:T(8,128)(2,1)} async-done(((bf16[4,28,16,128]{3,2,1,0:T(8,128)(2,1)}), bf16[32,28,16,128]{3,2,1,0:T(8,128)(2,1)}) %all-gather.12.cloned.1.call-update) | async-done | bytes 3670032 | tf_op jit(solution)/shard_map/all_gather | solution.py:702
  267.2 2.0 copy-done
  269.2 3.0 cross_later.5
  272.2 31.9 %all-reduce.9.cloned.1.call-done.refs_2_ = f32[40,512]{1,0:T(8,128)} async-done(((f32[40,512]{1,0:T(8,128)}), f32[40,512]{1,0:T(8,128)}) %all-reduce.9.cloned.1.call-update) | async-done | bytes 81936 | tf_op jit(solution)/shard_map/psum | solution.py:726
  304.1 36.4 %all-reduce.11.cloned.1.call-done.refs_3_ = f32[32,512]{1,0:T(8,128)} async-done(((f32[32,512]{1,0:T(8,128)}), f32[32,512]{1,0:T(8,128)}) %all-reduce.11.cloned.1.call-update) | async-done | bytes 65552 | tf_op jit(solution)/shard_map/psum | solution.py:726
  340.6 2.2 scores.1
  342.8 9.1 %all-gather = f32[8,2,512]{2,1,0:T(2,128)S(1)} all-gather(f32[1,2,512]{2,1,0:T(2,128)} %bitcast.9), channel_id=1, replica_groups=mesh['cls'=8,'prt'=4] {'cls'}, dimensions={0}, use_global_device_ids=true | all-gather | bytes 36864 | tf_op jit(solution)/shard_map/all_gather | solution.py:729
  352.0 2.0 copy-done.1
  355.7 24.1 %sums.1 = (f32[64,32,512]{2,1,0:T(8,128)}, f32[64,1]{1,0:T(8,128)S(1)}, f32[1,512]{1,0:T(1,128)S(1)}) custom-call(bf16[32,31,16,128]{3,2,1,0:T(8,128)(2,1)} %all-gather.6.cloned.1.call-done.p_ref.refs_0_.refs_1_.refs_2_.refs_4_.refs_5_, bf16[32,35,16,128]{3,2,1,0:T(8,128)(2,1)} %all-gather.8.cloned.1.call-done.p_ref.refs_1_, ...), custom_call_target="tpu_custom_call" | custom-call | flops 2164260864 | bytes 21102592 | tf_op jit(solution)/shard_map/sums/pallas_call | solution.py:662
  (51 shorter events, 8.1 us)
Async XLA Ops:
  7.2 56.2 %copy-start.12 = (bf16[2,256]{1,0:T(2,128)(2,1)S(1)}, bf16[2,256]{1,0:T(2,128)(2,1)}, u32[]{:S(2)}) copy-start(bf16[2,256]{1,0:T(2,128)(2,1)} %constant.27.clone.mask_ref) | copy-start | bytes 3076
  7.2 56.2 %copy-start.9 = (bf16[128,256]{1,0:T(8,128)(2,1)S(1)}, bf16[128,256]{1,0:T(8,128)(2,1)}, u32[]{:S(2)}) copy-start(bf16[128,256]{1,0:T(8,128)(2,1)} %constant.26.clone.sel_ref) | copy-start | bytes 196612
  7.2 71.6 %all-gather.6.cloned.1.call-start = ((), (), s32[]{:S(2)}) async-start(), calls=%async_computation.4 | async-start | bytes 4571136 | tf_op jit(solution)/shard_map/all_gather | solution.py:702
  8.9 1.6 copy-start.3
  10.5 0.8 copy-start.8
  41.9 75.8 %all-gather.8.cloned.1.call-start = ((), (), s32[]{:S(2)}) async-start(), calls=%async_computation.5 | async-start | bytes 5160960 | tf_op jit(solution)/shard_map/all_gather | solution.py:702
  59.8 24.9 %all-to-all-start.2 = ((bf16[4,35,16,128]{3,2,1,0:T(8,128)(2,1)}), bf16[4,35,16,128]{3,2,1,0:T(8,128)(2,1)S(1)}, u32[]{:S(2)}, u32[]{:S(2)}) async-start(bf16[4,35,16,128]{3,2,1,0:T(8,128)(2,1)} %get-tuple-element.24), calls=%async_computation.2 | async-start | bytes 1146880 | tf_op jit(solution)/shard_map/all_to_all | solution.py:701
  63.3 90.7 %all-reduce.5.cloned.1.call-start = ((), (), s32[]{:S(2)}) async-start(), calls=%async_computation.8 | async-start | bytes 131072 | tf_op jit(solution)/shard_map/psum | solution.py:722
  63.4 3.4 copy-start.2
  84.6 182.6 %copy-start.5 = (f32[8,512]{1,0:T(8,128)}, f32[8,512]{1,0:T(8,128)S(1)}, u32[]{:S(2)}) copy-start(f32[8,512]{1,0:T(8,128)S(1)} %get-tuple-element.28.cand_ref.refs_4_.refs_7_) | copy-start | bytes 49156
  84.7 109.9 %all-gather.10.cloned.1.call-start = ((), (), s32[]{:S(2)}) async-start(), calls=%async_computation.6 | async-start | bytes 5160960 | tf_op jit(solution)/shard_map/all_gather | solution.py:702
  84.7 0.8 copy-start.13
  85.6 68.5 %all-to-all-start.3 = ((bf16[4,28,16,128]{3,2,1,0:T(8,128)(2,1)}), bf16[4,28,16,128]{3,2,1,0:T(8,128)(2,1)S(1)}, u32[]{:S(2)}, u32[]{:S(2)}) async-start(bf16[4,28,16,128]{3,2,1,0:T(8,128)(2,1)} %get-tuple-element.25), calls=%async_computation.3 | async-start | bytes 917504 | tf_op jit(solution)/shard_map/all_to_all | solution.py:701
  90.6 140.3 %all-reduce.7.cloned.1.call-start = ((), (), s32[]{:S(2)}) async-start(), calls=%async_computation.9 | async-start | bytes 163840 | tf_op jit(solution)/shard_map/psum | solution.py:726
  154.0 113.2 %all-gather.12.cloned.1.call-start = ((), (), s32[]{:S(2)}) async-start(), calls=%async_computation.7 | async-start | bytes 4128768 | tf_op jit(solution)/shard_map/all_gather | solution.py:702
  154.1 0.8 copy-start.14
  154.9 149.2 %all-reduce.9.cloned.1.call-start = ((), (), s32[]{:S(2)}) async-start(), calls=%async_computation.10 | async-start | bytes 163840 | tf_op jit(solution)/shard_map/psum | solution.py:726
  194.6 157.3 %copy-start.4 = (f32[144,144]{1,0:T(8,128)S(1)}, f32[144,144]{1,0:T(8,128)}, u32[]{:S(2)}) copy-start(f32[144,144]{1,0:T(8,128)} %constant.29.clone.refs_5_.refs_9_) | copy-start | bytes 248836
  194.6 157.3 %copy-start.10 = (bf16[256,256]{1,0:T(8,128)(2,1)S(1)}, bf16[256,256]{1,0:T(8,128)(2,1)}, u32[]{:S(2)}) copy-start(bf16[256,256]{1,0:T(8,128)(2,1)} %constant.28.clone.refs_10_) | copy-start | bytes 393220
  230.9 109.6 %all-reduce.11.cloned.1.call-start = ((), (), s32[]{:S(2)}) async-start(), calls=%async_computation.11 | async-start | bytes 131072 | tf_op jit(solution)/shard_map/psum | solution.py:726
  267.2 2.0 copy-start
  351.9 2.0 copy-start.1
  354.0 0.7 copy-start.6
  354.7 1.0 copy-start.7
  (1 other events, 0.7 us)
Sparse Core Ops, SparseCore 0:
  42.1 35.2 all-gather.5
  79.2 38.3 all-gather.7
  120.0 33.9 all-reduce.4
  156.5 38.0 all-gather.9
  196.9 33.9 all-reduce.6
  232.6 34.5 all-gather.11
  270.1 33.9 all-reduce.8
  306.5 33.9 all-reduce.10

commit v3 on v2

--- a/solution.py
+++ b/solution.py
@@ -166,15 +166,8 @@
 CHUNKS = BODY + TAIL // 2
 EXTRA = TAIL // 2 + 1
 COEF = 2 * HALF * CAND_OWN
-PIECES = ((0, 4), (4, 9), (9, 14), (14, 18))
-
-
-def piece_chunks(piece):
-    first, last = PIECES[piece]
-    chunks = list(range(first * TURNS, last * TURNS))
-    if piece == 0:
-        chunks += list(range(BODY, CHUNKS + 1))
-    return chunks
+CROSS_STEP = 6
+SUM_STEP = 3
 
 
 def selector():
@@ -214,18 +207,19 @@
     return jnp.concatenate(parts, 0)
 
 
-def particle_body(x_ref, owner_ref, pick_ref, sel_ref, mask_ref, *refs):
+def particle_body(at_ref, x_ref, owner_ref, pick_ref, sel_ref, mask_ref, *refs):
     outs, scr = refs[:-1], refs[-1]
     count, cycles, _ = x_ref.shape
-    n_prt = outs[0].shape[0]
+    n_prt = len(outs)
     span = cycles // n_prt
     masks = mask_ref[...]
 
     def one(n, carry):
-        x = x_ref[n]
-        w = jnp.concatenate(
-            [masked_stack(x[p * span : (p + 1) * span], masks) for p in range(n_prt)], 0
-        )
+        parts = []
+        for d in range(n_prt):
+            start = pl.multiple_of((at_ref[0] ^ d) * span, span)
+            parts.append(masked_stack(x_ref[n, pl.ds(start, span), :], masks))
+        w = jnp.concatenate(parts, 0)
         y = nt_dot(sel_ref[...], w)
         for p in range(n_prt):
             scr[p, pl.ds(pl.multiple_of(n * CHUNKS, CHUNKS), CHUNKS), :] = y[
@@ -235,23 +229,12 @@
 
     lax.fori_loop(0, count, one, 0)
 
-    for piece, out_ref in enumerate(outs):
-        chunks = [c for c in piece_chunks(piece) if c < BODY]
-
-        def two(c, carry):
-            for p in range(n_prt):
-                out_ref[p, c] = scr[p, pl.ds(chunks[0] + c, count, stride=CHUNKS), :].astype(
-                    jnp.bfloat16
-                )
-            return carry
-
-        lax.fori_loop(0, len(chunks), two, 0)
-    base = PIECES[0][1] * TURNS
-    for c in range(BODY, CHUNKS):
+    def two(c, carry):
         for p in range(n_prt):
-            outs[0][p, base + c - BODY] = scr[p, pl.ds(c, count, stride=CHUNKS), :].astype(
-                jnp.bfloat16
-            )
+            outs[p][c] = scr[p, pl.ds(c, count, stride=CHUNKS), :].astype(jnp.bfloat16)
+        return carry
+
+    lax.fori_loop(0, CHUNKS, two, 0)
     lane = lax.broadcasted_iota(jnp.int32, (count, LANES), 1)
     label = jnp.full((count, LANES), -1, jnp.int32)
     for t in range(OWN_TOP):
@@ -263,24 +246,22 @@
             )
     label = label.astype(jnp.float32).astype(jnp.bfloat16)
     for p in range(n_prt):
-        outs[0][p, base + CHUNKS - BODY] = label
-
-
-def arrange_particles(particles, owner, picks, n_prt, sel, masks):
+        outs[p][CHUNKS] = label
+
+
+def arrange_particles(prt, particles, owner, picks, n_prt, sel, masks):
     count = particles.shape[0]
     return pl.pallas_call(
         particle_body,
-        out_shape=[
-            jax.ShapeDtypeStruct((n_prt, len(piece_chunks(i)), count, LANES), jnp.bfloat16)
-            for i in range(len(PIECES))
-        ],
+        in_specs=[pl.BlockSpec(memory_space=pltpu.SMEM)] + [pl.BlockSpec(memory_space=pltpu.VMEM)] * 5,
+        out_shape=[jax.ShapeDtypeStruct((CHUNKS + 1, count, LANES), jnp.bfloat16)] * n_prt,
         scratch_shapes=[pltpu.VMEM((n_prt, count * CHUNKS, LANES), jnp.float32)],
         compiler_params=pltpu.CompilerParams(vmem_limit_bytes=32 << 20),
         cost_estimate=pl.CostEstimate(
             flops=particles.size * 2 * CHUNKS, bytes_accessed=particles.size * 4, transcendentals=0
         ),
         name="arrange_particles",
-    )(particles, owner, picks, sel, masks)
+    )(prt, particles, owner, picks, sel, masks)
 
 
 def reference_body(at_ref, x_ref, sel_ref, mask_ref, out_ref, norm_ref, scr):
@@ -349,11 +330,10 @@
     return imag, odd
 
 
-def lanes_of(ref, first, number):
-    parts = []
-    for i in range(first, first + number):
-        part = ref[:, i]
-        parts.append(part.reshape(part.shape[0] * part.shape[1], LANES))
+def lanes_of(refs, first, number):
+    parts = [
+        jnp.concatenate([ref[i] for ref in refs], 0) for i in range(first, first + number)
+    ]
     return jnp.concatenate(parts, 1) if number > 1 else parts[0]
 
 
@@ -362,14 +342,14 @@
     return [rows == cand[q : q + 1] for q in range(CAND_OWN)]
 
 
-def residue_weights(q_ref, g, special):
+def residue_weights(q_ref, at, g):
     imag, odd = lane_signs()
     sign = jnp.where(imag == odd, -1.0, 1.0)
     first, second = [], []
     for i in range(TURNS):
-        q = q_ref[i].astype(jnp.float32)
+        q = q_ref[at * TURNS + i].astype(jnp.float32)
         turned = pltpu.roll(q, LANES // 2, 1) * sign
-        if special:
+        if at == 0:
             first.append(jnp.where((g == 0) & odd, 0.0, q))
             second.append(jnp.where(g == 0, jnp.where(odd, q, 0.0), turned))
         else:
@@ -391,16 +371,17 @@
     return jnp.concatenate(rows, 0)
 
 
-def cross_first_body(at_ref, p_ref, *refs):
-    tails, label_ref = refs[: TAIL // 2], refs[TAIL // 2]
-    q_ref, qt_ref, norm_ref, coef_ref, cand_ref, acc = refs[TAIL // 2 + 1 :]
-    g = pl.program_id(0)
+def cross_body(at_ref, *refs):
+    number = (len(refs) - 6) // 2
+    blocks, extras = refs[:number], refs[number : 2 * number]
+    q_ref, qt_ref, norm_ref, coef_ref, cand_ref, acc = refs[2 * number :]
+    step = pl.program_id(0)
     groups = q_ref.shape[1]
     imag, odd = lane_signs()
 
-    @pl.when(g == 0)
+    @pl.when(step == 0)
     def _():
-        label = lanes_of(label_ref, 0, 1).astype(jnp.float32).T
+        label = lanes_of(extras, TAIL // 2, 1).astype(jnp.float32).T
         row = lax.broadcasted_iota(jnp.int32, label.shape, 0)
         base = at_ref[0] * CAND_OWN
         for q in range(CAND_OWN):
@@ -411,109 +392,80 @@
             (cand_ref.shape[0] - CAND_OWN, cand_ref.shape[1]), -1.0, jnp.float32
         )
 
-    acc[...] = nt_dot(residue_weights(q_ref, g, True), lanes_of(p_ref, 0, TURNS))
-
-    for i in range(TAIL):
-
-        @pl.when(g == i)
-        def _():
-            q = qt_ref[i // 2].astype(jnp.float32)
-            keep = odd if i % 2 else ~odd
-            a = jnp.where(keep, q, 0.0)
-            b = jnp.where(keep, pltpu.roll(q, LANES // 2, 1) * jnp.where(imag, 1.0, -1.0), 0.0)
-            if i == 0:
-                b = jnp.zeros_like(b)
-            w = jnp.concatenate([a, b], 0).astype(jnp.bfloat16)
-            acc[...] += nt_dot(w, lanes_of(tails[i // 2], 0, 1))
-
-    @pl.when(g == 0)
-    def _():
-        acc[:groups, :] -= 0.5 * jnp.sum(norm_ref[...], axis=1, keepdims=True)
-
-    coef_ref[...] = chosen_rows(acc[...], cand_ref[...])
-
-
-def cross_body(p_ref, q_ref, cand_ref, coef_ref):
-    acc = nt_dot(residue_weights(q_ref, None, False), lanes_of(p_ref, 0, TURNS))
-    coef_ref[...] = chosen_rows(acc, cand_ref[...])
-
-
-def cross_cost(gathered, groups):
-    return pl.CostEstimate(
-        flops=4 * gathered.size * groups, bytes_accessed=2 * gathered.size, transcendentals=0
-    )
-
-
-def extra_specs(sources, count):
-    base = PIECES[0][1] * TURNS
-    return [
-        pl.BlockSpec((sources, 1, count, LANES), lambda g, *at, k=k: (0, base + k, 0, 0))
-        for k in range(EXTRA)
-    ]
-
-
-def cross_first(gathered, arranged, norms, cls):
-    sources, _, count, _ = gathered.shape
+    for u in range(CROSS_STEP):
+        g = step * CROSS_STEP + u
+        acc[...] = nt_dot(residue_weights(q_ref, u, g), lanes_of(blocks, u * TURNS, TURNS))
+
+        for i in range(TAIL):
+            if i % CROSS_STEP != u:
+                continue
+
+            @pl.when(g == i)
+            def _():
+                q = qt_ref[i // 2].astype(jnp.float32)
+                keep = odd if i % 2 else ~odd
+                a = jnp.where(keep, q, 0.0)
+                turned = pltpu.roll(q, LANES // 2, 1) * jnp.where(imag, 1.0, -1.0)
+                b = jnp.where(keep, turned, 0.0)
+                if i == 0:
+                    b = jnp.zeros_like(b)
+                w = jnp.concatenate([a, b], 0).astype(jnp.bfloat16)
+                acc[...] += nt_dot(w, lanes_of(extras, i // 2, 1))
+                if i == 0:
+                    acc[:groups, :] -= 0.5 * jnp.sum(norm_ref[...], axis=1, keepdims=True)
+
+        block = 2 * CAND_OWN
+        coef_ref[u * block : (u + 1) * block, :] = chosen_rows(acc[...], cand_ref[...])
+
+
+def cross_coefficients(blocks, arranged, norms, cls):
+    count = blocks[0].shape[1]
     groups = arranged.shape[1]
-    total = sources * count
+    total = len(blocks) * count
     half_tail = TAIL // 2
-    number = PIECES[0][1]
+    size = blocks[0].size * len(blocks)
     block = 2 * CAND_OWN
     return pl.pallas_call(
-        cross_first_body,
+        cross_body,
         grid_spec=pltpu.PrefetchScalarGridSpec(
             num_scalar_prefetch=1,
-            grid=(number,),
+            grid=(HALF // CROSS_STEP,),
             in_specs=[
-                pl.BlockSpec((sources, TURNS, count, LANES), lambda g, at: (0, g, 0, 0)),
-                *extra_specs(sources, count),
-                pl.BlockSpec((TURNS, groups, LANES), lambda g, at: (g, 0, 0)),
+                *[
+                    pl.BlockSpec((CROSS_STEP * TURNS, count, LANES), lambda g, at: (g, 0, 0))
+                    for _ in blocks
+                ],
+                *[
+                    pl.BlockSpec((EXTRA, count, LANES), lambda g, at: (BODY // EXTRA, 0, 0))
+                    for _ in blocks
+                ],
+                pl.BlockSpec((CROSS_STEP * TURNS, groups, LANES), lambda g, at: (g, 0, 0)),
                 pl.BlockSpec((half_tail, groups, LANES), lambda g, at: (BODY // half_tail, 0, 0)),
                 pl.BlockSpec((groups, LANES), lambda g, at: (0, 0)),
             ],
             out_specs=[
-                pl.BlockSpec((block, total), lambda g, at: (g, 0)),
+                pl.BlockSpec((CROSS_STEP * block, total), lambda g, at: (g, 0)),
                 pl.BlockSpec((block, total), lambda g, at: (0, 0)),
             ],
             scratch_shapes=[pltpu.VMEM((2 * groups, total), jnp.float32)],
         ),
         out_shape=[
-            jax.ShapeDtypeStruct((number * block, total), jnp.float32),
+            jax.ShapeDtypeStruct((COEF, total), jnp.float32),
             jax.ShapeDtypeStruct((block, total), jnp.float32),
         ],
-        compiler_params=pltpu.CompilerParams(vmem_limit_bytes=48 << 20),
-        cost_estimate=cross_cost(gathered, groups),
-        name="cross_first",
-    )(cls, gathered, *[gathered] * EXTRA, arranged, arranged, norms)
-
-
-def cross_later(gathered, arranged, cand, piece):
-    sources, _, count, _ = gathered.shape
-    groups = arranged.shape[1]
-    total = sources * count
-    first, last = PIECES[piece]
-    block = 2 * CAND_OWN
-    return pl.pallas_call(
-        cross_body,
-        grid=(last - first,),
-        in_specs=[
-            pl.BlockSpec((sources, TURNS, count, LANES), lambda g: (0, g, 0, 0)),
-            pl.BlockSpec((TURNS, groups, LANES), lambda g: (first + g, 0, 0)),
-            pl.BlockSpec((block, total), lambda g: (0, 0)),
-        ],
-        out_specs=pl.BlockSpec((block, total), lambda g: (g, 0)),
-        out_shape=jax.ShapeDtypeStruct(((last - first) * block, total), jnp.float32),
-        compiler_params=pltpu.CompilerParams(vmem_limit_bytes=48 << 20),
-        cost_estimate=cross_cost(gathered, groups),
-        name="cross_later",
-    )(gathered, arranged, cand)
+        compiler_params=pltpu.CompilerParams(vmem_limit_bytes=32 << 20),
+        cost_estimate=pl.CostEstimate(
+            flops=4 * size * groups, bytes_accessed=2 * size, transcendentals=0
+        ),
+        name="cross_coefficients",
+    )(cls, *blocks, *blocks, arranged, arranged, norms)
 
 
 def score_body(*refs, scale):
     *coefs, cand_ref, table_ref, score_ref, stat_ref = refs
     corr = lax.dot_general(
         table_ref[...],
-        jnp.concatenate([ref[...] for ref in coefs], 0),
+        functools.reduce(jnp.add, [ref[...] for ref in coefs]),
         (((0,), (0,)), ((), ())),
         precision=lax.Precision.HIGHEST,
         preferred_element_type=jnp.float32,
@@ -538,94 +490,129 @@
     )(*coefs, cand, table)
 
 
-def sums_body(*refs):
-    number = len(PIECES)
-    pieces, tails = refs[:number], refs[number : number + TAIL // 2]
-    score_ref, cand_ref, stat_ref, table_ref, back_ref = refs[number + TAIL // 2 : -5]
-    out_ref, weight_ref, norm_ref, mix, planes = refs[-5:]
+def swap_blocks(x, distance, width):
+    lane = lax.broadcasted_iota(jnp.int32, x.shape, 1)
+    bit = 1
+    while bit <= distance:
+        if distance & bit:
+            shift = bit * width
+            down = pltpu.roll(x, shift, 1)
+            up = pltpu.roll(x, x.shape[1] - shift, 1)
+            x = jnp.where((lane // shift) % 2 == 1, down, up)
+        bit *= 2
+    return x
+
+
+def weights_body(at_ref, score_ref, cand_ref, stat_ref, table_ref, mix_ref, norm_ref):
+    n_cls, _, total = stat_ref.shape
+    width = total // n_cls
+    tops, parts = [], []
+    for e in range(n_cls):
+        table = stat_ref[at_ref[0] ^ e]
+        table = swap_blocks(jnp.concatenate([table] * 4, 0), e, width)
+        tops.append(table[0:1])
+        parts.append(table[1:2])
+    top = functools.reduce(jnp.maximum, tops)
+    summed = jnp.zeros_like(top)
+    for other, part in zip(tops, parts):
+        summed += part * jnp.exp(other - top)
+    log_norm = top + jnp.log(summed)
+    norm_ref[...] = log_norm
+    weight = jnp.where(cand_ref[0:1, :] >= 0.0, jnp.exp(score_ref[...] - log_norm), 0.0)
+    mix_ref[...] = lax.dot_general(
+        table_ref[...],
+        weight,
+        (((1,), (0,)), ((), ())),
+        precision=lax.Precision.HIGHEST,
+        preferred_element_type=jnp.float32,
+    )
+
+
+def mixed_weights(cls, score, cand, stats, table):
+    total = score.shape[1]
+    return pl.pallas_call(
+        weights_body,
+        in_specs=[pl.BlockSpec(memory_space=pltpu.SMEM)] + [pl.BlockSpec(memory_space=pltpu.VMEM)] * 4,
+        out_shape=[
+            jax.ShapeDtypeStruct((COEF, total), jnp.float32),
+            jax.ShapeDtypeStruct((1, total), jnp.float32),
+        ],
+        name="mixed_weights",
+    )(cls, score, cand, stats, table)
+
+
+def sums_body(*refs, number, pieces):
+    blocks, extras = refs[:number], refs[number : 2 * number]
+    refs = refs[2 * number :]
+    mixes, cands = refs[:pieces], refs[pieces : 2 * pieces]
+    back_ref, out_ref, weight_ref, mix, cand, planes = refs[2 * pieces :]
     i = pl.program_id(0)
     groups = weight_ref.shape[0]
-    total = score_ref.shape[1]
+    total = mix.shape[1]
     imag, odd = lane_signs()
 
     @pl.when(i == 0)
     def _():
-        tops = [stat_ref[2 * j : 2 * j + 1, :] for j in range(stat_ref.shape[0] // 2)]
-        top = functools.reduce(jnp.maximum, tops)
-        summed = jnp.zeros_like(top)
-        for j, other in enumerate(tops):
-            summed += stat_ref[2 * j + 1 : 2 * j + 2, :] * jnp.exp(other - top)
-        log_norm = top + jnp.log(summed)
-        norm_ref[...] = log_norm
-        weight = jnp.where(
-            cand_ref[0:1, :] >= 0.0, jnp.exp(score_ref[...] - log_norm), 0.0
-        )
-        mixed = lax.dot_general(
-            table_ref[...],
-            weight,
-            (((1,), (0,)), ((), ())),
-            precision=lax.Precision.HIGHEST,
-            preferred_element_type=jnp.float32,
-        )
-        hot = hot_masks(cand_ref[...], groups)
+        mixed = jnp.concatenate([ref[...] for ref in mixes], 1)
+        chosen = jnp.concatenate([ref[...] for ref in cands], 1)
+        hot = hot_masks(chosen, groups)
         summed = jnp.zeros((groups, total), jnp.float32)
         for q in range(CAND_OWN):
             summed += jnp.where(hot[q], mixed[q : q + 1], 0.0)
         weight_ref[...] = jnp.sum(summed, axis=1, keepdims=True)
         mix[...] = mixed
-
-    @pl.when(i < HALF)
+        cand[...] = chosen
+
+    @pl.when(i < HALF // SUM_STEP)
     def _():
-        hot = hot_masks(cand_ref[...], groups)
+        hot = hot_masks(cand[...], groups)
         block = 2 * CAND_OWN
-        mine = mix[pl.ds(pl.multiple_of(i * block, block), block), :]
-        halves = []
-        for ab in range(2):
-            dense = jnp.zeros((groups, total), jnp.float32)
-            for q in range(CAND_OWN):
-                at = ab * CAND_OWN + q
-                dense = jnp.where(hot[q], mine[at : at + 1], dense)
-            halves.append(dense)
-        weights = jnp.concatenate(halves, 0).astype(jnp.bfloat16)
         sign = jnp.where(imag == odd, 1.0, -1.0)
-        for piece, (first, last) in enumerate(PIECES):
-
-            @pl.when((i >= first) & (i < last))
-            def _():
-                made = jnp.dot(
-                    weights,
-                    lanes_of(pieces[piece], 0, TURNS),
-                    preferred_element_type=jnp.float32,
-                )
-                for t in range(TURNS):
-                    g1 = made[:groups, t * LANES : (t + 1) * LANES]
-                    g2 = made[groups:, t * LANES : (t + 1) * LANES]
-                    value = g1 + sign * pltpu.roll(g2, LANES // 2, 1)
-                    if piece == 0:
-                        value = jnp.where(i == 0, jnp.where(odd, g2, g1), value)
-                    start = pl.multiple_of((i * TURNS + t) * groups, groups)
-                    planes[pl.ds(start, groups), :] = value
-
-        for t in range(TAIL):
-
-            @pl.when(i == t)
-            def _():
-                made = jnp.dot(
-                    weights, lanes_of(tails[t // 2], 0, 1), preferred_element_type=jnp.float32
-                )
-                g1, g2 = made[:groups], made[groups:]
-                value = g1
-                if t > 0:
-                    value = g1 + jnp.where(imag, -1.0, 1.0) * pltpu.roll(g2, LANES // 2, 1)
-                rows = pl.ds((BODY + t // 2) * groups, groups)
-                if t % 2:
-                    value = jnp.where(odd, value, planes[rows, :])
-                planes[rows, :] = value
-
-    @pl.when(i >= HALF)
+        for u in range(SUM_STEP):
+            g = i * SUM_STEP + u
+            mine = mix[pl.ds(pl.multiple_of(g * block, block), block), :]
+            halves = []
+            for ab in range(2):
+                dense = jnp.zeros((groups, total), jnp.float32)
+                for q in range(CAND_OWN):
+                    at = ab * CAND_OWN + q
+                    dense = jnp.where(hot[q], mine[at : at + 1], dense)
+                halves.append(dense)
+            weights = jnp.concatenate(halves, 0).astype(jnp.bfloat16)
+            made = jnp.dot(
+                weights, lanes_of(blocks, u * TURNS, TURNS), preferred_element_type=jnp.float32
+            )
+            for t in range(TURNS):
+                g1 = made[:groups, t * LANES : (t + 1) * LANES]
+                g2 = made[groups:, t * LANES : (t + 1) * LANES]
+                value = g1 + sign * pltpu.roll(g2, LANES // 2, 1)
+                if u == 0:
+                    value = jnp.where(i == 0, jnp.where(odd, g2, g1), value)
+                start = pl.multiple_of((g * TURNS + t) * groups, groups)
+                planes[pl.ds(start, groups), :] = value
+
+            for t in range(TAIL):
+                if t % SUM_STEP != u:
+                    continue
+
+                @pl.when(g == t)
+                def _():
+                    made = jnp.dot(
+                        weights, lanes_of(extras, t // 2, 1), preferred_element_type=jnp.float32
+                    )
+                    g1, g2 = made[:groups], made[groups:]
+                    value = g1
+                    if t > 0:
+                        value = g1 + jnp.where(imag, -1.0, 1.0) * pltpu.roll(g2, LANES // 2, 1)
+                    rows = pl.ds((BODY + t // 2) * groups, groups)
+                    if t % 2:
+                        value = jnp.where(odd, value, planes[rows, :])
+                    planes[rows, :] = value
+
+    @pl.when(i >= HALF // SUM_STEP)
     def _():
         block, span, _ = out_ref.shape
-        first = (i - HALF) * block
+        first = (i - HALF // SUM_STEP) * block
         back = back_ref[...]
         for c in range(block):
             turned = planes[pl.ds(first + c, CHUNKS, stride=groups), :].T
@@ -645,46 +632,42 @@
             out_ref[c, :, HARM:] = placed[span:]
 
 
-def piece_spec(piece, sources, count):
-    first, last = PIECES[piece]
-    return pl.BlockSpec(
-        (sources, TURNS, count, LANES),
-        lambda i: (0, jnp.clip(i, first, last - 1) - first, 0, 0),
-    )
-
-
-def sums(gathered, score, cand, stats, table, back, groups, span):
-    sources, _, count, _ = gathered[0].shape
-    total = sources * count
-    size = sum(piece.size for piece in gathered)
+def sums(blocks, mixes, cands, back, groups, span):
+    count = blocks[0].shape[1]
+    total = len(blocks) * count
+    size = blocks[0].size * len(blocks)
     block = 8
+    steps = HALF // SUM_STEP
     whole = lambda i: (0, 0)
     return pl.pallas_call(
-        sums_body,
-        grid=(HALF + groups // block,),
+        functools.partial(sums_body, number=len(blocks), pieces=len(mixes)),
+        grid=(steps + groups // block,),
         in_specs=[
-            *[piece_spec(piece, sources, count) for piece in range(len(PIECES))],
-            *extra_specs(sources, count)[: TAIL // 2],
-            pl.BlockSpec(score.shape, whole),
-            pl.BlockSpec(cand.shape, whole),
-            pl.BlockSpec(stats.shape, whole),
-            pl.BlockSpec(table.shape, whole),
-            pl.BlockSpec(back.shape, whole),
+            *[
+                pl.BlockSpec(
+                    (SUM_STEP * TURNS, count, LANES), lambda i: (jnp.minimum(i, steps - 1), 0, 0)
+                )
+                for _ in blocks
+            ],
+            *[
+                pl.BlockSpec((EXTRA, count, LANES), lambda i: (BODY // EXTRA, 0, 0))
+                for _ in blocks
+            ],
+            *[pl.BlockSpec(array.shape, whole) for array in (*mixes, *cands, back)],
         ],
         out_specs=[
             pl.BlockSpec(
-                (block, span, 2 * HARM), lambda i: (jnp.maximum(i - HALF, 0), 0, 0)
+                (block, span, 2 * HARM), lambda i: (jnp.maximum(i - steps, 0), 0, 0)
             ),
             pl.BlockSpec((groups, 1), whole),
-            pl.BlockSpec((1, total), whole),
         ],
         out_shape=[
             jax.ShapeDtypeStruct((groups, span, 2 * HARM), jnp.float32),
             jax.ShapeDtypeStruct((groups, 1), jnp.float32),
-            jax.ShapeDtypeStruct((1, total), jnp.float32),
         ],
         scratch_shapes=[
             pltpu.VMEM((COEF, total), jnp.float32),
+            pltpu.VMEM((2 * CAND_OWN, total), jnp.float32),
             pltpu.VMEM((CHUNKS * groups, LANES), jnp.float32),
         ],
         compiler_params=pltpu.CompilerParams(vmem_limit_bytes=48 << 20),
@@ -694,12 +677,24 @@
             transcendentals=0,
         ),
         name="sums",
-    )(*gathered, *[gathered[0]] * (TAIL // 2), score, cand, stats, table, back)
-
-
-def spread(outgoing):
-    arrived = lax.all_to_all(outgoing, "prt", split_axis=0, concat_axis=0, tiled=True)
-    return lax.all_gather(arrived, "cls", axis=0, tiled=True)
+    )(*blocks, *blocks, *mixes, *cands, back)
+
+
+def hop(value, axis, distance):
+    size = lax.axis_size(axis)
+    return lax.ppermute(value, axis, [(i, i ^ distance) for i in range(size)])
+
+
+def spread(own, d):
+    n_cls = lax.axis_size("cls")
+    blocks = {0: own}
+    for j in sorted(range(2, n_cls, 2), key=lambda j: bin(j).count("1")):
+        bits = [bit for bit in range(1, n_cls.bit_length()) if j >> bit & 1]
+        way = 1 << bits[d % len(bits)]
+        blocks[j] = hop(blocks[j ^ way], "cls", way)
+    for j in range(0, n_cls, 2):
+        blocks[j + 1] = hop(blocks[j], "cls", 1)
+    return [blocks[j] for j in range(n_cls)]
 
 
 def gather_device(particles, references, owner_groups, class_order):
@@ -713,24 +708,25 @@
     back = jnp.asarray(unselector(), jnp.bfloat16)
     table = jnp.asarray(rotation_table())
     picks = class_order[:, :, :CAND_OWN].reshape(count, OWN_TOP * CAND_OWN)
-    outgoing = arrange_particles(particles, owner_groups, picks, n_prt, sel, masks)
-    gathered = [spread(piece) for piece in outgoing]
-    arranged, norms = arrange_references(
-        references, prt.reshape(1).astype(jnp.int32), n_prt, sel, masks
-    )
-    coef, cand = cross_first(gathered[0], arranged, norms, cls.reshape(1).astype(jnp.int32))
-    coefs = [lax.psum(coef, "prt")]
-    for piece in range(1, len(PIECES)):
-        coef = cross_later(gathered[piece], arranged, cand, piece)
-        coef, coefs[-1] = lax.optimization_barrier((coef, coefs[-1]))
-        coefs.append(lax.psum(coef, "prt"))
+    cls, prt = (index.reshape(1).astype(jnp.int32) for index in (cls, prt))
+    outgoing = arrange_particles(prt, particles, owner_groups, picks, n_prt, sel, masks)
+    arrived = [hop(block, "prt", d) if d else block for d, block in enumerate(outgoing)]
+    blocks = [spread(block, d) for d, block in enumerate(arrived)]
+    arranged, norms = arrange_references(references, prt, n_prt, sel, masks)
     scale = 2.0 / math.sqrt(cycles * width)
-    score, stat = scores(coefs, cand, table, scale)
-    stats = lax.all_gather(stat, "cls", axis=0, tiled=True)
-    class_sums, class_weights, log_norm = sums(
-        gathered, score, cand, stats, table, back, groups, span
-    )
-    own = lax.dynamic_slice(log_norm[0], ((cls * n_prt + prt) * count,), (count,))
+    coefs, cands = [], []
+    for d in range(n_prt):
+        coef, cand = cross_coefficients(blocks[d], arranged, norms, cls)
+        coefs.append(hop(coef, "prt", d) if d else coef)
+        cands.append(cand)
+    score, stat = scores(coefs, cands[0], table, scale)
+    stats = lax.all_gather(stat.reshape(1, *stat.shape), "cls", axis=0, tiled=True)
+    mix, log_norm = mixed_weights(cls, score, cands[0], stats, table)
+    mixes = [hop(mix, "prt", d) if d else mix for d in range(n_prt)]
+    class_sums, class_weights = sums(
+        [block for piece in blocks for block in piece], mixes, cands, back, groups, span
+    )
+    own = log_norm[0, :count]
     return class_sums, class_weights[:, 0], own
 
 
@@ -739,7 +735,9 @@
     count, cycles, _ = particles.shape
     groups = references.shape[0]
     cap = max(2, 2 * count * OWN_TOP // n_cls)
+    powers = n_cls & (n_cls - 1) == 0 and n_prt & (n_prt - 1) == 0
     fits = 4 * cycles == LANES * n_prt and n_cls * CAND_OWN <= LANES and groups % 16 == 0
+    fits = fits and powers and n_cls * count == LANES
     plan = gather_device if cap >= count and fits else dispatch_device
     return plan(particles, references, owner_groups, class_order)
 

time: 389 us -> 220 us (0.57)
  waiting for transfers between devices: 232 us -> 68.8 us
  blocking collectives: 47.3 us -> 9.85 us
  starting transfers between devices: 8.77 us -> 40.8 us
  local copies, waits for them, and re-layouts: 16.1 us -> 29.8 us
  between operations: 14.3 us -> 1.09 us
    psum x4 -> x0, waiting for transfers between devices: 129 us -> none  [the longest x3 98.7 us: gather_device(): coefs.append(lax.psum(coef, 'prt'))]
    all_gather x4 -> x0, waiting for transfers between devices: 103 us -> none  [spread(): return lax.all_gather(arrived, 'cls', axis=0, tiled=True)]
    ppermute x0 -> x37, waiting for transfers between devices: none -> 68.8 us  [hop(): return lax.ppermute(value, axis, [(i, i ^ distance) for i in range(size)])]
    ppermute x0 -> x37, starting transfers between devices: none -> 40.8 us  [hop(): return lax.ppermute(value, axis, [(i, i ^ distance) for i in range(size)])]
    all_to_all x2 -> x0, blocking collectives: 38.1 us -> none  [spread(): lax.all_to_all(outgoing, 'prt', split_axis=0, concat_axis=0, tiled=True)]
    unnamed x32 -> x111, local copies, waits for them, and re-layouts: 14.6 us -> 27.7 us
    all_to_all x2 -> x0, starting transfers between devices: 8.49 us -> none  [spread(): lax.all_to_all(outgoing, 'prt', split_axis=0, concat_axis=0, tiled=True)]
    pallas_call x6 -> x7, Pallas kernels: 54.1 us -> 54.4 us  [the longest x4 23.3 us: cross_coefficients(): pl.pallas_call(cross_body, grid_spec=pltpu.PrefetchScalarGridSpec(num_sca...]
  transfers between devices with their start and end apart: 10 -> 37, of which waited for: 7 -> 10; matrix products, arithmetic and copies ran while one was open for 0% -> 1% of each run, Pallas kernels for 8% -> 16%
where the time goes in v3:
time: 220 us; the launch traced here: 219 us
  waiting for transfers between devices  68.8 us (31%)
  Pallas kernels  68.4 us (31%)
  starting transfers between devices  40.8 us (19%)
  local copies, waits for them, and re-layouts  29.8 us (14%)
  blocking collectives  9.85 us (4%)
    ppermute x37, waiting for transfers between devices, hop(): return lax.ppermute(value, axis, [(i, i ^ distance) for i in range(size)])  68.8 us
    ppermute x37, starting transfers between devices, hop(): return lax.ppermute(value, axis, [(i, i ^ distance) for i in range(size)])  40.8 us
    unnamed x111, local copies, waits for them, and re-layouts  27.7 us
    pallas_call x4, Pallas kernels, cross_coefficients(): pl.pallas_call(cross_body, grid_spec=pltpu.PrefetchScalarGridSpec(num_sca...  23.3 us
    pallas_call x1, Pallas kernels, sums(): pl.pallas_call(functools.partial(sums_body, number=len(blocks), pieces=le...  20 us
    pallas_call x1, Pallas kernels, arrange_references(): pl.pallas_call(reference_body, grid_spec=pltpu.PrefetchScalarGridSpec(num...  12 us
    all_gather x1, blocking collectives, gather_device(): lax.all_gather(stat.reshape(1, *stat.shape), 'cls', axis=0, tiled=True)  9.85 us
    pallas_call x1, Pallas kernels, arrange_particles(): pl.pallas_call(particle_body, in_specs=[pl.BlockSpec(memory_space=pltpu.S...  8.94 us
  transfers between devices with their start and end apart: 37, of which 10 were waited for; matrix products, arithmetic and copies ran while one was open for 1% of the time, Pallas kernels for 16%

profile of v3, /device:TPU:0, one launch (start us, length us, event | category | flops | bytes accessed | tf_op | source)
XLA Modules:
  0.0 219.4 jit_solution(16585582619889246818)
XLA Ops:
  5.4 8.9 %arrange_particles.1 = (bf16[129,16,128]{2,1,0:T(8,128)(2,1)S(1)}, bf16[129,16,128]{2,1,0:T(8,128)(2,1)S(1)}, bf16[129,16,128]{2,1,0:T(8,128)(2,1)S(1)}, bf16[129,16,128]{2,1,0:T(8,128)(2,1)S(1)}) custom-call(s32[1]{0:T(128)} %bitcast.at_ref, bf16[16,128,512]{2,1,0:T(8,128)(2,1)S(1)} %copy-done.42, s32[16,4]{1,0:T(8,128)S(1)} %copy.16.owner_ref, ...), custom_call_target="tpu_custom_call" | custom-call | flops 268435456 | bytes 4194304 | tf_op jit(solution)/shard_map/arrange_particles/pallas_call | solution.py:254
  14.4 3.1 %collective-permute-start.7 = (bf16[129,16,128]{2,1,0:T(8,128)(2,1)S(1)}, bf16[129,16,128]{2,1,0:T(8,128)(2,1)S(1)}, u32[]{:S(2)}, u32[]{:S(2)}) collective-permute-start(bf16[129,16,128]{2,1,0:T(8,128)(2,1)S(1)} %get-tuple-element.24), channel_id=1, source_target_pairs={{0,1},{1,0},{2,3},{3,2},{4,5},{5,4},{6,7},{7,6},{8,9},{9,8},{10,11... | collective-permute-start | bytes 1585160 | tf_op jit(solution)/shard_map/ppermute | solution.py:685
  17.5 2.6 %collective-permute-start.15 = (bf16[129,16,128]{2,1,0:T(8,128)(2,1)S(1)}, bf16[129,16,128]{2,1,0:T(8,128)(2,1)S(1)}, u32[]{:S(2)}, u32[]{:S(2)}) collective-permute-start(bf16[129,16,128]{2,1,0:T(8,128)(2,1)S(1)} %get-tuple-element.25), channel_id=1, source_target_pairs={{0,2},{1,3},{2,0},{3,1},{4,6},{5,7},{6,4},{7,5},{8,10},{9,11},{10,... | collective-permute-start | bytes 1585160 | tf_op jit(solution)/shard_map/ppermute | solution.py:685
  23.3 16.7 %collective-permute-done.7.refs_0_.refs_8_.refs_40_ = bf16[129,16,128]{2,1,0:T(8,128)(2,1)S(1)} collective-permute-done((bf16[129,16,128]{2,1,0:T(8,128)(2,1)S(1)}, bf16[129,16,128]{2,1,0:T(8,128)(2,1)S(1)}, u32[]{:S(2)}, u32[]{:S(2)}) %collective-permute-start.7) | collective-permute-done | bytes 528416 | tf_op jit(solution)/shard_map/ppermute | solution.py:685
  41.7 14.2 %collective-permute-done.15.refs_0_.refs_8_.refs_16_.refs_48_ = bf16[129,16,128]{2,1,0:T(8,128)(2,1)S(1)} collective-permute-done((bf16[129,16,128]{2,1,0:T(8,128)(2,1)S(1)}, bf16[129,16,128]{2,1,0:T(8,128)(2,1)S(1)}, u32[]{:S(2)}, u32[]{:S(2)}) %collective-permute-start.15) | collective-permute-done | bytes 528416 | tf_op jit(solution)/shard_map/ppermute | solution.py:685
  59.6 8.9 %collective-permute-done.9.refs_2_.refs_10_.refs_42_ = bf16[129,16,128]{2,1,0:T(8,128)(2,1)S(1)} collective-permute-done((bf16[129,16,128]{2,1,0:T(8,128)(2,1)S(1)}, bf16[129,16,128]{2,1,0:T(8,128)(2,1)S(1)}, u32[]{:S(2)}, u32[]{:S(2)}) %collective-permute-start.9) | collective-permute-done | bytes 528416 | tf_op jit(solution)/shard_map/ppermute | solution.py:685
  68.5 2.6 %collective-permute-start.27 = (bf16[129,16,128]{2,1,0:T(8,128)(2,1)S(1)}, bf16[129,16,128]{2,1,0:T(8,128)(2,1)S(1)}, u32[]{:S(2)}, u32[]{:S(2)}) collective-permute-start(bf16[129,16,128]{2,1,0:T(8,128)(2,1)S(1)} %collective-permute-done.23.refs_0_.refs_8_.refs_24_.refs_56_), channel_id=1, source_target_pairs={{0,16},{4,20},{8,24},{12,28},{16,0},{20,4},{24,8},{28,12},{1,17},{... | collective-permute-start | bytes 1585160 | tf_op jit(solution)/shard_map/ppermute | solution.py:685
  71.9 2.5 %collective-permute-start.25 = (bf16[129,16,128]{2,1,0:T(8,128)(2,1)S(1)}, bf16[129,16,128]{2,1,0:T(8,128)(2,1)S(1)}, u32[]{:S(2)}, u32[]{:S(2)}) collective-permute-start(bf16[129,16,128]{2,1,0:T(8,128)(2,1)S(1)} %collective-permute-done.23.refs_0_.refs_8_.refs_24_.refs_56_), channel_id=1, source_target_pairs={{0,8},{4,12},{8,0},{12,4},{16,24},{20,28},{24,16},{28,20},{1,9},{5... | collective-permute-start | bytes 1585160 | tf_op jit(solution)/shard_map/ppermute | solution.py:685
  74.3 5.5 %collective-permute-done.17.refs_2_.refs_10_.refs_18_.refs_50_ = bf16[129,16,128]{2,1,0:T(8,128)(2,1)S(1)} collective-permute-done((bf16[129,16,128]{2,1,0:T(8,128)(2,1)S(1)}, bf16[129,16,128]{2,1,0:T(8,128)(2,1)S(1)}, u32[]{:S(2)}, u32[]{:S(2)}) %collective-permute-start.17) | collective-permute-done | bytes 528416 | tf_op jit(solution)/shard_map/ppermute | solution.py:685
  83.9 2.6 %collective-permute-start.13 = (bf16[129,16,128]{2,1,0:T(8,128)(2,1)S(1)}, bf16[129,16,128]{2,1,0:T(8,128)(2,1)S(1)}, u32[]{:S(2)}, u32[]{:S(2)}) collective-permute-start(bf16[129,16,128]{2,1,0:T(8,128)(2,1)S(1)} %collective-permute-done.9.refs_2_.refs_10_.refs_42_), channel_id=1, source_target_pairs={{0,16},{4,20},{8,24},{12,28},{16,0},{20,4},{24,8},{28,12},{1,17},{... | collective-permute-start | bytes 1585160 | tf_op jit(solution)/shard_map/ppermute | solution.py:685
  86.5 4.6 %collective-permute-done.25.refs_2_.refs_10_.refs_26_.refs_58_ = bf16[129,16,128]{2,1,0:T(8,128)(2,1)S(1)} collective-permute-done((bf16[129,16,128]{2,1,0:T(8,128)(2,1)S(1)}, bf16[129,16,128]{2,1,0:T(8,128)(2,1)S(1)}, u32[]{:S(2)}, u32[]{:S(2)}) %collective-permute-start.25) | collective-permute-done | bytes 528416 | tf_op jit(solution)/shard_map/ppermute | solution.py:685
  95.3 6.5 %collective-permute-done.5.refs_6_.refs_14_.refs_38_ = bf16[129,16,128]{2,1,0:T(8,128)(2,1)} collective-permute-done((bf16[129,16,128]{2,1,0:T(8,128)(2,1)S(1)}, bf16[129,16,128]{2,1,0:T(8,128)(2,1)}, u32[]{:S(2)}, u32[]{:S(2)}) %collective-permute-start.5) | collective-permute-done | bytes 528416 | tf_op jit(solution)/shard_map/ppermute | solution.py:685
  106.8 3.8 %collective-permute-done.21.refs_6_.refs_14_.refs_22_.refs_54_ = bf16[129,16,128]{2,1,0:T(8,128)(2,1)} collective-permute-done((bf16[129,16,128]{2,1,0:T(8,128)(2,1)S(1)}, bf16[129,16,128]{2,1,0:T(8,128)(2,1)}, u32[]{:S(2)}, u32[]{:S(2)}) %collective-permute-start.21) | collective-permute-done | bytes 528416 | tf_op jit(solution)/shard_map/ppermute | solution.py:685
  113.6 4.2 %collective-permute-done.29.refs_6_.refs_14_.refs_30_.refs_62_ = bf16[129,16,128]{2,1,0:T(8,128)(2,1)S(1)} collective-permute-done((bf16[129,16,128]{2,1,0:T(8,128)(2,1)S(1)}, bf16[129,16,128]{2,1,0:T(8,128)(2,1)S(1)}, u32[]{:S(2)}, u32[]{:S(2)}) %collective-permute-start.29) | collective-permute-done | bytes 528416 | tf_op jit(solution)/shard_map/ppermute | solution.py:685
  124.1 3.4 %copy-done.41 = bf16[64,128,512]{2,1,0:T(8,128)(2,1)S(1)} copy-done((bf16[64,128,512]{2,1,0:T(8,128)(2,1)S(1)}, bf16[64,128,512]{2,1,0:T(8,128)(2,1)}, u32[]{:S(2)}) %copy-start.41) | copy-done | bytes 8388632
  129.1 12.0 %arrange_references.1 = (bf16[128,64,128]{2,1,0:T(8,128)(2,1)S(1)}, f32[64,128]{1,0:T(8,128)S(1)}) custom-call(s32[1]{0:T(128)} %bitcast.at_ref, bf16[64,128,512]{2,1,0:T(8,128)(2,1)S(1)} %copy-done.41, bf16[128,256]{1,0:T(8,128)(2,1)S(1)} %copy-done.44, bf16[2,256]{1,0:T(2,128)(2,1)S(1)} %copy-done.51), custom_call_target="tpu_custom_call" | custom-call | flops 268435456 | bytes 4194304 | tf_op jit(solution)/shard_map/arrange_references/pallas_call | solution.py:295
  141.3 5.3 %cross_coefficients.7 = (f32[144,128]{1,0:T(8,128)S(1)}, f32[8,128]{1,0:T(8,128)S(1)}) custom-call(s32[1]{0:T(128)} %bitcast.2.at_ref, bf16[129,16,128]{2,1,0:T(8,128)(2,1)S(1)} %collective-permute-done.23.refs_0_.refs_8_.refs_24_.refs_56_, bf16[129,16,128]{2,1,0:T(8,128)(2,1)S(1)} %copy-done.20, bf16[129,16,128]{2,1,0:T(8,128)(2,1)S(1)} %copy-done.18, ...), custom_call_target="tpu_custom_call" | custom-call | flops 541065216 | bytes 4227072 | tf_op jit(solution)/shard_map/cross_coefficients/pallas_call | solution.py:428
  146.6 5.2 %cross_coefficients.5 = (f32[144,128]{1,0:T(8,128)S(1)}, f32[8,128]{1,0:T(8,128)S(1)}) custom-call(s32[1]{0:T(128)} %bitcast.2.at_ref, bf16[129,16,128]{2,1,0:T(8,128)(2,1)S(1)} %collective-permute-done.7.refs_0_.refs_8_.refs_40_, bf16[129,16,128]{2,1,0:T(8,128)(2,1)S(1)} %copy-done.7, bf16[129,16,128]{2,1,0:T(8,128)(2,1)S(1)} %copy-done.5, ...), custom_call_target="tpu_custom_call" | custom-call | flops 541065216 | bytes 4227072 | tf_op jit(solution)/shard_map/cross_coefficients/pallas_call | solution.py:428
  151.9 4.0 %collective-permute-start.31 = (f32[144,128]{1,0:T(8,128)S(1)}, f32[144,128]{1,0:T(8,128)S(1)}, u32[]{:S(2)}, u32[]{:S(2)}) collective-permute-start(f32[144,128]{1,0:T(8,128)S(1)} %get-tuple-element.30), channel_id=1, source_target_pairs={{0,1},{1,0},{2,3},{3,2},{4,5},{5,4},{6,7},{7,6},{8,9},{9,8},{10,11... | collective-permute-start | bytes 221192 | tf_op jit(solution)/shard_map/ppermute | solution.py:685
  155.9 6.3 %cross_coefficients.6 = (f32[144,128]{1,0:T(8,128)S(1)}, f32[8,128]{1,0:T(8,128)S(1)}) custom-call(s32[1]{0:T(128)} %bitcast.2.at_ref, bf16[129,16,128]{2,1,0:T(8,128)(2,1)S(1)} %collective-permute-done.15.refs_0_.refs_8_.refs_16_.refs_48_, bf16[129,16,128]{2,1,0:T(8,128)(2,1)S(1)} %copy-done.14, bf16[129,16,128]{2,1,0:T(8,128)(2,1)S(1)} %copy-done.12, ...), custom_call_target="tpu_custom_call" | custom-call | flops 541065216 | bytes 4227072 | tf_op jit(solution)/shard_map/cross_coefficients/pallas_call | solution.py:428
  164.9 6.6 %cross_coefficients.4 = (f32[144,128]{1,0:T(8,128)S(1)}, f32[8,128]{1,0:T(8,128)S(1)}) custom-call(s32[1]{0:T(128)} %bitcast.2.at_ref, bf16[129,16,128]{2,1,0:T(8,128)(2,1)S(1)} %get-tuple-element.23.refs_0_.refs_8_.refs_32_, bf16[129,16,128]{2,1,0:T(8,128)(2,1)} %collective-permute-done.refs_1_.refs_9_.refs_33_, ...), custom_call_target="tpu_custom_call" | custom-call | flops 541065216 | bytes 4227072 | tf_op jit(solution)/shard_map/cross_coefficients/pallas_call | solution.py:428
  175.4 9.8 %all-gather.1.stat_ref = f32[8,2,128]{2,1,0:T(2,128)} all-gather(f32[1,2,128]{2,1,0:T(2,128)} %bitcast.9), channel_id=2, replica_groups=mesh['cls'=8,'prt'=4] {'cls'}, dimensions={0}, use_global_device_ids=true | all-gather | bytes 9216 | tf_op jit(solution)/shard_map/all_gather | solution.py:723
  194.5 2.6 %collective-permute-done.35.refs_66_ = f32[144,128]{1,0:T(8,128)S(1)} collective-permute-done((f32[144,128]{1,0:T(8,128)}, f32[144,128]{1,0:T(8,128)S(1)}, u32[]{:S(2)}, u32[]{:S(2)}) %collective-permute-start.35) | collective-permute-done | bytes 73760 | tf_op jit(solution)/shard_map/ppermute | solution.py:685
  198.7 20.0 %sums.1 = (f32[64,32,512]{2,1,0:T(8,128)}, f32[64,1]{1,0:T(8,128)S(1)}) custom-call(bf16[129,16,128]{2,1,0:T(8,128)(2,1)S(1)} %get-tuple-element.23.refs_0_.refs_8_.refs_32_, bf16[129,16,128]{2,1,0:T(8,128)(2,1)} %collective-permute-done.refs_1_.refs_9_.refs_33_, bf16[129,16,128]{2,1,0:T(8,128)(2,1)S(1)} %collective-permute-done.1.refs_2_.refs_10_.refs_34_, ...), custom_call_target="tpu_custom_call" | custom-call | flops 2164260864 | bytes 21102592 | tf_op jit(solution)/shard_map/sums/pallas_call | solution.py:642
  (175 shorter events, 56.4 us)
Async XLA Ops:
  14.4 25.6 %collective-permute-start.7 = (bf16[129,16,128]{2,1,0:T(8,128)(2,1)S(1)}, bf16[129,16,128]{2,1,0:T(8,128)(2,1)S(1)}, u32[]{:S(2)}, u32[]{:S(2)}) collective-permute-start(bf16[129,16,128]{2,1,0:T(8,128)(2,1)S(1)} %get-tuple-element.24), channel_id=1, source_target_pairs={{0,1},{1,0},{2,3},{3,2},{4,5},{5,4},{6,7},{7,6},{8,9},{9,8},{10,11... | collective-permute-start | bytes 1585160 | tf_op jit(solution)/shard_map/ppermute | solution.py:685
  17.5 38.5 %collective-permute-start.15 = (bf16[129,16,128]{2,1,0:T(8,128)(2,1)S(1)}, bf16[129,16,128]{2,1,0:T(8,128)(2,1)S(1)}, u32[]{:S(2)}, u32[]{:S(2)}) collective-permute-start(bf16[129,16,128]{2,1,0:T(8,128)(2,1)S(1)} %get-tuple-element.25), channel_id=1, source_target_pairs={{0,2},{1,3},{2,0},{3,1},{4,6},{5,7},{6,4},{7,5},{8,10},{9,11},{10,... | collective-permute-start | bytes 1585160 | tf_op jit(solution)/shard_map/ppermute | solution.py:685
  20.1 37.4 %collective-permute-start.23 = (bf16[129,16,128]{2,1,0:T(8,128)(2,1)S(1)}, bf16[129,16,128]{2,1,0:T(8,128)(2,1)S(1)}, u32[]{:S(2)}, u32[]{:S(2)}) collective-permute-start(bf16[129,16,128]{2,1,0:T(8,128)(2,1)S(1)} %get-tuple-element.26), channel_id=1, source_target_pairs={{0,3},{1,2},{2,1},{3,0},{4,7},{5,6},{6,5},{7,4},{8,11},{9,10},{10,... | collective-permute-start | bytes 1585160 | tf_op jit(solution)/shard_map/ppermute | solution.py:685
  20.1 37.4 %collective-permute-start.3 = (bf16[129,16,128]{2,1,0:T(8,128)(2,1)S(1)}, bf16[129,16,128]{2,1,0:T(8,128)(2,1)S(1)}, u32[]{:S(2)}, u32[]{:S(2)}) collective-permute-start(bf16[129,16,128]{2,1,0:T(8,128)(2,1)S(1)} %get-tuple-element.23.refs_0_.refs_8_.refs_32_), channel_id=1, source_target_pairs={{0,16},{4,20},{8,24},{12,28},{16,0},{20,4},{24,8},{28,12},{1,17},{... | collective-permute-start | bytes 1585160 | tf_op jit(solution)/shard_map/ppermute | solution.py:685
  21.8 37.3 %collective-permute-start.1 = (bf16[129,16,128]{2,1,0:T(8,128)(2,1)S(1)}, bf16[129,16,128]{2,1,0:T(8,128)(2,1)S(1)}, u32[]{:S(2)}, u32[]{:S(2)}) collective-permute-start(bf16[129,16,128]{2,1,0:T(8,128)(2,1)S(1)} %get-tuple-element.23.refs_0_.refs_8_.refs_32_), channel_id=1, source_target_pairs={{0,8},{4,12},{8,0},{12,4},{16,24},{20,28},{24,16},{28,20},{1,9},{5... | collective-permute-start | bytes 1585160 | tf_op jit(solution)/shard_map/ppermute | solution.py:685
  40.0 19.6 %collective-permute-start.11 = (bf16[129,16,128]{2,1,0:T(8,128)(2,1)S(1)}, bf16[129,16,128]{2,1,0:T(8,128)(2,1)S(1)}, u32[]{:S(2)}, u32[]{:S(2)}) collective-permute-start(bf16[129,16,128]{2,1,0:T(8,128)(2,1)S(1)} %collective-permute-done.7.refs_0_.refs_8_.refs_40_), channel_id=1, source_target_pairs={{0,16},{4,20},{8,24},{12,28},{16,0},{20,4},{24,8},{28,12},{1,17},{... | collective-permute-start | bytes 1585160 | tf_op jit(solution)/shard_map/ppermute | solution.py:685
  57.5 16.9 %collective-permute-start.19 = (bf16[129,16,128]{2,1,0:T(8,128)(2,1)S(1)}, bf16[129,16,128]{2,1,0:T(8,128)(2,1)S(1)}, u32[]{:S(2)}, u32[]{:S(2)}) collective-permute-start(bf16[129,16,128]{2,1,0:T(8,128)(2,1)S(1)} %collective-permute-done.15.refs_0_.refs_8_.refs_16_.refs_48_), channel_id=1, source_target_pairs={{0,16},{4,20},{8,24},{12,28},{16,0},{20,4},{24,8},{28,12},{1,17},{... | collective-permute-start | bytes 1585160 | tf_op jit(solution)/shard_map/ppermute | solution.py:685
  59.1 20.7 %collective-permute-start.17 = (bf16[129,16,128]{2,1,0:T(8,128)(2,1)S(1)}, bf16[129,16,128]{2,1,0:T(8,128)(2,1)S(1)}, u32[]{:S(2)}, u32[]{:S(2)}) collective-permute-start(bf16[129,16,128]{2,1,0:T(8,128)(2,1)S(1)} %collective-permute-done.15.refs_0_.refs_8_.refs_16_.refs_48_), channel_id=1, source_target_pairs={{0,8},{4,12},{8,0},{12,4},{16,24},{20,28},{24,16},{28,20},{1,9},{5... | collective-permute-start | bytes 1585160 | tf_op jit(solution)/shard_map/ppermute | solution.py:685
  59.6 22.7 %collective-permute-start.16 = (bf16[129,16,128]{2,1,0:T(8,128)(2,1)S(1)}, bf16[129,16,128]{2,1,0:T(8,128)(2,1)S(1)}, u32[]{:S(2)}, u32[]{:S(2)}) collective-permute-start(bf16[129,16,128]{2,1,0:T(8,128)(2,1)S(1)} %collective-permute-done.15.refs_0_.refs_8_.refs_16_.refs_48_), channel_id=1, source_target_pairs={{0,4},{4,0},{8,12},{12,8},{16,20},{20,16},{24,28},{28,24},{1,5},{5... | collective-permute-start | bytes 1585160 | tf_op jit(solution)/shard_map/ppermute | solution.py:685
  68.5 15.5 %collective-permute-start.27 = (bf16[129,16,128]{2,1,0:T(8,128)(2,1)S(1)}, bf16[129,16,128]{2,1,0:T(8,128)(2,1)S(1)}, u32[]{:S(2)}, u32[]{:S(2)}) collective-permute-start(bf16[129,16,128]{2,1,0:T(8,128)(2,1)S(1)} %collective-permute-done.23.refs_0_.refs_8_.refs_24_.refs_56_), channel_id=1, source_target_pairs={{0,16},{4,20},{8,24},{12,28},{16,0},{20,4},{24,8},{28,12},{1,17},{... | collective-permute-start | bytes 1585160 | tf_op jit(solution)/shard_map/ppermute | solution.py:685
  71.9 19.3 %collective-permute-start.25 = (bf16[129,16,128]{2,1,0:T(8,128)(2,1)S(1)}, bf16[129,16,128]{2,1,0:T(8,128)(2,1)S(1)}, u32[]{:S(2)}, u32[]{:S(2)}) collective-permute-start(bf16[129,16,128]{2,1,0:T(8,128)(2,1)S(1)} %collective-permute-done.23.refs_0_.refs_8_.refs_24_.refs_56_), channel_id=1, source_target_pairs={{0,8},{4,12},{8,0},{12,4},{16,24},{20,28},{24,16},{28,20},{1,9},{5... | collective-permute-start | bytes 1585160 | tf_op jit(solution)/shard_map/ppermute | solution.py:685
  74.3 17.6 %collective-permute-start.24 = (bf16[129,16,128]{2,1,0:T(8,128)(2,1)S(1)}, bf16[129,16,128]{2,1,0:T(8,128)(2,1)S(1)}, u32[]{:S(2)}, u32[]{:S(2)}) collective-permute-start(bf16[129,16,128]{2,1,0:T(8,128)(2,1)S(1)} %collective-permute-done.23.refs_0_.refs_8_.refs_24_.refs_56_), channel_id=1, source_target_pairs={{0,4},{4,0},{8,12},{12,8},{16,20},{20,16},{24,28},{28,24},{1,5},{5... | collective-permute-start | bytes 1585160 | tf_op jit(solution)/shard_map/ppermute | solution.py:685
  79.8 21.9 %collective-permute-start.5 = (bf16[129,16,128]{2,1,0:T(8,128)(2,1)S(1)}, bf16[129,16,128]{2,1,0:T(8,128)(2,1)}, u32[]{:S(2)}, u32[]{:S(2)}) collective-permute-start(bf16[129,16,128]{2,1,0:T(8,128)(2,1)S(1)} %collective-permute-done.3.refs_4_.refs_12_.refs_36_), channel_id=1, source_target_pairs={{0,8},{4,12},{8,0},{12,4},{16,24},{20,28},{24,16},{28,20},{1,9},{5... | collective-permute-start | bytes 1585160 | tf_op jit(solution)/shard_map/ppermute | solution.py:685
  83.1 19.5 %collective-permute-start.12 = (bf16[129,16,128]{2,1,0:T(8,128)(2,1)S(1)}, bf16[129,16,128]{2,1,0:T(8,128)(2,1)S(1)}, u32[]{:S(2)}, u32[]{:S(2)}) collective-permute-start(bf16[129,16,128]{2,1,0:T(8,128)(2,1)S(1)} %collective-permute-done.11.refs_4_.refs_12_.refs_44_), channel_id=1, source_target_pairs={{0,4},{4,0},{8,12},{12,8},{16,20},{20,16},{24,28},{28,24},{1,5},{5... | collective-permute-start | bytes 1585160 | tf_op jit(solution)/shard_map/ppermute | solution.py:685
  83.9 19.9 %collective-permute-start.13 = (bf16[129,16,128]{2,1,0:T(8,128)(2,1)S(1)}, bf16[129,16,128]{2,1,0:T(8,128)(2,1)S(1)}, u32[]{:S(2)}, u32[]{:S(2)}) collective-permute-start(bf16[129,16,128]{2,1,0:T(8,128)(2,1)S(1)} %collective-permute-done.9.refs_2_.refs_10_.refs_42_), channel_id=1, source_target_pairs={{0,16},{4,20},{8,24},{12,28},{16,0},{20,4},{24,8},{28,12},{1,17},{... | collective-permute-start | bytes 1585160 | tf_op jit(solution)/shard_map/ppermute | solution.py:685
  92.8 17.8 %collective-permute-start.21 = (bf16[129,16,128]{2,1,0:T(8,128)(2,1)S(1)}, bf16[129,16,128]{2,1,0:T(8,128)(2,1)}, u32[]{:S(2)}, u32[]{:S(2)}) collective-permute-start(bf16[129,16,128]{2,1,0:T(8,128)(2,1)S(1)} %collective-permute-done.19.refs_4_.refs_12_.refs_20_.refs_52_), channel_id=1, source_target_pairs={{0,8},{4,12},{8,0},{12,4},{16,24},{20,28},{24,16},{28,20},{1,9},{5... | collective-permute-start | bytes 1585160 | tf_op jit(solution)/shard_map/ppermute | solution.py:685
  103.4 14.4 %collective-permute-start.29 = (bf16[129,16,128]{2,1,0:T(8,128)(2,1)S(1)}, bf16[129,16,128]{2,1,0:T(8,128)(2,1)S(1)}, u32[]{:S(2)}, u32[]{:S(2)}) collective-permute-start(bf16[129,16,128]{2,1,0:T(8,128)(2,1)S(1)} %collective-permute-done.25.refs_2_.refs_10_.refs_26_.refs_58_), channel_id=1, source_target_pairs={{0,16},{4,20},{8,24},{12,28},{16,0},{20,4},{24,8},{28,12},{1,17},{... | collective-permute-start | bytes 1585160 | tf_op jit(solution)/shard_map/ppermute | solution.py:685
  103.8 14.8 %collective-permute-start.18 = (bf16[129,16,128]{2,1,0:T(8,128)(2,1)S(1)}, bf16[129,16,128]{2,1,0:T(8,128)(2,1)S(1)}, u32[]{:S(2)}, u32[]{:S(2)}) collective-permute-start(bf16[129,16,128]{2,1,0:T(8,128)(2,1)S(1)} %collective-permute-done.17.refs_2_.refs_10_.refs_18_.refs_50_), channel_id=1, source_target_pairs={{0,4},{4,0},{8,12},{12,8},{16,20},{20,16},{24,28},{28,24},{1,5},{5... | collective-permute-start | bytes 1585160 | tf_op jit(solution)/shard_map/ppermute | solution.py:685
  119.4 32.5 %collective-permute-start.22 = (bf16[129,16,128]{2,1,0:T(8,128)(2,1)}, bf16[129,16,128]{2,1,0:T(8,128)(2,1)}, u32[]{:S(2)}, u32[]{:S(2)}) collective-permute-start(bf16[129,16,128]{2,1,0:T(8,128)(2,1)} %collective-permute-done.21.refs_6_.refs_14_.refs_22_.refs_54_), channel_id=1, source_target_pairs={{0,4},{4,0},{8,12},{12,8},{16,20},{20,16},{24,28},{28,24},{1,5},{5... | collective-permute-start | bytes 1585160 | tf_op jit(solution)/shard_map/ppermute | solution.py:685
  120.7 41.4 %collective-permute-start = (bf16[129,16,128]{2,1,0:T(8,128)(2,1)S(1)}, bf16[129,16,128]{2,1,0:T(8,128)(2,1)}, u32[]{:S(2)}, u32[]{:S(2)}) collective-permute-start(bf16[129,16,128]{2,1,0:T(8,128)(2,1)S(1)} %get-tuple-element.23.refs_0_.refs_8_.refs_32_), channel_id=1, source_target_pairs={{0,4},{4,0},{8,12},{12,8},{16,20},{20,16},{24,28},{28,24},{1,5},{5... | collective-permute-start | bytes 1585160 | tf_op jit(solution)/shard_map/ppermute | solution.py:685
  121.5 41.8 %collective-permute-start.4 = (bf16[129,16,128]{2,1,0:T(8,128)(2,1)S(1)}, bf16[129,16,128]{2,1,0:T(8,128)(2,1)}, u32[]{:S(2)}, u32[]{:S(2)}) collective-permute-start(bf16[129,16,128]{2,1,0:T(8,128)(2,1)S(1)} %collective-permute-done.3.refs_4_.refs_12_.refs_36_), channel_id=1, source_target_pairs={{0,4},{4,0},{8,12},{12,8},{16,20},{20,16},{24,28},{28,24},{1,5},{5... | collective-permute-start | bytes 1585160 | tf_op jit(solution)/shard_map/ppermute | solution.py:685
  122.8 42.0 %collective-permute-start.2 = (bf16[129,16,128]{2,1,0:T(8,128)(2,1)S(1)}, bf16[129,16,128]{2,1,0:T(8,128)(2,1)}, u32[]{:S(2)}, u32[]{:S(2)}) collective-permute-start(bf16[129,16,128]{2,1,0:T(8,128)(2,1)S(1)} %collective-permute-done.1.refs_2_.refs_10_.refs_34_), channel_id=1, source_target_pairs={{0,4},{4,0},{8,12},{12,8},{16,20},{20,16},{24,28},{28,24},{1,5},{5... | collective-permute-start | bytes 1585160 | tf_op jit(solution)/shard_map/ppermute | solution.py:685
  123.6 41.2 %collective-permute-start.6 = (bf16[129,16,128]{2,1,0:T(8,128)(2,1)}, bf16[129,16,128]{2,1,0:T(8,128)(2,1)}, u32[]{:S(2)}, u32[]{:S(2)}) collective-permute-start(bf16[129,16,128]{2,1,0:T(8,128)(2,1)} %collective-permute-done.5.refs_6_.refs_14_.refs_38_), channel_id=1, source_target_pairs={{0,4},{4,0},{8,12},{12,8},{16,20},{20,16},{24,28},{28,24},{1,5},{5... | collective-permute-start | bytes 1585160 | tf_op jit(solution)/shard_map/ppermute | solution.py:685
  151.9 20.8 %collective-permute-start.31 = (f32[144,128]{1,0:T(8,128)S(1)}, f32[144,128]{1,0:T(8,128)S(1)}, u32[]{:S(2)}, u32[]{:S(2)}) collective-permute-start(f32[144,128]{1,0:T(8,128)S(1)} %get-tuple-element.30), channel_id=1, source_target_pairs={{0,1},{1,0},{2,3},{3,2},{4,5},{5,4},{6,7},{7,6},{8,9},{9,8},{10,11... | collective-permute-start | bytes 221192 | tf_op jit(solution)/shard_map/ppermute | solution.py:685
  (68 other events, 578.5 us)

commit v4 on v3

--- a/solution.py
+++ b/solution.py
@@ -453,7 +453,7 @@
             jax.ShapeDtypeStruct((COEF, total), jnp.float32),
             jax.ShapeDtypeStruct((block, total), jnp.float32),
         ],
-        compiler_params=pltpu.CompilerParams(vmem_limit_bytes=32 << 20),
+        compiler_params=pltpu.CompilerParams(vmem_limit_bytes=60 << 20),
         cost_estimate=pl.CostEstimate(
             flops=4 * size * groups, bytes_accessed=2 * size, transcendentals=0
         ),
@@ -670,7 +670,7 @@
             pltpu.VMEM((2 * CAND_OWN, total), jnp.float32),
             pltpu.VMEM((CHUNKS * groups, LANES), jnp.float32),
         ],
-        compiler_params=pltpu.CompilerParams(vmem_limit_bytes=48 << 20),
+        compiler_params=pltpu.CompilerParams(vmem_limit_bytes=60 << 20),
         cost_estimate=pl.CostEstimate(
             flops=4 * size * groups,
             bytes_accessed=2 * size + 8 * groups * span * HARM,
@@ -685,16 +685,32 @@
     return lax.ppermute(value, axis, [(i, i ^ distance) for i in range(size)])
 
 
-def spread(own, d):
+def after(value, *others):
+    return lax.optimization_barrier((value, *others))[0]
+
+
+def direct(own):
     n_cls = lax.axis_size("cls")
-    blocks = {0: own}
+    return {1 << bit: hop(own, "cls", 1 << bit) for bit in range(1, n_cls.bit_length() - 1)}
+
+
+def relayed(known, d, *others):
+    n_cls = lax.axis_size("cls")
     for j in sorted(range(2, n_cls, 2), key=lambda j: bin(j).count("1")):
-        bits = [bit for bit in range(1, n_cls.bit_length()) if j >> bit & 1]
-        way = 1 << bits[d % len(bits)]
-        blocks[j] = hop(blocks[j ^ way], "cls", way)
+        if j not in known:
+            bits = [bit for bit in range(1, n_cls.bit_length()) if j >> bit & 1]
+            way = 1 << bits[d % len(bits)]
+            known[j] = hop(after(known[j ^ way], *others), "cls", way)
+    return known
+
+
+def paired(known, *others):
+    n_cls = lax.axis_size("cls")
+    last = n_cls - 2
     for j in range(0, n_cls, 2):
-        blocks[j + 1] = hop(blocks[j], "cls", 1)
-    return [blocks[j] for j in range(n_cls)]
+        block = after(known[j], *others) if j == last and others else known[j]
+        known[j + 1] = hop(block, "cls", 1)
+    return [known[j] for j in range(n_cls)]
 
 
 def gather_device(particles, references, owner_groups, class_order):
@@ -710,16 +726,29 @@
     picks = class_order[:, :, :CAND_OWN].reshape(count, OWN_TOP * CAND_OWN)
     cls, prt = (index.reshape(1).astype(jnp.int32) for index in (cls, prt))
     outgoing = arrange_particles(prt, particles, owner_groups, picks, n_prt, sel, masks)
-    arrived = [hop(block, "prt", d) if d else block for d, block in enumerate(outgoing)]
-    blocks = [spread(block, d) for d, block in enumerate(arrived)]
+    arrived = list(outgoing)
+    known = []
+    for d in range(n_prt):
+        if d:
+            block = outgoing[d] if d < 3 else after(outgoing[d], arrived[d - 1])
+            arrived[d] = hop(block, "prt", d)
+        if d == 0:
+            known.append({0: arrived[0], **direct(arrived[0])})
     arranged, norms = arrange_references(references, prt, n_prt, sel, masks)
     scale = 2.0 / math.sqrt(cycles * width)
-    coefs, cands = [], []
+    coefs, cands, sent, blocks = [], [], [], []
     for d in range(n_prt):
+        if d:
+            own = after(arrived[d], coefs[0]) if d == 2 else arrived[d]
+            known.append({0: arrived[d], **direct(own)})
+        waits = [arranged] if d == 0 else [coefs[d - 1]] if d == 2 else []
+        relayed(known[d], d, *waits)
+        blocks.append(paired(known[d], *([coefs[d - 1]] if d == n_prt - 1 else [])))
         coef, cand = cross_coefficients(blocks[d], arranged, norms, cls)
-        coefs.append(hop(coef, "prt", d) if d else coef)
+        coefs.append(coef)
+        sent.append(hop(coef, "prt", d) if d else coef)
         cands.append(cand)
-    score, stat = scores(coefs, cands[0], table, scale)
+    score, stat = scores(sent, cands[0], table, scale)
     stats = lax.all_gather(stat.reshape(1, *stat.shape), "cls", axis=0, tiled=True)
     mix, log_norm = mixed_weights(cls, score, cands[0], stats, table)
     mixes = [hop(mix, "prt", d) if d else mix for d in range(n_prt)]

time: 220 us -> 218 us (level)
  local copies, waits for them, and re-layouts: 29.8 us -> 15.9 us
  Pallas kernels: 68.4 us -> 77 us
  waiting for transfers between devices: 68.8 us -> 72.1 us
    unnamed x111 -> x65, local copies, waits for them, and re-layouts: 27.7 us -> 13.8 us
    pallas_call x4, Pallas kernels: 23.3 us -> 30.9 us  [cross_coefficients(): pl.pallas_call(cross_body, grid_spec=pltpu.PrefetchScalarGridSpec(num_sca...]
    ppermute x37, waiting for transfers between devices: 68.8 us -> 72.1 us  [hop(): return lax.ppermute(value, axis, [(i, i ^ distance) for i in range(size)])]
  transfers between devices with their start and end apart: 37 -> 37, of which waited for: 10 -> 11; matrix products, arithmetic and copies ran while one was open for 1% -> 1% of each run, Pallas kernels for 16% -> 20%
where the time goes in v4:
time: 218 us; the launch traced here: 217 us
  Pallas kernels  77 us (35%)
  waiting for transfers between devices  72.1 us (33%)
  starting transfers between devices  39.3 us (18%)
  local copies, waits for them, and re-layouts  15.9 us (7%)
  blocking collectives  10.7 us (5%)
    ppermute x37, waiting for transfers between devices, hop(): return lax.ppermute(value, axis, [(i, i ^ distance) for i in range(size)])  72.1 us
    ppermute x37, starting transfers between devices, hop(): return lax.ppermute(value, axis, [(i, i ^ distance) for i in range(size)])  39.3 us
    pallas_call x4, Pallas kernels, cross_coefficients(): pl.pallas_call(cross_body, grid_spec=pltpu.PrefetchScalarGridSpec(num_sca...  30.9 us
    pallas_call x1, Pallas kernels, sums(): pl.pallas_call(functools.partial(sums_body, number=len(blocks), pieces=le...  21 us
    unnamed x65, local copies, waits for them, and re-layouts  13.8 us
    pallas_call x1, Pallas kernels, arrange_references(): pl.pallas_call(reference_body, grid_spec=pltpu.PrefetchScalarGridSpec(num...  12 us
    all_gather x1, blocking collectives, gather_device(): lax.all_gather(stat.reshape(1, *stat.shape), 'cls', axis=0, tiled=True)  10.7 us
    pallas_call x1, Pallas kernels, arrange_particles(): pl.pallas_call(particle_body, in_specs=[pl.BlockSpec(memory_space=pltpu.S...  8.95 us
  transfers between devices with their start and end apart: 37, of which 11 were waited for; matrix products, arithmetic and copies ran while one was open for 1% of the time, Pallas kernels for 20%

profile of v4, /device:TPU:0, one launch (start us, length us, event | category | flops | bytes accessed | tf_op | source)
XLA Modules:
  0.0 217.3 jit_solution(5870272650858395740)
XLA Ops:
  5.4 8.9 %arrange_particles.1 = (bf16[129,16,128]{2,1,0:T(8,128)(2,1)S(1)}, bf16[129,16,128]{2,1,0:T(8,128)(2,1)S(1)}, bf16[129,16,128]{2,1,0:T(8,128)(2,1)S(1)}, bf16[129,16,128]{2,1,0:T(8,128)(2,1)S(1)}) custom-call(s32[1]{0:T(128)} %bitcast.at_ref, bf16[16,128,512]{2,1,0:T(8,128)(2,1)S(1)} %copy-done.3, s32[16,4]{1,0:T(8,128)S(1)} %copy.16.owner_ref, ...), custom_call_target="tpu_custom_call" | custom-call | flops 268435456 | bytes 4194304 | tf_op jit(solution)/shard_map/arrange_particles/pallas_call | solution.py:254
  14.4 3.1 %collective-permute-start.7 = (bf16[129,16,128]{2,1,0:T(8,128)(2,1)S(1)}, bf16[129,16,128]{2,1,0:T(8,128)(2,1)S(1)}, u32[]{:S(2)}, u32[]{:S(2)}) collective-permute-start(bf16[129,16,128]{2,1,0:T(8,128)(2,1)S(1)} %get-tuple-element.31), channel_id=1, source_target_pairs={{0,1},{1,0},{2,3},{3,2},{4,5},{5,4},{6,7},{7,6},{8,9},{9,8},{10,11... | collective-permute-start | bytes 1585160 | tf_op jit(solution)/shard_map/ppermute | solution.py:685
  19.0 2.6 %collective-permute-start.15 = (bf16[129,16,128]{2,1,0:T(8,128)(2,1)S(1)}, bf16[129,16,128]{2,1,0:T(8,128)(2,1)S(1)}, u32[]{:S(2)}, u32[]{:S(2)}) collective-permute-start(bf16[129,16,128]{2,1,0:T(8,128)(2,1)S(1)} %get-tuple-element.32), channel_id=1, source_target_pairs={{0,2},{1,3},{2,0},{3,1},{4,6},{5,7},{6,4},{7,5},{8,10},{9,11},{10,... | collective-permute-start | bytes 1585160 | tf_op jit(solution)/shard_map/ppermute | solution.py:685
  23.1 16.4 %collective-permute-done.7.refs_0_.refs_8_.refs_40_ = bf16[129,16,128]{2,1,0:T(8,128)(2,1)S(1)} collective-permute-done((bf16[129,16,128]{2,1,0:T(8,128)(2,1)S(1)}, bf16[129,16,128]{2,1,0:T(8,128)(2,1)S(1)}, u32[]{:S(2)}, u32[]{:S(2)}) %collective-permute-start.7) | collective-permute-done | bytes 528416 | tf_op jit(solution)/shard_map/ppermute | solution.py:685
  41.1 3.4 %copy-done.2 = bf16[64,128,512]{2,1,0:T(8,128)(2,1)S(1)} copy-done((bf16[64,128,512]{2,1,0:T(8,128)(2,1)S(1)}, bf16[64,128,512]{2,1,0:T(8,128)(2,1)}, u32[]{:S(2)}) %copy-start.2) | copy-done | bytes 8388632
  46.0 12.0 %arrange_references.1 = (bf16[128,64,128]{2,1,0:T(8,128)(2,1)S(1)}, f32[64,128]{1,0:T(8,128)S(1)}) custom-call(s32[1]{0:T(128)} %bitcast.at_ref, bf16[64,128,512]{2,1,0:T(8,128)(2,1)S(1)} %copy-done.2, bf16[128,256]{1,0:T(8,128)(2,1)S(1)} %copy-done.6, bf16[2,256]{1,0:T(2,128)(2,1)S(1)} %copy-done.8), custom_call_target="tpu_custom_call" | custom-call | flops 268435456 | bytes 4194304 | tf_op jit(solution)/shard_map/arrange_references/pallas_call | solution.py:295
  60.3 2.7 %collective-permute-start.11 = (bf16[129,16,128]{2,1,0:T(8,128)(2,1)S(1)}, bf16[129,16,128]{2,1,0:T(8,128)(2,1)S(1)}, u32[]{:S(2)}, u32[]{:S(2)}) collective-permute-start(bf16[129,16,128]{2,1,0:T(8,128)(2,1)S(1)} %collective-permute-done.7.refs_0_.refs_8_.refs_40_), channel_id=1, source_target_pairs={{0,16},{4,20},{8,24},{12,28},{16,0},{20,4},{24,8},{28,12},{1,17},{... | collective-permute-start | bytes 1585160 | tf_op jit(solution)/shard_map/ppermute | solution.py:685
  63.6 9.0 %collective-permute-done.5.refs_6_.refs_14_.refs_38_ = bf16[129,16,128]{2,1,0:T(8,128)(2,1)} collective-permute-done((bf16[129,16,128]{2,1,0:T(8,128)(2,1)S(1)}, bf16[129,16,128]{2,1,0:T(8,128)(2,1)}, u32[]{:S(2)}, u32[]{:S(2)}) %collective-permute-start.5) | collective-permute-done | bytes 528416 | tf_op jit(solution)/shard_map/ppermute | solution.py:685
  72.7 3.3 %collective-permute-done.11.refs_4_.refs_12_.refs_44_ = bf16[129,16,128]{2,1,0:T(8,128)(2,1)S(1)} collective-permute-done((bf16[129,16,128]{2,1,0:T(8,128)(2,1)S(1)}, bf16[129,16,128]{2,1,0:T(8,128)(2,1)S(1)}, u32[]{:S(2)}, u32[]{:S(2)}) %collective-permute-start.11) | collective-permute-done | bytes 528416 | tf_op jit(solution)/shard_map/ppermute | solution.py:685
  76.1 2.6 %collective-permute-start.23 = (bf16[129,16,128]{2,1,0:T(8,128)(2,1)S(1)}, bf16[129,16,128]{2,1,0:T(8,128)(2,1)S(1)}, u32[]{:S(2)}, u32[]{:S(2)}) collective-permute-start(bf16[129,16,128]{2,1,0:T(8,128)(2,1)S(1)} %get-tuple-element.39), channel_id=1, source_target_pairs={{0,3},{1,2},{2,1},{3,0},{4,7},{5,6},{6,5},{7,4},{8,11},{9,10},{10,... | collective-permute-start | bytes 1585160 | tf_op jit(solution)/shard_map/ppermute | solution.py:685
  78.8 6.3 %collective-permute-done.13.refs_6_.refs_14_.refs_46_ = bf16[129,16,128]{2,1,0:T(8,128)(2,1)} collective-permute-done((bf16[129,16,128]{2,1,0:T(8,128)(2,1)}, bf16[129,16,128]{2,1,0:T(8,128)(2,1)}, u32[]{:S(2)}, u32[]{:S(2)}) %collective-permute-start.13) | collective-permute-done | bytes 528416 | tf_op jit(solution)/shard_map/ppermute | solution.py:685
  85.6 7.7 %cross_coefficients.4 = (f32[144,128]{1,0:T(8,128)}, f32[8,128]{1,0:T(8,128)}) custom-call(s32[1]{0:T(128)} %bitcast.2.at_ref, bf16[129,16,128]{2,1,0:T(8,128)(2,1)} %copy-done.1, bf16[129,16,128]{2,1,0:T(8,128)(2,1)} %copy-done.13, bf16[129,16,128]{2,1,0:T(8,128)(2,1)} %copy-done.12, bf16[129,16,128]{2,1,0:T(8,128)(2,1)} %collective-permute-done.2.refs_3_.refs_11_.refs_35_, ...), custom_call_target="tpu_custom_call" | custom-call | flops 541065216 | bytes 4227072 | tf_op jit(solution)/shard_map/cross_coefficients/pallas_call | solution.py:428
  97.1 7.7 %cross_coefficients.5 = (f32[144,128]{1,0:T(8,128)}, f32[8,128]{1,0:T(8,128)}) custom-call(s32[1]{0:T(128)} %bitcast.2.at_ref, bf16[129,16,128]{2,1,0:T(8,128)(2,1)} %copy-done.9, bf16[129,16,128]{2,1,0:T(8,128)(2,1)} %collective-permute-done.8.refs_1_.refs_9_.refs_41_, bf16[129,16,128]{2,1,0:T(8,128)(2,1)} %collective-permute-done.9.refs_2_.refs_10_.refs_42_, ...), custom_call_target="tpu_custom_call" | custom-call | flops 541065216 | bytes 4227072 | tf_op jit(solution)/shard_map/cross_coefficients/pallas_call | solution.py:428
  104.9 2.4 %collective-permute-done.19.refs_4_.refs_12_.refs_20_.refs_52_ = bf16[129,16,128]{2,1,0:T(8,128)(2,1)S(1)} collective-permute-done((bf16[129,16,128]{2,1,0:T(8,128)(2,1)S(1)}, bf16[129,16,128]{2,1,0:T(8,128)(2,1)S(1)}, u32[]{:S(2)}, u32[]{:S(2)}) %collective-permute-start.19) | collective-permute-done | bytes 528416 | tf_op jit(solution)/shard_map/ppermute | solution.py:685
  110.8 10.5 %collective-permute-done.17.refs_2_.refs_10_.refs_18_.refs_50_ = bf16[129,16,128]{2,1,0:T(8,128)(2,1)S(1)} collective-permute-done((bf16[129,16,128]{2,1,0:T(8,128)(2,1)S(1)}, bf16[129,16,128]{2,1,0:T(8,128)(2,1)S(1)}, u32[]{:S(2)}, u32[]{:S(2)}) %collective-permute-start.17) | collective-permute-done | bytes 528416 | tf_op jit(solution)/shard_map/ppermute | solution.py:685
  121.3 10.1 %collective-permute-done.21.refs_6_.refs_14_.refs_22_.refs_54_ = bf16[129,16,128]{2,1,0:T(8,128)(2,1)S(1)} collective-permute-done((bf16[129,16,128]{2,1,0:T(8,128)(2,1)S(1)}, bf16[129,16,128]{2,1,0:T(8,128)(2,1)S(1)}, u32[]{:S(2)}, u32[]{:S(2)}) %collective-permute-start.21) | collective-permute-done | bytes 528416 | tf_op jit(solution)/shard_map/ppermute | solution.py:685
  133.7 7.7 %cross_coefficients.6 = (f32[144,128]{1,0:T(8,128)}, f32[8,128]{1,0:T(8,128)}) custom-call(s32[1]{0:T(128)} %bitcast.2.at_ref, bf16[129,16,128]{2,1,0:T(8,128)(2,1)} %copy-done.11, bf16[129,16,128]{2,1,0:T(8,128)(2,1)} %copy-done.20, bf16[129,16,128]{2,1,0:T(8,128)(2,1)} %copy-done.18, bf16[129,16,128]{2,1,0:T(8,128)(2,1)} %copy-done.22, ...), custom_call_target="tpu_custom_call" | custom-call | flops 541065216 | bytes 4227072 | tf_op jit(solution)/shard_map/cross_coefficients/pallas_call | solution.py:428
  141.5 4.4 %collective-permute-done.29.refs_6_.refs_14_.refs_30_.refs_62_ = bf16[129,16,128]{2,1,0:T(8,128)(2,1)S(1)} collective-permute-done((bf16[129,16,128]{2,1,0:T(8,128)(2,1)S(1)}, bf16[129,16,128]{2,1,0:T(8,128)(2,1)S(1)}, u32[]{:S(2)}, u32[]{:S(2)}) %collective-permute-start.29) | collective-permute-done | bytes 528416 | tf_op jit(solution)/shard_map/ppermute | solution.py:685
  145.9 6.5 %collective-permute-start.31 = (f32[144,128]{1,0:T(8,128)S(1)}, f32[144,128]{1,0:T(8,128)S(1)}, u32[]{:S(2)}, u32[]{:S(2)}) collective-permute-start(f32[144,128]{1,0:T(8,128)S(1)} %copy-done.31), channel_id=1, source_target_pairs={{0,1},{1,0},{2,3},{3,2},{4,5},{5,4},{6,7},{7,6},{8,9},{9,8},{10,11... | collective-permute-start | bytes 221192 | tf_op jit(solution)/shard_map/ppermute | solution.py:685
  154.3 7.7 %cross_coefficients.7 = (f32[144,128]{1,0:T(8,128)}, f32[8,128]{1,0:T(8,128)}) custom-call(s32[1]{0:T(128)} %bitcast.2.at_ref, bf16[129,16,128]{2,1,0:T(8,128)(2,1)} %copy-done.15, bf16[129,16,128]{2,1,0:T(8,128)(2,1)} %collective-permute-done.24.refs_1_.refs_9_.refs_25_.refs_57_, bf16[129,16,128]{2,1,0:T(8,128)(2,1)} %copy-done.17, ...), custom_call_target="tpu_custom_call" | custom-call | flops 541065216 | bytes 4227072 | tf_op jit(solution)/shard_map/cross_coefficients/pallas_call | solution.py:428
  163.5 5.0 %collective-permute-done.33.refs_3_ = f32[144,128]{1,0:T(8,128)S(1)} collective-permute-done((f32[144,128]{1,0:T(8,128)}, f32[144,128]{1,0:T(8,128)S(1)}, u32[]{:S(2)}, u32[]{:S(2)}) %collective-permute-start.33) | collective-permute-done | bytes 73760 | tf_op jit(solution)/shard_map/ppermute | solution.py:685
  171.2 10.7 %all-gather.1.stat_ref = f32[8,2,128]{2,1,0:T(2,128)} all-gather(f32[1,2,128]{2,1,0:T(2,128)} %bitcast.9), channel_id=2, replica_groups=mesh['cls'=8,'prt'=4] {'cls'}, dimensions={0}, use_global_device_ids=true | all-gather | bytes 9216 | tf_op jit(solution)/shard_map/all_gather | solution.py:752
  191.3 3.0 %collective-permute-done.35.refs_66_ = f32[144,128]{1,0:T(8,128)S(1)} collective-permute-done((f32[144,128]{1,0:T(8,128)}, f32[144,128]{1,0:T(8,128)S(1)}, u32[]{:S(2)}, u32[]{:S(2)}) %collective-permute-start.35) | collective-permute-done | bytes 73760 | tf_op jit(solution)/shard_map/ppermute | solution.py:685
  194.9 21.0 %sums.1 = (f32[64,32,512]{2,1,0:T(8,128)}, f32[64,1]{1,0:T(8,128)}) custom-call(bf16[129,16,128]{2,1,0:T(8,128)(2,1)} %copy-done.1, bf16[129,16,128]{2,1,0:T(8,128)(2,1)} %copy-done.13, bf16[129,16,128]{2,1,0:T(8,128)(2,1)} %copy-done.12, bf16[129,16,128]{2,1,0:T(8,128)(2,1)} %collective-permute-done.2.refs_3_.refs_11_.refs_35_, ...), custom_call_target="tpu_custom_call" | custom-call | flops 2164260864 | bytes 21102592 | tf_op jit(solution)/shard_map/sums/pallas_call | solution.py:642
  (129 shorter events, 41.7 us)
Async XLA Ops:
  14.4 25.1 %collective-permute-start.7 = (bf16[129,16,128]{2,1,0:T(8,128)(2,1)S(1)}, bf16[129,16,128]{2,1,0:T(8,128)(2,1)S(1)}, u32[]{:S(2)}, u32[]{:S(2)}) collective-permute-start(bf16[129,16,128]{2,1,0:T(8,128)(2,1)S(1)} %get-tuple-element.31), channel_id=1, source_target_pairs={{0,1},{1,0},{2,3},{3,2},{4,5},{5,4},{6,7},{7,6},{8,9},{9,8},{10,11... | collective-permute-start | bytes 1585160 | tf_op jit(solution)/shard_map/ppermute | solution.py:685
  17.5 42.5 %collective-permute-start.3 = (bf16[129,16,128]{2,1,0:T(8,128)(2,1)S(1)}, bf16[129,16,128]{2,1,0:T(8,128)(2,1)S(1)}, u32[]{:S(2)}, u32[]{:S(2)}) collective-permute-start(bf16[129,16,128]{2,1,0:T(8,128)(2,1)S(1)} %get-tuple-element.28.refs_0_.refs_8_.refs_32_), channel_id=1, source_target_pairs={{0,16},{4,20},{8,24},{12,28},{16,0},{20,4},{24,8},{28,12},{1,17},{... | collective-permute-start | bytes 1585160 | tf_op jit(solution)/shard_map/ppermute | solution.py:685
  19.0 41.3 %collective-permute-start.15 = (bf16[129,16,128]{2,1,0:T(8,128)(2,1)S(1)}, bf16[129,16,128]{2,1,0:T(8,128)(2,1)S(1)}, u32[]{:S(2)}, u32[]{:S(2)}) collective-permute-start(bf16[129,16,128]{2,1,0:T(8,128)(2,1)S(1)} %get-tuple-element.32), channel_id=1, source_target_pairs={{0,2},{1,3},{2,0},{3,1},{4,6},{5,7},{6,4},{7,5},{8,10},{9,11},{10,... | collective-permute-start | bytes 1585160 | tf_op jit(solution)/shard_map/ppermute | solution.py:685
  21.6 41.4 %collective-permute-start.1 = (bf16[129,16,128]{2,1,0:T(8,128)(2,1)S(1)}, bf16[129,16,128]{2,1,0:T(8,128)(2,1)S(1)}, u32[]{:S(2)}, u32[]{:S(2)}) collective-permute-start(bf16[129,16,128]{2,1,0:T(8,128)(2,1)S(1)} %get-tuple-element.28.refs_0_.refs_8_.refs_32_), channel_id=1, source_target_pairs={{0,8},{4,12},{8,0},{12,4},{16,24},{20,28},{24,16},{28,20},{1,9},{5... | collective-permute-start | bytes 1585160 | tf_op jit(solution)/shard_map/ppermute | solution.py:685
  23.1 40.5 %collective-permute-start = (bf16[129,16,128]{2,1,0:T(8,128)(2,1)S(1)}, bf16[129,16,128]{2,1,0:T(8,128)(2,1)S(1)}, u32[]{:S(2)}, u32[]{:S(2)}) collective-permute-start(bf16[129,16,128]{2,1,0:T(8,128)(2,1)S(1)} %get-tuple-element.28.refs_0_.refs_8_.refs_32_), channel_id=1, source_target_pairs={{0,4},{4,0},{8,12},{12,8},{16,20},{20,16},{24,28},{28,24},{1,5},{5... | collective-permute-start | bytes 1585160 | tf_op jit(solution)/shard_map/ppermute | solution.py:685
  39.5 23.6 %collective-permute-start.9 = (bf16[129,16,128]{2,1,0:T(8,128)(2,1)S(1)}, bf16[129,16,128]{2,1,0:T(8,128)(2,1)}, u32[]{:S(2)}, u32[]{:S(2)}) collective-permute-start(bf16[129,16,128]{2,1,0:T(8,128)(2,1)S(1)} %collective-permute-done.7.refs_0_.refs_8_.refs_40_), channel_id=1, source_target_pairs={{0,8},{4,12},{8,0},{12,4},{16,24},{20,28},{24,16},{28,20},{1,9},{5... | collective-permute-start | bytes 1585160 | tf_op jit(solution)/shard_map/ppermute | solution.py:685
  60.3 15.6 %collective-permute-start.11 = (bf16[129,16,128]{2,1,0:T(8,128)(2,1)S(1)}, bf16[129,16,128]{2,1,0:T(8,128)(2,1)S(1)}, u32[]{:S(2)}, u32[]{:S(2)}) collective-permute-start(bf16[129,16,128]{2,1,0:T(8,128)(2,1)S(1)} %collective-permute-done.7.refs_0_.refs_8_.refs_40_), channel_id=1, source_target_pairs={{0,16},{4,20},{8,24},{12,28},{16,0},{20,4},{24,8},{28,12},{1,17},{... | collective-permute-start | bytes 1585160 | tf_op jit(solution)/shard_map/ppermute | solution.py:685
  63.1 15.6 %collective-permute-start.2 = (bf16[129,16,128]{2,1,0:T(8,128)(2,1)S(1)}, bf16[129,16,128]{2,1,0:T(8,128)(2,1)}, u32[]{:S(2)}, u32[]{:S(2)}) collective-permute-start(bf16[129,16,128]{2,1,0:T(8,128)(2,1)S(1)} %collective-permute-done.1.refs_2_.refs_10_.refs_34_), channel_id=1, source_target_pairs={{0,4},{4,0},{8,12},{12,8},{16,20},{20,16},{24,28},{28,24},{1,5},{5... | collective-permute-start | bytes 1585160 | tf_op jit(solution)/shard_map/ppermute | solution.py:685
  63.6 21.5 %collective-permute-start.13 = (bf16[129,16,128]{2,1,0:T(8,128)(2,1)}, bf16[129,16,128]{2,1,0:T(8,128)(2,1)}, u32[]{:S(2)}, u32[]{:S(2)}) collective-permute-start(bf16[129,16,128]{2,1,0:T(8,128)(2,1)} %collective-permute-done.9.refs_2_.refs_10_.refs_42_), channel_id=1, source_target_pairs={{0,16},{4,20},{8,24},{12,28},{16,0},{20,4},{24,8},{28,12},{1,17},{... | collective-permute-start | bytes 1585160 | tf_op jit(solution)/shard_map/ppermute | solution.py:685
  76.0 17.3 %collective-permute-start.8 = (bf16[129,16,128]{2,1,0:T(8,128)(2,1)S(1)}, bf16[129,16,128]{2,1,0:T(8,128)(2,1)}, u32[]{:S(2)}, u32[]{:S(2)}) collective-permute-start(bf16[129,16,128]{2,1,0:T(8,128)(2,1)S(1)} %collective-permute-done.7.refs_0_.refs_8_.refs_40_), channel_id=1, source_target_pairs={{0,4},{4,0},{8,12},{12,8},{16,20},{20,16},{24,28},{28,24},{1,5},{5... | collective-permute-start | bytes 1585160 | tf_op jit(solution)/shard_map/ppermute | solution.py:685
  76.1 19.0 %collective-permute-start.23 = (bf16[129,16,128]{2,1,0:T(8,128)(2,1)S(1)}, bf16[129,16,128]{2,1,0:T(8,128)(2,1)S(1)}, u32[]{:S(2)}, u32[]{:S(2)}) collective-permute-start(bf16[129,16,128]{2,1,0:T(8,128)(2,1)S(1)} %get-tuple-element.39), channel_id=1, source_target_pairs={{0,3},{1,2},{2,1},{3,0},{4,7},{5,6},{6,5},{7,4},{8,11},{9,10},{10,... | collective-permute-start | bytes 1585160 | tf_op jit(solution)/shard_map/ppermute | solution.py:685
  78.6 18.5 %collective-permute-start.10 = (bf16[129,16,128]{2,1,0:T(8,128)(2,1)}, bf16[129,16,128]{2,1,0:T(8,128)(2,1)}, u32[]{:S(2)}, u32[]{:S(2)}) collective-permute-start(bf16[129,16,128]{2,1,0:T(8,128)(2,1)} %collective-permute-done.9.refs_2_.refs_10_.refs_42_), channel_id=1, source_target_pairs={{0,4},{4,0},{8,12},{12,8},{16,20},{20,16},{24,28},{28,24},{1,5},{5... | collective-permute-start | bytes 1585160 | tf_op jit(solution)/shard_map/ppermute | solution.py:685
  93.3 14.0 %collective-permute-start.19 = (bf16[129,16,128]{2,1,0:T(8,128)(2,1)S(1)}, bf16[129,16,128]{2,1,0:T(8,128)(2,1)S(1)}, u32[]{:S(2)}, u32[]{:S(2)}) collective-permute-start(bf16[129,16,128]{2,1,0:T(8,128)(2,1)S(1)} %collective-permute-done.15.refs_0_.refs_8_.refs_16_.refs_48_), channel_id=1, source_target_pairs={{0,16},{4,20},{8,24},{12,28},{16,0},{20,4},{24,8},{28,12},{1,17},{... | collective-permute-start | bytes 1585160 | tf_op jit(solution)/shard_map/ppermute | solution.py:685
  95.1 15.5 %collective-permute-start.25 = (bf16[129,16,128]{2,1,0:T(8,128)(2,1)S(1)}, bf16[129,16,128]{2,1,0:T(8,128)(2,1)S(1)}, u32[]{:S(2)}, u32[]{:S(2)}) collective-permute-start(bf16[129,16,128]{2,1,0:T(8,128)(2,1)S(1)} %collective-permute-done.23.refs_0_.refs_8_.refs_24_.refs_56_), channel_id=1, source_target_pairs={{0,8},{4,12},{8,0},{12,4},{16,24},{20,28},{24,16},{28,20},{1,9},{5... | collective-permute-start | bytes 1585160 | tf_op jit(solution)/shard_map/ppermute | solution.py:685
  96.6 24.7 %collective-permute-start.17 = (bf16[129,16,128]{2,1,0:T(8,128)(2,1)S(1)}, bf16[129,16,128]{2,1,0:T(8,128)(2,1)S(1)}, u32[]{:S(2)}, u32[]{:S(2)}) collective-permute-start(bf16[129,16,128]{2,1,0:T(8,128)(2,1)S(1)} %collective-permute-done.15.refs_0_.refs_8_.refs_16_.refs_48_), channel_id=1, source_target_pairs={{0,8},{4,12},{8,0},{12,4},{16,24},{20,28},{24,16},{28,20},{1,9},{5... | collective-permute-start | bytes 1585160 | tf_op jit(solution)/shard_map/ppermute | solution.py:685
  107.3 24.1 %collective-permute-start.21 = (bf16[129,16,128]{2,1,0:T(8,128)(2,1)S(1)}, bf16[129,16,128]{2,1,0:T(8,128)(2,1)S(1)}, u32[]{:S(2)}, u32[]{:S(2)}) collective-permute-start(bf16[129,16,128]{2,1,0:T(8,128)(2,1)S(1)} %collective-permute-done.19.refs_4_.refs_12_.refs_20_.refs_52_), channel_id=1, source_target_pairs={{0,8},{4,12},{8,0},{12,4},{16,24},{20,28},{24,16},{28,20},{1,9},{5... | collective-permute-start | bytes 1585160 | tf_op jit(solution)/shard_map/ppermute | solution.py:685
  108.8 22.6 %collective-permute-start.16 = (bf16[129,16,128]{2,1,0:T(8,128)(2,1)S(1)}, bf16[129,16,128]{2,1,0:T(8,128)(2,1)S(1)}, u32[]{:S(2)}, u32[]{:S(2)}) collective-permute-start(bf16[129,16,128]{2,1,0:T(8,128)(2,1)S(1)} %collective-permute-done.15.refs_0_.refs_8_.refs_16_.refs_48_), channel_id=1, source_target_pairs={{0,4},{4,0},{8,12},{12,8},{16,20},{20,16},{24,28},{28,24},{1,5},{5... | collective-permute-start | bytes 1585160 | tf_op jit(solution)/shard_map/ppermute | solution.py:685
  108.8 23.0 %collective-permute-start.27 = (bf16[129,16,128]{2,1,0:T(8,128)(2,1)S(1)}, bf16[129,16,128]{2,1,0:T(8,128)(2,1)}, u32[]{:S(2)}, u32[]{:S(2)}) collective-permute-start(bf16[129,16,128]{2,1,0:T(8,128)(2,1)S(1)} %collective-permute-done.23.refs_0_.refs_8_.refs_24_.refs_56_), channel_id=1, source_target_pairs={{0,16},{4,20},{8,24},{12,28},{16,0},{20,4},{24,8},{28,12},{1,17},{... | collective-permute-start | bytes 1585160 | tf_op jit(solution)/shard_map/ppermute | solution.py:685
  110.6 21.5 %collective-permute-start.20 = (bf16[129,16,128]{2,1,0:T(8,128)(2,1)S(1)}, bf16[129,16,128]{2,1,0:T(8,128)(2,1)S(1)}, u32[]{:S(2)}, u32[]{:S(2)}) collective-permute-start(bf16[129,16,128]{2,1,0:T(8,128)(2,1)S(1)} %collective-permute-done.19.refs_4_.refs_12_.refs_20_.refs_52_), channel_id=1, source_target_pairs={{0,4},{4,0},{8,12},{12,8},{16,20},{20,16},{24,28},{28,24},{1,5},{5... | collective-permute-start | bytes 1585160 | tf_op jit(solution)/shard_map/ppermute | solution.py:685
  131.4 14.4 %collective-permute-start.29 = (bf16[129,16,128]{2,1,0:T(8,128)(2,1)S(1)}, bf16[129,16,128]{2,1,0:T(8,128)(2,1)S(1)}, u32[]{:S(2)}, u32[]{:S(2)}) collective-permute-start(bf16[129,16,128]{2,1,0:T(8,128)(2,1)S(1)} %collective-permute-done.25.refs_2_.refs_10_.refs_26_.refs_58_), channel_id=1, source_target_pairs={{0,16},{4,20},{8,24},{12,28},{16,0},{20,4},{24,8},{28,12},{1,17},{... | collective-permute-start | bytes 1585160 | tf_op jit(solution)/shard_map/ppermute | solution.py:685
  131.9 20.5 %collective-permute-start.24 = (bf16[129,16,128]{2,1,0:T(8,128)(2,1)S(1)}, bf16[129,16,128]{2,1,0:T(8,128)(2,1)}, u32[]{:S(2)}, u32[]{:S(2)}) collective-permute-start(bf16[129,16,128]{2,1,0:T(8,128)(2,1)S(1)} %collective-permute-done.23.refs_0_.refs_8_.refs_24_.refs_56_), channel_id=1, source_target_pairs={{0,4},{4,0},{8,12},{12,8},{16,20},{20,16},{24,28},{28,24},{1,5},{5... | collective-permute-start | bytes 1585160 | tf_op jit(solution)/shard_map/ppermute | solution.py:685
  132.1 21.4 %collective-permute-start.26 = (bf16[129,16,128]{2,1,0:T(8,128)(2,1)S(1)}, bf16[129,16,128]{2,1,0:T(8,128)(2,1)}, u32[]{:S(2)}, u32[]{:S(2)}) collective-permute-start(bf16[129,16,128]{2,1,0:T(8,128)(2,1)S(1)} %collective-permute-done.25.refs_2_.refs_10_.refs_26_.refs_58_), channel_id=1, source_target_pairs={{0,4},{4,0},{8,12},{12,8},{16,20},{20,16},{24,28},{28,24},{1,5},{5... | collective-permute-start | bytes 1585160 | tf_op jit(solution)/shard_map/ppermute | solution.py:685
  132.9 20.6 %collective-permute-start.28 = (bf16[129,16,128]{2,1,0:T(8,128)(2,1)}, bf16[129,16,128]{2,1,0:T(8,128)(2,1)}, u32[]{:S(2)}, u32[]{:S(2)}) collective-permute-start(bf16[129,16,128]{2,1,0:T(8,128)(2,1)} %collective-permute-done.27.refs_4_.refs_12_.refs_28_.refs_60_), channel_id=1, source_target_pairs={{0,4},{4,0},{8,12},{12,8},{16,20},{20,16},{24,28},{28,24},{1,5},{5... | collective-permute-start | bytes 1585160 | tf_op jit(solution)/shard_map/ppermute | solution.py:685
  145.9 17.6 %collective-permute-start.31 = (f32[144,128]{1,0:T(8,128)S(1)}, f32[144,128]{1,0:T(8,128)S(1)}, u32[]{:S(2)}, u32[]{:S(2)}) collective-permute-start(f32[144,128]{1,0:T(8,128)S(1)} %copy-done.31), channel_id=1, source_target_pairs={{0,1},{1,0},{2,3},{3,2},{4,5},{5,4},{6,7},{7,6},{8,9},{9,8},{10,11... | collective-permute-start | bytes 221192 | tf_op jit(solution)/shard_map/ppermute | solution.py:685
  (45 other events, 518.8 us)

commit v5 on v4

--- a/solution.py
+++ b/solution.py
@@ -207,21 +207,21 @@
     return jnp.concatenate(parts, 0)
 
 
-def particle_body(at_ref, x_ref, owner_ref, pick_ref, sel_ref, mask_ref, *refs):
+def particle_body(at_ref, x_ref, owner_ref, pick_ref, sel_ref, mask_ref, *refs, distances, n_prt):
     outs, scr = refs[:-1], refs[-1]
     count, cycles, _ = x_ref.shape
-    n_prt = len(outs)
+    number = len(outs)
     span = cycles // n_prt
     masks = mask_ref[...]
 
     def one(n, carry):
         parts = []
-        for d in range(n_prt):
+        for d in distances:
             start = pl.multiple_of((at_ref[0] ^ d) * span, span)
             parts.append(masked_stack(x_ref[n, pl.ds(start, span), :], masks))
         w = jnp.concatenate(parts, 0)
         y = nt_dot(sel_ref[...], w)
-        for p in range(n_prt):
+        for p in range(number):
             scr[p, pl.ds(pl.multiple_of(n * CHUNKS, CHUNKS), CHUNKS), :] = y[
                 :, p * LANES : (p + 1) * LANES
             ]
@@ -230,7 +230,7 @@
     lax.fori_loop(0, count, one, 0)
 
     def two(c, carry):
-        for p in range(n_prt):
+        for p in range(number):
             outs[p][c] = scr[p, pl.ds(c, count, stride=CHUNKS), :].astype(jnp.bfloat16)
         return carry
 
@@ -245,20 +245,22 @@
                 mine & (lane % CAND_OWN == q), pick_ref[:, at : at + 1], label
             )
     label = label.astype(jnp.float32).astype(jnp.bfloat16)
-    for p in range(n_prt):
+    for p in range(number):
         outs[p][CHUNKS] = label
 
 
-def arrange_particles(prt, particles, owner, picks, n_prt, sel, masks):
+def arrange_particles(prt, particles, owner, picks, n_prt, distances, sel, masks):
     count = particles.shape[0]
+    number = len(distances)
+    size = particles.size * number // n_prt
     return pl.pallas_call(
-        particle_body,
+        functools.partial(particle_body, distances=distances, n_prt=n_prt),
         in_specs=[pl.BlockSpec(memory_space=pltpu.SMEM)] + [pl.BlockSpec(memory_space=pltpu.VMEM)] * 5,
-        out_shape=[jax.ShapeDtypeStruct((CHUNKS + 1, count, LANES), jnp.bfloat16)] * n_prt,
-        scratch_shapes=[pltpu.VMEM((n_prt, count * CHUNKS, LANES), jnp.float32)],
+        out_shape=[jax.ShapeDtypeStruct((CHUNKS + 1, count, LANES), jnp.bfloat16)] * number,
+        scratch_shapes=[pltpu.VMEM((number, count * CHUNKS, LANES), jnp.float32)],
         compiler_params=pltpu.CompilerParams(vmem_limit_bytes=32 << 20),
         cost_estimate=pl.CostEstimate(
-            flops=particles.size * 2 * CHUNKS, bytes_accessed=particles.size * 4, transcendentals=0
+            flops=size * 2 * CHUNKS, bytes_accessed=size * 4, transcendentals=0
         ),
         name="arrange_particles",
     )(prt, particles, owner, picks, sel, masks)
@@ -312,7 +314,7 @@
             jax.ShapeDtypeStruct((CHUNKS, groups, LANES), jnp.bfloat16),
             jax.ShapeDtypeStruct((groups, LANES), jnp.float32),
         ],
-        compiler_params=pltpu.CompilerParams(vmem_limit_bytes=32 << 20),
+        compiler_params=pltpu.CompilerParams(vmem_limit_bytes=60 << 20),
         cost_estimate=pl.CostEstimate(
             flops=groups * span * width * 2 * CHUNKS,
             bytes_accessed=groups * span * width * 4,
@@ -725,26 +727,34 @@
     table = jnp.asarray(rotation_table())
     picks = class_order[:, :, :CAND_OWN].reshape(count, OWN_TOP * CAND_OWN)
     cls, prt = (index.reshape(1).astype(jnp.int32) for index in (cls, prt))
-    outgoing = arrange_particles(prt, particles, owner_groups, picks, n_prt, sel, masks)
-    arrived = list(outgoing)
-    known = []
-    for d in range(n_prt):
-        if d:
-            block = outgoing[d] if d < 3 else after(outgoing[d], arrived[d - 1])
-            arrived[d] = hop(block, "prt", d)
-        if d == 0:
-            known.append({0: arrived[0], **direct(arrived[0])})
+    outgoing = []
+    for first in range(0, n_prt, 2):
+        distances = tuple(range(first, min(first + 2, n_prt)))
+        place = after(prt, outgoing[0]) if outgoing else prt
+        outgoing += arrange_particles(
+            place, particles, owner_groups, picks, n_prt, distances, sel, masks
+        )
+    arrived = [outgoing[0]]
+    known = [{0: arrived[0], **direct(arrived[0])}]
     arranged, norms = arrange_references(references, prt, n_prt, sel, masks)
+    for d in range(1, n_prt):
+        block = after(outgoing[d], arrived[d - 1], arranged) if d > 2 else outgoing[d]
+        arrived.append(hop(block, "prt", d))
+    for d in range(1, n_prt):
+        own = after(arrived[d], arranged) if d < 3 else arrived[d]
+        known.append({0: own, **direct(own)})
+    relayed(known[0], 0, arranged)
+    for d in range(1, n_prt, 2):
+        relayed(known[d], d)
     scale = 2.0 / math.sqrt(cycles * width)
     coefs, cands, sent, blocks = [], [], [], []
     for d in range(n_prt):
-        if d:
-            own = after(arrived[d], coefs[0]) if d == 2 else arrived[d]
-            known.append({0: arrived[d], **direct(own)})
-        waits = [arranged] if d == 0 else [coefs[d - 1]] if d == 2 else []
-        relayed(known[d], d, *waits)
-        blocks.append(paired(known[d], *([coefs[d - 1]] if d == n_prt - 1 else [])))
-        coef, cand = cross_coefficients(blocks[d], arranged, norms, cls)
+        if d and d % 2 == 0:
+            relayed(known[d], d, coefs[0])
+        waits = [arrived[-1], known[1][2]] if d == 0 else [known[-1][2]] if d == 1 else []
+        blocks.append(paired(known[d], *(coefs[1:2] if d == n_prt - 1 else [])))
+        ready = after(arranged, *waits) if waits else arranged
+        coef, cand = cross_coefficients(blocks[d], ready, norms, cls)
         coefs.append(coef)
         sent.append(hop(coef, "prt", d) if d else coef)
         cands.append(cand)

time: 218 us -> 199 us (0.913)
  waiting for transfers between devices: 72.1 us -> 55.6 us
  local copies, waits for them, and re-layouts: 15.9 us -> 9.43 us
  Pallas kernels: 77 us -> 82.9 us
    ppermute x37, waiting for transfers between devices: 72.1 us -> 55.6 us  [hop(): return lax.ppermute(value, axis, [(i, i ^ distance) for i in range(size)])]
    unnamed x65 -> x57, local copies, waits for them, and re-layouts: 13.8 us -> 7.34 us
    pallas_call x1 -> x2, Pallas kernels: 8.95 us -> 12.9 us  [arrange_particles(): pl.pallas_call(functools.partial(particle_body, distances=distances, n_pr...]
  transfers between devices with their start and end apart: 37 -> 37, of which waited for: 11 -> 12; matrix products, arithmetic and copies ran while one was open for 1% -> 1% of each run, Pallas kernels for 20% -> 26%
where the time goes in v5:
time: 199 us; the launch traced here: 198 us
  Pallas kernels  82.9 us (42%)
  waiting for transfers between devices  55.6 us (28%)
  starting transfers between devices  38.1 us (19%)
  blocking collectives  9.8 us (5%)
  local copies, waits for them, and re-layouts  9.43 us (5%)
    ppermute x37, waiting for transfers between devices, hop(): return lax.ppermute(value, axis, [(i, i ^ distance) for i in range(size)])  55.6 us
    ppermute x37, starting transfers between devices, hop(): return lax.ppermute(value, axis, [(i, i ^ distance) for i in range(size)])  38.1 us
    pallas_call x4, Pallas kernels, cross_coefficients(): pl.pallas_call(cross_body, grid_spec=pltpu.PrefetchScalarGridSpec(num_sca...  30.9 us
    pallas_call x1, Pallas kernels, sums(): pl.pallas_call(functools.partial(sums_body, number=len(blocks), pieces=le...  21 us
    pallas_call x1, Pallas kernels, arrange_references(): pl.pallas_call(reference_body, grid_spec=pltpu.PrefetchScalarGridSpec(num...  14 us
    pallas_call x2, Pallas kernels, arrange_particles(): pl.pallas_call(functools.partial(particle_body, distances=distances, n_pr...  12.9 us
    all_gather x1, blocking collectives, gather_device(): lax.all_gather(stat.reshape(1, *stat.shape), 'cls', axis=0, tiled=True)  9.8 us
    unnamed x57, local copies, waits for them, and re-layouts  7.34 us
  transfers between devices with their start and end apart: 37, of which 12 were waited for; matrix products, arithmetic and copies ran while one was open for 1% of the time, Pallas kernels for 26%

profile of v5, /device:TPU:0, one launch (start us, length us, event | category | flops | bytes accessed | tf_op | source)
XLA Modules:
  0.0 198.1 jit_solution(12591250617961479017)
XLA Ops:
  5.4 6.4 %arrange_particles.2 = (bf16[129,16,128]{2,1,0:T(8,128)(2,1)S(1)}, bf16[129,16,128]{2,1,0:T(8,128)(2,1)S(1)}) custom-call(s32[1]{0:T(128)} %bitcast.at_ref, bf16[16,128,512]{2,1,0:T(8,128)(2,1)S(1)} %copy-done.1, s32[16,4]{1,0:T(8,128)S(1)} %copy.19.owner_ref, s32[16,16]{1,0:T(8,128)S(1)} %copy.20.pick_ref, bf16[128,256]{1,0:T(8,128)(2,1)S(1)} %copy-done.2, ...), custom_call_target="tpu_custom_call" | custom-call | flops 134217728 | bytes 2097152 | tf_op jit(solution)/shard_map/arrange_particles/pallas_call | solution.py:256
  11.9 3.0 %collective-permute-start.3 = (bf16[129,16,128]{2,1,0:T(8,128)(2,1)S(1)}, bf16[129,16,128]{2,1,0:T(8,128)(2,1)S(1)}, u32[]{:S(2)}, u32[]{:S(2)}) collective-permute-start(bf16[129,16,128]{2,1,0:T(8,128)(2,1)S(1)} %get-tuple-element.32.refs_0_.refs_8_.refs_32_), channel_id=1, source_target_pairs={{0,16},{4,20},{8,24},{12,28},{16,0},{20,4},{24,8},{28,12},{1,17},{... | collective-permute-start | bytes 1585160 | tf_op jit(solution)/shard_map/ppermute | solution.py:687
  16.5 6.4 %arrange_particles.3 = (bf16[129,16,128]{2,1,0:T(8,128)(2,1)S(1)}, bf16[129,16,128]{2,1,0:T(8,128)(2,1)S(1)}) custom-call(s32[1]{0:T(128)} %bitcast.at_ref, bf16[16,128,512]{2,1,0:T(8,128)(2,1)S(1)} %copy-done.1, s32[16,4]{1,0:T(8,128)S(1)} %copy.19.owner_ref, s32[16,16]{1,0:T(8,128)S(1)} %copy.20.pick_ref, bf16[128,256]{1,0:T(8,128)(2,1)S(1)} %copy-done.2, ...), custom_call_target="tpu_custom_call" | custom-call | flops 134217728 | bytes 2097152 | tf_op jit(solution)/shard_map/arrange_particles/pallas_call | solution.py:256
  22.9 2.7 %collective-permute-start.15 = (bf16[129,16,128]{2,1,0:T(8,128)(2,1)S(1)}, bf16[129,16,128]{2,1,0:T(8,128)(2,1)S(1)}, u32[]{:S(2)}, u32[]{:S(2)}) collective-permute-start(bf16[129,16,128]{2,1,0:T(8,128)(2,1)S(1)} %get-tuple-element.38), channel_id=1, source_target_pairs={{0,2},{1,3},{2,0},{3,1},{4,6},{5,7},{6,4},{7,5},{8,10},{9,11},{10,... | collective-permute-start | bytes 1585160 | tf_op jit(solution)/shard_map/ppermute | solution.py:687
  27.6 14.0 %arrange_references.1 = (bf16[128,64,128]{2,1,0:T(8,128)(2,1)}, f32[64,128]{1,0:T(8,128)}) custom-call(s32[1]{0:T(128)} %bitcast.at_ref, bf16[64,128,512]{2,1,0:T(8,128)(2,1)} %x_ref.4, bf16[128,256]{1,0:T(8,128)(2,1)} %constant.17.clone.sel_ref, bf16[2,256]{1,0:T(2,128)(2,1)} %constant.18.clone.mask_ref), custom_call_target="tpu_custom_call" | custom-call | flops 268435456 | bytes 4194304 | tf_op jit(solution)/shard_map/arrange_references/pallas_call | solution.py:297
  42.9 5.5 %collective-permute-done.15.refs_0_.refs_8_.refs_16_.refs_48_ = bf16[129,16,128]{2,1,0:T(8,128)(2,1)S(1)} collective-permute-done((bf16[129,16,128]{2,1,0:T(8,128)(2,1)S(1)}, bf16[129,16,128]{2,1,0:T(8,128)(2,1)S(1)}, u32[]{:S(2)}, u32[]{:S(2)}) %collective-permute-start.15) | collective-permute-done | bytes 528416 | tf_op jit(solution)/shard_map/ppermute | solution.py:687
  50.5 2.5 %collective-permute-start.21 = (bf16[129,16,128]{2,1,0:T(8,128)(2,1)S(1)}, bf16[129,16,128]{2,1,0:T(8,128)(2,1)}, u32[]{:S(2)}, u32[]{:S(2)}) collective-permute-start(bf16[129,16,128]{2,1,0:T(8,128)(2,1)S(1)} %get-tuple-element.41), channel_id=1, source_target_pairs={{0,3},{1,2},{2,1},{3,0},{4,7},{5,6},{6,5},{7,4},{8,11},{9,10},{10,... | collective-permute-start | bytes 1585160 | tf_op jit(solution)/shard_map/ppermute | solution.py:687
  53.0 3.5 %collective-permute-done.5.refs_6_.refs_14_.refs_38_ = bf16[129,16,128]{2,1,0:T(8,128)(2,1)S(1)} collective-permute-done((bf16[129,16,128]{2,1,0:T(8,128)(2,1)S(1)}, bf16[129,16,128]{2,1,0:T(8,128)(2,1)S(1)}, u32[]{:S(2)}, u32[]{:S(2)}) %collective-permute-start.5) | collective-permute-done | bytes 528416 | tf_op jit(solution)/shard_map/ppermute | solution.py:687
  56.5 10.6 %collective-permute-done.9.refs_2_.refs_10_.refs_42_ = bf16[129,16,128]{2,1,0:T(8,128)(2,1)S(1)} collective-permute-done((bf16[129,16,128]{2,1,0:T(8,128)(2,1)S(1)}, bf16[129,16,128]{2,1,0:T(8,128)(2,1)S(1)}, u32[]{:S(2)}, u32[]{:S(2)}) %collective-permute-start.9) | collective-permute-done | bytes 528416 | tf_op jit(solution)/shard_map/ppermute | solution.py:687
  71.6 7.7 %cross_coefficients.4 = (f32[144,128]{1,0:T(8,128)}, f32[8,128]{1,0:T(8,128)}) custom-call(s32[1]{0:T(128)} %bitcast.2.at_ref, bf16[129,16,128]{2,1,0:T(8,128)(2,1)} %copy-done, bf16[129,16,128]{2,1,0:T(8,128)(2,1)} %collective-permute-done.refs_1_.refs_9_.refs_33_, bf16[129,16,128]{2,1,0:T(8,128)(2,1)} %collective-permute-done.1.refs_2_.refs_10_.refs_34_, ...), custom_call_target="tpu_custom_call" | custom-call | flops 541065216 | bytes 4227072 | tf_op jit(solution)/shard_map/cross_coefficients/pallas_call | solution.py:430
  79.4 2.8 %collective-permute-done.19.refs_4_.refs_12_.refs_20_.refs_52_ = bf16[129,16,128]{2,1,0:T(8,128)(2,1)} collective-permute-done((bf16[129,16,128]{2,1,0:T(8,128)(2,1)S(1)}, bf16[129,16,128]{2,1,0:T(8,128)(2,1)}, u32[]{:S(2)}, u32[]{:S(2)}) %collective-permute-start.19) | collective-permute-done | bytes 528416 | tf_op jit(solution)/shard_map/ppermute | solution.py:687
  82.7 9.3 %collective-permute-done.13.refs_6_.refs_14_.refs_46_ = bf16[129,16,128]{2,1,0:T(8,128)(2,1)} collective-permute-done((bf16[129,16,128]{2,1,0:T(8,128)(2,1)S(1)}, bf16[129,16,128]{2,1,0:T(8,128)(2,1)}, u32[]{:S(2)}, u32[]{:S(2)}) %collective-permute-start.13) | collective-permute-done | bytes 528416 | tf_op jit(solution)/shard_map/ppermute | solution.py:687
  97.5 9.2 %collective-permute-done.22.refs_6_.refs_14_.refs_22_.refs_54_ = bf16[129,16,128]{2,1,0:T(8,128)(2,1)} collective-permute-done((bf16[129,16,128]{2,1,0:T(8,128)(2,1)}, bf16[129,16,128]{2,1,0:T(8,128)(2,1)}, u32[]{:S(2)}, u32[]{:S(2)}) %collective-permute-start.22) | collective-permute-done | bytes 528416 | tf_op jit(solution)/shard_map/ppermute | solution.py:687
  106.7 3.4 %collective-permute-done.29.refs_6_.refs_14_.refs_30_.refs_62_ = bf16[129,16,128]{2,1,0:T(8,128)(2,1)} collective-permute-done((bf16[129,16,128]{2,1,0:T(8,128)(2,1)}, bf16[129,16,128]{2,1,0:T(8,128)(2,1)}, u32[]{:S(2)}, u32[]{:S(2)}) %collective-permute-start.29) | collective-permute-done | bytes 528416 | tf_op jit(solution)/shard_map/ppermute | solution.py:687
  110.2 7.7 %cross_coefficients.5 = (f32[144,128]{1,0:T(8,128)}, f32[8,128]{1,0:T(8,128)}) custom-call(s32[1]{0:T(128)} %bitcast.2.at_ref, bf16[129,16,128]{2,1,0:T(8,128)(2,1)} %copy-done.5, bf16[129,16,128]{2,1,0:T(8,128)(2,1)} %collective-permute-done.8.refs_1_.refs_9_.refs_41_, bf16[129,16,128]{2,1,0:T(8,128)(2,1)} %copy-done.8, bf16[129,16,128]{2,1,0:T(8,128)(2,1)} %copy-done.14, ...), custom_call_target="tpu_custom_call" | custom-call | flops 541065216 | bytes 4227072 | tf_op jit(solution)/shard_map/cross_coefficients/pallas_call | solution.py:430
  120.2 6.2 %collective-permute-start.31 = (f32[144,128]{1,0:T(8,128)}, f32[144,128]{1,0:T(8,128)S(1)}, u32[]{:S(2)}, u32[]{:S(2)}) collective-permute-start(f32[144,128]{1,0:T(8,128)} %get-tuple-element.47), channel_id=1, source_target_pairs={{0,1},{1,0},{2,3},{3,2},{4,5},{5,4},{6,7},{7,6},{8,9},{9,8},{10,11... | collective-permute-start | bytes 221192 | tf_op jit(solution)/shard_map/ppermute | solution.py:687
  126.4 7.7 %cross_coefficients.6 = (f32[144,128]{1,0:T(8,128)}, f32[8,128]{1,0:T(8,128)}) custom-call(s32[1]{0:T(128)} %bitcast.2.at_ref, bf16[129,16,128]{2,1,0:T(8,128)(2,1)} %copy-done.6, bf16[129,16,128]{2,1,0:T(8,128)(2,1)} %copy-done.16, bf16[129,16,128]{2,1,0:T(8,128)(2,1)} %copy-done.12, ...), custom_call_target="tpu_custom_call" | custom-call | flops 541065216 | bytes 4227072 | tf_op jit(solution)/shard_map/cross_coefficients/pallas_call | solution.py:430
  136.1 7.7 %cross_coefficients.7 = (f32[144,128]{1,0:T(8,128)}, f32[8,128]{1,0:T(8,128)}) custom-call(s32[1]{0:T(128)} %bitcast.2.at_ref, bf16[129,16,128]{2,1,0:T(8,128)(2,1)} %collective-permute-done.21.refs_0_.refs_8_.refs_24_.refs_56_, bf16[129,16,128]{2,1,0:T(8,128)(2,1)} %copy-done.18, ...), custom_call_target="tpu_custom_call" | custom-call | flops 541065216 | bytes 4227072 | tf_op jit(solution)/shard_map/cross_coefficients/pallas_call | solution.py:430
  143.9 2.5 %collective-permute-start.33 = (f32[144,128]{1,0:T(8,128)}, f32[144,128]{1,0:T(8,128)S(1)}, u32[]{:S(2)}, u32[]{:S(2)}) collective-permute-start(f32[144,128]{1,0:T(8,128)} %get-tuple-element.50), channel_id=1, source_target_pairs={{0,3},{1,2},{2,1},{3,0},{4,7},{5,6},{6,5},{7,4},{8,11},{9,10},{10,... | collective-permute-start | bytes 221192 | tf_op jit(solution)/shard_map/ppermute | solution.py:687
  146.4 4.0 %collective-permute-done.33.refs_3_ = f32[144,128]{1,0:T(8,128)S(1)} collective-permute-done((f32[144,128]{1,0:T(8,128)}, f32[144,128]{1,0:T(8,128)S(1)}, u32[]{:S(2)}, u32[]{:S(2)}) %collective-permute-start.33) | collective-permute-done | bytes 73760 | tf_op jit(solution)/shard_map/ppermute | solution.py:687
  153.0 9.8 %all-gather.1.stat_ref = f32[8,2,128]{2,1,0:T(2,128)} all-gather(f32[1,2,128]{2,1,0:T(2,128)} %bitcast.9), channel_id=2, replica_groups=mesh['cls'=8,'prt'=4] {'cls'}, dimensions={0}, use_global_device_ids=true | all-gather | bytes 9216 | tf_op jit(solution)/shard_map/all_gather | solution.py:762
  164.9 2.4 %collective-permute-start.36 = (f32[144,128]{1,0:T(8,128)}, f32[144,128]{1,0:T(8,128)S(1)}, u32[]{:S(2)}, u32[]{:S(2)}) collective-permute-start(f32[144,128]{1,0:T(8,128)} %get-tuple-element.54.refs_64_), channel_id=1, source_target_pairs={{0,3},{1,2},{2,1},{3,0},{4,7},{5,6},{6,5},{7,4},{8,11},{9,10},{10,... | collective-permute-start | bytes 221192 | tf_op jit(solution)/shard_map/ppermute | solution.py:687
  172.1 3.0 %collective-permute-done.35.refs_66_ = f32[144,128]{1,0:T(8,128)S(1)} collective-permute-done((f32[144,128]{1,0:T(8,128)}, f32[144,128]{1,0:T(8,128)S(1)}, u32[]{:S(2)}, u32[]{:S(2)}) %collective-permute-start.35) | collective-permute-done | bytes 73760 | tf_op jit(solution)/shard_map/ppermute | solution.py:687
  175.7 21.0 %sums.1 = (f32[64,32,512]{2,1,0:T(8,128)}, f32[64,1]{1,0:T(8,128)}) custom-call(bf16[129,16,128]{2,1,0:T(8,128)(2,1)} %copy-done, bf16[129,16,128]{2,1,0:T(8,128)(2,1)} %collective-permute-done.refs_1_.refs_9_.refs_33_, bf16[129,16,128]{2,1,0:T(8,128)(2,1)} %collective-permute-done.1.refs_2_.refs_10_.refs_34_, bf16[129,16,128]{2,1,0:T(8,128)(2,1)} %copy-done.9, ...), custom_call_target="tpu_custom_call" | custom-call | flops 2164260864 | bytes 21102592 | tf_op jit(solution)/shard_map/sums/pallas_call | solution.py:644
  (122 shorter events, 38.1 us)
Async XLA Ops:
  11.9 15.2 %collective-permute-start.3 = (bf16[129,16,128]{2,1,0:T(8,128)(2,1)S(1)}, bf16[129,16,128]{2,1,0:T(8,128)(2,1)S(1)}, u32[]{:S(2)}, u32[]{:S(2)}) collective-permute-start(bf16[129,16,128]{2,1,0:T(8,128)(2,1)S(1)} %get-tuple-element.32.refs_0_.refs_8_.refs_32_), channel_id=1, source_target_pairs={{0,16},{4,20},{8,24},{12,28},{16,0},{20,4},{24,8},{28,12},{1,17},{... | collective-permute-start | bytes 1585160 | tf_op jit(solution)/shard_map/ppermute | solution.py:687
  14.9 26.7 %collective-permute-start.7 = (bf16[129,16,128]{2,1,0:T(8,128)(2,1)S(1)}, bf16[129,16,128]{2,1,0:T(8,128)(2,1)S(1)}, u32[]{:S(2)}, u32[]{:S(2)}) collective-permute-start(bf16[129,16,128]{2,1,0:T(8,128)(2,1)S(1)} %get-tuple-element.35), channel_id=1, source_target_pairs={{0,1},{1,0},{2,3},{3,2},{4,5},{5,4},{6,7},{7,6},{8,9},{9,8},{10,11... | collective-permute-start | bytes 1585160 | tf_op jit(solution)/shard_map/ppermute | solution.py:687
  22.9 25.5 %collective-permute-start.15 = (bf16[129,16,128]{2,1,0:T(8,128)(2,1)S(1)}, bf16[129,16,128]{2,1,0:T(8,128)(2,1)S(1)}, u32[]{:S(2)}, u32[]{:S(2)}) collective-permute-start(bf16[129,16,128]{2,1,0:T(8,128)(2,1)S(1)} %get-tuple-element.38), channel_id=1, source_target_pairs={{0,2},{1,3},{2,0},{3,1},{4,6},{5,7},{6,4},{7,5},{8,10},{9,11},{10,... | collective-permute-start | bytes 1585160 | tf_op jit(solution)/shard_map/ppermute | solution.py:687
  25.6 24.4 %collective-permute-start.1 = (bf16[129,16,128]{2,1,0:T(8,128)(2,1)S(1)}, bf16[129,16,128]{2,1,0:T(8,128)(2,1)}, u32[]{:S(2)}, u32[]{:S(2)}) collective-permute-start(bf16[129,16,128]{2,1,0:T(8,128)(2,1)S(1)} %get-tuple-element.32.refs_0_.refs_8_.refs_32_), channel_id=1, source_target_pairs={{0,8},{4,12},{8,0},{12,4},{16,24},{20,28},{24,16},{28,20},{1,9},{5... | collective-permute-start | bytes 1585160 | tf_op jit(solution)/shard_map/ppermute | solution.py:687
  27.1 22.9 %collective-permute-start = (bf16[129,16,128]{2,1,0:T(8,128)(2,1)S(1)}, bf16[129,16,128]{2,1,0:T(8,128)(2,1)}, u32[]{:S(2)}, u32[]{:S(2)}) collective-permute-start(bf16[129,16,128]{2,1,0:T(8,128)(2,1)S(1)} %get-tuple-element.32.refs_0_.refs_8_.refs_32_), channel_id=1, source_target_pairs={{0,4},{4,0},{8,12},{12,8},{16,20},{20,16},{24,28},{28,24},{1,5},{5... | collective-permute-start | bytes 1585160 | tf_op jit(solution)/shard_map/ppermute | solution.py:687
  27.1 23.5 %collective-permute-start.4 = (bf16[129,16,128]{2,1,0:T(8,128)(2,1)S(1)}, bf16[129,16,128]{2,1,0:T(8,128)(2,1)}, u32[]{:S(2)}, u32[]{:S(2)}) collective-permute-start(bf16[129,16,128]{2,1,0:T(8,128)(2,1)S(1)} %collective-permute-done.3.refs_4_.refs_12_.refs_36_), channel_id=1, source_target_pairs={{0,4},{4,0},{8,12},{12,8},{16,20},{20,16},{24,28},{28,24},{1,5},{5... | collective-permute-start | bytes 1585160 | tf_op jit(solution)/shard_map/ppermute | solution.py:687
  41.6 14.9 %collective-permute-start.5 = (bf16[129,16,128]{2,1,0:T(8,128)(2,1)S(1)}, bf16[129,16,128]{2,1,0:T(8,128)(2,1)S(1)}, u32[]{:S(2)}, u32[]{:S(2)}) collective-permute-start(bf16[129,16,128]{2,1,0:T(8,128)(2,1)S(1)} %collective-permute-done.3.refs_4_.refs_12_.refs_36_), channel_id=1, source_target_pairs={{0,8},{4,12},{8,0},{12,4},{16,24},{20,28},{24,16},{28,20},{1,9},{5... | collective-permute-start | bytes 1585160 | tf_op jit(solution)/shard_map/ppermute | solution.py:687
  48.5 18.7 %collective-permute-start.9 = (bf16[129,16,128]{2,1,0:T(8,128)(2,1)S(1)}, bf16[129,16,128]{2,1,0:T(8,128)(2,1)S(1)}, u32[]{:S(2)}, u32[]{:S(2)}) collective-permute-start(bf16[129,16,128]{2,1,0:T(8,128)(2,1)S(1)} %collective-permute-done.7.refs_0_.refs_8_.refs_40_), channel_id=1, source_target_pairs={{0,8},{4,12},{8,0},{12,4},{16,24},{20,28},{24,16},{28,20},{1,9},{5... | collective-permute-start | bytes 1585160 | tf_op jit(solution)/shard_map/ppermute | solution.py:687
  50.0 18.6 %collective-permute-start.2 = (bf16[129,16,128]{2,1,0:T(8,128)(2,1)}, bf16[129,16,128]{2,1,0:T(8,128)(2,1)S(1)}, u32[]{:S(2)}, u32[]{:S(2)}) collective-permute-start(bf16[129,16,128]{2,1,0:T(8,128)(2,1)} %collective-permute-done.1.refs_2_.refs_10_.refs_34_), channel_id=1, source_target_pairs={{0,4},{4,0},{8,12},{12,8},{16,20},{20,16},{24,28},{28,24},{1,5},{5... | collective-permute-start | bytes 1585160 | tf_op jit(solution)/shard_map/ppermute | solution.py:687
  50.0 18.6 %collective-permute-start.11 = (bf16[129,16,128]{2,1,0:T(8,128)(2,1)S(1)}, bf16[129,16,128]{2,1,0:T(8,128)(2,1)S(1)}, u32[]{:S(2)}, u32[]{:S(2)}) collective-permute-start(bf16[129,16,128]{2,1,0:T(8,128)(2,1)S(1)} %collective-permute-done.7.refs_0_.refs_8_.refs_40_), channel_id=1, source_target_pairs={{0,16},{4,20},{8,24},{12,28},{16,0},{20,4},{24,8},{28,12},{1,17},{... | collective-permute-start | bytes 1585160 | tf_op jit(solution)/shard_map/ppermute | solution.py:687
  50.5 18.7 %collective-permute-start.21 = (bf16[129,16,128]{2,1,0:T(8,128)(2,1)S(1)}, bf16[129,16,128]{2,1,0:T(8,128)(2,1)}, u32[]{:S(2)}, u32[]{:S(2)}) collective-permute-start(bf16[129,16,128]{2,1,0:T(8,128)(2,1)S(1)} %get-tuple-element.41), channel_id=1, source_target_pairs={{0,3},{1,2},{2,1},{3,0},{4,7},{5,6},{6,5},{7,4},{8,11},{9,10},{10,... | collective-permute-start | bytes 1585160 | tf_op jit(solution)/shard_map/ppermute | solution.py:687
  67.1 15.1 %collective-permute-start.19 = (bf16[129,16,128]{2,1,0:T(8,128)(2,1)S(1)}, bf16[129,16,128]{2,1,0:T(8,128)(2,1)}, u32[]{:S(2)}, u32[]{:S(2)}) collective-permute-start(bf16[129,16,128]{2,1,0:T(8,128)(2,1)S(1)} %collective-permute-done.15.refs_0_.refs_8_.refs_16_.refs_48_), channel_id=1, source_target_pairs={{0,16},{4,20},{8,24},{12,28},{16,0},{20,4},{24,8},{28,12},{1,17},{... | collective-permute-start | bytes 1585160 | tf_op jit(solution)/shard_map/ppermute | solution.py:687
  68.6 23.4 %collective-permute-start.13 = (bf16[129,16,128]{2,1,0:T(8,128)(2,1)S(1)}, bf16[129,16,128]{2,1,0:T(8,128)(2,1)}, u32[]{:S(2)}, u32[]{:S(2)}) collective-permute-start(bf16[129,16,128]{2,1,0:T(8,128)(2,1)S(1)} %collective-permute-done.9.refs_2_.refs_10_.refs_42_), channel_id=1, source_target_pairs={{0,16},{4,20},{8,24},{12,28},{16,0},{20,4},{24,8},{28,12},{1,17},{... | collective-permute-start | bytes 1585160 | tf_op jit(solution)/shard_map/ppermute | solution.py:687
  69.3 22.7 %collective-permute-start.25 = (bf16[129,16,128]{2,1,0:T(8,128)(2,1)}, bf16[129,16,128]{2,1,0:T(8,128)(2,1)}, u32[]{:S(2)}, u32[]{:S(2)}) collective-permute-start(bf16[129,16,128]{2,1,0:T(8,128)(2,1)} %collective-permute-done.21.refs_0_.refs_8_.refs_24_.refs_56_), channel_id=1, source_target_pairs={{0,8},{4,12},{8,0},{12,4},{16,24},{20,28},{24,16},{28,20},{1,9},{5... | collective-permute-start | bytes 1585160 | tf_op jit(solution)/shard_map/ppermute | solution.py:687
  70.8 24.0 %collective-permute-start.17 = (bf16[129,16,128]{2,1,0:T(8,128)(2,1)S(1)}, bf16[129,16,128]{2,1,0:T(8,128)(2,1)S(1)}, u32[]{:S(2)}, u32[]{:S(2)}) collective-permute-start(bf16[129,16,128]{2,1,0:T(8,128)(2,1)S(1)} %collective-permute-done.15.refs_0_.refs_8_.refs_16_.refs_48_), channel_id=1, source_target_pairs={{0,8},{4,12},{8,0},{12,4},{16,24},{20,28},{24,16},{28,20},{1,9},{5... | collective-permute-start | bytes 1585160 | tf_op jit(solution)/shard_map/ppermute | solution.py:687
  92.0 14.7 %collective-permute-start.22 = (bf16[129,16,128]{2,1,0:T(8,128)(2,1)}, bf16[129,16,128]{2,1,0:T(8,128)(2,1)}, u32[]{:S(2)}, u32[]{:S(2)}) collective-permute-start(bf16[129,16,128]{2,1,0:T(8,128)(2,1)} %collective-permute-done.19.refs_4_.refs_12_.refs_20_.refs_52_), channel_id=1, source_target_pairs={{0,8},{4,12},{8,0},{12,4},{16,24},{20,28},{24,16},{28,20},{1,9},{5... | collective-permute-start | bytes 1585160 | tf_op jit(solution)/shard_map/ppermute | solution.py:687
  94.9 15.3 %collective-permute-start.29 = (bf16[129,16,128]{2,1,0:T(8,128)(2,1)}, bf16[129,16,128]{2,1,0:T(8,128)(2,1)}, u32[]{:S(2)}, u32[]{:S(2)}) collective-permute-start(bf16[129,16,128]{2,1,0:T(8,128)(2,1)} %collective-permute-done.25.refs_2_.refs_10_.refs_26_.refs_58_), channel_id=1, source_target_pairs={{0,16},{4,20},{8,24},{12,28},{16,0},{20,4},{24,8},{28,12},{1,17},{... | collective-permute-start | bytes 1585160 | tf_op jit(solution)/shard_map/ppermute | solution.py:687
  96.3 21.6 %collective-permute-start.16 = (bf16[129,16,128]{2,1,0:T(8,128)(2,1)S(1)}, bf16[129,16,128]{2,1,0:T(8,128)(2,1)S(1)}, u32[]{:S(2)}, u32[]{:S(2)}) collective-permute-start(bf16[129,16,128]{2,1,0:T(8,128)(2,1)S(1)} %collective-permute-done.15.refs_0_.refs_8_.refs_16_.refs_48_), channel_id=1, source_target_pairs={{0,4},{4,0},{8,12},{12,8},{16,20},{20,16},{24,28},{28,24},{1,5},{5... | collective-permute-start | bytes 1585160 | tf_op jit(solution)/shard_map/ppermute | solution.py:687
  96.4 22.1 %collective-permute-start.20 = (bf16[129,16,128]{2,1,0:T(8,128)(2,1)}, bf16[129,16,128]{2,1,0:T(8,128)(2,1)S(1)}, u32[]{:S(2)}, u32[]{:S(2)}) collective-permute-start(bf16[129,16,128]{2,1,0:T(8,128)(2,1)} %collective-permute-done.19.refs_4_.refs_12_.refs_20_.refs_52_), channel_id=1, source_target_pairs={{0,4},{4,0},{8,12},{12,8},{16,20},{20,16},{24,28},{28,24},{1,5},{5... | collective-permute-start | bytes 1585160 | tf_op jit(solution)/shard_map/ppermute | solution.py:687
  96.9 22.8 %collective-permute-start.27 = (bf16[129,16,128]{2,1,0:T(8,128)(2,1)}, bf16[129,16,128]{2,1,0:T(8,128)(2,1)}, u32[]{:S(2)}, u32[]{:S(2)}) collective-permute-start(bf16[129,16,128]{2,1,0:T(8,128)(2,1)} %collective-permute-done.21.refs_0_.refs_8_.refs_24_.refs_56_), channel_id=1, source_target_pairs={{0,16},{4,20},{8,24},{12,28},{16,0},{20,4},{24,8},{28,12},{1,17},{... | collective-permute-start | bytes 1585160 | tf_op jit(solution)/shard_map/ppermute | solution.py:687
  117.9 16.2 %collective-permute-start.24 = (bf16[129,16,128]{2,1,0:T(8,128)(2,1)}, bf16[129,16,128]{2,1,0:T(8,128)(2,1)S(1)}, u32[]{:S(2)}, u32[]{:S(2)}) collective-permute-start(bf16[129,16,128]{2,1,0:T(8,128)(2,1)} %collective-permute-done.21.refs_0_.refs_8_.refs_24_.refs_56_), channel_id=1, source_target_pairs={{0,4},{4,0},{8,12},{12,8},{16,20},{20,16},{24,28},{28,24},{1,5},{5... | collective-permute-start | bytes 1585160 | tf_op jit(solution)/shard_map/ppermute | solution.py:687
  118.5 15.8 %collective-permute-start.26 = (bf16[129,16,128]{2,1,0:T(8,128)(2,1)}, bf16[129,16,128]{2,1,0:T(8,128)(2,1)S(1)}, u32[]{:S(2)}, u32[]{:S(2)}) collective-permute-start(bf16[129,16,128]{2,1,0:T(8,128)(2,1)} %collective-permute-done.25.refs_2_.refs_10_.refs_26_.refs_58_), channel_id=1, source_target_pairs={{0,4},{4,0},{8,12},{12,8},{16,20},{20,16},{24,28},{28,24},{1,5},{5... | collective-permute-start | bytes 1585160 | tf_op jit(solution)/shard_map/ppermute | solution.py:687
  119.7 14.6 %collective-permute-start.30 = (bf16[129,16,128]{2,1,0:T(8,128)(2,1)}, bf16[129,16,128]{2,1,0:T(8,128)(2,1)S(1)}, u32[]{:S(2)}, u32[]{:S(2)}) collective-permute-start(bf16[129,16,128]{2,1,0:T(8,128)(2,1)} %collective-permute-done.29.refs_6_.refs_14_.refs_30_.refs_62_), channel_id=1, source_target_pairs={{0,4},{4,0},{8,12},{12,8},{16,20},{20,16},{24,28},{28,24},{1,5},{5... | collective-permute-start | bytes 1585160 | tf_op jit(solution)/shard_map/ppermute | solution.py:687
  120.2 26.1 %collective-permute-start.31 = (f32[144,128]{1,0:T(8,128)}, f32[144,128]{1,0:T(8,128)S(1)}, u32[]{:S(2)}, u32[]{:S(2)}) collective-permute-start(f32[144,128]{1,0:T(8,128)} %get-tuple-element.47), channel_id=1, source_target_pairs={{0,1},{1,0},{2,3},{3,2},{4,5},{5,4},{6,7},{7,6},{8,9},{9,8},{10,11... | collective-permute-start | bytes 221192 | tf_op jit(solution)/shard_map/ppermute | solution.py:687
  (41 other events, 414.6 us)

commit v6 on v5

--- a/solution.py
+++ b/solution.py
@@ -174,10 +174,6 @@
     return (np.arange(CHUNKS)[:, None] == CHUNK_OF[None, :]).astype(np.float32)
 
 
-def side_masks():
-    return np.stack([SIDE_OF == 0, SIDE_OF == 1]).astype(np.float32)
-
-
 def unselector():
     sel = selector()
     return np.concatenate([sel * (SIDE_OF == 0), sel * (SIDE_OF == 1)], 0)
@@ -199,6 +195,24 @@
     return lax.dot_general(a, b, (((1,), (1,)), ((), ())), preferred_element_type=jnp.float32)
 
 
+def selector_masks():
+    m = lax.broadcasted_iota(jnp.int32, (1, HARM), 1)
+    turn = jnp.zeros((1, HARM), jnp.int32)
+    for t in range(1, TURNS + 1):
+        turn += jnp.where(m >= t * ROTS, 1, 0)
+    rest = m - ROTS * turn
+    back = jnp.where(rest == HALF, 0, ROTS - rest)
+    chunk = jnp.where(rest < HALF, rest, back) * TURNS + turn
+    side = jnp.where(rest < HALF, 0, 1)
+    chunk = jnp.where(turn == TURNS, BODY + rest // 2, chunk)
+    side = jnp.where(turn == TURNS, rest % 2, side)
+    rows = lax.broadcasted_iota(jnp.int32, (CHUNKS, HARM), 0)
+    sel = jnp.where(rows == chunk, 1.0, 0.0).astype(jnp.bfloat16)
+    sides = lax.broadcasted_iota(jnp.int32, (2, HARM), 0)
+    masks = jnp.where(sides == side, 1.0, 0.0).astype(jnp.bfloat16)
+    return sel, masks
+
+
 def masked_stack(piece, masks):
     parts = []
     for s in range(2):
@@ -207,12 +221,12 @@
     return jnp.concatenate(parts, 0)
 
 
-def particle_body(at_ref, x_ref, owner_ref, pick_ref, sel_ref, mask_ref, *refs, distances, n_prt):
+def particle_body(at_ref, x_ref, owner_ref, pick_ref, *refs, distances, n_prt):
     outs, scr = refs[:-1], refs[-1]
     count, cycles, _ = x_ref.shape
     number = len(outs)
     span = cycles // n_prt
-    masks = mask_ref[...]
+    sel, masks = selector_masks()
 
     def one(n, carry):
         parts = []
@@ -220,7 +234,7 @@
             start = pl.multiple_of((at_ref[0] ^ d) * span, span)
             parts.append(masked_stack(x_ref[n, pl.ds(start, span), :], masks))
         w = jnp.concatenate(parts, 0)
-        y = nt_dot(sel_ref[...], w)
+        y = nt_dot(sel, w)
         for p in range(number):
             scr[p, pl.ds(pl.multiple_of(n * CHUNKS, CHUNKS), CHUNKS), :] = y[
                 :, p * LANES : (p + 1) * LANES
@@ -249,13 +263,13 @@
         outs[p][CHUNKS] = label
 
 
-def arrange_particles(prt, particles, owner, picks, n_prt, distances, sel, masks):
+def arrange_particles(prt, particles, owner, picks, n_prt, distances):
     count = particles.shape[0]
     number = len(distances)
     size = particles.size * number // n_prt
     return pl.pallas_call(
         functools.partial(particle_body, distances=distances, n_prt=n_prt),
-        in_specs=[pl.BlockSpec(memory_space=pltpu.SMEM)] + [pl.BlockSpec(memory_space=pltpu.VMEM)] * 5,
+        in_specs=[pl.BlockSpec(memory_space=pltpu.SMEM)] + [pl.BlockSpec(memory_space=pltpu.VMEM)] * 3,
         out_shape=[jax.ShapeDtypeStruct((CHUNKS + 1, count, LANES), jnp.bfloat16)] * number,
         scratch_shapes=[pltpu.VMEM((number, count * CHUNKS, LANES), jnp.float32)],
         compiler_params=pltpu.CompilerParams(vmem_limit_bytes=32 << 20),
@@ -263,17 +277,17 @@
             flops=size * 2 * CHUNKS, bytes_accessed=size * 4, transcendentals=0
         ),
         name="arrange_particles",
-    )(prt, particles, owner, picks, sel, masks)
-
-
-def reference_body(at_ref, x_ref, sel_ref, mask_ref, out_ref, norm_ref, scr):
+    )(prt, particles, owner, picks)
+
+
+def reference_body(at_ref, x_ref, out_ref, norm_ref, scr):
     rows = x_ref.shape[0]
-    masks = mask_ref[...]
+    sel, masks = selector_masks()
     step = 4
 
     def one(n, carry):
         w = jnp.concatenate([masked_stack(x_ref[n * step + i], masks) for i in range(step)], 0)
-        y = nt_dot(sel_ref[...], w)
+        y = nt_dot(sel, w)
         for i in range(step):
             scr[pl.ds(pl.multiple_of((n * step + i) * CHUNKS, CHUNKS), CHUNKS), :] = y[
                 :, i * LANES : (i + 1) * LANES
@@ -290,7 +304,7 @@
     norm_ref[...] = lax.fori_loop(0, CHUNKS, two, jnp.zeros((rows, LANES), jnp.float32))
 
 
-def arrange_references(references, prt, n_prt, sel, masks):
+def arrange_references(references, prt, n_prt):
     groups, cycles, width = references.shape
     span = cycles // n_prt
     block = 16
@@ -301,8 +315,6 @@
             grid=(groups // block,),
             in_specs=[
                 pl.BlockSpec((block, span, width), lambda i, at: (i, at[0], 0)),
-                pl.BlockSpec(sel.shape, lambda i, at: (0, 0)),
-                pl.BlockSpec(masks.shape, lambda i, at: (0, 0)),
             ],
             out_specs=[
                 pl.BlockSpec((CHUNKS, block, LANES), lambda i, at: (0, i, 0)),
@@ -321,7 +333,7 @@
             transcendentals=0,
         ),
         name="arrange_references",
-    )(prt, references, sel, masks)
+    )(prt, references)
 
 
 def lane_signs():
@@ -519,7 +531,7 @@
     for other, part in zip(tops, parts):
         summed += part * jnp.exp(other - top)
     log_norm = top + jnp.log(summed)
-    norm_ref[...] = log_norm
+    norm_ref[...] = log_norm[:, : norm_ref.shape[1]]
     weight = jnp.where(cand_ref[0:1, :] >= 0.0, jnp.exp(score_ref[...] - log_norm), 0.0)
     mix_ref[...] = lax.dot_general(
         table_ref[...],
@@ -530,14 +542,14 @@
     )
 
 
-def mixed_weights(cls, score, cand, stats, table):
+def mixed_weights(cls, score, cand, stats, table, count):
     total = score.shape[1]
     return pl.pallas_call(
         weights_body,
         in_specs=[pl.BlockSpec(memory_space=pltpu.SMEM)] + [pl.BlockSpec(memory_space=pltpu.VMEM)] * 4,
         out_shape=[
             jax.ShapeDtypeStruct((COEF, total), jnp.float32),
-            jax.ShapeDtypeStruct((1, total), jnp.float32),
+            jax.ShapeDtypeStruct((1, count), jnp.float32),
         ],
         name="mixed_weights",
     )(cls, score, cand, stats, table)
@@ -549,7 +561,7 @@
     mixes, cands = refs[:pieces], refs[pieces : 2 * pieces]
     back_ref, out_ref, weight_ref, mix, cand, planes = refs[2 * pieces :]
     i = pl.program_id(0)
-    groups = weight_ref.shape[0]
+    groups = weight_ref.shape[1]
     total = mix.shape[1]
     imag, odd = lane_signs()
 
@@ -561,7 +573,13 @@
         summed = jnp.zeros((groups, total), jnp.float32)
         for q in range(CAND_OWN):
             summed += jnp.where(hot[q], mixed[q : q + 1], 0.0)
-        weight_ref[...] = jnp.sum(summed, axis=1, keepdims=True)
+        weight_ref[...] = lax.dot_general(
+            jnp.ones((1, total), jnp.float32),
+            summed,
+            (((1,), (1,)), ((), ())),
+            precision=lax.Precision.HIGHEST,
+            preferred_element_type=jnp.float32,
+        )
         mix[...] = mixed
         cand[...] = chosen
 
@@ -661,11 +679,11 @@
             pl.BlockSpec(
                 (block, span, 2 * HARM), lambda i: (jnp.maximum(i - steps, 0), 0, 0)
             ),
-            pl.BlockSpec((groups, 1), whole),
+            pl.BlockSpec((1, groups), whole),
         ],
         out_shape=[
             jax.ShapeDtypeStruct((groups, span, 2 * HARM), jnp.float32),
-            jax.ShapeDtypeStruct((groups, 1), jnp.float32),
+            jax.ShapeDtypeStruct((1, groups), jnp.float32),
         ],
         scratch_shapes=[
             pltpu.VMEM((COEF, total), jnp.float32),
@@ -706,11 +724,11 @@
     return known
 
 
-def paired(known, *others):
+def paired(known, each, last):
     n_cls = lax.axis_size("cls")
-    last = n_cls - 2
     for j in range(0, n_cls, 2):
-        block = after(known[j], *others) if j == last and others else known[j]
+        others = last if j == n_cls - 2 else each
+        block = after(known[j], *others) if others else known[j]
         known[j + 1] = hop(block, "cls", 1)
     return [known[j] for j in range(n_cls)]
 
@@ -721,8 +739,6 @@
     count, cycles, width = particles.shape
     groups = references.shape[0]
     span = cycles // n_prt
-    sel = jnp.asarray(selector(), jnp.bfloat16)
-    masks = jnp.asarray(side_masks(), jnp.bfloat16)
     back = jnp.asarray(unselector(), jnp.bfloat16)
     table = jnp.asarray(rotation_table())
     picks = class_order[:, :, :CAND_OWN].reshape(count, OWN_TOP * CAND_OWN)
@@ -732,27 +748,34 @@
         distances = tuple(range(first, min(first + 2, n_prt)))
         place = after(prt, outgoing[0]) if outgoing else prt
         outgoing += arrange_particles(
-            place, particles, owner_groups, picks, n_prt, distances, sel, masks
+            place, particles, owner_groups, picks, n_prt, distances
         )
     arrived = [outgoing[0]]
     known = [{0: arrived[0], **direct(arrived[0])}]
-    arranged, norms = arrange_references(references, prt, n_prt, sel, masks)
-    for d in range(1, n_prt):
-        block = after(outgoing[d], arrived[d - 1], arranged) if d > 2 else outgoing[d]
-        arrived.append(hop(block, "prt", d))
-    for d in range(1, n_prt):
-        own = after(arrived[d], arranged) if d < 3 else arrived[d]
+    for d in range(1, min(n_prt, 3)):
+        arrived.append(hop(outgoing[d], "prt", d))
+    early = after(arrived[1], outgoing[-1])
+    known.append({0: early, **direct(early)})
+    relayed(known[0], 0, outgoing[-1])
+    place = after(prt, *arrived[1:2], *[known[0][1 << b] for b in range(1, n_cls.bit_length() - 1)])
+    arranged, norms = arrange_references(references, place, n_prt)
+    for d in range(2, n_prt):
+        if d > 2:
+            arrived.append(hop(after(outgoing[d], arrived[d - 1], arranged), "prt", d))
+        own = after(arrived[d], arranged) if d == 2 else arrived[d]
         known.append({0: own, **direct(own)})
-    relayed(known[0], 0, arranged)
     for d in range(1, n_prt, 2):
         relayed(known[d], d)
     scale = 2.0 / math.sqrt(cycles * width)
     coefs, cands, sent, blocks = [], [], [], []
     for d in range(n_prt):
+        waits = []
+        if n_prt > 3:
+            waits = [[known[1][2]], [arrived[3], known[2][n_cls // 2]], [known[3][2]], []][min(d, 3)]
         if d and d % 2 == 0:
             relayed(known[d], d, coefs[0])
-        waits = [arrived[-1], known[1][2]] if d == 0 else [known[-1][2]] if d == 1 else []
-        blocks.append(paired(known[d], *(coefs[1:2] if d == n_prt - 1 else [])))
+        each = [arranged, known[1][n_cls // 2]] if d == 0 else coefs[:1] if d < 3 else []
+        blocks.append(paired(known[d], each, coefs[-1:]))
         ready = after(arranged, *waits) if waits else arranged
         coef, cand = cross_coefficients(blocks[d], ready, norms, cls)
         coefs.append(coef)
@@ -760,13 +783,13 @@
         cands.append(cand)
     score, stat = scores(sent, cands[0], table, scale)
     stats = lax.all_gather(stat.reshape(1, *stat.shape), "cls", axis=0, tiled=True)
-    mix, log_norm = mixed_weights(cls, score, cands[0], stats, table)
+    mix, log_norm = mixed_weights(cls, score, cands[0], stats, table, count)
     mixes = [hop(mix, "prt", d) if d else mix for d in range(n_prt)]
     class_sums, class_weights = sums(
         [block for piece in blocks for block in piece], mixes, cands, back, groups, span
     )
-    own = log_norm[0, :count]
-    return class_sums, class_weights[:, 0], own
+    own = log_norm[0]
+    return class_sums, class_weights[0], own
 
 
 def per_device(particles, references, owner_groups, class_order):
@@ -775,7 +798,7 @@
     groups = references.shape[0]
     cap = max(2, 2 * count * OWN_TOP // n_cls)
     powers = n_cls & (n_cls - 1) == 0 and n_prt & (n_prt - 1) == 0
-    fits = 4 * cycles == LANES * n_prt and n_cls * CAND_OWN <= LANES and groups % 16 == 0
+    fits = 4 * cycles == LANES * n_prt and n_cls * CAND_OWN <= LANES and groups % 16 == 0 and n_cls >= 4
     fits = fits and powers and n_cls * count == LANES
     plan = gather_device if cap >= count and fits else dispatch_device
     return plan(particles, references, owner_groups, class_order)

time: 199 us -> 186 us (0.935)
  waiting for transfers between devices: 55.6 us -> 45.3 us
    ppermute x37, waiting for transfers between devices: 55.6 us -> 45.3 us  [hop(): return lax.ppermute(value, axis, [(i, i ^ distance) for i in range(size)])]
    unnamed x57 -> x55, local copies, waits for them, and re-layouts: 7.34 us -> 7.68 us
  transfers between devices with their start and end apart: 37 -> 37, of which waited for: 12 -> 11; matrix products, arithmetic and copies ran while one was open for 1% -> 0% of each run, Pallas kernels for 26% -> 28%
where the time goes in v6:
time: 186 us; the launch traced here: 185 us
  Pallas kernels  83.6 us (45%)
  waiting for transfers between devices  45.3 us (24%)
  starting transfers between devices  36.9 us (20%)
  blocking collectives  9.93 us (5%)
  local copies, waits for them, and re-layouts  8.6 us (5%)
    ppermute x37, waiting for transfers between devices, hop(): return lax.ppermute(value, axis, [(i, i ^ distance) for i in range(size)])  45.3 us
    ppermute x37, starting transfers between devices, hop(): return lax.ppermute(value, axis, [(i, i ^ distance) for i in range(size)])  36.9 us
    pallas_call x4, Pallas kernels, cross_coefficients(): pl.pallas_call(cross_body, grid_spec=pltpu.PrefetchScalarGridSpec(num_sca...  30.9 us
    pallas_call x1, Pallas kernels, sums(): pl.pallas_call(functools.partial(sums_body, number=len(blocks), pieces=le...  21.1 us
    pallas_call x1, Pallas kernels, arrange_references(): pl.pallas_call(reference_body, grid_spec=pltpu.PrefetchScalarGridSpec(num...  14.3 us
    pallas_call x2, Pallas kernels, arrange_particles(): pl.pallas_call(functools.partial(particle_body, distances=distances, n_pr...  13.1 us
    all_gather x1, blocking collectives, gather_device(): lax.all_gather(stat.reshape(1, *stat.shape), 'cls', axis=0, tiled=True)  9.93 us
    unnamed x55, local copies, waits for them, and re-layouts  7.68 us
  transfers between devices with their start and end apart: 37, of which 11 were waited for; matrix products, arithmetic and copies ran while one was open for 0% of the time, Pallas kernels for 28%

profile of v6, /device:TPU:0, one launch (start us, length us, event | category | flops | bytes accessed | tf_op | source)
XLA Modules:
  0.0 185.3 jit_solution(11161017158023743698)
XLA Ops:
  3.9 6.5 %arrange_particles.2 = (bf16[129,16,128]{2,1,0:T(8,128)(2,1)S(1)}, bf16[129,16,128]{2,1,0:T(8,128)(2,1)S(1)}) custom-call(s32[1]{0:T(128)} %bitcast.at_ref, bf16[16,128,512]{2,1,0:T(8,128)(2,1)S(1)} %copy-done.1, s32[16,4]{1,0:T(8,128)S(1)} %copy.17.owner_ref, s32[16,16]{1,0:T(8,128)S(1)} %copy.18.pick_ref), custom_call_target="tpu_custom_call" | custom-call | flops 134217728 | bytes 2097152 | tf_op jit(solution)/shard_map/arrange_particles/pallas_call | solution.py:270
  10.5 3.1 %collective-permute-start = (bf16[129,16,128]{2,1,0:T(8,128)(2,1)S(1)}, bf16[129,16,128]{2,1,0:T(8,128)(2,1)S(1)}, u32[]{:S(2)}, u32[]{:S(2)}) collective-permute-start(bf16[129,16,128]{2,1,0:T(8,128)(2,1)S(1)} %get-tuple-element.45), channel_id=1, source_target_pairs={{0,1},{1,0},{2,3},{3,2},{4,5},{5,4},{6,7},{7,6},{8,9},{9,8},{10,11... | collective-permute-start | bytes 1585160 | tf_op jit(solution)/shard_map/ppermute | solution.py:705
  16.6 6.5 %arrange_particles.3 = (bf16[129,16,128]{2,1,0:T(8,128)(2,1)S(1)}, bf16[129,16,128]{2,1,0:T(8,128)(2,1)S(1)}) custom-call(s32[1]{0:T(128)} %bitcast.at_ref, bf16[16,128,512]{2,1,0:T(8,128)(2,1)S(1)} %copy-done.1, s32[16,4]{1,0:T(8,128)S(1)} %copy.17.owner_ref, s32[16,16]{1,0:T(8,128)S(1)} %copy.18.pick_ref), custom_call_target="tpu_custom_call" | custom-call | flops 134217728 | bytes 2097152 | tf_op jit(solution)/shard_map/arrange_particles/pallas_call | solution.py:270
  23.1 2.4 %collective-permute-done.refs_0_.refs_8_.refs_40_ = bf16[129,16,128]{2,1,0:T(8,128)(2,1)S(1)} collective-permute-done((bf16[129,16,128]{2,1,0:T(8,128)(2,1)S(1)}, bf16[129,16,128]{2,1,0:T(8,128)(2,1)S(1)}, u32[]{:S(2)}, u32[]{:S(2)}) %collective-permute-start) | collective-permute-done | bytes 528416 | tf_op jit(solution)/shard_map/ppermute | solution.py:705
  29.3 2.6 %collective-permute-start.15 = (bf16[129,16,128]{2,1,0:T(8,128)(2,1)S(1)}, bf16[129,16,128]{2,1,0:T(8,128)(2,1)}, u32[]{:S(2)}, u32[]{:S(2)}) collective-permute-start(bf16[129,16,128]{2,1,0:T(8,128)(2,1)S(1)} %get-tuple-element.62), channel_id=1, source_target_pairs={{0,2},{1,3},{2,0},{3,1},{4,6},{5,7},{6,4},{7,5},{8,10},{9,11},{10,... | collective-permute-start | bytes 1585160 | tf_op jit(solution)/shard_map/ppermute | solution.py:705
  31.9 14.3 %arrange_references.1 = (bf16[128,64,128]{2,1,0:T(8,128)(2,1)}, f32[64,128]{1,0:T(8,128)}) custom-call(s32[1]{0:T(128)} %bitcast.at_ref, bf16[64,128,512]{2,1,0:T(8,128)(2,1)} %x_ref.4), custom_call_target="tpu_custom_call" | custom-call | flops 268435456 | bytes 4194304 | tf_op jit(solution)/shard_map/arrange_references/pallas_call | solution.py:311
  46.9 4.4 %collective-permute-done.9.refs_2_.refs_10_.refs_42_ = bf16[129,16,128]{2,1,0:T(8,128)(2,1)} collective-permute-done((bf16[129,16,128]{2,1,0:T(8,128)(2,1)S(1)}, bf16[129,16,128]{2,1,0:T(8,128)(2,1)}, u32[]{:S(2)}, u32[]{:S(2)}) %collective-permute-start.9) | collective-permute-done | bytes 528416 | tf_op jit(solution)/shard_map/ppermute | solution.py:705
  51.3 2.4 %collective-permute-done.15.refs_0_.refs_8_.refs_16_.refs_48_ = bf16[129,16,128]{2,1,0:T(8,128)(2,1)} collective-permute-done((bf16[129,16,128]{2,1,0:T(8,128)(2,1)S(1)}, bf16[129,16,128]{2,1,0:T(8,128)(2,1)}, u32[]{:S(2)}, u32[]{:S(2)}) %collective-permute-start.15) | collective-permute-done | bytes 528416 | tf_op jit(solution)/shard_map/ppermute | solution.py:705
  57.2 3.5 %collective-permute-start.22 = (bf16[129,16,128]{2,1,0:T(8,128)(2,1)S(1)}, bf16[129,16,128]{2,1,0:T(8,128)(2,1)S(1)}, u32[]{:S(2)}, u32[]{:S(2)}) collective-permute-start(bf16[129,16,128]{2,1,0:T(8,128)(2,1)S(1)} %get-tuple-element.67), channel_id=1, source_target_pairs={{0,3},{1,2},{2,1},{3,0},{4,7},{5,6},{6,5},{7,4},{8,11},{9,10},{10,... | collective-permute-start | bytes 1585160 | tf_op jit(solution)/shard_map/ppermute | solution.py:705
  60.7 7.7 %cross_coefficients.4 = (f32[144,128]{1,0:T(8,128)}, f32[8,128]{1,0:T(8,128)}) custom-call(s32[1]{0:T(128)} %bitcast.2.at_ref, bf16[129,16,128]{2,1,0:T(8,128)(2,1)} %copy-done, bf16[129,16,128]{2,1,0:T(8,128)(2,1)} %collective-permute-done.4.refs_1_.refs_9_.refs_33_, bf16[129,16,128]{2,1,0:T(8,128)(2,1)} %copy-done.4, ...), custom_call_target="tpu_custom_call" | custom-call | flops 541065216 | bytes 4227072 | tf_op jit(solution)/shard_map/cross_coefficients/pallas_call | solution.py:442
  69.0 9.3 %collective-permute-done.19.refs_4_.refs_12_.refs_20_.refs_52_ = bf16[129,16,128]{2,1,0:T(8,128)(2,1)S(1)} collective-permute-done((bf16[129,16,128]{2,1,0:T(8,128)(2,1)}, bf16[129,16,128]{2,1,0:T(8,128)(2,1)S(1)}, u32[]{:S(2)}, u32[]{:S(2)}) %collective-permute-start.19) | collective-permute-done | bytes 528416 | tf_op jit(solution)/shard_map/ppermute | solution.py:705
  84.2 7.7 %cross_coefficients.5 = (f32[144,128]{1,0:T(8,128)}, f32[8,128]{1,0:T(8,128)}) custom-call(s32[1]{0:T(128)} %bitcast.2.at_ref, bf16[129,16,128]{2,1,0:T(8,128)(2,1)} %copy-done.2, bf16[129,16,128]{2,1,0:T(8,128)(2,1)} %copy-done.9, bf16[129,16,128]{2,1,0:T(8,128)(2,1)} %collective-permute-done.9.refs_2_.refs_10_.refs_42_, bf16[129,16,128]{2,1,0:T(8,128)(2,1)} %copy-done.10, ...), custom_call_target="tpu_custom_call" | custom-call | flops 541065216 | bytes 4227072 | tf_op jit(solution)/shard_map/cross_coefficients/pallas_call | solution.py:442
  93.7 10.4 %collective-permute-done.25.refs_2_.refs_10_.refs_26_.refs_58_ = bf16[129,16,128]{2,1,0:T(8,128)(2,1)S(1)} collective-permute-done((bf16[129,16,128]{2,1,0:T(8,128)(2,1)S(1)}, bf16[129,16,128]{2,1,0:T(8,128)(2,1)S(1)}, u32[]{:S(2)}, u32[]{:S(2)}) %collective-permute-start.25) | collective-permute-done | bytes 528416 | tf_op jit(solution)/shard_map/ppermute | solution.py:705
  107.4 7.7 %cross_coefficients.6 = (f32[144,128]{1,0:T(8,128)}, f32[8,128]{1,0:T(8,128)}) custom-call(s32[1]{0:T(128)} %bitcast.2.at_ref, bf16[129,16,128]{2,1,0:T(8,128)(2,1)} %collective-permute-done.15.refs_0_.refs_8_.refs_16_.refs_48_, bf16[129,16,128]{2,1,0:T(8,128)(2,1)} %collective-permute-done.16.refs_1_.refs_9_.refs_17_.refs_49_, ...), custom_call_target="tpu_custom_call" | custom-call | flops 541065216 | bytes 4227072 | tf_op jit(solution)/shard_map/cross_coefficients/pallas_call | solution.py:442
  115.1 3.6 %collective-permute-done.29.refs_6_.refs_14_.refs_30_.refs_62_ = bf16[129,16,128]{2,1,0:T(8,128)(2,1)} collective-permute-done((bf16[129,16,128]{2,1,0:T(8,128)(2,1)S(1)}, bf16[129,16,128]{2,1,0:T(8,128)(2,1)}, u32[]{:S(2)}, u32[]{:S(2)}) %collective-permute-start.29) | collective-permute-done | bytes 528416 | tf_op jit(solution)/shard_map/ppermute | solution.py:705
  120.2 3.4 %collective-permute-start.32 = (f32[144,128]{1,0:T(8,128)}, f32[144,128]{1,0:T(8,128)S(1)}, u32[]{:S(2)}, u32[]{:S(2)}) collective-permute-start(f32[144,128]{1,0:T(8,128)} %get-tuple-element.72), channel_id=1, source_target_pairs={{0,2},{1,3},{2,0},{3,1},{4,6},{5,7},{6,4},{7,5},{8,10},{9,11},{10,... | collective-permute-start | bytes 221192 | tf_op jit(solution)/shard_map/ppermute | solution.py:705
  125.4 7.7 %cross_coefficients.7 = (f32[144,128]{1,0:T(8,128)}, f32[8,128]{1,0:T(8,128)}) custom-call(s32[1]{0:T(128)} %bitcast.2.at_ref, bf16[129,16,128]{2,1,0:T(8,128)(2,1)} %copy-done.8, bf16[129,16,128]{2,1,0:T(8,128)(2,1)} %collective-permute-done.24.refs_1_.refs_9_.refs_25_.refs_57_, bf16[129,16,128]{2,1,0:T(8,128)(2,1)} %copy-done.14, ...), custom_call_target="tpu_custom_call" | custom-call | flops 541065216 | bytes 4227072 | tf_op jit(solution)/shard_map/cross_coefficients/pallas_call | solution.py:442
  133.8 5.8 %collective-permute-done.33.refs_3_ = f32[144,128]{1,0:T(8,128)S(1)} collective-permute-done((f32[144,128]{1,0:T(8,128)}, f32[144,128]{1,0:T(8,128)S(1)}, u32[]{:S(2)}, u32[]{:S(2)}) %collective-permute-start.33) | collective-permute-done | bytes 73760 | tf_op jit(solution)/shard_map/ppermute | solution.py:705
  140.2 2.0 %scores.1 = (f32[144,128]{1,0:T(8,128)}, f32[2,128]{1,0:T(2,128)}) custom-call(f32[144,128]{1,0:T(8,128)} %get-tuple-element.57.refs_0_, f32[144,128]{1,0:T(8,128)} %copy-done.23, f32[144,128]{1,0:T(8,128)} %copy-done.24, f32[144,128]{1,0:T(8,128)} %copy-done.25, f32[8,128]{1,0:T(8,128)} %get-tuple-element.75.refs_4_.cand_ref.refs_68_, ...), custom_call_target="tpu_custom_call" | custom-call | tf_op jit(solution)/shard_map/scores/pallas_call | solution.py:497
  142.2 9.9 %all-gather.1.stat_ref = f32[8,2,128]{2,1,0:T(2,128)} all-gather(f32[1,2,128]{2,1,0:T(2,128)} %bitcast.9), channel_id=2, replica_groups=mesh['cls'=8,'prt'=4] {'cls'}, dimensions={0}, use_global_device_ids=true | all-gather | bytes 9216 | tf_op jit(solution)/shard_map/all_gather | solution.py:785
  152.1 2.1 %mixed_weights.1 = (f32[144,128]{1,0:T(8,128)}, f32[1,16]{1,0:T(1,128)}) custom-call(s32[1]{0:T(128)} %bitcast.2.at_ref, f32[144,128]{1,0:T(8,128)} %get-tuple-element.76.score_ref, f32[8,128]{1,0:T(8,128)} %get-tuple-element.75.refs_4_.cand_ref.refs_68_, f32[8,2,128]{2,1,0:T(2,128)} %all-gather.1.stat_ref, f32[144,144]{1,0:T(8,128)} %constant.14.clone.refs_5_.table_ref), custom_call_target="tpu_custom_call" | custom-call | tf_op jit(solution)/shard_map/mixed_weights/pallas_call | solution.py:547
  154.9 3.7 %collective-permute-start.34 = (f32[144,128]{1,0:T(8,128)}, f32[144,128]{1,0:T(8,128)S(1)}, u32[]{:S(2)}, u32[]{:S(2)}) collective-permute-start(f32[144,128]{1,0:T(8,128)} %get-tuple-element.78.refs_64_), channel_id=1, source_target_pairs={{0,1},{1,0},{2,3},{3,2},{4,5},{5,4},{6,7},{7,6},{8,9},{9,8},{10,11... | collective-permute-start | bytes 221192 | tf_op jit(solution)/shard_map/ppermute | solution.py:705
  158.6 2.8 %collective-permute-done.36.refs_67_ = f32[144,128]{1,0:T(8,128)S(1)} collective-permute-done((f32[144,128]{1,0:T(8,128)}, f32[144,128]{1,0:T(8,128)S(1)}, u32[]{:S(2)}, u32[]{:S(2)}) %collective-permute-start.36) | collective-permute-done | bytes 73760 | tf_op jit(solution)/shard_map/ppermute | solution.py:705
  164.0 21.1 %sums.1 = (f32[64,32,512]{2,1,0:T(8,128)}, f32[1,64]{1,0:T(1,128)}) custom-call(bf16[129,16,128]{2,1,0:T(8,128)(2,1)} %copy-done, bf16[129,16,128]{2,1,0:T(8,128)(2,1)} %collective-permute-done.4.refs_1_.refs_9_.refs_33_, bf16[129,16,128]{2,1,0:T(8,128)(2,1)} %copy-done.4, bf16[129,16,128]{2,1,0:T(8,128)(2,1)} %collective-permute-done.5.refs_3_.refs_11_.refs_35_, ...), custom_call_target="tpu_custom_call" | custom-call | flops 2164260864 | bytes 21102592 | tf_op jit(solution)/shard_map/sums/pallas_call | solution.py:662
  (118 shorter events, 33.4 us)
Async XLA Ops:
  10.5 15.1 %collective-permute-start = (bf16[129,16,128]{2,1,0:T(8,128)(2,1)S(1)}, bf16[129,16,128]{2,1,0:T(8,128)(2,1)S(1)}, u32[]{:S(2)}, u32[]{:S(2)}) collective-permute-start(bf16[129,16,128]{2,1,0:T(8,128)(2,1)S(1)} %get-tuple-element.45), channel_id=1, source_target_pairs={{0,1},{1,0},{2,3},{3,2},{4,5},{5,4},{6,7},{7,6},{8,9},{9,8},{10,11... | collective-permute-start | bytes 1585160 | tf_op jit(solution)/shard_map/ppermute | solution.py:705
  13.6 13.7 %collective-permute-start.2 = (bf16[129,16,128]{2,1,0:T(8,128)(2,1)S(1)}, bf16[129,16,128]{2,1,0:T(8,128)(2,1)S(1)}, u32[]{:S(2)}, u32[]{:S(2)}) collective-permute-start(bf16[129,16,128]{2,1,0:T(8,128)(2,1)S(1)} %get-tuple-element.51.refs_0_.refs_8_.refs_32_), channel_id=1, source_target_pairs={{0,16},{4,20},{8,24},{12,28},{16,0},{20,4},{24,8},{28,12},{1,17},{... | collective-permute-start | bytes 1585160 | tf_op jit(solution)/shard_map/ppermute | solution.py:705
  15.1 16.8 %collective-permute-start.1 = (bf16[129,16,128]{2,1,0:T(8,128)(2,1)S(1)}, bf16[129,16,128]{2,1,0:T(8,128)(2,1)S(1)}, u32[]{:S(2)}, u32[]{:S(2)}) collective-permute-start(bf16[129,16,128]{2,1,0:T(8,128)(2,1)S(1)} %get-tuple-element.51.refs_0_.refs_8_.refs_32_), channel_id=1, source_target_pairs={{0,8},{4,12},{8,0},{12,4},{16,24},{20,28},{24,16},{28,20},{1,9},{5... | collective-permute-start | bytes 1585160 | tf_op jit(solution)/shard_map/ppermute | solution.py:705
  25.6 20.6 %collective-permute-start.3 = (bf16[129,16,128]{2,1,0:T(8,128)(2,1)S(1)}, bf16[129,16,128]{2,1,0:T(8,128)(2,1)S(1)}, u32[]{:S(2)}, u32[]{:S(2)}) collective-permute-start(bf16[129,16,128]{2,1,0:T(8,128)(2,1)S(1)} %collective-permute-done.refs_0_.refs_8_.refs_40_), channel_id=1, source_target_pairs={{0,16},{4,20},{8,24},{12,28},{16,0},{20,4},{24,8},{28,12},{1,17},{... | collective-permute-start | bytes 1585160 | tf_op jit(solution)/shard_map/ppermute | solution.py:705
  27.3 18.9 %collective-permute-start.7 = (bf16[129,16,128]{2,1,0:T(8,128)(2,1)S(1)}, bf16[129,16,128]{2,1,0:T(8,128)(2,1)}, u32[]{:S(2)}, u32[]{:S(2)}) collective-permute-start(bf16[129,16,128]{2,1,0:T(8,128)(2,1)S(1)} %collective-permute-done.2.refs_4_.refs_12_.refs_36_), channel_id=1, source_target_pairs={{0,8},{4,12},{8,0},{12,4},{16,24},{20,28},{24,16},{28,20},{1,9},{5... | collective-permute-start | bytes 1585160 | tf_op jit(solution)/shard_map/ppermute | solution.py:705
  28.8 22.5 %collective-permute-start.9 = (bf16[129,16,128]{2,1,0:T(8,128)(2,1)S(1)}, bf16[129,16,128]{2,1,0:T(8,128)(2,1)}, u32[]{:S(2)}, u32[]{:S(2)}) collective-permute-start(bf16[129,16,128]{2,1,0:T(8,128)(2,1)S(1)} %collective-permute-done.refs_0_.refs_8_.refs_40_), channel_id=1, source_target_pairs={{0,8},{4,12},{8,0},{12,4},{16,24},{20,28},{24,16},{28,20},{1,9},{5... | collective-permute-start | bytes 1585160 | tf_op jit(solution)/shard_map/ppermute | solution.py:705
  29.3 24.4 %collective-permute-start.15 = (bf16[129,16,128]{2,1,0:T(8,128)(2,1)S(1)}, bf16[129,16,128]{2,1,0:T(8,128)(2,1)}, u32[]{:S(2)}, u32[]{:S(2)}) collective-permute-start(bf16[129,16,128]{2,1,0:T(8,128)(2,1)S(1)} %get-tuple-element.62), channel_id=1, source_target_pairs={{0,2},{1,3},{2,0},{3,1},{4,6},{5,7},{6,4},{7,5},{8,10},{9,11},{10,... | collective-permute-start | bytes 1585160 | tf_op jit(solution)/shard_map/ppermute | solution.py:705
  53.6 15.3 %collective-permute-start.13 = (bf16[129,16,128]{2,1,0:T(8,128)(2,1)}, bf16[129,16,128]{2,1,0:T(8,128)(2,1)}, u32[]{:S(2)}, u32[]{:S(2)}) collective-permute-start(bf16[129,16,128]{2,1,0:T(8,128)(2,1)} %collective-permute-done.9.refs_2_.refs_10_.refs_42_), channel_id=1, source_target_pairs={{0,16},{4,20},{8,24},{12,28},{16,0},{20,4},{24,8},{28,12},{1,17},{... | collective-permute-start | bytes 1585160 | tf_op jit(solution)/shard_map/ppermute | solution.py:705
  54.9 23.4 %collective-permute-start.19 = (bf16[129,16,128]{2,1,0:T(8,128)(2,1)}, bf16[129,16,128]{2,1,0:T(8,128)(2,1)S(1)}, u32[]{:S(2)}, u32[]{:S(2)}) collective-permute-start(bf16[129,16,128]{2,1,0:T(8,128)(2,1)} %collective-permute-done.15.refs_0_.refs_8_.refs_16_.refs_48_), channel_id=1, source_target_pairs={{0,16},{4,20},{8,24},{12,28},{16,0},{20,4},{24,8},{28,12},{1,17},{... | collective-permute-start | bytes 1585160 | tf_op jit(solution)/shard_map/ppermute | solution.py:705
  55.7 22.6 %collective-permute-start.17 = (bf16[129,16,128]{2,1,0:T(8,128)(2,1)}, bf16[129,16,128]{2,1,0:T(8,128)(2,1)S(1)}, u32[]{:S(2)}, u32[]{:S(2)}) collective-permute-start(bf16[129,16,128]{2,1,0:T(8,128)(2,1)} %collective-permute-done.15.refs_0_.refs_8_.refs_16_.refs_48_), channel_id=1, source_target_pairs={{0,8},{4,12},{8,0},{12,4},{16,24},{20,28},{24,16},{28,20},{1,9},{5... | collective-permute-start | bytes 1585160 | tf_op jit(solution)/shard_map/ppermute | solution.py:705
  57.2 21.6 %collective-permute-start.22 = (bf16[129,16,128]{2,1,0:T(8,128)(2,1)S(1)}, bf16[129,16,128]{2,1,0:T(8,128)(2,1)S(1)}, u32[]{:S(2)}, u32[]{:S(2)}) collective-permute-start(bf16[129,16,128]{2,1,0:T(8,128)(2,1)S(1)} %get-tuple-element.67), channel_id=1, source_target_pairs={{0,3},{1,2},{2,1},{3,0},{4,7},{5,6},{6,5},{7,4},{8,11},{9,10},{10,... | collective-permute-start | bytes 1585160 | tf_op jit(solution)/shard_map/ppermute | solution.py:705
  68.9 11.9 %collective-permute-start.11 = (bf16[129,16,128]{2,1,0:T(8,128)(2,1)}, bf16[129,16,128]{2,1,0:T(8,128)(2,1)S(1)}, u32[]{:S(2)}, u32[]{:S(2)}) collective-permute-start(bf16[129,16,128]{2,1,0:T(8,128)(2,1)} %collective-permute-done.9.refs_2_.refs_10_.refs_42_), channel_id=1, source_target_pairs={{0,4},{4,0},{8,12},{12,8},{16,20},{20,16},{24,28},{28,24},{1,5},{5... | collective-permute-start | bytes 1585160 | tf_op jit(solution)/shard_map/ppermute | solution.py:705
  78.8 14.9 %collective-permute-start.21 = (bf16[129,16,128]{2,1,0:T(8,128)(2,1)S(1)}, bf16[129,16,128]{2,1,0:T(8,128)(2,1)S(1)}, u32[]{:S(2)}, u32[]{:S(2)}) collective-permute-start(bf16[129,16,128]{2,1,0:T(8,128)(2,1)S(1)} %collective-permute-done.19.refs_4_.refs_12_.refs_20_.refs_52_), channel_id=1, source_target_pairs={{0,8},{4,12},{8,0},{12,4},{16,24},{20,28},{24,16},{28,20},{1,9},{5... | collective-permute-start | bytes 1585160 | tf_op jit(solution)/shard_map/ppermute | solution.py:705
  80.3 23.8 %collective-permute-start.25 = (bf16[129,16,128]{2,1,0:T(8,128)(2,1)S(1)}, bf16[129,16,128]{2,1,0:T(8,128)(2,1)S(1)}, u32[]{:S(2)}, u32[]{:S(2)}) collective-permute-start(bf16[129,16,128]{2,1,0:T(8,128)(2,1)S(1)} %collective-permute-done.22.refs_0_.refs_8_.refs_24_.refs_56_), channel_id=1, source_target_pairs={{0,8},{4,12},{8,0},{12,4},{16,24},{20,28},{24,16},{28,20},{1,9},{5... | collective-permute-start | bytes 1585160 | tf_op jit(solution)/shard_map/ppermute | solution.py:705
  80.9 23.3 %collective-permute-start.27 = (bf16[129,16,128]{2,1,0:T(8,128)(2,1)S(1)}, bf16[129,16,128]{2,1,0:T(8,128)(2,1)}, u32[]{:S(2)}, u32[]{:S(2)}) collective-permute-start(bf16[129,16,128]{2,1,0:T(8,128)(2,1)S(1)} %collective-permute-done.22.refs_0_.refs_8_.refs_24_.refs_56_), channel_id=1, source_target_pairs={{0,16},{4,20},{8,24},{12,28},{16,0},{20,4},{24,8},{28,12},{1,17},{... | collective-permute-start | bytes 1585160 | tf_op jit(solution)/shard_map/ppermute | solution.py:705
  82.6 23.5 %collective-permute-start.20 = (bf16[129,16,128]{2,1,0:T(8,128)(2,1)S(1)}, bf16[129,16,128]{2,1,0:T(8,128)(2,1)S(1)}, u32[]{:S(2)}, u32[]{:S(2)}) collective-permute-start(bf16[129,16,128]{2,1,0:T(8,128)(2,1)S(1)} %collective-permute-done.19.refs_4_.refs_12_.refs_20_.refs_52_), channel_id=1, source_target_pairs={{0,4},{4,0},{8,12},{12,8},{16,20},{20,16},{24,28},{28,24},{1,5},{5... | collective-permute-start | bytes 1585160 | tf_op jit(solution)/shard_map/ppermute | solution.py:705
  84.2 21.7 %collective-permute-start.16 = (bf16[129,16,128]{2,1,0:T(8,128)(2,1)}, bf16[129,16,128]{2,1,0:T(8,128)(2,1)}, u32[]{:S(2)}, u32[]{:S(2)}) collective-permute-start(bf16[129,16,128]{2,1,0:T(8,128)(2,1)} %collective-permute-done.15.refs_0_.refs_8_.refs_16_.refs_48_), channel_id=1, source_target_pairs={{0,4},{4,0},{8,12},{12,8},{16,20},{20,16},{24,28},{28,24},{1,5},{5... | collective-permute-start | bytes 1585160 | tf_op jit(solution)/shard_map/ppermute | solution.py:705
  93.7 12.8 %collective-permute-start.18 = (bf16[129,16,128]{2,1,0:T(8,128)(2,1)S(1)}, bf16[129,16,128]{2,1,0:T(8,128)(2,1)S(1)}, u32[]{:S(2)}, u32[]{:S(2)}) collective-permute-start(bf16[129,16,128]{2,1,0:T(8,128)(2,1)S(1)} %collective-permute-done.17.refs_2_.refs_10_.refs_18_.refs_50_), channel_id=1, source_target_pairs={{0,4},{4,0},{8,12},{12,8},{16,20},{20,16},{24,28},{28,24},{1,5},{5... | collective-permute-start | bytes 1585160 | tf_op jit(solution)/shard_map/ppermute | solution.py:705
  104.2 14.5 %collective-permute-start.29 = (bf16[129,16,128]{2,1,0:T(8,128)(2,1)S(1)}, bf16[129,16,128]{2,1,0:T(8,128)(2,1)}, u32[]{:S(2)}, u32[]{:S(2)}) collective-permute-start(bf16[129,16,128]{2,1,0:T(8,128)(2,1)S(1)} %collective-permute-done.25.refs_2_.refs_10_.refs_26_.refs_58_), channel_id=1, source_target_pairs={{0,16},{4,20},{8,24},{12,28},{16,0},{20,4},{24,8},{28,12},{1,17},{... | collective-permute-start | bytes 1585160 | tf_op jit(solution)/shard_map/ppermute | solution.py:705
  106.0 14.2 %collective-permute-start.24 = (bf16[129,16,128]{2,1,0:T(8,128)(2,1)S(1)}, bf16[129,16,128]{2,1,0:T(8,128)(2,1)}, u32[]{:S(2)}, u32[]{:S(2)}) collective-permute-start(bf16[129,16,128]{2,1,0:T(8,128)(2,1)S(1)} %collective-permute-done.22.refs_0_.refs_8_.refs_24_.refs_56_), channel_id=1, source_target_pairs={{0,4},{4,0},{8,12},{12,8},{16,20},{20,16},{24,28},{28,24},{1,5},{5... | collective-permute-start | bytes 1585160 | tf_op jit(solution)/shard_map/ppermute | solution.py:705
  106.1 17.4 %collective-permute-start.26 = (bf16[129,16,128]{2,1,0:T(8,128)(2,1)S(1)}, bf16[129,16,128]{2,1,0:T(8,128)(2,1)S(1)}, u32[]{:S(2)}, u32[]{:S(2)}) collective-permute-start(bf16[129,16,128]{2,1,0:T(8,128)(2,1)S(1)} %collective-permute-done.25.refs_2_.refs_10_.refs_26_.refs_58_), channel_id=1, source_target_pairs={{0,4},{4,0},{8,12},{12,8},{16,20},{20,16},{24,28},{28,24},{1,5},{5... | collective-permute-start | bytes 1585160 | tf_op jit(solution)/shard_map/ppermute | solution.py:705
  106.5 17.1 %collective-permute-start.28 = (bf16[129,16,128]{2,1,0:T(8,128)(2,1)}, bf16[129,16,128]{2,1,0:T(8,128)(2,1)S(1)}, u32[]{:S(2)}, u32[]{:S(2)}) collective-permute-start(bf16[129,16,128]{2,1,0:T(8,128)(2,1)} %collective-permute-done.27.refs_4_.refs_12_.refs_28_.refs_60_), channel_id=1, source_target_pairs={{0,4},{4,0},{8,12},{12,8},{16,20},{20,16},{24,28},{28,24},{1,5},{5... | collective-permute-start | bytes 1585160 | tf_op jit(solution)/shard_map/ppermute | solution.py:705
  118.7 15.1 %collective-permute-start.31 = (f32[144,128]{1,0:T(8,128)S(1)}, f32[144,128]{1,0:T(8,128)S(1)}, u32[]{:S(2)}, u32[]{:S(2)}) collective-permute-start(f32[144,128]{1,0:T(8,128)S(1)} %copy-done.26), channel_id=1, source_target_pairs={{0,1},{1,0},{2,3},{3,2},{4,5},{5,4},{6,7},{7,6},{8,9},{9,8},{10,11... | collective-permute-start | bytes 221192 | tf_op jit(solution)/shard_map/ppermute | solution.py:705
  120.2 13.5 %collective-permute-start.32 = (f32[144,128]{1,0:T(8,128)}, f32[144,128]{1,0:T(8,128)S(1)}, u32[]{:S(2)}, u32[]{:S(2)}) collective-permute-start(f32[144,128]{1,0:T(8,128)} %get-tuple-element.72), channel_id=1, source_target_pairs={{0,2},{1,3},{2,0},{3,1},{4,6},{5,7},{6,4},{7,5},{8,10},{9,11},{10,... | collective-permute-start | bytes 221192 | tf_op jit(solution)/shard_map/ppermute | solution.py:705
  (40 other events, 380.4 us)

commit v7 on v6

--- a/solution.py
+++ b/solution.py
@@ -221,7 +221,16 @@
     return jnp.concatenate(parts, 0)
 
 
-def particle_body(at_ref, x_ref, owner_ref, pick_ref, *refs, distances, n_prt):
+def repeat(number, step, body, carry):
+    def several(i, carry):
+        for u in range(step):
+            carry = body(i * step + u, carry)
+        return carry
+
+    return lax.fori_loop(0, number // step, several, carry)
+
+
+def particle_body(at_ref, x_ref, meta_ref, *refs, distances, n_prt):
     outs, scr = refs[:-1], refs[-1]
     count, cycles, _ = x_ref.shape
     number = len(outs)
@@ -241,35 +250,35 @@
             ]
         return carry
 
-    lax.fori_loop(0, count, one, 0)
+    repeat(count, 4, one, 0)
 
     def two(c, carry):
         for p in range(number):
             outs[p][c] = scr[p, pl.ds(c, count, stride=CHUNKS), :].astype(jnp.bfloat16)
         return carry
 
-    lax.fori_loop(0, CHUNKS, two, 0)
+    repeat(CHUNKS, 8, two, 0)
     lane = lax.broadcasted_iota(jnp.int32, (count, LANES), 1)
     label = jnp.full((count, LANES), -1, jnp.int32)
     for t in range(OWN_TOP):
-        mine = (lane // CAND_OWN) == owner_ref[:, t : t + 1]
+        mine = (lane // CAND_OWN) == meta_ref[:, t : t + 1]
         for q in range(CAND_OWN):
-            at = t * CAND_OWN + q
+            at = OWN_TOP + t * CAND_OWN + q
             label = jnp.where(
-                mine & (lane % CAND_OWN == q), pick_ref[:, at : at + 1], label
+                mine & (lane % CAND_OWN == q), meta_ref[:, at : at + 1], label
             )
     label = label.astype(jnp.float32).astype(jnp.bfloat16)
     for p in range(number):
         outs[p][CHUNKS] = label
 
 
-def arrange_particles(prt, particles, owner, picks, n_prt, distances):
+def arrange_particles(prt, particles, meta, n_prt, distances):
     count = particles.shape[0]
     number = len(distances)
     size = particles.size * number // n_prt
     return pl.pallas_call(
         functools.partial(particle_body, distances=distances, n_prt=n_prt),
-        in_specs=[pl.BlockSpec(memory_space=pltpu.SMEM)] + [pl.BlockSpec(memory_space=pltpu.VMEM)] * 3,
+        in_specs=[pl.BlockSpec(memory_space=pltpu.SMEM)] + [pl.BlockSpec(memory_space=pltpu.VMEM)] * 2,
         out_shape=[jax.ShapeDtypeStruct((CHUNKS + 1, count, LANES), jnp.bfloat16)] * number,
         scratch_shapes=[pltpu.VMEM((number, count * CHUNKS, LANES), jnp.float32)],
         compiler_params=pltpu.CompilerParams(vmem_limit_bytes=32 << 20),
@@ -277,7 +286,7 @@
             flops=size * 2 * CHUNKS, bytes_accessed=size * 4, transcendentals=0
         ),
         name="arrange_particles",
-    )(prt, particles, owner, picks)
+    )(prt, particles, meta)
 
 
 def reference_body(at_ref, x_ref, out_ref, norm_ref, scr):
@@ -294,14 +303,14 @@
             ]
         return carry
 
-    lax.fori_loop(0, rows // step, one, 0)
+    repeat(rows // step, 2, one, 0)
 
     def two(c, carry):
         value = scr[pl.ds(c, rows, stride=CHUNKS), :]
         out_ref[c] = value.astype(jnp.bfloat16)
         return carry + value * value
 
-    norm_ref[...] = lax.fori_loop(0, CHUNKS, two, jnp.zeros((rows, LANES), jnp.float32))
+    norm_ref[...] = repeat(CHUNKS, 8, two, jnp.zeros((rows, LANES), jnp.float32))
 
 
 def arrange_references(references, prt, n_prt):
@@ -634,22 +643,26 @@
         block, span, _ = out_ref.shape
         first = (i - HALF // SUM_STEP) * block
         back = back_ref[...]
+        values = []
         for c in range(block):
             turned = planes[pl.ds(first + c, CHUNKS, stride=groups), :].T
-            parts = []
             for s in range(2):
                 at = 2 * s * span
-                parts.append(
+                values.append(
                     jnp.concatenate([turned[at : at + span], turned[at + span : at + 2 * span]], 1)
                 )
-            value = jnp.concatenate(parts, 0)
-            high = value.astype(jnp.bfloat16)
-            low = (value - high.astype(jnp.float32)).astype(jnp.bfloat16)
-            placed = jnp.dot(high, back, preferred_element_type=jnp.float32) + jnp.dot(
-                low, back, preferred_element_type=jnp.float32
-            )
-            out_ref[c, :, :HARM] = placed[:span]
-            out_ref[c, :, HARM:] = placed[span:]
+        value = jnp.concatenate(values, 0)
+        high = value.astype(jnp.bfloat16)
+        low = (value - high.astype(jnp.float32)).astype(jnp.bfloat16)
+        both = jnp.dot(
+            jnp.concatenate([high, low], 0), back, preferred_element_type=jnp.float32
+        )
+        rows = value.shape[0]
+        placed = both[:rows] + both[rows:]
+        for c in range(block):
+            for s in range(2):
+                at = (2 * c + s) * span
+                out_ref[c, :, s * HARM : (s + 1) * HARM] = placed[at : at + span]
 
 
 def sums(blocks, mixes, cands, back, groups, span):
@@ -742,40 +755,36 @@
     back = jnp.asarray(unselector(), jnp.bfloat16)
     table = jnp.asarray(rotation_table())
     picks = class_order[:, :, :CAND_OWN].reshape(count, OWN_TOP * CAND_OWN)
+    meta = jnp.concatenate([owner_groups, picks], 1)
     cls, prt = (index.reshape(1).astype(jnp.int32) for index in (cls, prt))
-    outgoing = []
+    order = [d for d in range(n_prt) if d % 2 == 0] + [d for d in range(n_prt) if d % 2]
+    outgoing = {}
+    place = prt
     for first in range(0, n_prt, 2):
-        distances = tuple(range(first, min(first + 2, n_prt)))
-        place = after(prt, outgoing[0]) if outgoing else prt
-        outgoing += arrange_particles(
-            place, particles, owner_groups, picks, n_prt, distances
-        )
-    arrived = [outgoing[0]]
-    known = [{0: arrived[0], **direct(arrived[0])}]
+        distances = tuple(order[first : first + 2])
+        made = arrange_particles(place, particles, meta, n_prt, distances)
+        outgoing.update(zip(distances, made))
+        place = after(prt, made[0])
+    last = outgoing[order[-1]]
+    arrived = {d: hop(outgoing[d], "prt", d) if d else outgoing[d] for d in order}
+    known = {0: {0: arrived[0], **direct(arrived[0])}}
     for d in range(1, min(n_prt, 3)):
-        arrived.append(hop(outgoing[d], "prt", d))
-    early = after(arrived[1], outgoing[-1])
-    known.append({0: early, **direct(early)})
-    relayed(known[0], 0, outgoing[-1])
-    place = after(prt, *arrived[1:2], *[known[0][1 << b] for b in range(1, n_cls.bit_length() - 1)])
+        own = after(arrived[d], last) if d == 2 else arrived[d]
+        known[d] = {0: own, **direct(own)}
+    place = after(prt, *[arrived[d] for d in range(1, min(n_prt, 3))])
     arranged, norms = arrange_references(references, place, n_prt)
-    for d in range(2, n_prt):
-        if d > 2:
-            arrived.append(hop(after(outgoing[d], arrived[d - 1], arranged), "prt", d))
-        own = after(arrived[d], arranged) if d == 2 else arrived[d]
-        known.append({0: own, **direct(own)})
-    for d in range(1, n_prt, 2):
+    for d in range(3, n_prt):
+        arrived[d] = after(arrived[d], arranged)
+        known[d] = {0: arrived[d], **direct(arrived[d])}
+    relayed(known[0], 0, arranged)
+    for d in range(1, n_prt):
         relayed(known[d], d)
     scale = 2.0 / math.sqrt(cycles * width)
     coefs, cands, sent, blocks = [], [], [], []
     for d in range(n_prt):
-        waits = []
-        if n_prt > 3:
-            waits = [[known[1][2]], [arrived[3], known[2][n_cls // 2]], [known[3][2]], []][min(d, 3)]
-        if d and d % 2 == 0:
-            relayed(known[d], d, coefs[0])
-        each = [arranged, known[1][n_cls // 2]] if d == 0 else coefs[:1] if d < 3 else []
-        blocks.append(paired(known[d], each, coefs[-1:]))
+        waits = [known[n_prt - 1][2]] if d == 1 else []
+        each = [arranged] if d == 0 else [arranged, arrived[n_prt - 1]] if d == 1 else coefs[:1]
+        blocks.append(paired(known[d], each, coefs[-1:] if d > 1 else []))
         ready = after(arranged, *waits) if waits else arranged
         coef, cand = cross_coefficients(blocks[d], ready, norms, cls)
         coefs.append(coef)

time: 186 us -> 193 us (1.038)
  Pallas kernels: 83.6 us -> 68.2 us
  waiting for transfers between devices: 45.3 us -> 59.8 us
  starting transfers between devices: 36.9 us -> 47 us
    ppermute x37, waiting for transfers between devices: 45.3 us -> 59.8 us  [hop(): return lax.ppermute(value, axis, [(i, i ^ distance) for i in range(size)])]
    ppermute x37, starting transfers between devices: 36.9 us -> 47 us  [hop(): return lax.ppermute(value, axis, [(i, i ^ distance) for i in range(size)])]
    pallas_call x2, Pallas kernels: 13.1 us -> 5.35 us  [arrange_particles(): pl.pallas_call(functools.partial(particle_body, distances=distances, n_pr...]
    pallas_call x1, Pallas kernels: 14.3 us -> 7.45 us  [arrange_references(): pl.pallas_call(reference_body, grid_spec=pltpu.PrefetchScalarGridSpec(num...]
    unnamed x55 -> x59, local copies, waits for them, and re-layouts: 7.68 us -> 6.35 us
  transfers between devices with their start and end apart: 37 -> 37, of which waited for: 11 -> 13; matrix products, arithmetic and copies ran while one was open for 0% -> 0% of each run, Pallas kernels for 28% -> 21%
where the time goes in v7:
time: 193 us
  Pallas kernels  68.2 us (35%)
  waiting for transfers between devices  59.8 us (31%)
  starting transfers between devices  47 us (24%)
  blocking collectives  9.23 us (5%)
  local copies, waits for them, and re-layouts  7.28 us (4%)
    ppermute x37, waiting for transfers between devices, hop(): return lax.ppermute(value, axis, [(i, i ^ distance) for i in range(size)])  59.8 us
    ppermute x37, starting transfers between devices, hop(): return lax.ppermute(value, axis, [(i, i ^ distance) for i in range(size)])  47 us
    pallas_call x4, Pallas kernels, cross_coefficients(): pl.pallas_call(cross_body, grid_spec=pltpu.PrefetchScalarGridSpec(num_sca...  30.9 us
    pallas_call x1, Pallas kernels, sums(): pl.pallas_call(functools.partial(sums_body, number=len(blocks), pieces=le...  20.4 us
    all_gather x1, blocking collectives, gather_device(): lax.all_gather(stat.reshape(1, *stat.shape), 'cls', axis=0, tiled=True)  9.23 us
    pallas_call x1, Pallas kernels, arrange_references(): pl.pallas_call(reference_body, grid_spec=pltpu.PrefetchScalarGridSpec(num...  7.45 us
    unnamed x59, local copies, waits for them, and re-layouts  6.35 us
    pallas_call x2, Pallas kernels, arrange_particles(): pl.pallas_call(functools.partial(particle_body, distances=distances, n_pr...  5.35 us
  transfers between devices with their start and end apart: 37, of which 13 were waited for; matrix products, arithmetic and copies ran while one was open for 0% of the time, Pallas kernels for 21%

profile of v7, /device:TPU:0, one launch (start us, length us, event | category | flops | bytes accessed | tf_op | source)
XLA Modules:
  0.0 192.6 jit_solution(7602727336287903967)
XLA Ops:
  4.0 2.7 %arrange_particles.2 = (bf16[129,16,128]{2,1,0:T(8,128)(2,1)S(1)}, bf16[129,16,128]{2,1,0:T(8,128)(2,1)S(1)}) custom-call(s32[1]{0:T(128)} %bitcast.at_ref, bf16[16,128,512]{2,1,0:T(8,128)(2,1)S(1)} %copy-done.1, s32[16,20]{1,0:T(8,128)S(1)} %pad_add_fusion.meta_ref), custom_call_target="tpu_custom_call" | custom-call | flops 134217728 | bytes 2097152 | tf_op jit(solution)/shard_map/arrange_particles/pallas_call | solution.py:279
  6.7 4.1 %collective-permute-start.1 = (bf16[129,16,128]{2,1,0:T(8,128)(2,1)S(1)}, bf16[129,16,128]{2,1,0:T(8,128)(2,1)S(1)}, u32[]{:S(2)}, u32[]{:S(2)}) collective-permute-start(bf16[129,16,128]{2,1,0:T(8,128)(2,1)S(1)} %get-tuple-element.45), channel_id=1, source_target_pairs={{0,2},{1,3},{2,0},{3,1},{4,6},{5,7},{6,4},{7,5},{8,10},{9,11},{10,... | collective-permute-start | bytes 1585160 | tf_op jit(solution)/shard_map/ppermute | solution.py:718
  10.8 2.7 %arrange_particles.3 = (bf16[129,16,128]{2,1,0:T(8,128)(2,1)S(1)}, bf16[129,16,128]{2,1,0:T(8,128)(2,1)S(1)}) custom-call(s32[1]{0:T(128)} %bitcast.at_ref, bf16[16,128,512]{2,1,0:T(8,128)(2,1)S(1)} %copy-done.1, s32[16,20]{1,0:T(8,128)S(1)} %pad_add_fusion.meta_ref), custom_call_target="tpu_custom_call" | custom-call | flops 134217728 | bytes 2097152 | tf_op jit(solution)/shard_map/arrange_particles/pallas_call | solution.py:279
  18.4 17.5 %collective-permute-done.1.refs_0_.refs_8_.refs_16_.refs_48_ = bf16[129,16,128]{2,1,0:T(8,128)(2,1)S(1)} collective-permute-done((bf16[129,16,128]{2,1,0:T(8,128)(2,1)S(1)}, bf16[129,16,128]{2,1,0:T(8,128)(2,1)S(1)}, u32[]{:S(2)}, u32[]{:S(2)}) %collective-permute-start.1) | collective-permute-done | bytes 528416 | tf_op jit(solution)/shard_map/ppermute | solution.py:718
  35.9 12.4 %collective-permute-start.20 = (bf16[129,16,128]{2,1,0:T(8,128)(2,1)S(1)}, bf16[129,16,128]{2,1,0:T(8,128)(2,1)}, u32[]{:S(2)}, u32[]{:S(2)}) collective-permute-start(bf16[129,16,128]{2,1,0:T(8,128)(2,1)S(1)} %collective-permute-done.1.refs_0_.refs_8_.refs_16_.refs_48_), channel_id=1, source_target_pairs={{0,16},{4,20},{8,24},{12,28},{16,0},{20,4},{24,8},{28,12},{1,17},{... | collective-permute-start | bytes 1585160 | tf_op jit(solution)/shard_map/ppermute | solution.py:718
  50.0 7.5 %arrange_references.1 = (bf16[128,64,128]{2,1,0:T(8,128)(2,1)}, f32[64,128]{1,0:T(8,128)}) custom-call(s32[1]{0:T(128)} %bitcast.at_ref, bf16[64,128,512]{2,1,0:T(8,128)(2,1)} %x_ref.5), custom_call_target="tpu_custom_call" | custom-call | flops 268435456 | bytes 4194304 | tf_op jit(solution)/shard_map/arrange_references/pallas_call | solution.py:320
  62.4 2.6 %collective-permute-start.7 = (bf16[129,16,128]{2,1,0:T(8,128)(2,1)S(1)}, bf16[129,16,128]{2,1,0:T(8,128)(2,1)S(1)}, u32[]{:S(2)}, u32[]{:S(2)}) collective-permute-start(bf16[129,16,128]{2,1,0:T(8,128)(2,1)S(1)} %collective-permute-done.5.refs_4_.refs_12_.refs_36_), channel_id=1, source_target_pairs={{0,8},{4,12},{8,0},{12,4},{16,24},{20,28},{24,16},{28,20},{1,9},{5... | collective-permute-start | bytes 1585160 | tf_op jit(solution)/shard_map/ppermute | solution.py:718
  65.0 5.0 %collective-permute-done.13.refs_4_.refs_12_.refs_44_ = bf16[129,16,128]{2,1,0:T(8,128)(2,1)} collective-permute-done((bf16[129,16,128]{2,1,0:T(8,128)(2,1)S(1)}, bf16[129,16,128]{2,1,0:T(8,128)(2,1)}, u32[]{:S(2)}, u32[]{:S(2)}) %collective-permute-start.13) | collective-permute-done | bytes 528416 | tf_op jit(solution)/shard_map/ppermute | solution.py:718
  70.0 4.2 %collective-permute-done.11.refs_2_.refs_10_.refs_42_ = bf16[129,16,128]{2,1,0:T(8,128)(2,1)} collective-permute-done((bf16[129,16,128]{2,1,0:T(8,128)(2,1)S(1)}, bf16[129,16,128]{2,1,0:T(8,128)(2,1)}, u32[]{:S(2)}, u32[]{:S(2)}) %collective-permute-start.11) | collective-permute-done | bytes 528416 | tf_op jit(solution)/shard_map/ppermute | solution.py:718
  78.0 7.3 %collective-permute-done.7.refs_6_.refs_14_.refs_38_ = bf16[129,16,128]{2,1,0:T(8,128)(2,1)S(1)} collective-permute-done((bf16[129,16,128]{2,1,0:T(8,128)(2,1)S(1)}, bf16[129,16,128]{2,1,0:T(8,128)(2,1)S(1)}, u32[]{:S(2)}, u32[]{:S(2)}) %collective-permute-start.7) | collective-permute-done | bytes 528416 | tf_op jit(solution)/shard_map/ppermute | solution.py:718
  86.0 3.3 %collective-permute-done.15.refs_6_.refs_14_.refs_46_ = bf16[129,16,128]{2,1,0:T(8,128)(2,1)S(1)} collective-permute-done((bf16[129,16,128]{2,1,0:T(8,128)(2,1)}, bf16[129,16,128]{2,1,0:T(8,128)(2,1)S(1)}, u32[]{:S(2)}, u32[]{:S(2)}) %collective-permute-start.15) | collective-permute-done | bytes 528416 | tf_op jit(solution)/shard_map/ppermute | solution.py:718
  89.2 5.8 %collective-permute-done.23.refs_2_.refs_10_.refs_26_.refs_58_ = bf16[129,16,128]{2,1,0:T(8,128)(2,1)S(1)} collective-permute-done((bf16[129,16,128]{2,1,0:T(8,128)(2,1)S(1)}, bf16[129,16,128]{2,1,0:T(8,128)(2,1)S(1)}, u32[]{:S(2)}, u32[]{:S(2)}) %collective-permute-start.23) | collective-permute-done | bytes 528416 | tf_op jit(solution)/shard_map/ppermute | solution.py:718
  98.9 7.7 %cross_coefficients.4 = (f32[144,128]{1,0:T(8,128)}, f32[8,128]{1,0:T(8,128)}) custom-call(s32[1]{0:T(128)} %bitcast.2.at_ref, bf16[129,16,128]{2,1,0:T(8,128)(2,1)} %copy-done, bf16[129,16,128]{2,1,0:T(8,128)(2,1)} %copy-done.7, bf16[129,16,128]{2,1,0:T(8,128)(2,1)} %copy-done.5, bf16[129,16,128]{2,1,0:T(8,128)(2,1)} %copy-done.8, ...), custom_call_target="tpu_custom_call" | custom-call | flops 541065216 | bytes 4227072 | tf_op jit(solution)/shard_map/cross_coefficients/pallas_call | solution.py:451
  107.4 7.7 %cross_coefficients.5 = (f32[144,128]{1,0:T(8,128)}, f32[8,128]{1,0:T(8,128)}) custom-call(s32[1]{0:T(128)} %bitcast.2.at_ref, bf16[129,16,128]{2,1,0:T(8,128)(2,1)} %copy-done.3, bf16[129,16,128]{2,1,0:T(8,128)(2,1)} %copy-done.11, bf16[129,16,128]{2,1,0:T(8,128)(2,1)} %collective-permute-done.11.refs_2_.refs_10_.refs_42_, ...), custom_call_target="tpu_custom_call" | custom-call | flops 541065216 | bytes 4227072 | tf_op jit(solution)/shard_map/cross_coefficients/pallas_call | solution.py:451
  118.4 7.7 %cross_coefficients.6 = (f32[144,128]{1,0:T(8,128)}, f32[8,128]{1,0:T(8,128)}) custom-call(s32[1]{0:T(128)} %bitcast.2.at_ref, bf16[129,16,128]{2,1,0:T(8,128)(2,1)} %copy-done.2, bf16[129,16,128]{2,1,0:T(8,128)(2,1)} %copy-done.16, bf16[129,16,128]{2,1,0:T(8,128)(2,1)} %collective-permute-done.18.refs_2_.refs_10_.refs_18_.refs_50_, ...), custom_call_target="tpu_custom_call" | custom-call | flops 541065216 | bytes 4227072 | tf_op jit(solution)/shard_map/cross_coefficients/pallas_call | solution.py:451
  126.1 3.6 %collective-permute-done.29.refs_6_.refs_14_.refs_30_.refs_62_ = bf16[129,16,128]{2,1,0:T(8,128)(2,1)} collective-permute-done((bf16[129,16,128]{2,1,0:T(8,128)(2,1)S(1)}, bf16[129,16,128]{2,1,0:T(8,128)(2,1)}, u32[]{:S(2)}, u32[]{:S(2)}) %collective-permute-start.29) | collective-permute-done | bytes 528416 | tf_op jit(solution)/shard_map/ppermute | solution.py:718
  129.8 3.0 %collective-permute-start.32 = (f32[144,128]{1,0:T(8,128)}, f32[144,128]{1,0:T(8,128)S(1)}, u32[]{:S(2)}, u32[]{:S(2)}) collective-permute-start(f32[144,128]{1,0:T(8,128)} %get-tuple-element.68), channel_id=1, source_target_pairs={{0,2},{1,3},{2,0},{3,1},{4,6},{5,7},{6,4},{7,5},{8,10},{9,11},{10,... | collective-permute-start | bytes 221192 | tf_op jit(solution)/shard_map/ppermute | solution.py:718
  133.6 7.7 %cross_coefficients.7 = (f32[144,128]{1,0:T(8,128)}, f32[8,128]{1,0:T(8,128)}) custom-call(s32[1]{0:T(128)} %bitcast.2.at_ref, bf16[129,16,128]{2,1,0:T(8,128)(2,1)} %copy-done.6, bf16[129,16,128]{2,1,0:T(8,128)(2,1)} %copy-done.20, bf16[129,16,128]{2,1,0:T(8,128)(2,1)} %copy-done.13, ...), custom_call_target="tpu_custom_call" | custom-call | flops 541065216 | bytes 4227072 | tf_op jit(solution)/shard_map/cross_coefficients/pallas_call | solution.py:451
  143.0 4.8 %collective-permute-done.33.refs_3_ = f32[144,128]{1,0:T(8,128)S(1)} collective-permute-done((f32[144,128]{1,0:T(8,128)}, f32[144,128]{1,0:T(8,128)S(1)}, u32[]{:S(2)}, u32[]{:S(2)}) %collective-permute-start.33) | collective-permute-done | bytes 73760 | tf_op jit(solution)/shard_map/ppermute | solution.py:718
  150.4 9.2 %all-gather.1.stat_ref = f32[8,2,128]{2,1,0:T(2,128)} all-gather(f32[1,2,128]{2,1,0:T(2,128)} %bitcast.9), channel_id=2, replica_groups=mesh['cls'=8,'prt'=4] {'cls'}, dimensions={0}, use_global_device_ids=true | all-gather | bytes 9216 | tf_op jit(solution)/shard_map/all_gather | solution.py:794
  163.3 2.9 %collective-permute-start.34 = (f32[144,128]{1,0:T(8,128)}, f32[144,128]{1,0:T(8,128)S(1)}, u32[]{:S(2)}, u32[]{:S(2)}) collective-permute-start(f32[144,128]{1,0:T(8,128)} %get-tuple-element.74.refs_64_), channel_id=1, source_target_pairs={{0,1},{1,0},{2,3},{3,2},{4,5},{5,4},{6,7},{7,6},{8,9},{9,8},{10,11... | collective-permute-start | bytes 221192 | tf_op jit(solution)/shard_map/ppermute | solution.py:718
  166.2 2.8 %collective-permute-done.36.refs_67_ = f32[144,128]{1,0:T(8,128)S(1)} collective-permute-done((f32[144,128]{1,0:T(8,128)}, f32[144,128]{1,0:T(8,128)S(1)}, u32[]{:S(2)}, u32[]{:S(2)}) %collective-permute-start.36) | collective-permute-done | bytes 73760 | tf_op jit(solution)/shard_map/ppermute | solution.py:718
  169.0 2.5 %collective-permute-done.35.refs_66_ = f32[144,128]{1,0:T(8,128)S(1)} collective-permute-done((f32[144,128]{1,0:T(8,128)}, f32[144,128]{1,0:T(8,128)S(1)}, u32[]{:S(2)}, u32[]{:S(2)}) %collective-permute-start.35) | collective-permute-done | bytes 73760 | tf_op jit(solution)/shard_map/ppermute | solution.py:718
  172.1 20.4 %sums.1 = (f32[64,32,512]{2,1,0:T(8,128)}, f32[1,64]{1,0:T(1,128)}) custom-call(bf16[129,16,128]{2,1,0:T(8,128)(2,1)} %copy-done, bf16[129,16,128]{2,1,0:T(8,128)(2,1)} %copy-done.7, bf16[129,16,128]{2,1,0:T(8,128)(2,1)} %copy-done.5, bf16[129,16,128]{2,1,0:T(8,128)(2,1)} %copy-done.8, bf16[129,16,128]{2,1,0:T(8,128)(2,1)} %copy-done.4, ...), custom_call_target="tpu_custom_call" | custom-call | flops 2164260864 | bytes 21102592 | tf_op jit(solution)/shard_map/sums/pallas_call | solution.py:675
  (123 shorter events, 36.5 us)
Async XLA Ops:
  6.7 29.2 %collective-permute-start.1 = (bf16[129,16,128]{2,1,0:T(8,128)(2,1)S(1)}, bf16[129,16,128]{2,1,0:T(8,128)(2,1)S(1)}, u32[]{:S(2)}, u32[]{:S(2)}) collective-permute-start(bf16[129,16,128]{2,1,0:T(8,128)(2,1)S(1)} %get-tuple-element.45), channel_id=1, source_target_pairs={{0,2},{1,3},{2,0},{3,1},{4,6},{5,7},{6,4},{7,5},{8,10},{9,11},{10,... | collective-permute-start | bytes 1585160 | tf_op jit(solution)/shard_map/ppermute | solution.py:718
  13.5 35.0 %collective-permute-start = (bf16[129,16,128]{2,1,0:T(8,128)(2,1)S(1)}, bf16[129,16,128]{2,1,0:T(8,128)(2,1)S(1)}, u32[]{:S(2)}, u32[]{:S(2)}) collective-permute-start(bf16[129,16,128]{2,1,0:T(8,128)(2,1)S(1)} %get-tuple-element.44), channel_id=1, source_target_pairs={{0,1},{1,0},{2,3},{3,2},{4,5},{5,4},{6,7},{7,6},{8,9},{9,8},{10,11... | collective-permute-start | bytes 1585160 | tf_op jit(solution)/shard_map/ppermute | solution.py:718
  15.1 42.4 %collective-permute-start.5 = (bf16[129,16,128]{2,1,0:T(8,128)(2,1)S(1)}, bf16[129,16,128]{2,1,0:T(8,128)(2,1)S(1)}, u32[]{:S(2)}, u32[]{:S(2)}) collective-permute-start(bf16[129,16,128]{2,1,0:T(8,128)(2,1)S(1)} %get-tuple-element.48.refs_0_.refs_8_.refs_32_), channel_id=1, source_target_pairs={{0,16},{4,20},{8,24},{12,28},{16,0},{20,4},{24,8},{28,12},{1,17},{... | collective-permute-start | bytes 1585160 | tf_op jit(solution)/shard_map/ppermute | solution.py:718
  16.6 42.4 %collective-permute-start.3 = (bf16[129,16,128]{2,1,0:T(8,128)(2,1)S(1)}, bf16[129,16,128]{2,1,0:T(8,128)(2,1)S(1)}, u32[]{:S(2)}, u32[]{:S(2)}) collective-permute-start(bf16[129,16,128]{2,1,0:T(8,128)(2,1)S(1)} %get-tuple-element.48.refs_0_.refs_8_.refs_32_), channel_id=1, source_target_pairs={{0,8},{4,12},{8,0},{12,4},{16,24},{20,28},{24,16},{28,20},{1,9},{5... | collective-permute-start | bytes 1585160 | tf_op jit(solution)/shard_map/ppermute | solution.py:718
  18.1 41.5 %collective-permute-start.9 = (bf16[129,16,128]{2,1,0:T(8,128)(2,1)S(1)}, bf16[129,16,128]{2,1,0:T(8,128)(2,1)S(1)}, u32[]{:S(2)}, u32[]{:S(2)}) collective-permute-start(bf16[129,16,128]{2,1,0:T(8,128)(2,1)S(1)} %get-tuple-element.51), channel_id=1, source_target_pairs={{0,3},{1,2},{2,1},{3,0},{4,7},{5,6},{6,5},{7,4},{8,11},{9,10},{10,... | collective-permute-start | bytes 1585160 | tf_op jit(solution)/shard_map/ppermute | solution.py:718
  35.9 23.8 %collective-permute-start.20 = (bf16[129,16,128]{2,1,0:T(8,128)(2,1)S(1)}, bf16[129,16,128]{2,1,0:T(8,128)(2,1)}, u32[]{:S(2)}, u32[]{:S(2)}) collective-permute-start(bf16[129,16,128]{2,1,0:T(8,128)(2,1)S(1)} %collective-permute-done.1.refs_0_.refs_8_.refs_16_.refs_48_), channel_id=1, source_target_pairs={{0,16},{4,20},{8,24},{12,28},{16,0},{20,4},{24,8},{28,12},{1,17},{... | collective-permute-start | bytes 1585160 | tf_op jit(solution)/shard_map/ppermute | solution.py:718
  48.5 13.9 %collective-permute-start.18 = (bf16[129,16,128]{2,1,0:T(8,128)(2,1)S(1)}, bf16[129,16,128]{2,1,0:T(8,128)(2,1)}, u32[]{:S(2)}, u32[]{:S(2)}) collective-permute-start(bf16[129,16,128]{2,1,0:T(8,128)(2,1)S(1)} %collective-permute-done.1.refs_0_.refs_8_.refs_16_.refs_48_), channel_id=1, source_target_pairs={{0,8},{4,12},{8,0},{12,4},{16,24},{20,28},{24,16},{28,20},{1,9},{5... | collective-permute-start | bytes 1585160 | tf_op jit(solution)/shard_map/ppermute | solution.py:718
  59.1 15.1 %collective-permute-start.11 = (bf16[129,16,128]{2,1,0:T(8,128)(2,1)S(1)}, bf16[129,16,128]{2,1,0:T(8,128)(2,1)}, u32[]{:S(2)}, u32[]{:S(2)}) collective-permute-start(bf16[129,16,128]{2,1,0:T(8,128)(2,1)S(1)} %collective-permute-done.refs_0_.refs_8_.refs_40_), channel_id=1, source_target_pairs={{0,8},{4,12},{8,0},{12,4},{16,24},{20,28},{24,16},{28,20},{1,9},{5... | collective-permute-start | bytes 1585160 | tf_op jit(solution)/shard_map/ppermute | solution.py:718
  59.6 14.5 %collective-permute-start.2 = (bf16[129,16,128]{2,1,0:T(8,128)(2,1)S(1)}, bf16[129,16,128]{2,1,0:T(8,128)(2,1)S(1)}, u32[]{:S(2)}, u32[]{:S(2)}) collective-permute-start(bf16[129,16,128]{2,1,0:T(8,128)(2,1)S(1)} %get-tuple-element.48.refs_0_.refs_8_.refs_32_), channel_id=1, source_target_pairs={{0,4},{4,0},{8,12},{12,8},{16,20},{20,16},{24,28},{28,24},{1,5},{5... | collective-permute-start | bytes 1585160 | tf_op jit(solution)/shard_map/ppermute | solution.py:718
  59.7 16.7 %collective-permute-start.4 = (bf16[129,16,128]{2,1,0:T(8,128)(2,1)S(1)}, bf16[129,16,128]{2,1,0:T(8,128)(2,1)S(1)}, u32[]{:S(2)}, u32[]{:S(2)}) collective-permute-start(bf16[129,16,128]{2,1,0:T(8,128)(2,1)S(1)} %collective-permute-done.3.refs_2_.refs_10_.refs_34_), channel_id=1, source_target_pairs={{0,4},{4,0},{8,12},{12,8},{16,20},{20,16},{24,28},{28,24},{1,5},{5... | collective-permute-start | bytes 1585160 | tf_op jit(solution)/shard_map/ppermute | solution.py:718
  62.4 23.0 %collective-permute-start.7 = (bf16[129,16,128]{2,1,0:T(8,128)(2,1)S(1)}, bf16[129,16,128]{2,1,0:T(8,128)(2,1)S(1)}, u32[]{:S(2)}, u32[]{:S(2)}) collective-permute-start(bf16[129,16,128]{2,1,0:T(8,128)(2,1)S(1)} %collective-permute-done.5.refs_4_.refs_12_.refs_36_), channel_id=1, source_target_pairs={{0,8},{4,12},{8,0},{12,4},{16,24},{20,28},{24,16},{28,20},{1,9},{5... | collective-permute-start | bytes 1585160 | tf_op jit(solution)/shard_map/ppermute | solution.py:718
  70.0 15.4 %collective-permute-start.6 = (bf16[129,16,128]{2,1,0:T(8,128)(2,1)S(1)}, bf16[129,16,128]{2,1,0:T(8,128)(2,1)S(1)}, u32[]{:S(2)}, u32[]{:S(2)}) collective-permute-start(bf16[129,16,128]{2,1,0:T(8,128)(2,1)S(1)} %collective-permute-done.5.refs_4_.refs_12_.refs_36_), channel_id=1, source_target_pairs={{0,4},{4,0},{8,12},{12,8},{16,20},{20,16},{24,28},{28,24},{1,5},{5... | collective-permute-start | bytes 1585160 | tf_op jit(solution)/shard_map/ppermute | solution.py:718
  74.2 15.1 %collective-permute-start.15 = (bf16[129,16,128]{2,1,0:T(8,128)(2,1)}, bf16[129,16,128]{2,1,0:T(8,128)(2,1)S(1)}, u32[]{:S(2)}, u32[]{:S(2)}) collective-permute-start(bf16[129,16,128]{2,1,0:T(8,128)(2,1)} %collective-permute-done.11.refs_2_.refs_10_.refs_42_), channel_id=1, source_target_pairs={{0,16},{4,20},{8,24},{12,28},{16,0},{20,4},{24,8},{28,12},{1,17},{... | collective-permute-start | bytes 1585160 | tf_op jit(solution)/shard_map/ppermute | solution.py:718
  76.4 18.6 %collective-permute-start.23 = (bf16[129,16,128]{2,1,0:T(8,128)(2,1)S(1)}, bf16[129,16,128]{2,1,0:T(8,128)(2,1)S(1)}, u32[]{:S(2)}, u32[]{:S(2)}) collective-permute-start(bf16[129,16,128]{2,1,0:T(8,128)(2,1)S(1)} %collective-permute-done.9.refs_0_.refs_8_.refs_24_.refs_56_), channel_id=1, source_target_pairs={{0,8},{4,12},{8,0},{12,4},{16,24},{20,28},{24,16},{28,20},{1,9},{5... | collective-permute-start | bytes 1585160 | tf_op jit(solution)/shard_map/ppermute | solution.py:718
  85.4 21.3 %collective-permute-start.12 = (bf16[129,16,128]{2,1,0:T(8,128)(2,1)}, bf16[129,16,128]{2,1,0:T(8,128)(2,1)}, u32[]{:S(2)}, u32[]{:S(2)}) collective-permute-start(bf16[129,16,128]{2,1,0:T(8,128)(2,1)} %collective-permute-done.11.refs_2_.refs_10_.refs_42_), channel_id=1, source_target_pairs={{0,4},{4,0},{8,12},{12,8},{16,20},{20,16},{24,28},{28,24},{1,5},{5... | collective-permute-start | bytes 1585160 | tf_op jit(solution)/shard_map/ppermute | solution.py:718
  85.9 20.9 %collective-permute-start.14 = (bf16[129,16,128]{2,1,0:T(8,128)(2,1)}, bf16[129,16,128]{2,1,0:T(8,128)(2,1)}, u32[]{:S(2)}, u32[]{:S(2)}) collective-permute-start(bf16[129,16,128]{2,1,0:T(8,128)(2,1)} %collective-permute-done.13.refs_4_.refs_12_.refs_44_), channel_id=1, source_target_pairs={{0,4},{4,0},{8,12},{12,8},{16,20},{20,16},{24,28},{28,24},{1,5},{5... | collective-permute-start | bytes 1585160 | tf_op jit(solution)/shard_map/ppermute | solution.py:718
  89.2 18.0 %collective-permute-start.16 = (bf16[129,16,128]{2,1,0:T(8,128)(2,1)S(1)}, bf16[129,16,128]{2,1,0:T(8,128)(2,1)}, u32[]{:S(2)}, u32[]{:S(2)}) collective-permute-start(bf16[129,16,128]{2,1,0:T(8,128)(2,1)S(1)} %collective-permute-done.15.refs_6_.refs_14_.refs_46_), channel_id=1, source_target_pairs={{0,4},{4,0},{8,12},{12,8},{16,20},{20,16},{24,28},{28,24},{1,5},{5... | collective-permute-start | bytes 1585160 | tf_op jit(solution)/shard_map/ppermute | solution.py:718
  95.0 20.1 %collective-permute-start.22 = (bf16[129,16,128]{2,1,0:T(8,128)(2,1)}, bf16[129,16,128]{2,1,0:T(8,128)(2,1)}, u32[]{:S(2)}, u32[]{:S(2)}) collective-permute-start(bf16[129,16,128]{2,1,0:T(8,128)(2,1)} %collective-permute-done.20.refs_4_.refs_12_.refs_20_.refs_52_), channel_id=1, source_target_pairs={{0,8},{4,12},{8,0},{12,4},{16,24},{20,28},{24,16},{28,20},{1,9},{5... | collective-permute-start | bytes 1585160 | tf_op jit(solution)/shard_map/ppermute | solution.py:718
  97.4 18.2 %collective-permute-start.27 = (bf16[129,16,128]{2,1,0:T(8,128)(2,1)S(1)}, bf16[129,16,128]{2,1,0:T(8,128)(2,1)}, u32[]{:S(2)}, u32[]{:S(2)}) collective-permute-start(bf16[129,16,128]{2,1,0:T(8,128)(2,1)S(1)} %collective-permute-done.9.refs_0_.refs_8_.refs_24_.refs_56_), channel_id=1, source_target_pairs={{0,16},{4,20},{8,24},{12,28},{16,0},{20,4},{24,8},{28,12},{1,17},{... | collective-permute-start | bytes 1585160 | tf_op jit(solution)/shard_map/ppermute | solution.py:718
  115.6 14.1 %collective-permute-start.29 = (bf16[129,16,128]{2,1,0:T(8,128)(2,1)S(1)}, bf16[129,16,128]{2,1,0:T(8,128)(2,1)}, u32[]{:S(2)}, u32[]{:S(2)}) collective-permute-start(bf16[129,16,128]{2,1,0:T(8,128)(2,1)S(1)} %copy-done.14), channel_id=1, source_target_pairs={{0,16},{4,20},{8,24},{12,28},{16,0},{20,4},{24,8},{28,12},{1,17},{... | collective-permute-start | bytes 1585160 | tf_op jit(solution)/shard_map/ppermute | solution.py:718
  116.2 13.6 %collective-permute-start.25 = (bf16[129,16,128]{2,1,0:T(8,128)(2,1)S(1)}, bf16[129,16,128]{2,1,0:T(8,128)(2,1)S(1)}, u32[]{:S(2)}, u32[]{:S(2)}) collective-permute-start(bf16[129,16,128]{2,1,0:T(8,128)(2,1)S(1)} %collective-permute-done.9.refs_0_.refs_8_.refs_24_.refs_56_), channel_id=1, source_target_pairs={{0,4},{4,0},{8,12},{12,8},{16,20},{20,16},{24,28},{28,24},{1,5},{5... | collective-permute-start | bytes 1585160 | tf_op jit(solution)/shard_map/ppermute | solution.py:718
  116.3 16.5 %collective-permute-start.28 = (bf16[129,16,128]{2,1,0:T(8,128)(2,1)}, bf16[129,16,128]{2,1,0:T(8,128)(2,1)}, u32[]{:S(2)}, u32[]{:S(2)}) collective-permute-start(bf16[129,16,128]{2,1,0:T(8,128)(2,1)} %collective-permute-done.27.refs_4_.refs_12_.refs_28_.refs_60_), channel_id=1, source_target_pairs={{0,4},{4,0},{8,12},{12,8},{16,20},{20,16},{24,28},{28,24},{1,5},{5... | collective-permute-start | bytes 1585160 | tf_op jit(solution)/shard_map/ppermute | solution.py:718
  116.8 16.0 %collective-permute-start.26 = (bf16[129,16,128]{2,1,0:T(8,128)(2,1)S(1)}, bf16[129,16,128]{2,1,0:T(8,128)(2,1)}, u32[]{:S(2)}, u32[]{:S(2)}) collective-permute-start(bf16[129,16,128]{2,1,0:T(8,128)(2,1)S(1)} %copy-done.14), channel_id=1, source_target_pairs={{0,4},{4,0},{8,12},{12,8},{16,20},{20,16},{24,28},{28,24},{1,5},{5... | collective-permute-start | bytes 1585160 | tf_op jit(solution)/shard_map/ppermute | solution.py:718
  129.7 13.2 %collective-permute-start.31 = (f32[144,128]{1,0:T(8,128)S(1)}, f32[144,128]{1,0:T(8,128)S(1)}, u32[]{:S(2)}, u32[]{:S(2)}) collective-permute-start(f32[144,128]{1,0:T(8,128)S(1)} %copy-done.28), channel_id=1, source_target_pairs={{0,1},{1,0},{2,3},{3,2},{4,5},{5,4},{6,7},{7,6},{8,9},{9,8},{10,11... | collective-permute-start | bytes 221192 | tf_op jit(solution)/shard_map/ppermute | solution.py:718
  (42 other events, 542.3 us)

commit v8 on v7

--- a/solution.py
+++ b/solution.py
@@ -766,7 +766,10 @@
         outgoing.update(zip(distances, made))
         place = after(prt, made[0])
     last = outgoing[order[-1]]
-    arrived = {d: hop(outgoing[d], "prt", d) if d else outgoing[d] for d in order}
+    arrived = {0: outgoing[0]}
+    for d in order[1:]:
+        block = after(outgoing[d], arrived[2]) if d > 2 else outgoing[d]
+        arrived[d] = hop(block, "prt", d)
     known = {0: {0: arrived[0], **direct(arrived[0])}}
     for d in range(1, min(n_prt, 3)):
         own = after(arrived[d], last) if d == 2 else arrived[d]

time: 193 us -> 187 us (0.969)
  starting transfers between devices: 47 us -> 34 us
  waiting for transfers between devices: 59.8 us -> 65.3 us
    ppermute x37, starting transfers between devices: 47 us -> 34 us  [hop(): return lax.ppermute(value, axis, [(i, i ^ distance) for i in range(size)])]
    ppermute x37, waiting for transfers between devices: 59.8 us -> 65.3 us  [hop(): return lax.ppermute(value, axis, [(i, i ^ distance) for i in range(size)])]
    unnamed x59 -> x57, local copies, waits for them, and re-layouts: 6.35 us -> 6.03 us
  transfers between devices with their start and end apart: 37 -> 37, of which waited for: 13 -> 13; matrix products, arithmetic and copies ran while one was open for 0% -> 0% of each run, Pallas kernels for 21% -> 22%
where the time goes in v8:
time: 187 us; the launch traced here: 186 us
  Pallas kernels  68.2 us (36%)
  waiting for transfers between devices  65.3 us (35%)
  starting transfers between devices  34 us (18%)
  blocking collectives  10.6 us (6%)
  local copies, waits for them, and re-layouts  6.95 us (4%)
    ppermute x37, waiting for transfers between devices, hop(): return lax.ppermute(value, axis, [(i, i ^ distance) for i in range(size)])  65.3 us
    ppermute x37, starting transfers between devices, hop(): return lax.ppermute(value, axis, [(i, i ^ distance) for i in range(size)])  34 us
    pallas_call x4, Pallas kernels, cross_coefficients(): pl.pallas_call(cross_body, grid_spec=pltpu.PrefetchScalarGridSpec(num_sca...  30.9 us
    pallas_call x1, Pallas kernels, sums(): pl.pallas_call(functools.partial(sums_body, number=len(blocks), pieces=le...  20.4 us
    all_gather x1, blocking collectives, gather_device(): lax.all_gather(stat.reshape(1, *stat.shape), 'cls', axis=0, tiled=True)  10.6 us
    pallas_call x1, Pallas kernels, arrange_references(): pl.pallas_call(reference_body, grid_spec=pltpu.PrefetchScalarGridSpec(num...  7.45 us
    unnamed x57, local copies, waits for them, and re-layouts  6.03 us
    pallas_call x2, Pallas kernels, arrange_particles(): pl.pallas_call(functools.partial(particle_body, distances=distances, n_pr...  5.35 us
  transfers between devices with their start and end apart: 37, of which 13 were waited for; matrix products, arithmetic and copies ran while one was open for 0% of the time, Pallas kernels for 22%

profile of v8, /device:TPU:0, one launch (start us, length us, event | category | flops | bytes accessed | tf_op | source)
XLA Modules:
  0.0 186.3 jit_solution(8959974548278658923)
XLA Ops:
  4.0 2.7 %arrange_particles.2 = (bf16[129,16,128]{2,1,0:T(8,128)(2,1)S(1)}, bf16[129,16,128]{2,1,0:T(8,128)(2,1)S(1)}) custom-call(s32[1]{0:T(128)} %bitcast.at_ref, bf16[16,128,512]{2,1,0:T(8,128)(2,1)S(1)} %copy-done.1, s32[16,20]{1,0:T(8,128)S(1)} %pad_add_fusion.meta_ref), custom_call_target="tpu_custom_call" | custom-call | flops 134217728 | bytes 2097152 | tf_op jit(solution)/shard_map/arrange_particles/pallas_call | solution.py:279
  6.7 4.1 %collective-permute-start.1 = (bf16[129,16,128]{2,1,0:T(8,128)(2,1)S(1)}, bf16[129,16,128]{2,1,0:T(8,128)(2,1)S(1)}, u32[]{:S(2)}, u32[]{:S(2)}) collective-permute-start(bf16[129,16,128]{2,1,0:T(8,128)(2,1)S(1)} %get-tuple-element.46), channel_id=1, source_target_pairs={{0,2},{1,3},{2,0},{3,1},{4,6},{5,7},{6,4},{7,5},{8,10},{9,11},{10,... | collective-permute-start | bytes 1585160 | tf_op jit(solution)/shard_map/ppermute | solution.py:718
  10.8 2.7 %arrange_particles.3 = (bf16[129,16,128]{2,1,0:T(8,128)(2,1)S(1)}, bf16[129,16,128]{2,1,0:T(8,128)(2,1)S(1)}) custom-call(s32[1]{0:T(128)} %bitcast.at_ref, bf16[16,128,512]{2,1,0:T(8,128)(2,1)S(1)} %copy-done.1, s32[16,20]{1,0:T(8,128)S(1)} %pad_add_fusion.meta_ref), custom_call_target="tpu_custom_call" | custom-call | flops 134217728 | bytes 2097152 | tf_op jit(solution)/shard_map/arrange_particles/pallas_call | solution.py:279
  18.1 16.1 %collective-permute-done.1.refs_0_.refs_8_.refs_16_.refs_48_ = bf16[129,16,128]{2,1,0:T(8,128)(2,1)S(1)} collective-permute-done((bf16[129,16,128]{2,1,0:T(8,128)(2,1)S(1)}, bf16[129,16,128]{2,1,0:T(8,128)(2,1)S(1)}, u32[]{:S(2)}, u32[]{:S(2)}) %collective-permute-start.1) | collective-permute-done | bytes 528416 | tf_op jit(solution)/shard_map/ppermute | solution.py:718
  34.2 3.5 %collective-permute-start.9 = (bf16[129,16,128]{2,1,0:T(8,128)(2,1)S(1)}, bf16[129,16,128]{2,1,0:T(8,128)(2,1)S(1)}, u32[]{:S(2)}, u32[]{:S(2)}) collective-permute-start(bf16[129,16,128]{2,1,0:T(8,128)(2,1)S(1)} %get-tuple-element.53), channel_id=1, source_target_pairs={{0,3},{1,2},{2,1},{3,0},{4,7},{5,6},{6,5},{7,4},{8,11},{9,10},{10,... | collective-permute-start | bytes 1585160 | tf_op jit(solution)/shard_map/ppermute | solution.py:718
  40.8 7.5 %arrange_references.1 = (bf16[128,64,128]{2,1,0:T(8,128)(2,1)}, f32[64,128]{1,0:T(8,128)}) custom-call(s32[1]{0:T(128)} %bitcast.at_ref, bf16[64,128,512]{2,1,0:T(8,128)(2,1)} %x_ref.5), custom_call_target="tpu_custom_call" | custom-call | flops 268435456 | bytes 4194304 | tf_op jit(solution)/shard_map/arrange_references/pallas_call | solution.py:320
  54.4 11.3 %collective-permute-done.11.refs_2_.refs_10_.refs_42_ = bf16[129,16,128]{2,1,0:T(8,128)(2,1)} collective-permute-done((bf16[129,16,128]{2,1,0:T(8,128)(2,1)S(1)}, bf16[129,16,128]{2,1,0:T(8,128)(2,1)}, u32[]{:S(2)}, u32[]{:S(2)}) %collective-permute-start.11) | collective-permute-done | bytes 528416 | tf_op jit(solution)/shard_map/ppermute | solution.py:718
  66.2 9.1 %collective-permute-done.7.refs_6_.refs_14_.refs_38_ = bf16[129,16,128]{2,1,0:T(8,128)(2,1)S(1)} collective-permute-done((bf16[129,16,128]{2,1,0:T(8,128)(2,1)S(1)}, bf16[129,16,128]{2,1,0:T(8,128)(2,1)S(1)}, u32[]{:S(2)}, u32[]{:S(2)}) %collective-permute-start.7) | collective-permute-done | bytes 528416 | tf_op jit(solution)/shard_map/ppermute | solution.py:718
  77.3 3.1 %collective-permute-done.15.refs_6_.refs_14_.refs_46_ = bf16[129,16,128]{2,1,0:T(8,128)(2,1)} collective-permute-done((bf16[129,16,128]{2,1,0:T(8,128)(2,1)}, bf16[129,16,128]{2,1,0:T(8,128)(2,1)}, u32[]{:S(2)}, u32[]{:S(2)}) %collective-permute-start.15) | collective-permute-done | bytes 528416 | tf_op jit(solution)/shard_map/ppermute | solution.py:718
  82.4 8.3 %collective-permute-done.23.refs_2_.refs_10_.refs_26_.refs_58_ = bf16[129,16,128]{2,1,0:T(8,128)(2,1)S(1)} collective-permute-done((bf16[129,16,128]{2,1,0:T(8,128)(2,1)S(1)}, bf16[129,16,128]{2,1,0:T(8,128)(2,1)S(1)}, u32[]{:S(2)}, u32[]{:S(2)}) %collective-permute-start.23) | collective-permute-done | bytes 528416 | tf_op jit(solution)/shard_map/ppermute | solution.py:718
  92.1 7.7 %cross_coefficients.4 = (f32[144,128]{1,0:T(8,128)}, f32[8,128]{1,0:T(8,128)}) custom-call(s32[1]{0:T(128)} %bitcast.2.at_ref, bf16[129,16,128]{2,1,0:T(8,128)(2,1)} %copy-done, bf16[129,16,128]{2,1,0:T(8,128)(2,1)} %copy-done.8, bf16[129,16,128]{2,1,0:T(8,128)(2,1)} %copy-done.5, bf16[129,16,128]{2,1,0:T(8,128)(2,1)} %copy-done.9, ...), custom_call_target="tpu_custom_call" | custom-call | flops 541065216 | bytes 4227072 | tf_op jit(solution)/shard_map/cross_coefficients/pallas_call | solution.py:451
  100.5 7.7 %cross_coefficients.5 = (f32[144,128]{1,0:T(8,128)}, f32[8,128]{1,0:T(8,128)}) custom-call(s32[1]{0:T(128)} %bitcast.2.at_ref, bf16[129,16,128]{2,1,0:T(8,128)(2,1)} %copy-done.3, bf16[129,16,128]{2,1,0:T(8,128)(2,1)} %copy-done.12, bf16[129,16,128]{2,1,0:T(8,128)(2,1)} %collective-permute-done.11.refs_2_.refs_10_.refs_42_, ...), custom_call_target="tpu_custom_call" | custom-call | flops 541065216 | bytes 4227072 | tf_op jit(solution)/shard_map/cross_coefficients/pallas_call | solution.py:451
  111.6 7.7 %cross_coefficients.6 = (f32[144,128]{1,0:T(8,128)}, f32[8,128]{1,0:T(8,128)}) custom-call(s32[1]{0:T(128)} %bitcast.2.at_ref, bf16[129,16,128]{2,1,0:T(8,128)(2,1)} %copy-done.2, bf16[129,16,128]{2,1,0:T(8,128)(2,1)} %copy-done.16, bf16[129,16,128]{2,1,0:T(8,128)(2,1)} %collective-permute-done.18.refs_2_.refs_10_.refs_18_.refs_50_, ...), custom_call_target="tpu_custom_call" | custom-call | flops 541065216 | bytes 4227072 | tf_op jit(solution)/shard_map/cross_coefficients/pallas_call | solution.py:451
  119.4 3.5 %collective-permute-done.29.refs_6_.refs_14_.refs_30_.refs_62_ = bf16[129,16,128]{2,1,0:T(8,128)(2,1)} collective-permute-done((bf16[129,16,128]{2,1,0:T(8,128)(2,1)S(1)}, bf16[129,16,128]{2,1,0:T(8,128)(2,1)}, u32[]{:S(2)}, u32[]{:S(2)}) %collective-permute-start.29) | collective-permute-done | bytes 528416 | tf_op jit(solution)/shard_map/ppermute | solution.py:718
  125.8 7.7 %cross_coefficients.7 = (f32[144,128]{1,0:T(8,128)}, f32[8,128]{1,0:T(8,128)}) custom-call(s32[1]{0:T(128)} %bitcast.2.at_ref, bf16[129,16,128]{2,1,0:T(8,128)(2,1)} %copy-done.6, bf16[129,16,128]{2,1,0:T(8,128)(2,1)} %copy-done.19, bf16[129,16,128]{2,1,0:T(8,128)(2,1)} %copy-done.13, ...), custom_call_target="tpu_custom_call" | custom-call | flops 541065216 | bytes 4227072 | tf_op jit(solution)/shard_map/cross_coefficients/pallas_call | solution.py:451
  133.6 2.3 %collective-permute-start.33 = (f32[144,128]{1,0:T(8,128)}, f32[144,128]{1,0:T(8,128)S(1)}, u32[]{:S(2)}, u32[]{:S(2)}) collective-permute-start(f32[144,128]{1,0:T(8,128)} %get-tuple-element.72), channel_id=1, source_target_pairs={{0,3},{1,2},{2,1},{3,0},{4,7},{5,6},{6,5},{7,4},{8,11},{9,10},{10,... | collective-permute-start | bytes 221192 | tf_op jit(solution)/shard_map/ppermute | solution.py:718
  135.9 4.1 %collective-permute-done.33.refs_3_ = f32[144,128]{1,0:T(8,128)S(1)} collective-permute-done((f32[144,128]{1,0:T(8,128)}, f32[144,128]{1,0:T(8,128)S(1)}, u32[]{:S(2)}, u32[]{:S(2)}) %collective-permute-start.33) | collective-permute-done | bytes 73760 | tf_op jit(solution)/shard_map/ppermute | solution.py:718
  142.7 10.6 %all-gather.1.stat_ref = f32[8,2,128]{2,1,0:T(2,128)} all-gather(f32[1,2,128]{2,1,0:T(2,128)} %bitcast.9), channel_id=2, replica_groups=mesh['cls'=8,'prt'=4] {'cls'}, dimensions={0}, use_global_device_ids=true | all-gather | bytes 9216 | tf_op jit(solution)/shard_map/all_gather | solution.py:797
  153.3 2.1 %mixed_weights.1 = (f32[144,128]{1,0:T(8,128)}, f32[1,16]{1,0:T(1,128)}) custom-call(s32[1]{0:T(128)} %bitcast.2.at_ref, f32[144,128]{1,0:T(8,128)} %get-tuple-element.74.score_ref, f32[8,128]{1,0:T(8,128)} %get-tuple-element.73.refs_4_.cand_ref.refs_68_, f32[8,2,128]{2,1,0:T(2,128)} %all-gather.1.stat_ref, f32[144,144]{1,0:T(8,128)} %constant.14.clone.refs_5_.table_ref), custom_call_target="tpu_custom_call" | custom-call | tf_op jit(solution)/shard_map/mixed_weights/pallas_call | solution.py:556
  155.4 2.3 %collective-permute-start.36 = (f32[144,128]{1,0:T(8,128)}, f32[144,128]{1,0:T(8,128)S(1)}, u32[]{:S(2)}, u32[]{:S(2)}) collective-permute-start(f32[144,128]{1,0:T(8,128)} %get-tuple-element.76.refs_64_), channel_id=1, source_target_pairs={{0,3},{1,2},{2,1},{3,0},{4,7},{5,6},{6,5},{7,4},{8,11},{9,10},{10,... | collective-permute-start | bytes 221192 | tf_op jit(solution)/shard_map/ppermute | solution.py:718
  157.7 2.1 %collective-permute-start.34 = (f32[144,128]{1,0:T(8,128)}, f32[144,128]{1,0:T(8,128)S(1)}, u32[]{:S(2)}, u32[]{:S(2)}) collective-permute-start(f32[144,128]{1,0:T(8,128)} %get-tuple-element.76.refs_64_), channel_id=1, source_target_pairs={{0,1},{1,0},{2,3},{3,2},{4,5},{5,4},{6,7},{7,6},{8,9},{9,8},{10,11... | collective-permute-start | bytes 221192 | tf_op jit(solution)/shard_map/ppermute | solution.py:718
  159.8 2.8 %collective-permute-done.36.refs_67_ = f32[144,128]{1,0:T(8,128)S(1)} collective-permute-done((f32[144,128]{1,0:T(8,128)}, f32[144,128]{1,0:T(8,128)S(1)}, u32[]{:S(2)}, u32[]{:S(2)}) %collective-permute-start.36) | collective-permute-done | bytes 73760 | tf_op jit(solution)/shard_map/ppermute | solution.py:718
  162.6 2.5 %collective-permute-done.35.refs_66_ = f32[144,128]{1,0:T(8,128)S(1)} collective-permute-done((f32[144,128]{1,0:T(8,128)}, f32[144,128]{1,0:T(8,128)S(1)}, u32[]{:S(2)}, u32[]{:S(2)}) %collective-permute-start.35) | collective-permute-done | bytes 73760 | tf_op jit(solution)/shard_map/ppermute | solution.py:718
  165.7 20.4 %sums.1 = (f32[64,32,512]{2,1,0:T(8,128)}, f32[1,64]{1,0:T(1,128)}) custom-call(bf16[129,16,128]{2,1,0:T(8,128)(2,1)} %copy-done, bf16[129,16,128]{2,1,0:T(8,128)(2,1)} %copy-done.8, bf16[129,16,128]{2,1,0:T(8,128)(2,1)} %copy-done.5, bf16[129,16,128]{2,1,0:T(8,128)(2,1)} %copy-done.9, bf16[129,16,128]{2,1,0:T(8,128)(2,1)} %copy-done.4, ...), custom_call_target="tpu_custom_call" | custom-call | flops 2164260864 | bytes 21102592 | tf_op jit(solution)/shard_map/sums/pallas_call | solution.py:675
  (121 shorter events, 33.3 us)
Async XLA Ops:
  6.7 27.5 %collective-permute-start.1 = (bf16[129,16,128]{2,1,0:T(8,128)(2,1)S(1)}, bf16[129,16,128]{2,1,0:T(8,128)(2,1)S(1)}, u32[]{:S(2)}, u32[]{:S(2)}) collective-permute-start(bf16[129,16,128]{2,1,0:T(8,128)(2,1)S(1)} %get-tuple-element.46), channel_id=1, source_target_pairs={{0,2},{1,3},{2,0},{3,1},{4,6},{5,7},{6,4},{7,5},{8,10},{9,11},{10,... | collective-permute-start | bytes 1585160 | tf_op jit(solution)/shard_map/ppermute | solution.py:718
  13.5 25.8 %collective-permute-start = (bf16[129,16,128]{2,1,0:T(8,128)(2,1)S(1)}, bf16[129,16,128]{2,1,0:T(8,128)(2,1)S(1)}, u32[]{:S(2)}, u32[]{:S(2)}) collective-permute-start(bf16[129,16,128]{2,1,0:T(8,128)(2,1)S(1)} %get-tuple-element.45), channel_id=1, source_target_pairs={{0,1},{1,0},{2,3},{3,2},{4,5},{5,4},{6,7},{7,6},{8,9},{9,8},{10,11... | collective-permute-start | bytes 1585160 | tf_op jit(solution)/shard_map/ppermute | solution.py:718
  15.1 33.1 %collective-permute-start.5 = (bf16[129,16,128]{2,1,0:T(8,128)(2,1)S(1)}, bf16[129,16,128]{2,1,0:T(8,128)(2,1)S(1)}, u32[]{:S(2)}, u32[]{:S(2)}) collective-permute-start(bf16[129,16,128]{2,1,0:T(8,128)(2,1)S(1)} %get-tuple-element.49.refs_0_.refs_8_.refs_32_), channel_id=1, source_target_pairs={{0,16},{4,20},{8,24},{12,28},{16,0},{20,4},{24,8},{28,12},{1,17},{... | collective-permute-start | bytes 1585160 | tf_op jit(solution)/shard_map/ppermute | solution.py:718
  16.6 32.2 %collective-permute-start.3 = (bf16[129,16,128]{2,1,0:T(8,128)(2,1)S(1)}, bf16[129,16,128]{2,1,0:T(8,128)(2,1)S(1)}, u32[]{:S(2)}, u32[]{:S(2)}) collective-permute-start(bf16[129,16,128]{2,1,0:T(8,128)(2,1)S(1)} %get-tuple-element.49.refs_0_.refs_8_.refs_32_), channel_id=1, source_target_pairs={{0,8},{4,12},{8,0},{12,4},{16,24},{20,28},{24,16},{28,20},{1,9},{5... | collective-permute-start | bytes 1585160 | tf_op jit(solution)/shard_map/ppermute | solution.py:718
  34.2 15.8 %collective-permute-start.9 = (bf16[129,16,128]{2,1,0:T(8,128)(2,1)S(1)}, bf16[129,16,128]{2,1,0:T(8,128)(2,1)S(1)}, u32[]{:S(2)}, u32[]{:S(2)}) collective-permute-start(bf16[129,16,128]{2,1,0:T(8,128)(2,1)S(1)} %get-tuple-element.53), channel_id=1, source_target_pairs={{0,3},{1,2},{2,1},{3,0},{4,7},{5,6},{6,5},{7,4},{8,11},{9,10},{10,... | collective-permute-start | bytes 1585160 | tf_op jit(solution)/shard_map/ppermute | solution.py:718
  37.8 14.7 %collective-permute-start.20 = (bf16[129,16,128]{2,1,0:T(8,128)(2,1)S(1)}, bf16[129,16,128]{2,1,0:T(8,128)(2,1)}, u32[]{:S(2)}, u32[]{:S(2)}) collective-permute-start(bf16[129,16,128]{2,1,0:T(8,128)(2,1)S(1)} %collective-permute-done.1.refs_0_.refs_8_.refs_16_.refs_48_), channel_id=1, source_target_pairs={{0,16},{4,20},{8,24},{12,28},{16,0},{20,4},{24,8},{28,12},{1,17},{... | collective-permute-start | bytes 1585160 | tf_op jit(solution)/shard_map/ppermute | solution.py:718
  39.3 15.1 %collective-permute-start.18 = (bf16[129,16,128]{2,1,0:T(8,128)(2,1)S(1)}, bf16[129,16,128]{2,1,0:T(8,128)(2,1)}, u32[]{:S(2)}, u32[]{:S(2)}) collective-permute-start(bf16[129,16,128]{2,1,0:T(8,128)(2,1)S(1)} %collective-permute-done.1.refs_0_.refs_8_.refs_16_.refs_48_), channel_id=1, source_target_pairs={{0,8},{4,12},{8,0},{12,4},{16,24},{20,28},{24,16},{28,20},{1,9},{5... | collective-permute-start | bytes 1585160 | tf_op jit(solution)/shard_map/ppermute | solution.py:718
  48.2 17.4 %collective-permute-start.11 = (bf16[129,16,128]{2,1,0:T(8,128)(2,1)S(1)}, bf16[129,16,128]{2,1,0:T(8,128)(2,1)}, u32[]{:S(2)}, u32[]{:S(2)}) collective-permute-start(bf16[129,16,128]{2,1,0:T(8,128)(2,1)S(1)} %collective-permute-done.refs_0_.refs_8_.refs_40_), channel_id=1, source_target_pairs={{0,8},{4,12},{8,0},{12,4},{16,24},{20,28},{24,16},{28,20},{1,9},{5... | collective-permute-start | bytes 1585160 | tf_op jit(solution)/shard_map/ppermute | solution.py:718
  48.8 16.8 %collective-permute-start.13 = (bf16[129,16,128]{2,1,0:T(8,128)(2,1)S(1)}, bf16[129,16,128]{2,1,0:T(8,128)(2,1)}, u32[]{:S(2)}, u32[]{:S(2)}) collective-permute-start(bf16[129,16,128]{2,1,0:T(8,128)(2,1)S(1)} %collective-permute-done.refs_0_.refs_8_.refs_40_), channel_id=1, source_target_pairs={{0,16},{4,20},{8,24},{12,28},{16,0},{20,4},{24,8},{28,12},{1,17},{... | collective-permute-start | bytes 1585160 | tf_op jit(solution)/shard_map/ppermute | solution.py:718
  50.0 25.2 %collective-permute-start.7 = (bf16[129,16,128]{2,1,0:T(8,128)(2,1)S(1)}, bf16[129,16,128]{2,1,0:T(8,128)(2,1)S(1)}, u32[]{:S(2)}, u32[]{:S(2)}) collective-permute-start(bf16[129,16,128]{2,1,0:T(8,128)(2,1)S(1)} %collective-permute-done.5.refs_4_.refs_12_.refs_36_), channel_id=1, source_target_pairs={{0,8},{4,12},{8,0},{12,4},{16,24},{20,28},{24,16},{28,20},{1,9},{5... | collective-permute-start | bytes 1585160 | tf_op jit(solution)/shard_map/ppermute | solution.py:718
  52.5 22.8 %collective-permute-start.2 = (bf16[129,16,128]{2,1,0:T(8,128)(2,1)S(1)}, bf16[129,16,128]{2,1,0:T(8,128)(2,1)S(1)}, u32[]{:S(2)}, u32[]{:S(2)}) collective-permute-start(bf16[129,16,128]{2,1,0:T(8,128)(2,1)S(1)} %get-tuple-element.49.refs_0_.refs_8_.refs_32_), channel_id=1, source_target_pairs={{0,4},{4,0},{8,12},{12,8},{16,20},{20,16},{24,28},{28,24},{1,5},{5... | collective-permute-start | bytes 1585160 | tf_op jit(solution)/shard_map/ppermute | solution.py:718
  54.4 21.5 %collective-permute-start.4 = (bf16[129,16,128]{2,1,0:T(8,128)(2,1)S(1)}, bf16[129,16,128]{2,1,0:T(8,128)(2,1)S(1)}, u32[]{:S(2)}, u32[]{:S(2)}) collective-permute-start(bf16[129,16,128]{2,1,0:T(8,128)(2,1)S(1)} %collective-permute-done.3.refs_2_.refs_10_.refs_34_), channel_id=1, source_target_pairs={{0,4},{4,0},{8,12},{12,8},{16,20},{20,16},{24,28},{28,24},{1,5},{5... | collective-permute-start | bytes 1585160 | tf_op jit(solution)/shard_map/ppermute | solution.py:718
  65.7 14.7 %collective-permute-start.15 = (bf16[129,16,128]{2,1,0:T(8,128)(2,1)}, bf16[129,16,128]{2,1,0:T(8,128)(2,1)}, u32[]{:S(2)}, u32[]{:S(2)}) collective-permute-start(bf16[129,16,128]{2,1,0:T(8,128)(2,1)} %collective-permute-done.11.refs_2_.refs_10_.refs_42_), channel_id=1, source_target_pairs={{0,16},{4,20},{8,24},{12,28},{16,0},{20,4},{24,8},{28,12},{1,17},{... | collective-permute-start | bytes 1585160 | tf_op jit(solution)/shard_map/ppermute | solution.py:718
  75.8 14.9 %collective-permute-start.23 = (bf16[129,16,128]{2,1,0:T(8,128)(2,1)S(1)}, bf16[129,16,128]{2,1,0:T(8,128)(2,1)S(1)}, u32[]{:S(2)}, u32[]{:S(2)}) collective-permute-start(bf16[129,16,128]{2,1,0:T(8,128)(2,1)S(1)} %collective-permute-done.9.refs_0_.refs_8_.refs_24_.refs_56_), channel_id=1, source_target_pairs={{0,8},{4,12},{8,0},{12,4},{16,24},{20,28},{24,16},{28,20},{1,9},{5... | collective-permute-start | bytes 1585160 | tf_op jit(solution)/shard_map/ppermute | solution.py:718
  77.3 22.5 %collective-permute-start.12 = (bf16[129,16,128]{2,1,0:T(8,128)(2,1)}, bf16[129,16,128]{2,1,0:T(8,128)(2,1)}, u32[]{:S(2)}, u32[]{:S(2)}) collective-permute-start(bf16[129,16,128]{2,1,0:T(8,128)(2,1)} %collective-permute-done.11.refs_2_.refs_10_.refs_42_), channel_id=1, source_target_pairs={{0,4},{4,0},{8,12},{12,8},{16,20},{20,16},{24,28},{28,24},{1,5},{5... | collective-permute-start | bytes 1585160 | tf_op jit(solution)/shard_map/ppermute | solution.py:718
  80.4 19.5 %collective-permute-start.14 = (bf16[129,16,128]{2,1,0:T(8,128)(2,1)}, bf16[129,16,128]{2,1,0:T(8,128)(2,1)}, u32[]{:S(2)}, u32[]{:S(2)}) collective-permute-start(bf16[129,16,128]{2,1,0:T(8,128)(2,1)} %collective-permute-done.13.refs_4_.refs_12_.refs_44_), channel_id=1, source_target_pairs={{0,4},{4,0},{8,12},{12,8},{16,20},{20,16},{24,28},{28,24},{1,5},{5... | collective-permute-start | bytes 1585160 | tf_op jit(solution)/shard_map/ppermute | solution.py:718
  80.4 20.0 %collective-permute-start.16 = (bf16[129,16,128]{2,1,0:T(8,128)(2,1)}, bf16[129,16,128]{2,1,0:T(8,128)(2,1)}, u32[]{:S(2)}, u32[]{:S(2)}) collective-permute-start(bf16[129,16,128]{2,1,0:T(8,128)(2,1)} %collective-permute-done.15.refs_6_.refs_14_.refs_46_), channel_id=1, source_target_pairs={{0,4},{4,0},{8,12},{12,8},{16,20},{20,16},{24,28},{28,24},{1,5},{5... | collective-permute-start | bytes 1585160 | tf_op jit(solution)/shard_map/ppermute | solution.py:718
  80.9 27.3 %collective-permute-start.22 = (bf16[129,16,128]{2,1,0:T(8,128)(2,1)}, bf16[129,16,128]{2,1,0:T(8,128)(2,1)S(1)}, u32[]{:S(2)}, u32[]{:S(2)}) collective-permute-start(bf16[129,16,128]{2,1,0:T(8,128)(2,1)} %collective-permute-done.20.refs_4_.refs_12_.refs_20_.refs_52_), channel_id=1, source_target_pairs={{0,8},{4,12},{8,0},{12,4},{16,24},{20,28},{24,16},{28,20},{1,9},{5... | collective-permute-start | bytes 1585160 | tf_op jit(solution)/shard_map/ppermute | solution.py:718
  91.6 17.2 %collective-permute-start.27 = (bf16[129,16,128]{2,1,0:T(8,128)(2,1)S(1)}, bf16[129,16,128]{2,1,0:T(8,128)(2,1)}, u32[]{:S(2)}, u32[]{:S(2)}) collective-permute-start(bf16[129,16,128]{2,1,0:T(8,128)(2,1)S(1)} %collective-permute-done.9.refs_0_.refs_8_.refs_24_.refs_56_), channel_id=1, source_target_pairs={{0,16},{4,20},{8,24},{12,28},{16,0},{20,4},{24,8},{28,12},{1,17},{... | collective-permute-start | bytes 1585160 | tf_op jit(solution)/shard_map/ppermute | solution.py:718
  108.7 14.1 %collective-permute-start.29 = (bf16[129,16,128]{2,1,0:T(8,128)(2,1)S(1)}, bf16[129,16,128]{2,1,0:T(8,128)(2,1)}, u32[]{:S(2)}, u32[]{:S(2)}) collective-permute-start(bf16[129,16,128]{2,1,0:T(8,128)(2,1)S(1)} %copy-done.14), channel_id=1, source_target_pairs={{0,16},{4,20},{8,24},{12,28},{16,0},{20,4},{24,8},{28,12},{1,17},{... | collective-permute-start | bytes 1585160 | tf_op jit(solution)/shard_map/ppermute | solution.py:718
  110.4 13.6 %collective-permute-start.28 = (bf16[129,16,128]{2,1,0:T(8,128)(2,1)}, bf16[129,16,128]{2,1,0:T(8,128)(2,1)}, u32[]{:S(2)}, u32[]{:S(2)}) collective-permute-start(bf16[129,16,128]{2,1,0:T(8,128)(2,1)} %collective-permute-done.27.refs_4_.refs_12_.refs_28_.refs_60_), channel_id=1, source_target_pairs={{0,4},{4,0},{8,12},{12,8},{16,20},{20,16},{24,28},{28,24},{1,5},{5... | collective-permute-start | bytes 1585160 | tf_op jit(solution)/shard_map/ppermute | solution.py:718
  110.9 13.2 %collective-permute-start.26 = (bf16[129,16,128]{2,1,0:T(8,128)(2,1)S(1)}, bf16[129,16,128]{2,1,0:T(8,128)(2,1)}, u32[]{:S(2)}, u32[]{:S(2)}) collective-permute-start(bf16[129,16,128]{2,1,0:T(8,128)(2,1)S(1)} %copy-done.14), channel_id=1, source_target_pairs={{0,4},{4,0},{8,12},{12,8},{16,20},{20,16},{24,28},{28,24},{1,5},{5... | collective-permute-start | bytes 1585160 | tf_op jit(solution)/shard_map/ppermute | solution.py:718
  122.9 13.1 %collective-permute-start.31 = (f32[144,128]{1,0:T(8,128)S(1)}, f32[144,128]{1,0:T(8,128)S(1)}, u32[]{:S(2)}, u32[]{:S(2)}) collective-permute-start(f32[144,128]{1,0:T(8,128)S(1)} %copy-done.27), channel_id=1, source_target_pairs={{0,1},{1,0},{2,3},{3,2},{4,5},{5,4},{6,7},{7,6},{8,9},{9,8},{10,11... | collective-permute-start | bytes 221192 | tf_op jit(solution)/shard_map/ppermute | solution.py:718
  122.9 13.0 %collective-permute-start.32 = (f32[144,128]{1,0:T(8,128)}, f32[144,128]{1,0:T(8,128)S(1)}, u32[]{:S(2)}, u32[]{:S(2)}) collective-permute-start(f32[144,128]{1,0:T(8,128)} %get-tuple-element.70), channel_id=1, source_target_pairs={{0,2},{1,3},{2,0},{3,1},{4,6},{5,7},{6,4},{7,5},{8,10},{9,11},{10,... | collective-permute-start | bytes 221192 | tf_op jit(solution)/shard_map/ppermute | solution.py:718
  (41 other events, 529.3 us)

commit v9 on v8

--- a/solution.py
+++ b/solution.py
@@ -774,7 +774,8 @@
     for d in range(1, min(n_prt, 3)):
         own = after(arrived[d], last) if d == 2 else arrived[d]
         known[d] = {0: own, **direct(own)}
-    place = after(prt, *[arrived[d] for d in range(1, min(n_prt, 3))])
+    place = after(prt, known[0][2], known[0][n_cls // 2])
+    place = after(place, *[arrived[d] for d in range(1, min(n_prt, 3))])
     arranged, norms = arrange_references(references, place, n_prt)
     for d in range(3, n_prt):
         arrived[d] = after(arrived[d], arranged)
@@ -786,7 +787,8 @@
     coefs, cands, sent, blocks = [], [], [], []
     for d in range(n_prt):
         waits = [known[n_prt - 1][2]] if d == 1 else []
-        each = [arranged] if d == 0 else [arranged, arrived[n_prt - 1]] if d == 1 else coefs[:1]
+        first = [known[e][j] for e in range(1, n_prt) for j in (2, n_cls // 2)]
+        each = first if d < 2 else coefs[:1]
         blocks.append(paired(known[d], each, coefs[-1:] if d > 1 else []))
         ready = after(arranged, *waits) if waits else arranged
         coef, cand = cross_coefficients(blocks[d], ready, norms, cls)

time: 187 us -> 188 us (level)
  starting transfers between devices: 34 us -> 36.8 us
    ppermute x37, starting transfers between devices: 34 us -> 36.8 us  [hop(): return lax.ppermute(value, axis, [(i, i ^ distance) for i in range(size)])]
  transfers between devices with their start and end apart: 37 -> 37, of which waited for: 13 -> 17; matrix products, arithmetic and copies ran while one was open for 0% -> 0% of each run, Pallas kernels for 22% -> 22%
where the time goes in v9:
time: 188 us
  Pallas kernels  68.4 us (36%)
  waiting for transfers between devices  64.3 us (34%)
  starting transfers between devices  36.8 us (20%)
  blocking collectives  9.97 us (5%)
  local copies, waits for them, and re-layouts  7.17 us (4%)
    ppermute x37, waiting for transfers between devices, hop(): return lax.ppermute(value, axis, [(i, i ^ distance) for i in range(size)])  64.3 us
    ppermute x37, starting transfers between devices, hop(): return lax.ppermute(value, axis, [(i, i ^ distance) for i in range(size)])  36.8 us
    pallas_call x4, Pallas kernels, cross_coefficients(): pl.pallas_call(cross_body, grid_spec=pltpu.PrefetchScalarGridSpec(num_sca...  31 us
    pallas_call x1, Pallas kernels, sums(): pl.pallas_call(functools.partial(sums_body, number=len(blocks), pieces=le...  20.4 us
    all_gather x1, blocking collectives, gather_device(): lax.all_gather(stat.reshape(1, *stat.shape), 'cls', axis=0, tiled=True)  9.97 us
    pallas_call x1, Pallas kernels, arrange_references(): pl.pallas_call(reference_body, grid_spec=pltpu.PrefetchScalarGridSpec(num...  7.45 us
    unnamed x57, local copies, waits for them, and re-layouts  6.24 us
    pallas_call x2, Pallas kernels, arrange_particles(): pl.pallas_call(functools.partial(particle_body, distances=distances, n_pr...  5.35 us
  transfers between devices with their start and end apart: 37, of which 17 were waited for; matrix products, arithmetic and copies ran while one was open for 0% of the time, Pallas kernels for 22%

profile of v9, /device:TPU:0, one launch (start us, length us, event | category | flops | bytes accessed | tf_op | source)
XLA Modules:
  0.0 187.7 jit_solution(5599762706636004700)
XLA Ops:
  4.0 2.7 %arrange_particles.2 = (bf16[129,16,128]{2,1,0:T(8,128)(2,1)S(1)}, bf16[129,16,128]{2,1,0:T(8,128)(2,1)S(1)}) custom-call(s32[1]{0:T(128)} %bitcast.at_ref, bf16[16,128,512]{2,1,0:T(8,128)(2,1)S(1)} %copy-done.1, s32[16,20]{1,0:T(8,128)S(1)} %pad_add_fusion.meta_ref), custom_call_target="tpu_custom_call" | custom-call | flops 134217728 | bytes 2097152 | tf_op jit(solution)/shard_map/arrange_particles/pallas_call | solution.py:279
  6.7 4.1 %collective-permute-start.3 = (bf16[129,16,128]{2,1,0:T(8,128)(2,1)S(1)}, bf16[129,16,128]{2,1,0:T(8,128)(2,1)S(1)}, u32[]{:S(2)}, u32[]{:S(2)}) collective-permute-start(bf16[129,16,128]{2,1,0:T(8,128)(2,1)S(1)} %get-tuple-element.48), channel_id=1, source_target_pairs={{0,2},{1,3},{2,0},{3,1},{4,6},{5,7},{6,4},{7,5},{8,10},{9,11},{10,... | collective-permute-start | bytes 1585160 | tf_op jit(solution)/shard_map/ppermute | solution.py:718
  10.8 2.7 %arrange_particles.3 = (bf16[129,16,128]{2,1,0:T(8,128)(2,1)S(1)}, bf16[129,16,128]{2,1,0:T(8,128)(2,1)S(1)}) custom-call(s32[1]{0:T(128)} %bitcast.at_ref, bf16[16,128,512]{2,1,0:T(8,128)(2,1)S(1)} %copy-done.1, s32[16,20]{1,0:T(8,128)S(1)} %pad_add_fusion.meta_ref), custom_call_target="tpu_custom_call" | custom-call | flops 134217728 | bytes 2097152 | tf_op jit(solution)/shard_map/arrange_particles/pallas_call | solution.py:279
  13.5 1.6 collective-permute-start
  18.1 16.1 %collective-permute-done.3.refs_0_.refs_8_.refs_16_.refs_48_ = bf16[129,16,128]{2,1,0:T(8,128)(2,1)S(1)} collective-permute-done((bf16[129,16,128]{2,1,0:T(8,128)(2,1)S(1)}, bf16[129,16,128]{2,1,0:T(8,128)(2,1)S(1)}, u32[]{:S(2)}, u32[]{:S(2)}) %collective-permute-start.3) | collective-permute-done | bytes 528416 | tf_op jit(solution)/shard_map/ppermute | solution.py:718
  34.2 3.5 %collective-permute-start.6 = (bf16[129,16,128]{2,1,0:T(8,128)(2,1)S(1)}, bf16[129,16,128]{2,1,0:T(8,128)(2,1)S(1)}, u32[]{:S(2)}, u32[]{:S(2)}) collective-permute-start(bf16[129,16,128]{2,1,0:T(8,128)(2,1)S(1)} %get-tuple-element.51), channel_id=1, source_target_pairs={{0,3},{1,2},{2,1},{3,0},{4,7},{5,6},{6,5},{7,4},{8,11},{9,10},{10,... | collective-permute-start | bytes 1585160 | tf_op jit(solution)/shard_map/ppermute | solution.py:718
  41.8 7.4 %arrange_references.1 = (bf16[128,64,128]{2,1,0:T(8,128)(2,1)}, f32[64,128]{1,0:T(8,128)}) custom-call(s32[1]{0:T(128)} %bitcast.at_ref, bf16[64,128,512]{2,1,0:T(8,128)(2,1)} %x_ref.5), custom_call_target="tpu_custom_call" | custom-call | flops 268435456 | bytes 4194304 | tf_op jit(solution)/shard_map/arrange_references/pallas_call | solution.py:320
  55.8 8.3 %collective-permute-done.4.refs_2_.refs_10_.refs_18_.refs_50_ = bf16[129,16,128]{2,1,0:T(8,128)(2,1)} collective-permute-done((bf16[129,16,128]{2,1,0:T(8,128)(2,1)S(1)}, bf16[129,16,128]{2,1,0:T(8,128)(2,1)}, u32[]{:S(2)}, u32[]{:S(2)}) %collective-permute-start.4) | collective-permute-done | bytes 528416 | tf_op jit(solution)/shard_map/ppermute | solution.py:718
  65.7 11.2 %collective-permute-done.10.refs_4_.refs_12_.refs_28_.refs_60_ = bf16[129,16,128]{2,1,0:T(8,128)(2,1)S(1)} collective-permute-done((bf16[129,16,128]{2,1,0:T(8,128)(2,1)S(1)}, bf16[129,16,128]{2,1,0:T(8,128)(2,1)S(1)}, u32[]{:S(2)}, u32[]{:S(2)}) %collective-permute-start.10) | collective-permute-done | bytes 528416 | tf_op jit(solution)/shard_map/ppermute | solution.py:718
  76.9 9.7 %collective-permute-done.19.refs_6_.refs_14_.refs_46_ = bf16[129,16,128]{2,1,0:T(8,128)(2,1)S(1)} collective-permute-done((bf16[129,16,128]{2,1,0:T(8,128)(2,1)}, bf16[129,16,128]{2,1,0:T(8,128)(2,1)S(1)}, u32[]{:S(2)}, u32[]{:S(2)}) %collective-permute-start.19) | collective-permute-done | bytes 528416 | tf_op jit(solution)/shard_map/ppermute | solution.py:718
  92.7 7.7 %cross_coefficients.5 = (f32[144,128]{1,0:T(8,128)}, f32[8,128]{1,0:T(8,128)}) custom-call(s32[1]{0:T(128)} %bitcast.2.at_ref, bf16[129,16,128]{2,1,0:T(8,128)(2,1)} %copy-done.3, bf16[129,16,128]{2,1,0:T(8,128)(2,1)} %copy-done.13, bf16[129,16,128]{2,1,0:T(8,128)(2,1)} %collective-permute-done.1.refs_2_.refs_10_.refs_42_, bf16[129,16,128]{2,1,0:T(8,128)(2,1)} %copy-done.14, ...), custom_call_target="tpu_custom_call" | custom-call | flops 541065216 | bytes 4227072 | tf_op jit(solution)/shard_map/cross_coefficients/pallas_call | solution.py:451
  101.9 7.9 %cross_coefficients.4 = (f32[144,128]{1,0:T(8,128)}, f32[8,128]{1,0:T(8,128)}) custom-call(s32[1]{0:T(128)} %bitcast.2.at_ref, bf16[129,16,128]{2,1,0:T(8,128)(2,1)} %copy-done, bf16[129,16,128]{2,1,0:T(8,128)(2,1)} %collective-permute-done.11.refs_1_.refs_9_.refs_33_, bf16[129,16,128]{2,1,0:T(8,128)(2,1)} %copy-done.5, ...), custom_call_target="tpu_custom_call" | custom-call | flops 541065216 | bytes 4227072 | tf_op jit(solution)/shard_map/cross_coefficients/pallas_call | solution.py:451
  114.4 7.7 %cross_coefficients.6 = (f32[144,128]{1,0:T(8,128)}, f32[8,128]{1,0:T(8,128)}) custom-call(s32[1]{0:T(128)} %bitcast.2.at_ref, bf16[129,16,128]{2,1,0:T(8,128)(2,1)} %copy-done.2, bf16[129,16,128]{2,1,0:T(8,128)(2,1)} %copy-done.16, bf16[129,16,128]{2,1,0:T(8,128)(2,1)} %collective-permute-done.4.refs_2_.refs_10_.refs_18_.refs_50_, ...), custom_call_target="tpu_custom_call" | custom-call | flops 541065216 | bytes 4227072 | tf_op jit(solution)/shard_map/cross_coefficients/pallas_call | solution.py:451
  122.1 2.8 %collective-permute-done.29.refs_6_.refs_14_.refs_30_.refs_62_ = bf16[129,16,128]{2,1,0:T(8,128)(2,1)} collective-permute-done((bf16[129,16,128]{2,1,0:T(8,128)(2,1)S(1)}, bf16[129,16,128]{2,1,0:T(8,128)(2,1)}, u32[]{:S(2)}, u32[]{:S(2)}) %collective-permute-start.29) | collective-permute-done | bytes 528416 | tf_op jit(solution)/shard_map/ppermute | solution.py:718
  127.9 7.7 %cross_coefficients.7 = (f32[144,128]{1,0:T(8,128)}, f32[8,128]{1,0:T(8,128)}) custom-call(s32[1]{0:T(128)} %bitcast.2.at_ref, bf16[129,16,128]{2,1,0:T(8,128)(2,1)} %copy-done.6, bf16[129,16,128]{2,1,0:T(8,128)(2,1)} %collective-permute-done.26.refs_1_.refs_9_.refs_25_.refs_57_, bf16[129,16,128]{2,1,0:T(8,128)(2,1)} %copy-done.9, ...), custom_call_target="tpu_custom_call" | custom-call | flops 541065216 | bytes 4227072 | tf_op jit(solution)/shard_map/cross_coefficients/pallas_call | solution.py:451
  135.6 3.1 %collective-permute-start.33 = (f32[144,128]{1,0:T(8,128)}, f32[144,128]{1,0:T(8,128)S(1)}, u32[]{:S(2)}, u32[]{:S(2)}) collective-permute-start(f32[144,128]{1,0:T(8,128)} %get-tuple-element.76), channel_id=1, source_target_pairs={{0,3},{1,2},{2,1},{3,0},{4,7},{5,6},{6,5},{7,4},{8,11},{9,10},{10,... | collective-permute-start | bytes 221192 | tf_op jit(solution)/shard_map/ppermute | solution.py:718
  138.8 3.3 %collective-permute-done.33.refs_3_ = f32[144,128]{1,0:T(8,128)S(1)} collective-permute-done((f32[144,128]{1,0:T(8,128)}, f32[144,128]{1,0:T(8,128)S(1)}, u32[]{:S(2)}, u32[]{:S(2)}) %collective-permute-start.33) | collective-permute-done | bytes 73760 | tf_op jit(solution)/shard_map/ppermute | solution.py:718
  142.7 2.0 %scores.1 = (f32[144,128]{1,0:T(8,128)}, f32[2,128]{1,0:T(2,128)}) custom-call(f32[144,128]{1,0:T(8,128)} %get-tuple-element.64.refs_0_, f32[144,128]{1,0:T(8,128)} %copy-done.24, f32[144,128]{1,0:T(8,128)} %copy-done.25, f32[144,128]{1,0:T(8,128)} %copy-done.26, f32[8,128]{1,0:T(8,128)} %get-tuple-element.77.refs_4_.cand_ref.refs_68_, ...), custom_call_target="tpu_custom_call" | custom-call | tf_op jit(solution)/shard_map/scores/pallas_call | solution.py:506
  144.7 10.0 %all-gather.1.stat_ref = f32[8,2,128]{2,1,0:T(2,128)} all-gather(f32[1,2,128]{2,1,0:T(2,128)} %bitcast.9), channel_id=2, replica_groups=mesh['cls'=8,'prt'=4] {'cls'}, dimensions={0}, use_global_device_ids=true | all-gather | bytes 9216 | tf_op jit(solution)/shard_map/all_gather | solution.py:799
  154.7 2.1 %mixed_weights.1 = (f32[144,128]{1,0:T(8,128)}, f32[1,16]{1,0:T(1,128)}) custom-call(s32[1]{0:T(128)} %bitcast.2.at_ref, f32[144,128]{1,0:T(8,128)} %get-tuple-element.78.score_ref, f32[8,128]{1,0:T(8,128)} %get-tuple-element.77.refs_4_.cand_ref.refs_68_, f32[8,2,128]{2,1,0:T(2,128)} %all-gather.1.stat_ref, f32[144,144]{1,0:T(8,128)} %constant.14.clone.refs_5_.table_ref), custom_call_target="tpu_custom_call" | custom-call | tf_op jit(solution)/shard_map/mixed_weights/pallas_call | solution.py:556
  156.8 3.1 %collective-permute-start.36 = (f32[144,128]{1,0:T(8,128)}, f32[144,128]{1,0:T(8,128)S(1)}, u32[]{:S(2)}, u32[]{:S(2)}) collective-permute-start(f32[144,128]{1,0:T(8,128)} %get-tuple-element.80.refs_64_), channel_id=1, source_target_pairs={{0,3},{1,2},{2,1},{3,0},{4,7},{5,6},{6,5},{7,4},{8,11},{9,10},{10,... | collective-permute-start | bytes 221192 | tf_op jit(solution)/shard_map/ppermute | solution.py:718
  161.2 2.7 %collective-permute-done.36.refs_67_ = f32[144,128]{1,0:T(8,128)S(1)} collective-permute-done((f32[144,128]{1,0:T(8,128)}, f32[144,128]{1,0:T(8,128)S(1)}, u32[]{:S(2)}, u32[]{:S(2)}) %collective-permute-start.36) | collective-permute-done | bytes 73760 | tf_op jit(solution)/shard_map/ppermute | solution.py:718
  163.9 2.5 %collective-permute-done.35.refs_66_ = f32[144,128]{1,0:T(8,128)S(1)} collective-permute-done((f32[144,128]{1,0:T(8,128)}, f32[144,128]{1,0:T(8,128)S(1)}, u32[]{:S(2)}, u32[]{:S(2)}) %collective-permute-start.35) | collective-permute-done | bytes 73760 | tf_op jit(solution)/shard_map/ppermute | solution.py:718
  167.1 20.4 %sums.1 = (f32[64,32,512]{2,1,0:T(8,128)}, f32[1,64]{1,0:T(1,128)}) custom-call(bf16[129,16,128]{2,1,0:T(8,128)(2,1)} %copy-done, bf16[129,16,128]{2,1,0:T(8,128)(2,1)} %collective-permute-done.11.refs_1_.refs_9_.refs_33_, bf16[129,16,128]{2,1,0:T(8,128)(2,1)} %copy-done.5, bf16[129,16,128]{2,1,0:T(8,128)(2,1)} %collective-permute-done.12.refs_3_.refs_11_.refs_35_, ...), custom_call_target="tpu_custom_call" | custom-call | flops 2164260864 | bytes 21102592 | tf_op jit(solution)/shard_map/sums/pallas_call | solution.py:675
  (121 shorter events, 36.2 us)
Async XLA Ops:
  6.7 27.5 %collective-permute-start.3 = (bf16[129,16,128]{2,1,0:T(8,128)(2,1)S(1)}, bf16[129,16,128]{2,1,0:T(8,128)(2,1)S(1)}, u32[]{:S(2)}, u32[]{:S(2)}) collective-permute-start(bf16[129,16,128]{2,1,0:T(8,128)(2,1)S(1)} %get-tuple-element.48), channel_id=1, source_target_pairs={{0,2},{1,3},{2,0},{3,1},{4,6},{5,7},{6,4},{7,5},{8,10},{9,11},{10,... | collective-permute-start | bytes 1585160 | tf_op jit(solution)/shard_map/ppermute | solution.py:718
  13.5 24.3 %collective-permute-start = (bf16[129,16,128]{2,1,0:T(8,128)(2,1)S(1)}, bf16[129,16,128]{2,1,0:T(8,128)(2,1)S(1)}, u32[]{:S(2)}, u32[]{:S(2)}) collective-permute-start(bf16[129,16,128]{2,1,0:T(8,128)(2,1)S(1)} %get-tuple-element.47), channel_id=1, source_target_pairs={{0,1},{1,0},{2,3},{3,2},{4,5},{5,4},{6,7},{7,6},{8,9},{9,8},{10,11... | collective-permute-start | bytes 1585160 | tf_op jit(solution)/shard_map/ppermute | solution.py:718
  15.1 25.7 %collective-permute-start.8 = (bf16[129,16,128]{2,1,0:T(8,128)(2,1)S(1)}, bf16[129,16,128]{2,1,0:T(8,128)(2,1)S(1)}, u32[]{:S(2)}, u32[]{:S(2)}) collective-permute-start(bf16[129,16,128]{2,1,0:T(8,128)(2,1)S(1)} %get-tuple-element.56.refs_0_.refs_8_.refs_32_), channel_id=1, source_target_pairs={{0,16},{4,20},{8,24},{12,28},{16,0},{20,4},{24,8},{28,12},{1,17},{... | collective-permute-start | bytes 1585160 | tf_op jit(solution)/shard_map/ppermute | solution.py:718
  16.6 24.7 %collective-permute-start.7 = (bf16[129,16,128]{2,1,0:T(8,128)(2,1)S(1)}, bf16[129,16,128]{2,1,0:T(8,128)(2,1)S(1)}, u32[]{:S(2)}, u32[]{:S(2)}) collective-permute-start(bf16[129,16,128]{2,1,0:T(8,128)(2,1)S(1)} %get-tuple-element.56.refs_0_.refs_8_.refs_32_), channel_id=1, source_target_pairs={{0,8},{4,12},{8,0},{12,4},{16,24},{20,28},{24,16},{28,20},{1,9},{5... | collective-permute-start | bytes 1585160 | tf_op jit(solution)/shard_map/ppermute | solution.py:718
  34.2 15.8 %collective-permute-start.6 = (bf16[129,16,128]{2,1,0:T(8,128)(2,1)S(1)}, bf16[129,16,128]{2,1,0:T(8,128)(2,1)S(1)}, u32[]{:S(2)}, u32[]{:S(2)}) collective-permute-start(bf16[129,16,128]{2,1,0:T(8,128)(2,1)S(1)} %get-tuple-element.51), channel_id=1, source_target_pairs={{0,3},{1,2},{2,1},{3,0},{4,7},{5,6},{6,5},{7,4},{8,11},{9,10},{10,... | collective-permute-start | bytes 1585160 | tf_op jit(solution)/shard_map/ppermute | solution.py:718
  37.8 15.0 %collective-permute-start.1 = (bf16[129,16,128]{2,1,0:T(8,128)(2,1)S(1)}, bf16[129,16,128]{2,1,0:T(8,128)(2,1)}, u32[]{:S(2)}, u32[]{:S(2)}) collective-permute-start(bf16[129,16,128]{2,1,0:T(8,128)(2,1)S(1)} %collective-permute-done.refs_0_.refs_8_.refs_40_), channel_id=1, source_target_pairs={{0,8},{4,12},{8,0},{12,4},{16,24},{20,28},{24,16},{28,20},{1,9},{5... | collective-permute-start | bytes 1585160 | tf_op jit(solution)/shard_map/ppermute | solution.py:718
  39.3 15.1 %collective-permute-start.5 = (bf16[129,16,128]{2,1,0:T(8,128)(2,1)S(1)}, bf16[129,16,128]{2,1,0:T(8,128)(2,1)}, u32[]{:S(2)}, u32[]{:S(2)}) collective-permute-start(bf16[129,16,128]{2,1,0:T(8,128)(2,1)S(1)} %collective-permute-done.3.refs_0_.refs_8_.refs_16_.refs_48_), channel_id=1, source_target_pairs={{0,16},{4,20},{8,24},{12,28},{16,0},{20,4},{24,8},{28,12},{1,17},{... | collective-permute-start | bytes 1585160 | tf_op jit(solution)/shard_map/ppermute | solution.py:718
  40.8 23.4 %collective-permute-start.4 = (bf16[129,16,128]{2,1,0:T(8,128)(2,1)S(1)}, bf16[129,16,128]{2,1,0:T(8,128)(2,1)}, u32[]{:S(2)}, u32[]{:S(2)}) collective-permute-start(bf16[129,16,128]{2,1,0:T(8,128)(2,1)S(1)} %collective-permute-done.3.refs_0_.refs_8_.refs_16_.refs_48_), channel_id=1, source_target_pairs={{0,8},{4,12},{8,0},{12,4},{16,24},{20,28},{24,16},{28,20},{1,9},{5... | collective-permute-start | bytes 1585160 | tf_op jit(solution)/shard_map/ppermute | solution.py:718
  41.3 24.3 %collective-permute-start.2 = (bf16[129,16,128]{2,1,0:T(8,128)(2,1)S(1)}, bf16[129,16,128]{2,1,0:T(8,128)(2,1)}, u32[]{:S(2)}, u32[]{:S(2)}) collective-permute-start(bf16[129,16,128]{2,1,0:T(8,128)(2,1)S(1)} %collective-permute-done.refs_0_.refs_8_.refs_40_), channel_id=1, source_target_pairs={{0,16},{4,20},{8,24},{12,28},{16,0},{20,4},{24,8},{28,12},{1,17},{... | collective-permute-start | bytes 1585160 | tf_op jit(solution)/shard_map/ppermute | solution.py:718
  50.0 26.9 %collective-permute-start.10 = (bf16[129,16,128]{2,1,0:T(8,128)(2,1)S(1)}, bf16[129,16,128]{2,1,0:T(8,128)(2,1)S(1)}, u32[]{:S(2)}, u32[]{:S(2)}) collective-permute-start(bf16[129,16,128]{2,1,0:T(8,128)(2,1)S(1)} %collective-permute-done.6.refs_0_.refs_8_.refs_24_.refs_56_), channel_id=1, source_target_pairs={{0,16},{4,20},{8,24},{12,28},{16,0},{20,4},{24,8},{28,12},{1,17},{... | collective-permute-start | bytes 1585160 | tf_op jit(solution)/shard_map/ppermute | solution.py:718
  52.8 24.1 %collective-permute-start.9 = (bf16[129,16,128]{2,1,0:T(8,128)(2,1)S(1)}, bf16[129,16,128]{2,1,0:T(8,128)(2,1)S(1)}, u32[]{:S(2)}, u32[]{:S(2)}) collective-permute-start(bf16[129,16,128]{2,1,0:T(8,128)(2,1)S(1)} %collective-permute-done.6.refs_0_.refs_8_.refs_24_.refs_56_), channel_id=1, source_target_pairs={{0,8},{4,12},{8,0},{12,4},{16,24},{20,28},{24,16},{28,20},{1,9},{5... | collective-permute-start | bytes 1585160 | tf_op jit(solution)/shard_map/ppermute | solution.py:718
  54.3 32.2 %collective-permute-start.19 = (bf16[129,16,128]{2,1,0:T(8,128)(2,1)}, bf16[129,16,128]{2,1,0:T(8,128)(2,1)S(1)}, u32[]{:S(2)}, u32[]{:S(2)}) collective-permute-start(bf16[129,16,128]{2,1,0:T(8,128)(2,1)} %collective-permute-done.1.refs_2_.refs_10_.refs_42_), channel_id=1, source_target_pairs={{0,16},{4,20},{8,24},{12,28},{16,0},{20,4},{24,8},{28,12},{1,17},{... | collective-permute-start | bytes 1585160 | tf_op jit(solution)/shard_map/ppermute | solution.py:718
  64.1 23.4 %collective-permute-start.14 = (bf16[129,16,128]{2,1,0:T(8,128)(2,1)S(1)}, bf16[129,16,128]{2,1,0:T(8,128)(2,1)}, u32[]{:S(2)}, u32[]{:S(2)}) collective-permute-start(bf16[129,16,128]{2,1,0:T(8,128)(2,1)S(1)} %collective-permute-done.8.refs_4_.refs_12_.refs_36_), channel_id=1, source_target_pairs={{0,8},{4,12},{8,0},{12,4},{16,24},{20,28},{24,16},{28,20},{1,9},{5... | collective-permute-start | bytes 1585160 | tf_op jit(solution)/shard_map/ppermute | solution.py:718
  87.6 14.3 %collective-permute-start.24 = (bf16[129,16,128]{2,1,0:T(8,128)(2,1)}, bf16[129,16,128]{2,1,0:T(8,128)(2,1)}, u32[]{:S(2)}, u32[]{:S(2)}) collective-permute-start(bf16[129,16,128]{2,1,0:T(8,128)(2,1)} %collective-permute-done.5.refs_4_.refs_12_.refs_20_.refs_52_), channel_id=1, source_target_pairs={{0,8},{4,12},{8,0},{12,4},{16,24},{20,28},{24,16},{28,20},{1,9},{5... | collective-permute-start | bytes 1585160 | tf_op jit(solution)/shard_map/ppermute | solution.py:718
  88.5 13.4 %collective-permute-start.15 = (bf16[129,16,128]{2,1,0:T(8,128)(2,1)}, bf16[129,16,128]{2,1,0:T(8,128)(2,1)}, u32[]{:S(2)}, u32[]{:S(2)}) collective-permute-start(bf16[129,16,128]{2,1,0:T(8,128)(2,1)} %collective-permute-done.14.refs_6_.refs_14_.refs_38_), channel_id=1, source_target_pairs={{0,4},{4,0},{8,12},{12,8},{16,20},{20,16},{24,28},{28,24},{1,5},{5... | collective-permute-start | bytes 1585160 | tf_op jit(solution)/shard_map/ppermute | solution.py:718
  90.0 11.9 %collective-permute-start.11 = (bf16[129,16,128]{2,1,0:T(8,128)(2,1)S(1)}, bf16[129,16,128]{2,1,0:T(8,128)(2,1)}, u32[]{:S(2)}, u32[]{:S(2)}) collective-permute-start(bf16[129,16,128]{2,1,0:T(8,128)(2,1)S(1)} %get-tuple-element.56.refs_0_.refs_8_.refs_32_), channel_id=1, source_target_pairs={{0,4},{4,0},{8,12},{12,8},{16,20},{20,16},{24,28},{28,24},{1,5},{5... | collective-permute-start | bytes 1585160 | tf_op jit(solution)/shard_map/ppermute | solution.py:718
  90.2 11.7 %collective-permute-start.12 = (bf16[129,16,128]{2,1,0:T(8,128)(2,1)S(1)}, bf16[129,16,128]{2,1,0:T(8,128)(2,1)}, u32[]{:S(2)}, u32[]{:S(2)}) collective-permute-start(bf16[129,16,128]{2,1,0:T(8,128)(2,1)S(1)} %collective-permute-done.7.refs_2_.refs_10_.refs_34_), channel_id=1, source_target_pairs={{0,4},{4,0},{8,12},{12,8},{16,20},{20,16},{24,28},{28,24},{1,5},{5... | collective-permute-start | bytes 1585160 | tf_op jit(solution)/shard_map/ppermute | solution.py:718
  101.9 10.4 %collective-permute-start.25 = (bf16[129,16,128]{2,1,0:T(8,128)(2,1)}, bf16[129,16,128]{2,1,0:T(8,128)(2,1)}, u32[]{:S(2)}, u32[]{:S(2)}) collective-permute-start(bf16[129,16,128]{2,1,0:T(8,128)(2,1)} %collective-permute-done.24.refs_6_.refs_14_.refs_22_.refs_54_), channel_id=1, source_target_pairs={{0,4},{4,0},{8,12},{12,8},{16,20},{20,16},{24,28},{28,24},{1,5},{5... | collective-permute-start | bytes 1585160 | tf_op jit(solution)/shard_map/ppermute | solution.py:718
  110.8 14.1 %collective-permute-start.29 = (bf16[129,16,128]{2,1,0:T(8,128)(2,1)S(1)}, bf16[129,16,128]{2,1,0:T(8,128)(2,1)}, u32[]{:S(2)}, u32[]{:S(2)}) collective-permute-start(bf16[129,16,128]{2,1,0:T(8,128)(2,1)S(1)} %copy-done.10), channel_id=1, source_target_pairs={{0,16},{4,20},{8,24},{12,28},{16,0},{20,4},{24,8},{28,12},{1,17},{... | collective-permute-start | bytes 1585160 | tf_op jit(solution)/shard_map/ppermute | solution.py:718
  112.3 12.7 %collective-permute-start.26 = (bf16[129,16,128]{2,1,0:T(8,128)(2,1)S(1)}, bf16[129,16,128]{2,1,0:T(8,128)(2,1)}, u32[]{:S(2)}, u32[]{:S(2)}) collective-permute-start(bf16[129,16,128]{2,1,0:T(8,128)(2,1)S(1)} %collective-permute-done.6.refs_0_.refs_8_.refs_24_.refs_56_), channel_id=1, source_target_pairs={{0,4},{4,0},{8,12},{12,8},{16,20},{20,16},{24,28},{28,24},{1,5},{5... | collective-permute-start | bytes 1585160 | tf_op jit(solution)/shard_map/ppermute | solution.py:718
  112.3 13.9 %collective-permute-start.27 = (bf16[129,16,128]{2,1,0:T(8,128)(2,1)S(1)}, bf16[129,16,128]{2,1,0:T(8,128)(2,1)S(1)}, u32[]{:S(2)}, u32[]{:S(2)}) collective-permute-start(bf16[129,16,128]{2,1,0:T(8,128)(2,1)S(1)} %copy-done.10), channel_id=1, source_target_pairs={{0,4},{4,0},{8,12},{12,8},{16,20},{20,16},{24,28},{28,24},{1,5},{5... | collective-permute-start | bytes 1585160 | tf_op jit(solution)/shard_map/ppermute | solution.py:718
  112.8 13.4 %collective-permute-start.28 = (bf16[129,16,128]{2,1,0:T(8,128)(2,1)S(1)}, bf16[129,16,128]{2,1,0:T(8,128)(2,1)}, u32[]{:S(2)}, u32[]{:S(2)}) collective-permute-start(bf16[129,16,128]{2,1,0:T(8,128)(2,1)S(1)} %copy-done.8), channel_id=1, source_target_pairs={{0,4},{4,0},{8,12},{12,8},{16,20},{20,16},{24,28},{28,24},{1,5},{5... | collective-permute-start | bytes 1585160 | tf_op jit(solution)/shard_map/ppermute | solution.py:718
  124.9 13.8 %collective-permute-start.31 = (f32[144,128]{1,0:T(8,128)S(1)}, f32[144,128]{1,0:T(8,128)S(1)}, u32[]{:S(2)}, u32[]{:S(2)}) collective-permute-start(f32[144,128]{1,0:T(8,128)S(1)} %copy-done.27), channel_id=1, source_target_pairs={{0,1},{1,0},{2,3},{3,2},{4,5},{5,4},{6,7},{7,6},{8,9},{9,8},{10,11... | collective-permute-start | bytes 221192 | tf_op jit(solution)/shard_map/ppermute | solution.py:718
  124.9 13.8 %collective-permute-start.32 = (f32[144,128]{1,0:T(8,128)}, f32[144,128]{1,0:T(8,128)S(1)}, u32[]{:S(2)}, u32[]{:S(2)}) collective-permute-start(f32[144,128]{1,0:T(8,128)} %get-tuple-element.74), channel_id=1, source_target_pairs={{0,2},{1,3},{2,0},{3,1},{4,6},{5,7},{6,4},{7,5},{8,10},{9,11},{10,... | collective-permute-start | bytes 221192 | tf_op jit(solution)/shard_map/ppermute | solution.py:718
  (41 other events, 522.3 us)

commit v10 on v9

--- a/solution.py
+++ b/solution.py
@@ -166,7 +166,7 @@
 CHUNKS = BODY + TAIL // 2
 EXTRA = TAIL // 2 + 1
 COEF = 2 * HALF * CAND_OWN
-CROSS_STEP = 6
+CROSS_STEP = 3
 SUM_STEP = 3
 
 
@@ -337,7 +337,7 @@
         ],
         compiler_params=pltpu.CompilerParams(vmem_limit_bytes=60 << 20),
         cost_estimate=pl.CostEstimate(
-            flops=groups * span * width * 2 * CHUNKS,
+            flops=groups * span * width * 64 * CHUNKS,
             bytes_accessed=groups * span * width * 4,
             transcendentals=0,
         ),
@@ -478,7 +478,7 @@
         ],
         compiler_params=pltpu.CompilerParams(vmem_limit_bytes=60 << 20),
         cost_estimate=pl.CostEstimate(
-            flops=4 * size * groups, bytes_accessed=2 * size, transcendentals=0
+            flops=128 * size * groups, bytes_accessed=2 * size, transcendentals=0
         ),
         name="cross_coefficients",
     )(cls, *blocks, *blocks, arranged, arranged, norms)
@@ -788,8 +788,7 @@
     for d in range(n_prt):
         waits = [known[n_prt - 1][2]] if d == 1 else []
         first = [known[e][j] for e in range(1, n_prt) for j in (2, n_cls // 2)]
-        each = first if d < 2 else coefs[:1]
-        blocks.append(paired(known[d], each, coefs[-1:] if d > 1 else []))
+        blocks.append(paired(known[d], first if d < 2 else [], []))
         ready = after(arranged, *waits) if waits else arranged
         coef, cand = cross_coefficients(blocks[d], ready, norms, cls)
         coefs.append(coef)

time: 188 us -> 193 us (1.027)
  waiting for transfers between devices: 64.3 us -> 71.4 us
  Pallas kernels: 68.4 us -> 73 us
  starting transfers between devices: 36.8 us -> 32.3 us
    ppermute x37, waiting for transfers between devices: 64.3 us -> 71.4 us  [hop(): return lax.ppermute(value, axis, [(i, i ^ distance) for i in range(size)])]
    pallas_call x4, Pallas kernels: 31 us -> 35.7 us  [cross_coefficients(): pl.pallas_call(cross_body, grid_spec=pltpu.PrefetchScalarGridSpec(num_sca...]
    ppermute x37, starting transfers between devices: 36.8 us -> 32.3 us  [hop(): return lax.ppermute(value, axis, [(i, i ^ distance) for i in range(size)])]
    unnamed x57 -> x43, local copies, waits for them, and re-layouts: 6.24 us -> 4.94 us
  transfers between devices with their start and end apart: 37 -> 37, of which waited for: 17 -> 11; matrix products, arithmetic and copies ran while one was open for 0% -> 0% of each run, Pallas kernels for 22% -> 24%
where the time goes in v10:
time: 193 us; the launch traced here: 192 us
  Pallas kernels  73 us (38%)
  waiting for transfers between devices  71.4 us (37%)
  starting transfers between devices  32.3 us (17%)
  blocking collectives  8.82 us (5%)
  local copies, waits for them, and re-layouts  5.87 us (3%)
    ppermute x37, waiting for transfers between devices, hop(): return lax.ppermute(value, axis, [(i, i ^ distance) for i in range(size)])  71.4 us
    pallas_call x4, Pallas kernels, cross_coefficients(): pl.pallas_call(cross_body, grid_spec=pltpu.PrefetchScalarGridSpec(num_sca...  35.7 us
    ppermute x37, starting transfers between devices, hop(): return lax.ppermute(value, axis, [(i, i ^ distance) for i in range(size)])  32.3 us
    pallas_call x1, Pallas kernels, sums(): pl.pallas_call(functools.partial(sums_body, number=len(blocks), pieces=le...  20.4 us
    all_gather x1, blocking collectives, gather_device(): lax.all_gather(stat.reshape(1, *stat.shape), 'cls', axis=0, tiled=True)  8.82 us
    pallas_call x1, Pallas kernels, arrange_references(): pl.pallas_call(reference_body, grid_spec=pltpu.PrefetchScalarGridSpec(num...  7.45 us
    pallas_call x2, Pallas kernels, arrange_particles(): pl.pallas_call(functools.partial(particle_body, distances=distances, n_pr...  5.34 us
    unnamed x43, local copies, waits for them, and re-layouts  4.94 us
  transfers between devices with their start and end apart: 37, of which 11 were waited for; matrix products, arithmetic and copies ran while one was open for 0% of the time, Pallas kernels for 24%

profile of v10, /device:TPU:0, one launch (start us, length us, event | category | flops | bytes accessed | tf_op | source)
XLA Modules:
  0.0 192.4 jit_solution(5589980542997476866)
XLA Ops:
  4.0 2.7 %arrange_particles.2 = (bf16[129,16,128]{2,1,0:T(8,128)(2,1)S(1)}, bf16[129,16,128]{2,1,0:T(8,128)(2,1)S(1)}) custom-call(s32[1]{0:T(128)} %bitcast.at_ref, bf16[16,128,512]{2,1,0:T(8,128)(2,1)S(1)} %copy-done, s32[16,20]{1,0:T(8,128)S(1)} %pad_add_fusion.meta_ref), custom_call_target="tpu_custom_call" | custom-call | flops 134217728 | bytes 2097152 | tf_op jit(solution)/shard_map/arrange_particles/pallas_call | solution.py:279
  6.7 3.0 %collective-permute-start.8 = (bf16[129,16,128]{2,1,0:T(8,128)(2,1)S(1)}, bf16[129,16,128]{2,1,0:T(8,128)(2,1)S(1)}, u32[]{:S(2)}, u32[]{:S(2)}) collective-permute-start(bf16[129,16,128]{2,1,0:T(8,128)(2,1)S(1)} %get-tuple-element.48.refs_0_.refs_8_.refs_32_), channel_id=1, source_target_pairs={{0,16},{4,20},{8,24},{12,28},{16,0},{20,4},{24,8},{28,12},{1,17},{... | collective-permute-start | bytes 1585160 | tf_op jit(solution)/shard_map/ppermute | solution.py:718
  11.2 2.6 %collective-permute-start.3 = (bf16[129,16,128]{2,1,0:T(8,128)(2,1)S(1)}, bf16[129,16,128]{2,1,0:T(8,128)(2,1)S(1)}, u32[]{:S(2)}, u32[]{:S(2)}) collective-permute-start(bf16[129,16,128]{2,1,0:T(8,128)(2,1)S(1)} %get-tuple-element.40), channel_id=1, source_target_pairs={{0,2},{1,3},{2,0},{3,1},{4,6},{5,7},{6,4},{7,5},{8,10},{9,11},{10,... | collective-permute-start | bytes 1585160 | tf_op jit(solution)/shard_map/ppermute | solution.py:718
  13.8 2.7 %arrange_particles.3 = (bf16[129,16,128]{2,1,0:T(8,128)(2,1)S(1)}, bf16[129,16,128]{2,1,0:T(8,128)(2,1)S(1)}) custom-call(s32[1]{0:T(128)} %bitcast.at_ref, bf16[16,128,512]{2,1,0:T(8,128)(2,1)S(1)} %copy-done, s32[16,20]{1,0:T(8,128)S(1)} %pad_add_fusion.meta_ref), custom_call_target="tpu_custom_call" | custom-call | flops 134217728 | bytes 2097152 | tf_op jit(solution)/shard_map/arrange_particles/pallas_call | solution.py:279
  18.1 18.6 %collective-permute-done.3.refs_0_.refs_8_.refs_16_.refs_48_ = bf16[129,16,128]{2,1,0:T(8,128)(2,1)S(1)} collective-permute-done((bf16[129,16,128]{2,1,0:T(8,128)(2,1)S(1)}, bf16[129,16,128]{2,1,0:T(8,128)(2,1)S(1)}, u32[]{:S(2)}, u32[]{:S(2)}) %collective-permute-start.3) | collective-permute-done | bytes 528416 | tf_op jit(solution)/shard_map/ppermute | solution.py:718
  37.7 3.5 %collective-permute-start.6 = (bf16[129,16,128]{2,1,0:T(8,128)(2,1)S(1)}, bf16[129,16,128]{2,1,0:T(8,128)(2,1)}, u32[]{:S(2)}, u32[]{:S(2)}) collective-permute-start(bf16[129,16,128]{2,1,0:T(8,128)(2,1)S(1)} %get-tuple-element.43), channel_id=1, source_target_pairs={{0,3},{1,2},{2,1},{3,0},{4,7},{5,6},{6,5},{7,4},{8,11},{9,10},{10,... | collective-permute-start | bytes 1585160 | tf_op jit(solution)/shard_map/ppermute | solution.py:718
  42.8 7.4 %arrange_references.1 = (bf16[128,64,128]{2,1,0:T(8,128)(2,1)}, f32[64,128]{1,0:T(8,128)}) custom-call(s32[1]{0:T(128)} %bitcast.at_ref, bf16[64,128,512]{2,1,0:T(8,128)(2,1)} %x_ref.5), custom_call_target="tpu_custom_call" | custom-call | flops 8589934592 | bytes 4194304 | tf_op jit(solution)/shard_map/arrange_references/pallas_call | solution.py:320
  57.2 5.7 %collective-permute-done.2.refs_4_.refs_12_.refs_44_ = bf16[129,16,128]{2,1,0:T(8,128)(2,1)} collective-permute-done((bf16[129,16,128]{2,1,0:T(8,128)(2,1)S(1)}, bf16[129,16,128]{2,1,0:T(8,128)(2,1)}, u32[]{:S(2)}, u32[]{:S(2)}) %collective-permute-start.2) | collective-permute-done | bytes 528416 | tf_op jit(solution)/shard_map/ppermute | solution.py:718
  63.5 3.2 %collective-permute-done.1.refs_2_.refs_10_.refs_42_ = bf16[129,16,128]{2,1,0:T(8,128)(2,1)} collective-permute-done((bf16[129,16,128]{2,1,0:T(8,128)(2,1)S(1)}, bf16[129,16,128]{2,1,0:T(8,128)(2,1)}, u32[]{:S(2)}, u32[]{:S(2)}) %collective-permute-start.1) | collective-permute-done | bytes 528416 | tf_op jit(solution)/shard_map/ppermute | solution.py:718
  66.7 11.3 %collective-permute-done.24.refs_6_.refs_14_.refs_22_.refs_54_ = bf16[129,16,128]{2,1,0:T(8,128)(2,1)} collective-permute-done((bf16[129,16,128]{2,1,0:T(8,128)(2,1)}, bf16[129,16,128]{2,1,0:T(8,128)(2,1)}, u32[]{:S(2)}, u32[]{:S(2)}) %collective-permute-start.24) | collective-permute-done | bytes 528416 | tf_op jit(solution)/shard_map/ppermute | solution.py:718
  78.5 10.7 %collective-permute-done.9.refs_2_.refs_10_.refs_26_.refs_58_ = bf16[129,16,128]{2,1,0:T(8,128)(2,1)S(1)} collective-permute-done((bf16[129,16,128]{2,1,0:T(8,128)(2,1)}, bf16[129,16,128]{2,1,0:T(8,128)(2,1)S(1)}, u32[]{:S(2)}, u32[]{:S(2)}) %collective-permute-start.9) | collective-permute-done | bytes 528416 | tf_op jit(solution)/shard_map/ppermute | solution.py:718
  89.2 9.7 %collective-permute-done.14.refs_6_.refs_14_.refs_38_ = bf16[129,16,128]{2,1,0:T(8,128)(2,1)} collective-permute-done((bf16[129,16,128]{2,1,0:T(8,128)(2,1)S(1)}, bf16[129,16,128]{2,1,0:T(8,128)(2,1)}, u32[]{:S(2)}, u32[]{:S(2)}) %collective-permute-start.14) | collective-permute-done | bytes 528416 | tf_op jit(solution)/shard_map/ppermute | solution.py:718
  100.3 8.9 %cross_coefficients.6 = (f32[144,128]{1,0:T(8,128)}, f32[8,128]{1,0:T(8,128)}) custom-call(s32[1]{0:T(128)} %bitcast.2.at_ref, bf16[129,16,128]{2,1,0:T(8,128)(2,1)} %copy-done.4, bf16[129,16,128]{2,1,0:T(8,128)(2,1)} %copy-done.6, bf16[129,16,128]{2,1,0:T(8,128)(2,1)} %collective-permute-done.4.refs_2_.refs_10_.refs_18_.refs_50_, ...), custom_call_target="tpu_custom_call" | custom-call | flops 17314086912 | bytes 4227072 | tf_op jit(solution)/shard_map/cross_coefficients/pallas_call | solution.py:451
  110.3 3.7 %collective-permute-done.29.refs_6_.refs_14_.refs_30_.refs_62_ = bf16[129,16,128]{2,1,0:T(8,128)(2,1)} collective-permute-done((bf16[129,16,128]{2,1,0:T(8,128)(2,1)S(1)}, bf16[129,16,128]{2,1,0:T(8,128)(2,1)}, u32[]{:S(2)}, u32[]{:S(2)}) %collective-permute-start.29) | collective-permute-done | bytes 528416 | tf_op jit(solution)/shard_map/ppermute | solution.py:718
  114.0 8.9 %cross_coefficients.5 = (f32[144,128]{1,0:T(8,128)}, f32[8,128]{1,0:T(8,128)}) custom-call(s32[1]{0:T(128)} %bitcast.2.at_ref, bf16[129,16,128]{2,1,0:T(8,128)(2,1)} %copy-done.5, bf16[129,16,128]{2,1,0:T(8,128)(2,1)} %copy-done.8, bf16[129,16,128]{2,1,0:T(8,128)(2,1)} %collective-permute-done.1.refs_2_.refs_10_.refs_42_, ...), custom_call_target="tpu_custom_call" | custom-call | flops 17314086912 | bytes 4227072 | tf_op jit(solution)/shard_map/cross_coefficients/pallas_call | solution.py:451
  124.9 8.9 %cross_coefficients.7 = (f32[144,128]{1,0:T(8,128)}, f32[8,128]{1,0:T(8,128)}) custom-call(s32[1]{0:T(128)} %bitcast.2.at_ref, bf16[129,16,128]{2,1,0:T(8,128)(2,1)} %collective-permute-done.6.refs_0_.refs_8_.refs_24_.refs_56_, bf16[129,16,128]{2,1,0:T(8,128)(2,1)} %copy-done.9, bf16[129,16,128]{2,1,0:T(8,128)(2,1)} %copy-done.7, ...), custom_call_target="tpu_custom_call" | custom-call | flops 17314086912 | bytes 4227072 | tf_op jit(solution)/shard_map/cross_coefficients/pallas_call | solution.py:451
  133.8 3.4 %collective-permute-start.31 = (f32[144,128]{1,0:T(8,128)S(1)}, f32[144,128]{1,0:T(8,128)S(1)}, u32[]{:S(2)}, u32[]{:S(2)}) collective-permute-start(f32[144,128]{1,0:T(8,128)S(1)} %copy-done.20), channel_id=1, source_target_pairs={{0,1},{1,0},{2,3},{3,2},{4,5},{5,4},{6,7},{7,6},{8,9},{9,8},{10,11... | collective-permute-start | bytes 221192 | tf_op jit(solution)/shard_map/ppermute | solution.py:718
  138.9 8.9 %cross_coefficients.4 = (f32[144,128]{1,0:T(8,128)}, f32[8,128]{1,0:T(8,128)}) custom-call(s32[1]{0:T(128)} %bitcast.2.at_ref, bf16[129,16,128]{2,1,0:T(8,128)(2,1)} %copy-done.1, bf16[129,16,128]{2,1,0:T(8,128)(2,1)} %copy-done.11, bf16[129,16,128]{2,1,0:T(8,128)(2,1)} %copy-done.3, bf16[129,16,128]{2,1,0:T(8,128)(2,1)} %collective-permute-done.12.refs_3_.refs_11_.refs_35_, ...), custom_call_target="tpu_custom_call" | custom-call | flops 17314086912 | bytes 4227072 | tf_op jit(solution)/shard_map/cross_coefficients/pallas_call | solution.py:451
  150.5 8.8 %all-gather.1.stat_ref = f32[8,2,128]{2,1,0:T(2,128)} all-gather(f32[1,2,128]{2,1,0:T(2,128)} %bitcast.9), channel_id=2, replica_groups=mesh['cls'=8,'prt'=4] {'cls'}, dimensions={0}, use_global_device_ids=true | all-gather | bytes 9216 | tf_op jit(solution)/shard_map/all_gather | solution.py:798
  159.3 2.1 %mixed_weights.1 = (f32[144,128]{1,0:T(8,128)}, f32[1,16]{1,0:T(1,128)}) custom-call(s32[1]{0:T(128)} %bitcast.2.at_ref, f32[144,128]{1,0:T(8,128)} %get-tuple-element.62.score_ref, f32[8,128]{1,0:T(8,128)} %get-tuple-element.61.refs_4_.cand_ref.refs_68_, f32[8,2,128]{2,1,0:T(2,128)} %all-gather.1.stat_ref, f32[144,144]{1,0:T(8,128)} %constant.14.clone.refs_5_.table_ref), custom_call_target="tpu_custom_call" | custom-call | tf_op jit(solution)/shard_map/mixed_weights/pallas_call | solution.py:556
  161.4 3.1 %collective-permute-start.36 = (f32[144,128]{1,0:T(8,128)}, f32[144,128]{1,0:T(8,128)S(1)}, u32[]{:S(2)}, u32[]{:S(2)}) collective-permute-start(f32[144,128]{1,0:T(8,128)} %get-tuple-element.64.refs_64_), channel_id=1, source_target_pairs={{0,3},{1,2},{2,1},{3,0},{4,7},{5,6},{6,5},{7,4},{8,11},{9,10},{10,... | collective-permute-start | bytes 221192 | tf_op jit(solution)/shard_map/ppermute | solution.py:718
  165.8 2.8 %collective-permute-done.36.refs_67_ = f32[144,128]{1,0:T(8,128)S(1)} collective-permute-done((f32[144,128]{1,0:T(8,128)}, f32[144,128]{1,0:T(8,128)S(1)}, u32[]{:S(2)}, u32[]{:S(2)}) %collective-permute-start.36) | collective-permute-done | bytes 73760 | tf_op jit(solution)/shard_map/ppermute | solution.py:718
  168.6 2.7 %collective-permute-done.35.refs_66_ = f32[144,128]{1,0:T(8,128)S(1)} collective-permute-done((f32[144,128]{1,0:T(8,128)}, f32[144,128]{1,0:T(8,128)S(1)}, u32[]{:S(2)}, u32[]{:S(2)}) %collective-permute-start.35) | collective-permute-done | bytes 73760 | tf_op jit(solution)/shard_map/ppermute | solution.py:718
  172.0 20.4 %sums.1 = (f32[64,32,512]{2,1,0:T(8,128)}, f32[1,64]{1,0:T(1,128)}) custom-call(bf16[129,16,128]{2,1,0:T(8,128)(2,1)} %copy-done.1, bf16[129,16,128]{2,1,0:T(8,128)(2,1)} %copy-done.11, bf16[129,16,128]{2,1,0:T(8,128)(2,1)} %copy-done.3, bf16[129,16,128]{2,1,0:T(8,128)(2,1)} %collective-permute-done.12.refs_3_.refs_11_.refs_35_, ...), custom_call_target="tpu_custom_call" | custom-call | flops 2164260864 | bytes 21102592 | tf_op jit(solution)/shard_map/sums/pallas_call | solution.py:675
  (107 shorter events, 27.6 us)
Async XLA Ops:
  6.7 30.6 %collective-permute-start.8 = (bf16[129,16,128]{2,1,0:T(8,128)(2,1)S(1)}, bf16[129,16,128]{2,1,0:T(8,128)(2,1)S(1)}, u32[]{:S(2)}, u32[]{:S(2)}) collective-permute-start(bf16[129,16,128]{2,1,0:T(8,128)(2,1)S(1)} %get-tuple-element.48.refs_0_.refs_8_.refs_32_), channel_id=1, source_target_pairs={{0,16},{4,20},{8,24},{12,28},{16,0},{20,4},{24,8},{28,12},{1,17},{... | collective-permute-start | bytes 1585160 | tf_op jit(solution)/shard_map/ppermute | solution.py:718
  9.7 28.0 %collective-permute-start.7 = (bf16[129,16,128]{2,1,0:T(8,128)(2,1)S(1)}, bf16[129,16,128]{2,1,0:T(8,128)(2,1)S(1)}, u32[]{:S(2)}, u32[]{:S(2)}) collective-permute-start(bf16[129,16,128]{2,1,0:T(8,128)(2,1)S(1)} %get-tuple-element.48.refs_0_.refs_8_.refs_32_), channel_id=1, source_target_pairs={{0,8},{4,12},{8,0},{12,4},{16,24},{20,28},{24,16},{28,20},{1,9},{5... | collective-permute-start | bytes 1585160 | tf_op jit(solution)/shard_map/ppermute | solution.py:718
  11.2 25.5 %collective-permute-start.3 = (bf16[129,16,128]{2,1,0:T(8,128)(2,1)S(1)}, bf16[129,16,128]{2,1,0:T(8,128)(2,1)S(1)}, u32[]{:S(2)}, u32[]{:S(2)}) collective-permute-start(bf16[129,16,128]{2,1,0:T(8,128)(2,1)S(1)} %get-tuple-element.40), channel_id=1, source_target_pairs={{0,2},{1,3},{2,0},{3,1},{4,6},{5,7},{6,4},{7,5},{8,10},{9,11},{10,... | collective-permute-start | bytes 1585160 | tf_op jit(solution)/shard_map/ppermute | solution.py:718
  16.5 24.8 %collective-permute-start = (bf16[129,16,128]{2,1,0:T(8,128)(2,1)S(1)}, bf16[129,16,128]{2,1,0:T(8,128)(2,1)S(1)}, u32[]{:S(2)}, u32[]{:S(2)}) collective-permute-start(bf16[129,16,128]{2,1,0:T(8,128)(2,1)S(1)} %get-tuple-element.39), channel_id=1, source_target_pairs={{0,1},{1,0},{2,3},{3,2},{4,5},{5,4},{6,7},{7,6},{8,9},{9,8},{10,11... | collective-permute-start | bytes 1585160 | tf_op jit(solution)/shard_map/ppermute | solution.py:718
  36.7 18.4 %collective-permute-start.21 = (bf16[129,16,128]{2,1,0:T(8,128)(2,1)S(1)}, bf16[129,16,128]{2,1,0:T(8,128)(2,1)S(1)}, u32[]{:S(2)}, u32[]{:S(2)}) collective-permute-start(bf16[129,16,128]{2,1,0:T(8,128)(2,1)S(1)} %collective-permute-done.3.refs_0_.refs_8_.refs_16_.refs_48_), channel_id=1, source_target_pairs={{0,4},{4,0},{8,12},{12,8},{16,20},{20,16},{24,28},{28,24},{1,5},{5... | collective-permute-start | bytes 1585160 | tf_op jit(solution)/shard_map/ppermute | solution.py:718
  36.7 14.9 %collective-permute-start.5 = (bf16[129,16,128]{2,1,0:T(8,128)(2,1)S(1)}, bf16[129,16,128]{2,1,0:T(8,128)(2,1)}, u32[]{:S(2)}, u32[]{:S(2)}) collective-permute-start(bf16[129,16,128]{2,1,0:T(8,128)(2,1)S(1)} %collective-permute-done.3.refs_0_.refs_8_.refs_16_.refs_48_), channel_id=1, source_target_pairs={{0,16},{4,20},{8,24},{12,28},{16,0},{20,4},{24,8},{28,12},{1,17},{... | collective-permute-start | bytes 1585160 | tf_op jit(solution)/shard_map/ppermute | solution.py:718
  37.2 19.4 %collective-permute-start.4 = (bf16[129,16,128]{2,1,0:T(8,128)(2,1)S(1)}, bf16[129,16,128]{2,1,0:T(8,128)(2,1)}, u32[]{:S(2)}, u32[]{:S(2)}) collective-permute-start(bf16[129,16,128]{2,1,0:T(8,128)(2,1)S(1)} %collective-permute-done.3.refs_0_.refs_8_.refs_16_.refs_48_), channel_id=1, source_target_pairs={{0,8},{4,12},{8,0},{12,4},{16,24},{20,28},{24,16},{28,20},{1,9},{5... | collective-permute-start | bytes 1585160 | tf_op jit(solution)/shard_map/ppermute | solution.py:718
  37.7 15.9 %collective-permute-start.6 = (bf16[129,16,128]{2,1,0:T(8,128)(2,1)S(1)}, bf16[129,16,128]{2,1,0:T(8,128)(2,1)}, u32[]{:S(2)}, u32[]{:S(2)}) collective-permute-start(bf16[129,16,128]{2,1,0:T(8,128)(2,1)S(1)} %get-tuple-element.43), channel_id=1, source_target_pairs={{0,3},{1,2},{2,1},{3,0},{4,7},{5,6},{6,5},{7,4},{8,11},{9,10},{10,... | collective-permute-start | bytes 1585160 | tf_op jit(solution)/shard_map/ppermute | solution.py:718
  41.3 21.7 %collective-permute-start.2 = (bf16[129,16,128]{2,1,0:T(8,128)(2,1)S(1)}, bf16[129,16,128]{2,1,0:T(8,128)(2,1)}, u32[]{:S(2)}, u32[]{:S(2)}) collective-permute-start(bf16[129,16,128]{2,1,0:T(8,128)(2,1)S(1)} %collective-permute-done.refs_0_.refs_8_.refs_40_), channel_id=1, source_target_pairs={{0,16},{4,20},{8,24},{12,28},{16,0},{20,4},{24,8},{28,12},{1,17},{... | collective-permute-start | bytes 1585160 | tf_op jit(solution)/shard_map/ppermute | solution.py:718
  51.6 15.1 %collective-permute-start.1 = (bf16[129,16,128]{2,1,0:T(8,128)(2,1)S(1)}, bf16[129,16,128]{2,1,0:T(8,128)(2,1)}, u32[]{:S(2)}, u32[]{:S(2)}) collective-permute-start(bf16[129,16,128]{2,1,0:T(8,128)(2,1)S(1)} %collective-permute-done.refs_0_.refs_8_.refs_40_), channel_id=1, source_target_pairs={{0,8},{4,12},{8,0},{12,4},{16,24},{20,28},{24,16},{28,20},{1,9},{5... | collective-permute-start | bytes 1585160 | tf_op jit(solution)/shard_map/ppermute | solution.py:718
  53.6 24.4 %collective-permute-start.24 = (bf16[129,16,128]{2,1,0:T(8,128)(2,1)}, bf16[129,16,128]{2,1,0:T(8,128)(2,1)}, u32[]{:S(2)}, u32[]{:S(2)}) collective-permute-start(bf16[129,16,128]{2,1,0:T(8,128)(2,1)} %collective-permute-done.5.refs_4_.refs_12_.refs_20_.refs_52_), channel_id=1, source_target_pairs={{0,8},{4,12},{8,0},{12,4},{16,24},{20,28},{24,16},{28,20},{1,9},{5... | collective-permute-start | bytes 1585160 | tf_op jit(solution)/shard_map/ppermute | solution.py:718
  55.2 22.9 %collective-permute-start.10 = (bf16[129,16,128]{2,1,0:T(8,128)(2,1)}, bf16[129,16,128]{2,1,0:T(8,128)(2,1)}, u32[]{:S(2)}, u32[]{:S(2)}) collective-permute-start(bf16[129,16,128]{2,1,0:T(8,128)(2,1)} %collective-permute-done.6.refs_0_.refs_8_.refs_24_.refs_56_), channel_id=1, source_target_pairs={{0,16},{4,20},{8,24},{12,28},{16,0},{20,4},{24,8},{28,12},{1,17},{... | collective-permute-start | bytes 1585160 | tf_op jit(solution)/shard_map/ppermute | solution.py:718
  56.7 32.6 %collective-permute-start.9 = (bf16[129,16,128]{2,1,0:T(8,128)(2,1)}, bf16[129,16,128]{2,1,0:T(8,128)(2,1)S(1)}, u32[]{:S(2)}, u32[]{:S(2)}) collective-permute-start(bf16[129,16,128]{2,1,0:T(8,128)(2,1)} %collective-permute-done.6.refs_0_.refs_8_.refs_24_.refs_56_), channel_id=1, source_target_pairs={{0,8},{4,12},{8,0},{12,4},{16,24},{20,28},{24,16},{28,20},{1,9},{5... | collective-permute-start | bytes 1585160 | tf_op jit(solution)/shard_map/ppermute | solution.py:718
  63.0 36.0 %collective-permute-start.14 = (bf16[129,16,128]{2,1,0:T(8,128)(2,1)S(1)}, bf16[129,16,128]{2,1,0:T(8,128)(2,1)}, u32[]{:S(2)}, u32[]{:S(2)}) collective-permute-start(bf16[129,16,128]{2,1,0:T(8,128)(2,1)S(1)} %collective-permute-done.8.refs_4_.refs_12_.refs_36_), channel_id=1, source_target_pairs={{0,8},{4,12},{8,0},{12,4},{16,24},{20,28},{24,16},{28,20},{1,9},{5... | collective-permute-start | bytes 1585160 | tf_op jit(solution)/shard_map/ppermute | solution.py:718
  66.7 32.3 %collective-permute-start.23 = (bf16[129,16,128]{2,1,0:T(8,128)(2,1)}, bf16[129,16,128]{2,1,0:T(8,128)(2,1)}, u32[]{:S(2)}, u32[]{:S(2)}) collective-permute-start(bf16[129,16,128]{2,1,0:T(8,128)(2,1)} %collective-permute-done.5.refs_4_.refs_12_.refs_20_.refs_52_), channel_id=1, source_target_pairs={{0,4},{4,0},{8,12},{12,8},{16,20},{20,16},{24,28},{28,24},{1,5},{5... | collective-permute-start | bytes 1585160 | tf_op jit(solution)/shard_map/ppermute | solution.py:718
  78.0 21.5 %collective-permute-start.22 = (bf16[129,16,128]{2,1,0:T(8,128)(2,1)}, bf16[129,16,128]{2,1,0:T(8,128)(2,1)}, u32[]{:S(2)}, u32[]{:S(2)}) collective-permute-start(bf16[129,16,128]{2,1,0:T(8,128)(2,1)} %collective-permute-done.4.refs_2_.refs_10_.refs_18_.refs_50_), channel_id=1, source_target_pairs={{0,4},{4,0},{8,12},{12,8},{16,20},{20,16},{24,28},{28,24},{1,5},{5... | collective-permute-start | bytes 1585160 | tf_op jit(solution)/shard_map/ppermute | solution.py:718
  78.0 21.5 %collective-permute-start.19 = (bf16[129,16,128]{2,1,0:T(8,128)(2,1)}, bf16[129,16,128]{2,1,0:T(8,128)(2,1)}, u32[]{:S(2)}, u32[]{:S(2)}) collective-permute-start(bf16[129,16,128]{2,1,0:T(8,128)(2,1)} %collective-permute-done.1.refs_2_.refs_10_.refs_42_), channel_id=1, source_target_pairs={{0,16},{4,20},{8,24},{12,28},{16,0},{20,4},{24,8},{28,12},{1,17},{... | collective-permute-start | bytes 1585160 | tf_op jit(solution)/shard_map/ppermute | solution.py:718
  99.6 14.5 %collective-permute-start.29 = (bf16[129,16,128]{2,1,0:T(8,128)(2,1)S(1)}, bf16[129,16,128]{2,1,0:T(8,128)(2,1)}, u32[]{:S(2)}, u32[]{:S(2)}) collective-permute-start(bf16[129,16,128]{2,1,0:T(8,128)(2,1)S(1)} %collective-permute-done.9.refs_2_.refs_10_.refs_26_.refs_58_), channel_id=1, source_target_pairs={{0,16},{4,20},{8,24},{12,28},{16,0},{20,4},{24,8},{28,12},{1,17},{... | collective-permute-start | bytes 1585160 | tf_op jit(solution)/shard_map/ppermute | solution.py:718
  109.6 24.2 %collective-permute-start.15 = (bf16[129,16,128]{2,1,0:T(8,128)(2,1)}, bf16[129,16,128]{2,1,0:T(8,128)(2,1)S(1)}, u32[]{:S(2)}, u32[]{:S(2)}) collective-permute-start(bf16[129,16,128]{2,1,0:T(8,128)(2,1)} %collective-permute-done.14.refs_6_.refs_14_.refs_38_), channel_id=1, source_target_pairs={{0,4},{4,0},{8,12},{12,8},{16,20},{20,16},{24,28},{28,24},{1,5},{5... | collective-permute-start | bytes 1585160 | tf_op jit(solution)/shard_map/ppermute | solution.py:718
  123.0 14.2 %collective-permute-start.11 = (bf16[129,16,128]{2,1,0:T(8,128)(2,1)S(1)}, bf16[129,16,128]{2,1,0:T(8,128)(2,1)S(1)}, u32[]{:S(2)}, u32[]{:S(2)}) collective-permute-start(bf16[129,16,128]{2,1,0:T(8,128)(2,1)S(1)} %get-tuple-element.48.refs_0_.refs_8_.refs_32_), channel_id=1, source_target_pairs={{0,4},{4,0},{8,12},{12,8},{16,20},{20,16},{24,28},{28,24},{1,5},{5... | collective-permute-start | bytes 1585160 | tf_op jit(solution)/shard_map/ppermute | solution.py:718
  123.6 14.0 %collective-permute-start.12 = (bf16[129,16,128]{2,1,0:T(8,128)(2,1)S(1)}, bf16[129,16,128]{2,1,0:T(8,128)(2,1)}, u32[]{:S(2)}, u32[]{:S(2)}) collective-permute-start(bf16[129,16,128]{2,1,0:T(8,128)(2,1)S(1)} %collective-permute-done.7.refs_2_.refs_10_.refs_34_), channel_id=1, source_target_pairs={{0,4},{4,0},{8,12},{12,8},{16,20},{20,16},{24,28},{28,24},{1,5},{5... | collective-permute-start | bytes 1585160 | tf_op jit(solution)/shard_map/ppermute | solution.py:718
  123.7 13.9 %collective-permute-start.13 = (bf16[129,16,128]{2,1,0:T(8,128)(2,1)S(1)}, bf16[129,16,128]{2,1,0:T(8,128)(2,1)S(1)}, u32[]{:S(2)}, u32[]{:S(2)}) collective-permute-start(bf16[129,16,128]{2,1,0:T(8,128)(2,1)S(1)} %collective-permute-done.8.refs_4_.refs_12_.refs_36_), channel_id=1, source_target_pairs={{0,4},{4,0},{8,12},{12,8},{16,20},{20,16},{24,28},{28,24},{1,5},{5... | collective-permute-start | bytes 1585160 | tf_op jit(solution)/shard_map/ppermute | solution.py:718
  124.1 23.7 %collective-permute-start.32 = (f32[144,128]{1,0:T(8,128)S(1)}, f32[144,128]{1,0:T(8,128)S(1)}, u32[]{:S(2)}, u32[]{:S(2)}) collective-permute-start(f32[144,128]{1,0:T(8,128)S(1)} %copy-done.19), channel_id=1, source_target_pairs={{0,2},{1,3},{2,0},{3,1},{4,6},{5,7},{6,4},{7,5},{8,10},{9,11},{10,... | collective-permute-start | bytes 221192 | tf_op jit(solution)/shard_map/ppermute | solution.py:718
  133.8 14.0 %collective-permute-start.31 = (f32[144,128]{1,0:T(8,128)S(1)}, f32[144,128]{1,0:T(8,128)S(1)}, u32[]{:S(2)}, u32[]{:S(2)}) collective-permute-start(f32[144,128]{1,0:T(8,128)S(1)} %copy-done.20), channel_id=1, source_target_pairs={{0,1},{1,0},{2,3},{3,2},{4,5},{5,4},{6,7},{7,6},{8,9},{9,8},{10,11... | collective-permute-start | bytes 221192 | tf_op jit(solution)/shard_map/ppermute | solution.py:718
  (34 other events, 604.3 us)

commit v11 on v7

--- a/solution.py
+++ b/solution.py
@@ -166,8 +166,10 @@
 CHUNKS = BODY + TAIL // 2
 EXTRA = TAIL // 2 + 1
 COEF = 2 * HALF * CAND_OWN
-CROSS_STEP = 6
-SUM_STEP = 3
+RANGE = 6
+RANGES = ((BODY, CHUNKS + 1),) + tuple(
+    (first * TURNS, (first + RANGE) * TURNS) for first in range(0, HALF, RANGE)
+)
 
 
 def selector():
@@ -353,11 +355,27 @@
     return imag, odd
 
 
-def lanes_of(refs, first, number):
-    parts = [
-        jnp.concatenate([ref[i] for ref in refs], 0) for i in range(first, first + number)
-    ]
+def lanes_of(held, first, number):
+    parts = []
+    for i in range(number):
+        parts.append(jnp.concatenate([held[j, first + i] for j in range(held.shape[0])], 0))
     return jnp.concatenate(parts, 1) if number > 1 else parts[0]
+
+
+def fetch(blocks, held, sems):
+    copies = []
+    for r, (first, last) in enumerate(RANGES):
+        chunks = pl.ds(first, last - first)
+        copies.append(
+            [
+                pltpu.make_async_copy(block.at[chunks], held.at[j, chunks], sems.at[r, j])
+                for j, block in enumerate(blocks)
+            ]
+        )
+    for group in copies:
+        for copy in group:
+            copy.start()
+    return copies
 
 
 def hot_masks(cand, groups):
@@ -365,14 +383,14 @@
     return [rows == cand[q : q + 1] for q in range(CAND_OWN)]
 
 
-def residue_weights(q_ref, at, g):
+def residue_weights(q_ref, g, special):
     imag, odd = lane_signs()
     sign = jnp.where(imag == odd, -1.0, 1.0)
     first, second = [], []
     for i in range(TURNS):
-        q = q_ref[at * TURNS + i].astype(jnp.float32)
+        q = q_ref[g * TURNS + i].astype(jnp.float32)
         turned = pltpu.roll(q, LANES // 2, 1) * sign
-        if at == 0:
+        if special:
             first.append(jnp.where((g == 0) & odd, 0.0, q))
             second.append(jnp.where(g == 0, jnp.where(odd, q, 0.0), turned))
         else:
@@ -395,93 +413,83 @@
 
 
 def cross_body(at_ref, *refs):
-    number = (len(refs) - 6) // 2
-    blocks, extras = refs[:number], refs[number : 2 * number]
-    q_ref, qt_ref, norm_ref, coef_ref, cand_ref, acc = refs[2 * number :]
-    step = pl.program_id(0)
+    blocks = refs[:-7]
+    q_ref, norm_ref, coef_ref, cand_ref, held, acc, sems = refs[-7:]
     groups = q_ref.shape[1]
     imag, odd = lane_signs()
-
-    @pl.when(step == 0)
-    def _():
-        label = lanes_of(extras, TAIL // 2, 1).astype(jnp.float32).T
-        row = lax.broadcasted_iota(jnp.int32, label.shape, 0)
-        base = at_ref[0] * CAND_OWN
-        for q in range(CAND_OWN):
-            cand_ref[q : q + 1, :] = jnp.sum(
-                jnp.where(row == base + q, label, 0.0), axis=0, keepdims=True
+    copies = fetch(blocks, held, sems)
+    for copy in copies[0]:
+        copy.wait()
+    label = lanes_of(held, CHUNKS, 1).astype(jnp.float32).T
+    row = lax.broadcasted_iota(jnp.int32, label.shape, 0)
+    base = at_ref[0] * CAND_OWN
+    for q in range(CAND_OWN):
+        cand_ref[q : q + 1, :] = jnp.sum(
+            jnp.where(row == base + q, label, 0.0), axis=0, keepdims=True
+        )
+    cand_ref[CAND_OWN:, :] = jnp.full(
+        (cand_ref.shape[0] - CAND_OWN, cand_ref.shape[1]), -1.0, jnp.float32
+    )
+
+    def tail(i):
+        q = q_ref[BODY + i // 2].astype(jnp.float32)
+        keep = odd if i % 2 else ~odd
+        a = jnp.where(keep, q, 0.0)
+        turned = pltpu.roll(q, LANES // 2, 1) * jnp.where(imag, 1.0, -1.0)
+        b = jnp.where(keep, turned, 0.0)
+        if i == 0:
+            b = jnp.zeros_like(b)
+        w = jnp.concatenate([a, b], 0).astype(jnp.bfloat16)
+        acc[...] += nt_dot(w, lanes_of(held, BODY + i // 2, 1))
+        if i == 0:
+            acc[:groups, :] -= 0.5 * jnp.sum(norm_ref[...], axis=1, keepdims=True)
+
+    for r in range(1, len(RANGES)):
+        for copy in copies[r]:
+            copy.wait()
+
+        def one(u, carry):
+            g = (r - 1) * RANGE + u
+            acc[...] = nt_dot(residue_weights(q_ref, g, r == 1), lanes_of(held, g * TURNS, TURNS))
+            if r == 1:
+                for i in range(TAIL):
+                    pl.when(g == i)(functools.partial(tail, i))
+            block = 2 * CAND_OWN
+            coef_ref[pl.ds(pl.multiple_of(g * block, block), block), :] = chosen_rows(
+                acc[...], cand_ref[...]
             )
-        cand_ref[CAND_OWN:, :] = jnp.full(
-            (cand_ref.shape[0] - CAND_OWN, cand_ref.shape[1]), -1.0, jnp.float32
-        )
-
-    for u in range(CROSS_STEP):
-        g = step * CROSS_STEP + u
-        acc[...] = nt_dot(residue_weights(q_ref, u, g), lanes_of(blocks, u * TURNS, TURNS))
-
-        for i in range(TAIL):
-            if i % CROSS_STEP != u:
-                continue
-
-            @pl.when(g == i)
-            def _():
-                q = qt_ref[i // 2].astype(jnp.float32)
-                keep = odd if i % 2 else ~odd
-                a = jnp.where(keep, q, 0.0)
-                turned = pltpu.roll(q, LANES // 2, 1) * jnp.where(imag, 1.0, -1.0)
-                b = jnp.where(keep, turned, 0.0)
-                if i == 0:
-                    b = jnp.zeros_like(b)
-                w = jnp.concatenate([a, b], 0).astype(jnp.bfloat16)
-                acc[...] += nt_dot(w, lanes_of(extras, i // 2, 1))
-                if i == 0:
-                    acc[:groups, :] -= 0.5 * jnp.sum(norm_ref[...], axis=1, keepdims=True)
-
-        block = 2 * CAND_OWN
-        coef_ref[u * block : (u + 1) * block, :] = chosen_rows(acc[...], cand_ref[...])
+            return carry
+
+        lax.fori_loop(0, RANGE, one, 0)
 
 
 def cross_coefficients(blocks, arranged, norms, cls):
+    number = len(blocks)
     count = blocks[0].shape[1]
     groups = arranged.shape[1]
-    total = len(blocks) * count
-    half_tail = TAIL // 2
-    size = blocks[0].size * len(blocks)
+    total = number * count
+    size = blocks[0].size * number
     block = 2 * CAND_OWN
     return pl.pallas_call(
         cross_body,
-        grid_spec=pltpu.PrefetchScalarGridSpec(
-            num_scalar_prefetch=1,
-            grid=(HALF // CROSS_STEP,),
-            in_specs=[
-                *[
-                    pl.BlockSpec((CROSS_STEP * TURNS, count, LANES), lambda g, at: (g, 0, 0))
-                    for _ in blocks
-                ],
-                *[
-                    pl.BlockSpec((EXTRA, count, LANES), lambda g, at: (BODY // EXTRA, 0, 0))
-                    for _ in blocks
-                ],
-                pl.BlockSpec((CROSS_STEP * TURNS, groups, LANES), lambda g, at: (g, 0, 0)),
-                pl.BlockSpec((half_tail, groups, LANES), lambda g, at: (BODY // half_tail, 0, 0)),
-                pl.BlockSpec((groups, LANES), lambda g, at: (0, 0)),
-            ],
-            out_specs=[
-                pl.BlockSpec((CROSS_STEP * block, total), lambda g, at: (g, 0)),
-                pl.BlockSpec((block, total), lambda g, at: (0, 0)),
-            ],
-            scratch_shapes=[pltpu.VMEM((2 * groups, total), jnp.float32)],
-        ),
+        in_specs=[pl.BlockSpec(memory_space=pltpu.SMEM)]
+        + [pl.BlockSpec(memory_space=pl.ANY)] * number
+        + [pl.BlockSpec(memory_space=pltpu.VMEM)] * 2,
         out_shape=[
             jax.ShapeDtypeStruct((COEF, total), jnp.float32),
             jax.ShapeDtypeStruct((block, total), jnp.float32),
+        ],
+        scratch_shapes=[
+            pltpu.VMEM((number, *blocks[0].shape), jnp.bfloat16),
+            pltpu.VMEM((2 * groups, total), jnp.float32),
+            pltpu.SemaphoreType.DMA((len(RANGES), number)),
         ],
         compiler_params=pltpu.CompilerParams(vmem_limit_bytes=60 << 20),
         cost_estimate=pl.CostEstimate(
             flops=4 * size * groups, bytes_accessed=2 * size, transcendentals=0
         ),
         name="cross_coefficients",
-    )(cls, *blocks, *blocks, arranged, arranged, norms)
+    )(cls, *blocks, arranged, norms)
 
 
 def score_body(*refs, scale):
@@ -565,17 +573,18 @@
 
 
 def sums_body(*refs, number, pieces):
-    blocks, extras = refs[:number], refs[number : 2 * number]
-    refs = refs[2 * number :]
+    blocks = refs[:number]
+    refs = refs[number:]
     mixes, cands = refs[:pieces], refs[pieces : 2 * pieces]
-    back_ref, out_ref, weight_ref, mix, cand, planes = refs[2 * pieces :]
-    i = pl.program_id(0)
+    back_ref, out_ref, weight_ref, mix, cand, planes, held, sems = refs[2 * pieces :]
+    step = pl.program_id(0)
     groups = weight_ref.shape[1]
     total = mix.shape[1]
     imag, odd = lane_signs()
 
-    @pl.when(i == 0)
+    @pl.when(step == 0)
     def _():
+        copies = fetch(blocks, held, sems)
         mixed = jnp.concatenate([ref[...] for ref in mixes], 1)
         chosen = jnp.concatenate([ref[...] for ref in cands], 1)
         hot = hot_masks(chosen, groups)
@@ -591,57 +600,62 @@
         )
         mix[...] = mixed
         cand[...] = chosen
-
-    @pl.when(i < HALF // SUM_STEP)
-    def _():
-        hot = hot_masks(cand[...], groups)
-        block = 2 * CAND_OWN
         sign = jnp.where(imag == odd, 1.0, -1.0)
-        for u in range(SUM_STEP):
-            g = i * SUM_STEP + u
-            mine = mix[pl.ds(pl.multiple_of(g * block, block), block), :]
-            halves = []
-            for ab in range(2):
-                dense = jnp.zeros((groups, total), jnp.float32)
-                for q in range(CAND_OWN):
-                    at = ab * CAND_OWN + q
-                    dense = jnp.where(hot[q], mine[at : at + 1], dense)
-                halves.append(dense)
-            weights = jnp.concatenate(halves, 0).astype(jnp.bfloat16)
+        for copy in copies[0]:
+            copy.wait()
+
+        def tail(t, weights):
             made = jnp.dot(
-                weights, lanes_of(blocks, u * TURNS, TURNS), preferred_element_type=jnp.float32
+                weights, lanes_of(held, BODY + t // 2, 1), preferred_element_type=jnp.float32
             )
-            for t in range(TURNS):
-                g1 = made[:groups, t * LANES : (t + 1) * LANES]
-                g2 = made[groups:, t * LANES : (t + 1) * LANES]
-                value = g1 + sign * pltpu.roll(g2, LANES // 2, 1)
-                if u == 0:
-                    value = jnp.where(i == 0, jnp.where(odd, g2, g1), value)
-                start = pl.multiple_of((g * TURNS + t) * groups, groups)
-                planes[pl.ds(start, groups), :] = value
-
-            for t in range(TAIL):
-                if t % SUM_STEP != u:
-                    continue
-
-                @pl.when(g == t)
-                def _():
-                    made = jnp.dot(
-                        weights, lanes_of(extras, t // 2, 1), preferred_element_type=jnp.float32
-                    )
-                    g1, g2 = made[:groups], made[groups:]
-                    value = g1
-                    if t > 0:
-                        value = g1 + jnp.where(imag, -1.0, 1.0) * pltpu.roll(g2, LANES // 2, 1)
-                    rows = pl.ds((BODY + t // 2) * groups, groups)
-                    if t % 2:
-                        value = jnp.where(odd, value, planes[rows, :])
-                    planes[rows, :] = value
-
-    @pl.when(i >= HALF // SUM_STEP)
+            g1, g2 = made[:groups], made[groups:]
+            value = g1
+            if t > 0:
+                value = g1 + jnp.where(imag, -1.0, 1.0) * pltpu.roll(g2, LANES // 2, 1)
+            rows = pl.ds((BODY + t // 2) * groups, groups)
+            if t % 2:
+                value = jnp.where(odd, value, planes[rows, :])
+            planes[rows, :] = value
+
+        for r in range(1, len(RANGES)):
+            for copy in copies[r]:
+                copy.wait()
+
+            def one(u, carry):
+                g = (r - 1) * RANGE + u
+                hot = hot_masks(cand[...], groups)
+                block = 2 * CAND_OWN
+                mine = mix[pl.ds(pl.multiple_of(g * block, block), block), :]
+                halves = []
+                for ab in range(2):
+                    dense = jnp.zeros((groups, total), jnp.float32)
+                    for q in range(CAND_OWN):
+                        at = ab * CAND_OWN + q
+                        dense = jnp.where(hot[q], mine[at : at + 1], dense)
+                    halves.append(dense)
+                weights = jnp.concatenate(halves, 0).astype(jnp.bfloat16)
+                made = jnp.dot(
+                    weights, lanes_of(held, g * TURNS, TURNS), preferred_element_type=jnp.float32
+                )
+                for t in range(TURNS):
+                    g1 = made[:groups, t * LANES : (t + 1) * LANES]
+                    g2 = made[groups:, t * LANES : (t + 1) * LANES]
+                    value = g1 + sign * pltpu.roll(g2, LANES // 2, 1)
+                    if r == 1:
+                        value = jnp.where(g == 0, jnp.where(odd, g2, g1), value)
+                    start = pl.multiple_of((g * TURNS + t) * groups, groups)
+                    planes[pl.ds(start, groups), :] = value
+                if r == 1:
+                    for t in range(TAIL):
+                        pl.when(g == t)(functools.partial(tail, t, weights))
+                return carry
+
+            lax.fori_loop(0, RANGE, one, 0)
+
+    @pl.when(step > 0)
     def _():
         block, span, _ = out_ref.shape
-        first = (i - HALF // SUM_STEP) * block
+        first = (step - 1) * block
         back = back_ref[...]
         values = []
         for c in range(block):
@@ -666,32 +680,21 @@
 
 
 def sums(blocks, mixes, cands, back, groups, span):
+    number = len(blocks)
     count = blocks[0].shape[1]
-    total = len(blocks) * count
-    size = blocks[0].size * len(blocks)
+    total = number * count
+    size = blocks[0].size * number
     block = 8
-    steps = HALF // SUM_STEP
     whole = lambda i: (0, 0)
     return pl.pallas_call(
-        functools.partial(sums_body, number=len(blocks), pieces=len(mixes)),
-        grid=(steps + groups // block,),
+        functools.partial(sums_body, number=number, pieces=len(mixes)),
+        grid=(1 + groups // block,),
         in_specs=[
-            *[
-                pl.BlockSpec(
-                    (SUM_STEP * TURNS, count, LANES), lambda i: (jnp.minimum(i, steps - 1), 0, 0)
-                )
-                for _ in blocks
-            ],
-            *[
-                pl.BlockSpec((EXTRA, count, LANES), lambda i: (BODY // EXTRA, 0, 0))
-                for _ in blocks
-            ],
+            *[pl.BlockSpec(memory_space=pl.ANY)] * number,
             *[pl.BlockSpec(array.shape, whole) for array in (*mixes, *cands, back)],
         ],
         out_specs=[
-            pl.BlockSpec(
-                (block, span, 2 * HARM), lambda i: (jnp.maximum(i - steps, 0), 0, 0)
-            ),
+            pl.BlockSpec((block, span, 2 * HARM), lambda i: (jnp.maximum(i - 1, 0), 0, 0)),
             pl.BlockSpec((1, groups), whole),
         ],
         out_shape=[
@@ -702,6 +705,8 @@
             pltpu.VMEM((COEF, total), jnp.float32),
             pltpu.VMEM((2 * CAND_OWN, total), jnp.float32),
             pltpu.VMEM((CHUNKS * groups, LANES), jnp.float32),
+            pltpu.VMEM((number, *blocks[0].shape), jnp.bfloat16),
+            pltpu.SemaphoreType.DMA((len(RANGES), number)),
         ],
         compiler_params=pltpu.CompilerParams(vmem_limit_bytes=60 << 20),
         cost_estimate=pl.CostEstimate(
@@ -710,7 +715,7 @@
             transcendentals=0,
         ),
         name="sums",
-    )(*blocks, *blocks, *mixes, *cands, back)
+    )(*blocks, *mixes, *cands, back)
 
 
 def hop(value, axis, distance):
@@ -757,34 +762,39 @@
     picks = class_order[:, :, :CAND_OWN].reshape(count, OWN_TOP * CAND_OWN)
     meta = jnp.concatenate([owner_groups, picks], 1)
     cls, prt = (index.reshape(1).astype(jnp.int32) for index in (cls, prt))
-    order = [d for d in range(n_prt) if d % 2 == 0] + [d for d in range(n_prt) if d % 2]
-    outgoing = {}
-    place = prt
+    outgoing = []
     for first in range(0, n_prt, 2):
-        distances = tuple(order[first : first + 2])
-        made = arrange_particles(place, particles, meta, n_prt, distances)
-        outgoing.update(zip(distances, made))
-        place = after(prt, made[0])
-    last = outgoing[order[-1]]
-    arrived = {d: hop(outgoing[d], "prt", d) if d else outgoing[d] for d in order}
-    known = {0: {0: arrived[0], **direct(arrived[0])}}
+        distances = tuple(range(first, min(first + 2, n_prt)))
+        place = after(prt, outgoing[0]) if outgoing else prt
+        outgoing += arrange_particles(
+            place, particles, meta, n_prt, distances
+        )
+    arrived = [outgoing[0]]
+    known = [{0: arrived[0], **direct(arrived[0])}]
     for d in range(1, min(n_prt, 3)):
-        own = after(arrived[d], last) if d == 2 else arrived[d]
-        known[d] = {0: own, **direct(own)}
-    place = after(prt, *[arrived[d] for d in range(1, min(n_prt, 3))])
+        arrived.append(hop(outgoing[d], "prt", d))
+    early = after(arrived[1], outgoing[-1])
+    known.append({0: early, **direct(early)})
+    relayed(known[0], 0, outgoing[-1])
+    place = after(prt, *arrived[1:2], *[known[0][1 << b] for b in range(1, n_cls.bit_length() - 1)])
     arranged, norms = arrange_references(references, place, n_prt)
-    for d in range(3, n_prt):
-        arrived[d] = after(arrived[d], arranged)
-        known[d] = {0: arrived[d], **direct(arrived[d])}
-    relayed(known[0], 0, arranged)
-    for d in range(1, n_prt):
+    for d in range(2, n_prt):
+        if d > 2:
+            arrived.append(hop(after(outgoing[d], arrived[d - 1], arranged), "prt", d))
+        own = after(arrived[d], arranged) if d == 2 else arrived[d]
+        known.append({0: own, **direct(own)})
+    for d in range(1, n_prt, 2):
         relayed(known[d], d)
     scale = 2.0 / math.sqrt(cycles * width)
     coefs, cands, sent, blocks = [], [], [], []
     for d in range(n_prt):
-        waits = [known[n_prt - 1][2]] if d == 1 else []
-        each = [arranged] if d == 0 else [arranged, arrived[n_prt - 1]] if d == 1 else coefs[:1]
-        blocks.append(paired(known[d], each, coefs[-1:] if d > 1 else []))
+        waits = []
+        if n_prt > 3:
+            waits = [[known[1][2]], [arrived[3], known[2][n_cls // 2]], [known[3][2]], []][min(d, 3)]
+        if d and d % 2 == 0:
+            relayed(known[d], d, coefs[0])
+        each = [arranged, known[1][n_cls // 2]] if d == 0 else coefs[:1] if d < 3 else []
+        blocks.append(paired(known[d], each, coefs[-1:]))
         ready = after(arranged, *waits) if waits else arranged
         coef, cand = cross_coefficients(blocks[d], ready, norms, cls)
         coefs.append(coef)

time: 193 us -> 182 us (0.943)
  waiting for transfers between devices: 59.8 us -> 46.9 us
  Pallas kernels: 68.2 us -> 76.8 us
  starting transfers between devices: 47 us -> 38.8 us
    ppermute x37, waiting for transfers between devices: 59.8 us -> 46.9 us  [hop(): return lax.ppermute(value, axis, [(i, i ^ distance) for i in range(size)])]
    pallas_call x5, Pallas kernels: 51.3 us -> 59.7 us  [the longest x4 40 us: cross_coefficients(): pl.pallas_call(cross_body, in_specs=[pl.BlockSpec(memory_space=pltpu.SMEM...]
    ppermute x37, starting transfers between devices: 47 us -> 38.8 us  [hop(): return lax.ppermute(value, axis, [(i, i ^ distance) for i in range(size)])]
    unnamed x59 -> x51, local copies, waits for them, and re-layouts: 6.35 us -> 7.45 us
  transfers between devices with their start and end apart: 37 -> 37, of which waited for: 13 -> 10; matrix products, arithmetic and copies ran while one was open for 0% -> 0% of each run, Pallas kernels for 21% -> 28%
where the time goes in v11:
time: 182 us
  Pallas kernels  76.8 us (42%)
  waiting for transfers between devices  46.9 us (26%)
  starting transfers between devices  38.8 us (21%)
  blocking collectives  9.77 us (5%)
  local copies, waits for them, and re-layouts  8.38 us (5%)
    ppermute x37, waiting for transfers between devices, hop(): return lax.ppermute(value, axis, [(i, i ^ distance) for i in range(size)])  46.9 us
    pallas_call x4, Pallas kernels, cross_coefficients(): pl.pallas_call(cross_body, in_specs=[pl.BlockSpec(memory_space=pltpu.SMEM...  40 us
    ppermute x37, starting transfers between devices, hop(): return lax.ppermute(value, axis, [(i, i ^ distance) for i in range(size)])  38.8 us
    pallas_call x1, Pallas kernels, sums(): pl.pallas_call(functools.partial(sums_body, number=number, pieces=len(mix...  19.7 us
    all_gather x1, blocking collectives, gather_device(): lax.all_gather(stat.reshape(1, *stat.shape), 'cls', axis=0, tiled=True)  9.77 us
    pallas_call x1, Pallas kernels, arrange_references(): pl.pallas_call(reference_body, grid_spec=pltpu.PrefetchScalarGridSpec(num...  7.65 us
    unnamed x51, local copies, waits for them, and re-layouts  7.45 us
    pallas_call x2, Pallas kernels, arrange_particles(): pl.pallas_call(functools.partial(particle_body, distances=distances, n_pr...  5.35 us
  transfers between devices with their start and end apart: 37, of which 10 were waited for; matrix products, arithmetic and copies ran while one was open for 0% of the time, Pallas kernels for 28%

profile of v11, /device:TPU:0, one launch (start us, length us, event | category | flops | bytes accessed | tf_op | source)
XLA Modules:
  0.0 181.6 jit_solution(17831156722932801975)
XLA Ops:
  4.0 2.7 %arrange_particles.2 = (bf16[129,16,128]{2,1,0:T(8,128)(2,1)S(1)}, bf16[129,16,128]{2,1,0:T(8,128)(2,1)S(1)}) custom-call(s32[1]{0:T(128)} %bitcast.at_ref, bf16[16,128,512]{2,1,0:T(8,128)(2,1)S(1)} %copy-done, s32[16,20]{1,0:T(8,128)S(1)} %pad_add_fusion.meta_ref), custom_call_target="tpu_custom_call" | custom-call | flops 134217728 | bytes 2097152 | tf_op jit(solution)/shard_map/arrange_particles/pallas_call | solution.py:281
  6.7 3.1 %collective-permute-start = (bf16[129,16,128]{2,1,0:T(8,128)(2,1)S(1)}, bf16[129,16,128]{2,1,0:T(8,128)(2,1)S(1)}, u32[]{:S(2)}, u32[]{:S(2)}) collective-permute-start(bf16[129,16,128]{2,1,0:T(8,128)(2,1)S(1)} %get-tuple-element.45), channel_id=1, source_target_pairs={{0,1},{1,0},{2,3},{3,2},{4,5},{5,4},{6,7},{7,6},{8,9},{9,8},{10,11... | collective-permute-start | bytes 1585160 | tf_op jit(solution)/shard_map/ppermute | solution.py:723
  12.8 2.7 %arrange_particles.3 = (bf16[129,16,128]{2,1,0:T(8,128)(2,1)S(1)}, bf16[129,16,128]{2,1,0:T(8,128)(2,1)S(1)}) custom-call(s32[1]{0:T(128)} %bitcast.at_ref, bf16[16,128,512]{2,1,0:T(8,128)(2,1)S(1)} %copy-done, s32[16,20]{1,0:T(8,128)S(1)} %pad_add_fusion.meta_ref), custom_call_target="tpu_custom_call" | custom-call | flops 134217728 | bytes 2097152 | tf_op jit(solution)/shard_map/arrange_particles/pallas_call | solution.py:281
  15.5 6.3 %collective-permute-done.refs_0_.refs_8_ = bf16[129,16,128]{2,1,0:T(8,128)(2,1)S(1)} collective-permute-done((bf16[129,16,128]{2,1,0:T(8,128)(2,1)S(1)}, bf16[129,16,128]{2,1,0:T(8,128)(2,1)S(1)}, u32[]{:S(2)}, u32[]{:S(2)}) %collective-permute-start) | collective-permute-done | bytes 528416 | tf_op jit(solution)/shard_map/ppermute | solution.py:723
  25.5 2.6 %collective-permute-start.15 = (bf16[129,16,128]{2,1,0:T(8,128)(2,1)S(1)}, bf16[129,16,128]{2,1,0:T(8,128)(2,1)}, u32[]{:S(2)}, u32[]{:S(2)}) collective-permute-start(bf16[129,16,128]{2,1,0:T(8,128)(2,1)S(1)} %get-tuple-element.62), channel_id=1, source_target_pairs={{0,2},{1,3},{2,0},{3,1},{4,6},{5,7},{6,4},{7,5},{8,10},{9,11},{10,... | collective-permute-start | bytes 1585160 | tf_op jit(solution)/shard_map/ppermute | solution.py:723
  28.1 7.7 %arrange_references.1 = (bf16[128,64,128]{2,1,0:T(8,128)(2,1)}, f32[64,128]{1,0:T(8,128)}) custom-call(s32[1]{0:T(128)} %bitcast.at_ref, bf16[64,128,512]{2,1,0:T(8,128)(2,1)} %x_ref.4), custom_call_target="tpu_custom_call" | custom-call | flops 268435456 | bytes 4194304 | tf_op jit(solution)/shard_map/arrange_references/pallas_call | solution.py:322
  35.8 2.8 %collective-permute-done.7.refs_6_ = bf16[129,16,128]{2,1,0:T(8,128)(2,1)} collective-permute-done((bf16[129,16,128]{2,1,0:T(8,128)(2,1)S(1)}, bf16[129,16,128]{2,1,0:T(8,128)(2,1)}, u32[]{:S(2)}, u32[]{:S(2)}) %collective-permute-start.7) | collective-permute-done | bytes 528416 | tf_op jit(solution)/shard_map/ppermute | solution.py:723
  39.1 8.4 %collective-permute-done.9.refs_2_.refs_10_ = bf16[129,16,128]{2,1,0:T(8,128)(2,1)} collective-permute-done((bf16[129,16,128]{2,1,0:T(8,128)(2,1)S(1)}, bf16[129,16,128]{2,1,0:T(8,128)(2,1)}, u32[]{:S(2)}, u32[]{:S(2)}) %collective-permute-start.9) | collective-permute-done | bytes 528416 | tf_op jit(solution)/shard_map/ppermute | solution.py:723
  47.5 2.4 %collective-permute-done.15.refs_0_.refs_16_ = bf16[129,16,128]{2,1,0:T(8,128)(2,1)} collective-permute-done((bf16[129,16,128]{2,1,0:T(8,128)(2,1)S(1)}, bf16[129,16,128]{2,1,0:T(8,128)(2,1)}, u32[]{:S(2)}, u32[]{:S(2)}) %collective-permute-start.15) | collective-permute-done | bytes 528416 | tf_op jit(solution)/shard_map/ppermute | solution.py:723
  53.4 3.5 %collective-permute-start.22 = (bf16[129,16,128]{2,1,0:T(8,128)(2,1)S(1)}, bf16[129,16,128]{2,1,0:T(8,128)(2,1)S(1)}, u32[]{:S(2)}, u32[]{:S(2)}) collective-permute-start(bf16[129,16,128]{2,1,0:T(8,128)(2,1)S(1)} %get-tuple-element.67), channel_id=1, source_target_pairs={{0,3},{1,2},{2,1},{3,0},{4,7},{5,6},{6,5},{7,4},{8,11},{9,10},{10,... | collective-permute-start | bytes 1585160 | tf_op jit(solution)/shard_map/ppermute | solution.py:723
  56.9 10.0 %cross_coefficients.4 = (f32[144,128]{1,0:T(8,128)}, f32[8,128]{1,0:T(8,128)}) custom-call(s32[1]{0:T(128)} %bitcast.2.at_ref, bf16[129,16,128]{2,1,0:T(8,128)(2,1)} %copy-done.1, bf16[129,16,128]{2,1,0:T(8,128)(2,1)} %collective-permute-done.4.refs_1_, bf16[129,16,128]{2,1,0:T(8,128)(2,1)} %copy-done.4, ...), custom_call_target="tpu_custom_call" | custom-call | flops 541065216 | bytes 4227072 | tf_op jit(solution)/shard_map/cross_coefficients/pallas_call | solution.py:473
  67.5 7.1 %collective-permute-done.19.refs_4_.refs_20_ = bf16[129,16,128]{2,1,0:T(8,128)(2,1)S(1)} collective-permute-done((bf16[129,16,128]{2,1,0:T(8,128)(2,1)}, bf16[129,16,128]{2,1,0:T(8,128)(2,1)S(1)}, u32[]{:S(2)}, u32[]{:S(2)}) %collective-permute-start.19) | collective-permute-done | bytes 528416 | tf_op jit(solution)/shard_map/ppermute | solution.py:723
  80.5 10.0 %cross_coefficients.5 = (f32[144,128]{1,0:T(8,128)}, f32[8,128]{1,0:T(8,128)}) custom-call(s32[1]{0:T(128)} %bitcast.2.at_ref, bf16[129,16,128]{2,1,0:T(8,128)(2,1)} %copy-done.2, bf16[129,16,128]{2,1,0:T(8,128)(2,1)} %copy-done.9, bf16[129,16,128]{2,1,0:T(8,128)(2,1)} %collective-permute-done.9.refs_2_.refs_10_, bf16[129,16,128]{2,1,0:T(8,128)(2,1)} %copy-done.10, ...), custom_call_target="tpu_custom_call" | custom-call | flops 541065216 | bytes 4227072 | tf_op jit(solution)/shard_map/cross_coefficients/pallas_call | solution.py:473
  91.1 9.3 %collective-permute-done.25.refs_2_.refs_26_ = bf16[129,16,128]{2,1,0:T(8,128)(2,1)S(1)} collective-permute-done((bf16[129,16,128]{2,1,0:T(8,128)(2,1)S(1)}, bf16[129,16,128]{2,1,0:T(8,128)(2,1)S(1)}, u32[]{:S(2)}, u32[]{:S(2)}) %collective-permute-start.25) | collective-permute-done | bytes 528416 | tf_op jit(solution)/shard_map/ppermute | solution.py:723
  104.3 10.0 %cross_coefficients.6 = (f32[144,128]{1,0:T(8,128)}, f32[8,128]{1,0:T(8,128)}) custom-call(s32[1]{0:T(128)} %bitcast.2.at_ref, bf16[129,16,128]{2,1,0:T(8,128)(2,1)} %collective-permute-done.15.refs_0_.refs_16_, bf16[129,16,128]{2,1,0:T(8,128)(2,1)} %collective-permute-done.16.refs_1_.refs_17_, bf16[129,16,128]{2,1,0:T(8,128)(2,1)} %copy-done.7, ...), custom_call_target="tpu_custom_call" | custom-call | flops 541065216 | bytes 4227072 | tf_op jit(solution)/shard_map/cross_coefficients/pallas_call | solution.py:473
  116.4 3.3 %collective-permute-start.32 = (f32[144,128]{1,0:T(8,128)}, f32[144,128]{1,0:T(8,128)S(1)}, u32[]{:S(2)}, u32[]{:S(2)}) collective-permute-start(f32[144,128]{1,0:T(8,128)} %get-tuple-element.72), channel_id=1, source_target_pairs={{0,2},{1,3},{2,0},{3,1},{4,6},{5,7},{6,4},{7,5},{8,10},{9,11},{10,... | collective-permute-start | bytes 221192 | tf_op jit(solution)/shard_map/ppermute | solution.py:723
  120.6 10.0 %cross_coefficients.7 = (f32[144,128]{1,0:T(8,128)}, f32[8,128]{1,0:T(8,128)}) custom-call(s32[1]{0:T(128)} %bitcast.2.at_ref, bf16[129,16,128]{2,1,0:T(8,128)(2,1)} %copy-done.8, bf16[129,16,128]{2,1,0:T(8,128)(2,1)} %collective-permute-done.24.refs_1_.refs_25_, bf16[129,16,128]{2,1,0:T(8,128)(2,1)} %copy-done.14, ...), custom_call_target="tpu_custom_call" | custom-call | flops 541065216 | bytes 4227072 | tf_op jit(solution)/shard_map/cross_coefficients/pallas_call | solution.py:473
  132.2 4.8 %collective-permute-done.33.refs_3_ = f32[144,128]{1,0:T(8,128)S(1)} collective-permute-done((f32[144,128]{1,0:T(8,128)}, f32[144,128]{1,0:T(8,128)S(1)}, u32[]{:S(2)}, u32[]{:S(2)}) %collective-permute-start.33) | collective-permute-done | bytes 73760 | tf_op jit(solution)/shard_map/ppermute | solution.py:723
  139.7 9.8 %all-gather.1.stat_ref = f32[8,2,128]{2,1,0:T(2,128)} all-gather(f32[1,2,128]{2,1,0:T(2,128)} %bitcast.9), channel_id=2, replica_groups=mesh['cls'=8,'prt'=4] {'cls'}, dimensions={0}, use_global_device_ids=true | all-gather | bytes 9216 | tf_op jit(solution)/shard_map/all_gather | solution.py:804
  149.5 2.1 %mixed_weights.1 = (f32[144,128]{1,0:T(8,128)}, f32[1,16]{1,0:T(1,128)}) custom-call(s32[1]{0:T(128)} %bitcast.2.at_ref, f32[144,128]{1,0:T(8,128)} %get-tuple-element.76.score_ref, f32[8,128]{1,0:T(8,128)} %get-tuple-element.75.refs_4_.cand_ref.refs_36_, f32[8,2,128]{2,1,0:T(2,128)} %all-gather.1.stat_ref, f32[144,144]{1,0:T(8,128)} %constant.14.clone.refs_5_.table_ref), custom_call_target="tpu_custom_call" | custom-call | tf_op jit(solution)/shard_map/mixed_weights/pallas_call | solution.py:564
  153.1 2.9 %collective-permute-start.34 = (f32[144,128]{1,0:T(8,128)}, f32[144,128]{1,0:T(8,128)S(1)}, u32[]{:S(2)}, u32[]{:S(2)}) collective-permute-start(f32[144,128]{1,0:T(8,128)} %get-tuple-element.78.refs_32_), channel_id=1, source_target_pairs={{0,1},{1,0},{2,3},{3,2},{4,5},{5,4},{6,7},{7,6},{8,9},{9,8},{10,11... | collective-permute-start | bytes 221192 | tf_op jit(solution)/shard_map/ppermute | solution.py:723
  156.0 2.8 %collective-permute-done.36.refs_35_ = f32[144,128]{1,0:T(8,128)S(1)} collective-permute-done((f32[144,128]{1,0:T(8,128)}, f32[144,128]{1,0:T(8,128)S(1)}, u32[]{:S(2)}, u32[]{:S(2)}) %collective-permute-start.36) | collective-permute-done | bytes 73760 | tf_op jit(solution)/shard_map/ppermute | solution.py:723
  158.8 2.5 %collective-permute-done.35.refs_34_ = f32[144,128]{1,0:T(8,128)S(1)} collective-permute-done((f32[144,128]{1,0:T(8,128)}, f32[144,128]{1,0:T(8,128)S(1)}, u32[]{:S(2)}, u32[]{:S(2)}) %collective-permute-start.35) | collective-permute-done | bytes 73760 | tf_op jit(solution)/shard_map/ppermute | solution.py:723
  161.9 19.7 %sums.1 = (f32[64,32,512]{2,1,0:T(8,128)}, f32[1,64]{1,0:T(1,128)}) custom-call(bf16[129,16,128]{2,1,0:T(8,128)(2,1)} %copy-done.1, bf16[129,16,128]{2,1,0:T(8,128)(2,1)} %collective-permute-done.4.refs_1_, bf16[129,16,128]{2,1,0:T(8,128)(2,1)} %copy-done.4, bf16[129,16,128]{2,1,0:T(8,128)(2,1)} %collective-permute-done.5.refs_3_, ...), custom_call_target="tpu_custom_call" | custom-call | flops 2164260864 | bytes 21102592 | tf_op jit(solution)/shard_map/sums/pallas_call | solution.py:689
  (115 shorter events, 34.5 us)
Async XLA Ops:
  6.7 15.1 %collective-permute-start = (bf16[129,16,128]{2,1,0:T(8,128)(2,1)S(1)}, bf16[129,16,128]{2,1,0:T(8,128)(2,1)S(1)}, u32[]{:S(2)}, u32[]{:S(2)}) collective-permute-start(bf16[129,16,128]{2,1,0:T(8,128)(2,1)S(1)} %get-tuple-element.45), channel_id=1, source_target_pairs={{0,1},{1,0},{2,3},{3,2},{4,5},{5,4},{6,7},{7,6},{8,9},{9,8},{10,11... | collective-permute-start | bytes 1585160 | tf_op jit(solution)/shard_map/ppermute | solution.py:723
  9.8 13.7 %collective-permute-start.2 = (bf16[129,16,128]{2,1,0:T(8,128)(2,1)S(1)}, bf16[129,16,128]{2,1,0:T(8,128)(2,1)S(1)}, u32[]{:S(2)}, u32[]{:S(2)}) collective-permute-start(bf16[129,16,128]{2,1,0:T(8,128)(2,1)S(1)} %get-tuple-element.51.refs_0_), channel_id=1, source_target_pairs={{0,16},{4,20},{8,24},{12,28},{16,0},{20,4},{24,8},{28,12},{1,17},{... | collective-permute-start | bytes 1585160 | tf_op jit(solution)/shard_map/ppermute | solution.py:723
  11.3 16.8 %collective-permute-start.1 = (bf16[129,16,128]{2,1,0:T(8,128)(2,1)S(1)}, bf16[129,16,128]{2,1,0:T(8,128)(2,1)S(1)}, u32[]{:S(2)}, u32[]{:S(2)}) collective-permute-start(bf16[129,16,128]{2,1,0:T(8,128)(2,1)S(1)} %get-tuple-element.51.refs_0_), channel_id=1, source_target_pairs={{0,8},{4,12},{8,0},{12,4},{16,24},{20,28},{24,16},{28,20},{1,9},{5... | collective-permute-start | bytes 1585160 | tf_op jit(solution)/shard_map/ppermute | solution.py:723
  21.8 14.0 %collective-permute-start.3 = (bf16[129,16,128]{2,1,0:T(8,128)(2,1)S(1)}, bf16[129,16,128]{2,1,0:T(8,128)(2,1)S(1)}, u32[]{:S(2)}, u32[]{:S(2)}) collective-permute-start(bf16[129,16,128]{2,1,0:T(8,128)(2,1)S(1)} %collective-permute-done.refs_0_.refs_8_), channel_id=1, source_target_pairs={{0,16},{4,20},{8,24},{12,28},{16,0},{20,4},{24,8},{28,12},{1,17},{... | collective-permute-start | bytes 1585160 | tf_op jit(solution)/shard_map/ppermute | solution.py:723
  23.5 15.1 %collective-permute-start.7 = (bf16[129,16,128]{2,1,0:T(8,128)(2,1)S(1)}, bf16[129,16,128]{2,1,0:T(8,128)(2,1)}, u32[]{:S(2)}, u32[]{:S(2)}) collective-permute-start(bf16[129,16,128]{2,1,0:T(8,128)(2,1)S(1)} %collective-permute-done.2.refs_4_), channel_id=1, source_target_pairs={{0,8},{4,12},{8,0},{12,4},{16,24},{20,28},{24,16},{28,20},{1,9},{5... | collective-permute-start | bytes 1585160 | tf_op jit(solution)/shard_map/ppermute | solution.py:723
  25.0 22.5 %collective-permute-start.9 = (bf16[129,16,128]{2,1,0:T(8,128)(2,1)S(1)}, bf16[129,16,128]{2,1,0:T(8,128)(2,1)}, u32[]{:S(2)}, u32[]{:S(2)}) collective-permute-start(bf16[129,16,128]{2,1,0:T(8,128)(2,1)S(1)} %collective-permute-done.refs_0_.refs_8_), channel_id=1, source_target_pairs={{0,8},{4,12},{8,0},{12,4},{16,24},{20,28},{24,16},{28,20},{1,9},{5... | collective-permute-start | bytes 1585160 | tf_op jit(solution)/shard_map/ppermute | solution.py:723
  25.5 24.4 %collective-permute-start.15 = (bf16[129,16,128]{2,1,0:T(8,128)(2,1)S(1)}, bf16[129,16,128]{2,1,0:T(8,128)(2,1)}, u32[]{:S(2)}, u32[]{:S(2)}) collective-permute-start(bf16[129,16,128]{2,1,0:T(8,128)(2,1)S(1)} %get-tuple-element.62), channel_id=1, source_target_pairs={{0,2},{1,3},{2,0},{3,1},{4,6},{5,7},{6,4},{7,5},{8,10},{9,11},{10,... | collective-permute-start | bytes 1585160 | tf_op jit(solution)/shard_map/ppermute | solution.py:723
  38.5 13.4 %collective-permute-start.4 = (bf16[129,16,128]{2,1,0:T(8,128)(2,1)S(1)}, bf16[129,16,128]{2,1,0:T(8,128)(2,1)}, u32[]{:S(2)}, u32[]{:S(2)}) collective-permute-start(bf16[129,16,128]{2,1,0:T(8,128)(2,1)S(1)} %get-tuple-element.51.refs_0_), channel_id=1, source_target_pairs={{0,4},{4,0},{8,12},{12,8},{16,20},{20,16},{24,28},{28,24},{1,5},{5... | collective-permute-start | bytes 1585160 | tf_op jit(solution)/shard_map/ppermute | solution.py:723
  39.0 14.3 %collective-permute-start.5 = (bf16[129,16,128]{2,1,0:T(8,128)(2,1)S(1)}, bf16[129,16,128]{2,1,0:T(8,128)(2,1)}, u32[]{:S(2)}, u32[]{:S(2)}) collective-permute-start(bf16[129,16,128]{2,1,0:T(8,128)(2,1)S(1)} %collective-permute-done.1.refs_2_), channel_id=1, source_target_pairs={{0,4},{4,0},{8,12},{12,8},{16,20},{20,16},{24,28},{28,24},{1,5},{5... | collective-permute-start | bytes 1585160 | tf_op jit(solution)/shard_map/ppermute | solution.py:723
  49.9 17.1 %collective-permute-start.13 = (bf16[129,16,128]{2,1,0:T(8,128)(2,1)}, bf16[129,16,128]{2,1,0:T(8,128)(2,1)}, u32[]{:S(2)}, u32[]{:S(2)}) collective-permute-start(bf16[129,16,128]{2,1,0:T(8,128)(2,1)} %collective-permute-done.9.refs_2_.refs_10_), channel_id=1, source_target_pairs={{0,16},{4,20},{8,24},{12,28},{16,0},{20,4},{24,8},{28,12},{1,17},{... | collective-permute-start | bytes 1585160 | tf_op jit(solution)/shard_map/ppermute | solution.py:723
  51.1 23.4 %collective-permute-start.19 = (bf16[129,16,128]{2,1,0:T(8,128)(2,1)}, bf16[129,16,128]{2,1,0:T(8,128)(2,1)S(1)}, u32[]{:S(2)}, u32[]{:S(2)}) collective-permute-start(bf16[129,16,128]{2,1,0:T(8,128)(2,1)} %collective-permute-done.15.refs_0_.refs_16_), channel_id=1, source_target_pairs={{0,16},{4,20},{8,24},{12,28},{16,0},{20,4},{24,8},{28,12},{1,17},{... | collective-permute-start | bytes 1585160 | tf_op jit(solution)/shard_map/ppermute | solution.py:723
  51.9 22.6 %collective-permute-start.17 = (bf16[129,16,128]{2,1,0:T(8,128)(2,1)}, bf16[129,16,128]{2,1,0:T(8,128)(2,1)S(1)}, u32[]{:S(2)}, u32[]{:S(2)}) collective-permute-start(bf16[129,16,128]{2,1,0:T(8,128)(2,1)} %collective-permute-done.15.refs_0_.refs_16_), channel_id=1, source_target_pairs={{0,8},{4,12},{8,0},{12,4},{16,24},{20,28},{24,16},{28,20},{1,9},{5... | collective-permute-start | bytes 1585160 | tf_op jit(solution)/shard_map/ppermute | solution.py:723
  53.4 21.7 %collective-permute-start.22 = (bf16[129,16,128]{2,1,0:T(8,128)(2,1)S(1)}, bf16[129,16,128]{2,1,0:T(8,128)(2,1)S(1)}, u32[]{:S(2)}, u32[]{:S(2)}) collective-permute-start(bf16[129,16,128]{2,1,0:T(8,128)(2,1)S(1)} %get-tuple-element.67), channel_id=1, source_target_pairs={{0,3},{1,2},{2,1},{3,0},{4,7},{5,6},{6,5},{7,4},{8,11},{9,10},{10,... | collective-permute-start | bytes 1585160 | tf_op jit(solution)/shard_map/ppermute | solution.py:723
  75.0 15.5 %collective-permute-start.21 = (bf16[129,16,128]{2,1,0:T(8,128)(2,1)S(1)}, bf16[129,16,128]{2,1,0:T(8,128)(2,1)S(1)}, u32[]{:S(2)}, u32[]{:S(2)}) collective-permute-start(bf16[129,16,128]{2,1,0:T(8,128)(2,1)S(1)} %collective-permute-done.19.refs_4_.refs_20_), channel_id=1, source_target_pairs={{0,8},{4,12},{8,0},{12,4},{16,24},{20,28},{24,16},{28,20},{1,9},{5... | collective-permute-start | bytes 1585160 | tf_op jit(solution)/shard_map/ppermute | solution.py:723
  76.6 23.8 %collective-permute-start.25 = (bf16[129,16,128]{2,1,0:T(8,128)(2,1)S(1)}, bf16[129,16,128]{2,1,0:T(8,128)(2,1)S(1)}, u32[]{:S(2)}, u32[]{:S(2)}) collective-permute-start(bf16[129,16,128]{2,1,0:T(8,128)(2,1)S(1)} %collective-permute-done.22.refs_0_.refs_24_), channel_id=1, source_target_pairs={{0,8},{4,12},{8,0},{12,4},{16,24},{20,28},{24,16},{28,20},{1,9},{5... | collective-permute-start | bytes 1585160 | tf_op jit(solution)/shard_map/ppermute | solution.py:723
  77.1 23.3 %collective-permute-start.27 = (bf16[129,16,128]{2,1,0:T(8,128)(2,1)S(1)}, bf16[129,16,128]{2,1,0:T(8,128)(2,1)}, u32[]{:S(2)}, u32[]{:S(2)}) collective-permute-start(bf16[129,16,128]{2,1,0:T(8,128)(2,1)S(1)} %collective-permute-done.22.refs_0_.refs_24_), channel_id=1, source_target_pairs={{0,16},{4,20},{8,24},{12,28},{16,0},{20,4},{24,8},{28,12},{1,17},{... | collective-permute-start | bytes 1585160 | tf_op jit(solution)/shard_map/ppermute | solution.py:723
  78.8 23.5 %collective-permute-start.20 = (bf16[129,16,128]{2,1,0:T(8,128)(2,1)S(1)}, bf16[129,16,128]{2,1,0:T(8,128)(2,1)}, u32[]{:S(2)}, u32[]{:S(2)}) collective-permute-start(bf16[129,16,128]{2,1,0:T(8,128)(2,1)S(1)} %collective-permute-done.19.refs_4_.refs_20_), channel_id=1, source_target_pairs={{0,4},{4,0},{8,12},{12,8},{16,20},{20,16},{24,28},{28,24},{1,5},{5... | collective-permute-start | bytes 1585160 | tf_op jit(solution)/shard_map/ppermute | solution.py:723
  80.4 21.8 %collective-permute-start.16 = (bf16[129,16,128]{2,1,0:T(8,128)(2,1)}, bf16[129,16,128]{2,1,0:T(8,128)(2,1)}, u32[]{:S(2)}, u32[]{:S(2)}) collective-permute-start(bf16[129,16,128]{2,1,0:T(8,128)(2,1)} %collective-permute-done.15.refs_0_.refs_16_), channel_id=1, source_target_pairs={{0,4},{4,0},{8,12},{12,8},{16,20},{20,16},{24,28},{28,24},{1,5},{5... | collective-permute-start | bytes 1585160 | tf_op jit(solution)/shard_map/ppermute | solution.py:723
  100.4 14.5 %collective-permute-start.29 = (bf16[129,16,128]{2,1,0:T(8,128)(2,1)S(1)}, bf16[129,16,128]{2,1,0:T(8,128)(2,1)}, u32[]{:S(2)}, u32[]{:S(2)}) collective-permute-start(bf16[129,16,128]{2,1,0:T(8,128)(2,1)S(1)} %collective-permute-done.25.refs_2_.refs_26_), channel_id=1, source_target_pairs={{0,16},{4,20},{8,24},{12,28},{16,0},{20,4},{24,8},{28,12},{1,17},{... | collective-permute-start | bytes 1585160 | tf_op jit(solution)/shard_map/ppermute | solution.py:723
  102.2 14.2 %collective-permute-start.24 = (bf16[129,16,128]{2,1,0:T(8,128)(2,1)S(1)}, bf16[129,16,128]{2,1,0:T(8,128)(2,1)}, u32[]{:S(2)}, u32[]{:S(2)}) collective-permute-start(bf16[129,16,128]{2,1,0:T(8,128)(2,1)S(1)} %collective-permute-done.22.refs_0_.refs_24_), channel_id=1, source_target_pairs={{0,4},{4,0},{8,12},{12,8},{16,20},{20,16},{24,28},{28,24},{1,5},{5... | collective-permute-start | bytes 1585160 | tf_op jit(solution)/shard_map/ppermute | solution.py:723
  102.4 17.4 %collective-permute-start.26 = (bf16[129,16,128]{2,1,0:T(8,128)(2,1)S(1)}, bf16[129,16,128]{2,1,0:T(8,128)(2,1)}, u32[]{:S(2)}, u32[]{:S(2)}) collective-permute-start(bf16[129,16,128]{2,1,0:T(8,128)(2,1)S(1)} %collective-permute-done.25.refs_2_.refs_26_), channel_id=1, source_target_pairs={{0,4},{4,0},{8,12},{12,8},{16,20},{20,16},{24,28},{28,24},{1,5},{5... | collective-permute-start | bytes 1585160 | tf_op jit(solution)/shard_map/ppermute | solution.py:723
  102.7 17.1 %collective-permute-start.28 = (bf16[129,16,128]{2,1,0:T(8,128)(2,1)}, bf16[129,16,128]{2,1,0:T(8,128)(2,1)}, u32[]{:S(2)}, u32[]{:S(2)}) collective-permute-start(bf16[129,16,128]{2,1,0:T(8,128)(2,1)} %collective-permute-done.27.refs_4_.refs_28_), channel_id=1, source_target_pairs={{0,4},{4,0},{8,12},{12,8},{16,20},{20,16},{24,28},{28,24},{1,5},{5... | collective-permute-start | bytes 1585160 | tf_op jit(solution)/shard_map/ppermute | solution.py:723
  114.9 17.3 %collective-permute-start.31 = (f32[144,128]{1,0:T(8,128)S(1)}, f32[144,128]{1,0:T(8,128)S(1)}, u32[]{:S(2)}, u32[]{:S(2)}) collective-permute-start(f32[144,128]{1,0:T(8,128)S(1)} %copy-done.24), channel_id=1, source_target_pairs={{0,1},{1,0},{2,3},{3,2},{4,5},{5,4},{6,7},{7,6},{8,9},{9,8},{10,11... | collective-permute-start | bytes 221192 | tf_op jit(solution)/shard_map/ppermute | solution.py:723
  116.4 15.8 %collective-permute-start.32 = (f32[144,128]{1,0:T(8,128)}, f32[144,128]{1,0:T(8,128)S(1)}, u32[]{:S(2)}, u32[]{:S(2)}) collective-permute-start(f32[144,128]{1,0:T(8,128)} %get-tuple-element.72), channel_id=1, source_target_pairs={{0,2},{1,3},{2,0},{3,1},{4,6},{5,7},{6,4},{7,5},{8,10},{9,11},{10,... | collective-permute-start | bytes 221192 | tf_op jit(solution)/shard_map/ppermute | solution.py:723
  (38 other events, 434.8 us)

commit v12 on v11

--- a/solution.py
+++ b/solution.py
@@ -383,16 +383,16 @@
     return [rows == cand[q : q + 1] for q in range(CAND_OWN)]
 
 
-def residue_weights(q_ref, g, special):
+def residue_weights(q_ref, g):
     imag, odd = lane_signs()
     sign = jnp.where(imag == odd, -1.0, 1.0)
     first, second = [], []
     for i in range(TURNS):
         q = q_ref[g * TURNS + i].astype(jnp.float32)
         turned = pltpu.roll(q, LANES // 2, 1) * sign
-        if special:
-            first.append(jnp.where((g == 0) & odd, 0.0, q))
-            second.append(jnp.where(g == 0, jnp.where(odd, q, 0.0), turned))
+        if g == 0:
+            first.append(jnp.where(odd, 0.0, q))
+            second.append(jnp.where(odd, q, 0.0))
         else:
             first.append(q)
             second.append(turned)
@@ -413,8 +413,8 @@
 
 
 def cross_body(at_ref, *refs):
-    blocks = refs[:-7]
-    q_ref, norm_ref, coef_ref, cand_ref, held, acc, sems = refs[-7:]
+    blocks = refs[:-6]
+    q_ref, norm_ref, coef_ref, cand_ref, held, sems = refs[-6:]
     groups = q_ref.shape[1]
     imag, odd = lane_signs()
     copies = fetch(blocks, held, sems)
@@ -440,27 +440,21 @@
         if i == 0:
             b = jnp.zeros_like(b)
         w = jnp.concatenate([a, b], 0).astype(jnp.bfloat16)
-        acc[...] += nt_dot(w, lanes_of(held, BODY + i // 2, 1))
-        if i == 0:
-            acc[:groups, :] -= 0.5 * jnp.sum(norm_ref[...], axis=1, keepdims=True)
+        return nt_dot(w, lanes_of(held, BODY + i // 2, 1))
 
     for r in range(1, len(RANGES)):
         for copy in copies[r]:
             copy.wait()
 
-        def one(u, carry):
-            g = (r - 1) * RANGE + u
-            acc[...] = nt_dot(residue_weights(q_ref, g, r == 1), lanes_of(held, g * TURNS, TURNS))
-            if r == 1:
-                for i in range(TAIL):
-                    pl.when(g == i)(functools.partial(tail, i))
+        for g in range((r - 1) * RANGE, r * RANGE):
+            acc = nt_dot(residue_weights(q_ref, g), lanes_of(held, g * TURNS, TURNS))
+            if g < TAIL:
+                acc += tail(g)
+            if g == 0:
+                half_norm = 0.5 * jnp.sum(norm_ref[...], axis=1, keepdims=True)
+                acc = jnp.concatenate([acc[:groups] - half_norm, acc[groups:]], 0)
             block = 2 * CAND_OWN
-            coef_ref[pl.ds(pl.multiple_of(g * block, block), block), :] = chosen_rows(
-                acc[...], cand_ref[...]
-            )
-            return carry
-
-        lax.fori_loop(0, RANGE, one, 0)
+            coef_ref[g * block : (g + 1) * block, :] = chosen_rows(acc, cand_ref[...])
 
 
 def cross_coefficients(blocks, arranged, norms, cls):
@@ -481,7 +475,6 @@
         ],
         scratch_shapes=[
             pltpu.VMEM((number, *blocks[0].shape), jnp.bfloat16),
-            pltpu.VMEM((2 * groups, total), jnp.float32),
             pltpu.SemaphoreType.DMA((len(RANGES), number)),
         ],
         compiler_params=pltpu.CompilerParams(vmem_limit_bytes=60 << 20),
@@ -621,11 +614,10 @@
             for copy in copies[r]:
                 copy.wait()
 
-            def one(u, carry):
-                g = (r - 1) * RANGE + u
-                hot = hot_masks(cand[...], groups)
-                block = 2 * CAND_OWN
-                mine = mix[pl.ds(pl.multiple_of(g * block, block), block), :]
+            hot = hot_masks(cand[...], groups)
+            block = 2 * CAND_OWN
+            for g in range((r - 1) * RANGE, r * RANGE):
+                mine = mix[g * block : (g + 1) * block, :]
                 halves = []
                 for ab in range(2):
                     dense = jnp.zeros((groups, total), jnp.float32)
@@ -640,17 +632,14 @@
                 for t in range(TURNS):
                     g1 = made[:groups, t * LANES : (t + 1) * LANES]
                     g2 = made[groups:, t * LANES : (t + 1) * LANES]
-                    value = g1 + sign * pltpu.roll(g2, LANES // 2, 1)
-                    if r == 1:
-                        value = jnp.where(g == 0, jnp.where(odd, g2, g1), value)
-                    start = pl.multiple_of((g * TURNS + t) * groups, groups)
-                    planes[pl.ds(start, groups), :] = value
-                if r == 1:
-                    for t in range(TAIL):
-                        pl.when(g == t)(functools.partial(tail, t, weights))
-                return carry
-
-            lax.fori_loop(0, RANGE, one, 0)
+                    if g == 0:
+                        value = jnp.where(odd, g2, g1)
+                    else:
+                        value = g1 + sign * pltpu.roll(g2, LANES // 2, 1)
+                    start = (g * TURNS + t) * groups
+                    planes[start : start + groups, :] = value
+                if g < TAIL:
+                    tail(g, weights)
 
     @pl.when(step > 0)
     def _():
@@ -737,7 +726,7 @@
     for j in sorted(range(2, n_cls, 2), key=lambda j: bin(j).count("1")):
         if j not in known:
             bits = [bit for bit in range(1, n_cls.bit_length()) if j >> bit & 1]
-            way = 1 << bits[d % len(bits)]
+            way = 1 << bits[(1 - d // 2) % len(bits)]
             known[j] = hop(after(known[j ^ way], *others), "cls", way)
     return known
 
@@ -762,44 +751,52 @@
     picks = class_order[:, :, :CAND_OWN].reshape(count, OWN_TOP * CAND_OWN)
     meta = jnp.concatenate([owner_groups, picks], 1)
     cls, prt = (index.reshape(1).astype(jnp.int32) for index in (cls, prt))
-    outgoing = []
+    order = [d for d in range(n_prt) if d % 2 == 0] + [d for d in range(n_prt) if d % 2]
+    outgoing = {}
+    place = prt
     for first in range(0, n_prt, 2):
-        distances = tuple(range(first, min(first + 2, n_prt)))
-        place = after(prt, outgoing[0]) if outgoing else prt
-        outgoing += arrange_particles(
-            place, particles, meta, n_prt, distances
-        )
-    arrived = [outgoing[0]]
-    known = [{0: arrived[0], **direct(arrived[0])}]
-    for d in range(1, min(n_prt, 3)):
-        arrived.append(hop(outgoing[d], "prt", d))
-    early = after(arrived[1], outgoing[-1])
-    known.append({0: early, **direct(early)})
-    relayed(known[0], 0, outgoing[-1])
-    place = after(prt, *arrived[1:2], *[known[0][1 << b] for b in range(1, n_cls.bit_length() - 1)])
+        distances = tuple(order[first : first + 2])
+        made = arrange_particles(place, particles, meta, n_prt, distances)
+        outgoing.update(zip(distances, made))
+        place = after(prt, made[0])
+    lead, second, *others = order[1:]
+    final = outgoing[order[-1]]
+    arrived = {d: outgoing[d] if d == 0 else hop(outgoing[d], "prt", d) for d in order[:3]}
+    known = {0: {0: arrived[0], **direct(arrived[0])}}
+    early = after(arrived[lead], final)
+    known[lead] = {0: early, **direct(early)}
+    relayed(known[0], 0, final)
+    far = n_cls // 2
+    place = after(prt, arrived[lead], known[0][2], known[0][far])
     arranged, norms = arrange_references(references, place, n_prt)
-    for d in range(2, n_prt):
-        if d > 2:
-            arrived.append(hop(after(outgoing[d], arrived[d - 1], arranged), "prt", d))
-        own = after(arrived[d], arranged) if d == 2 else arrived[d]
-        known.append({0: own, **direct(own)})
-    for d in range(1, n_prt, 2):
+    previous = arrived[lead]
+    for d in others:
+        previous = arrived[d] = hop(after(outgoing[d], previous), "prt", d)
+    own = after(arrived[second], arranged)
+    known[second] = {0: own, **direct(own)}
+    for d in others:
+        known[d] = {0: arrived[d], **direct(arrived[d])}
+    for d in (lead, *others):
         relayed(known[d], d)
     scale = 2.0 / math.sqrt(cycles * width)
-    coefs, cands, sent, blocks = [], [], [], []
-    for d in range(n_prt):
-        waits = []
-        if n_prt > 3:
-            waits = [[known[1][2]], [arrived[3], known[2][n_cls // 2]], [known[3][2]], []][min(d, 3)]
-        if d and d % 2 == 0:
-            relayed(known[d], d, coefs[0])
-        each = [arranged, known[1][n_cls // 2]] if d == 0 else coefs[:1] if d < 3 else []
-        blocks.append(paired(known[d], each, coefs[-1:]))
+    made, blocks, done = {}, {}, []
+    for d in (0, lead, second, *others):
+        waits = {
+            0: [known[lead][2]],
+            lead: [previous, known[second][far]],
+            second: [known[others[0]][2]],
+        }.get(d, [])
+        if d == second:
+            relayed(known[d], d, done[0])
+        each = [arranged, known[lead][far]] if d == 0 else [] if d in others else done[:1]
+        blocks[d] = paired(known[d], each, done[-1:])
         ready = after(arranged, *waits) if waits else arranged
-        coef, cand = cross_coefficients(blocks[d], ready, norms, cls)
-        coefs.append(coef)
-        sent.append(hop(coef, "prt", d) if d else coef)
-        cands.append(cand)
+        made[d] = cross_coefficients(blocks[d], ready, norms, cls)
+        done.append(made[d][0])
+    distances = range(n_prt)
+    sent = [hop(made[d][0], "prt", d) if d else made[d][0] for d in distances]
+    cands = [made[d][1] for d in distances]
+    blocks = [blocks[d] for d in distances]
     score, stat = scores(sent, cands[0], table, scale)
     stats = lax.all_gather(stat.reshape(1, *stat.shape), "cls", axis=0, tiled=True)
     mix, log_norm = mixed_weights(cls, score, cands[0], stats, table, count)
@@ -817,7 +814,7 @@
     groups = references.shape[0]
     cap = max(2, 2 * count * OWN_TOP // n_cls)
     powers = n_cls & (n_cls - 1) == 0 and n_prt & (n_prt - 1) == 0
-    fits = 4 * cycles == LANES * n_prt and n_cls * CAND_OWN <= LANES and groups % 16 == 0 and n_cls >= 4
+    fits = 4 * cycles == LANES * n_prt and n_cls * CAND_OWN <= LANES and groups % 16 == 0 and n_cls >= 4 and n_prt >= 4
     fits = fits and powers and n_cls * count == LANES
     plan = gather_device if cap >= count and fits else dispatch_device
     return plan(particles, references, owner_groups, class_order)

time: 182 us -> 185 us (1.016)
  waiting for transfers between devices: 46.9 us -> 71.9 us
  Pallas kernels: 76.8 us -> 56.5 us
    ppermute x37, waiting for transfers between devices: 46.9 us -> 71.9 us  [hop(): return lax.ppermute(value, axis, [(i, i ^ distance) for i in range(size)])]
    pallas_call x4, Pallas kernels: 40 us -> 24.2 us  [cross_coefficients(): pl.pallas_call(cross_body, in_specs=[pl.BlockSpec(memory_space=pltpu.SMEM...]
    pallas_call x1, Pallas kernels: 19.7 us -> 15.2 us  [sums(): pl.pallas_call(functools.partial(sums_body, number=number, pieces=len(mix...]
    unnamed x51 -> x49, local copies, waits for them, and re-layouts: 7.45 us -> 5.64 us
  transfers between devices with their start and end apart: 37 -> 37, of which waited for: 10 -> 13; matrix products, arithmetic and copies ran while one was open for 0% -> 0% of each run, Pallas kernels for 28% -> 19%
where the time goes in v12:
time: 185 us
  waiting for transfers between devices  71.9 us (39%)
  Pallas kernels  56.5 us (31%)
  starting transfers between devices  37.9 us (20%)
  blocking collectives  10.7 us (6%)
  local copies, waits for them, and re-layouts  6.56 us (4%)
    ppermute x37, waiting for transfers between devices, hop(): return lax.ppermute(value, axis, [(i, i ^ distance) for i in range(size)])  71.9 us
    ppermute x37, starting transfers between devices, hop(): return lax.ppermute(value, axis, [(i, i ^ distance) for i in range(size)])  37.9 us
    pallas_call x4, Pallas kernels, cross_coefficients(): pl.pallas_call(cross_body, in_specs=[pl.BlockSpec(memory_space=pltpu.SMEM...  24.2 us
    pallas_call x1, Pallas kernels, sums(): pl.pallas_call(functools.partial(sums_body, number=number, pieces=len(mix...  15.2 us
    all_gather x1, blocking collectives, gather_device(): lax.all_gather(stat.reshape(1, *stat.shape), 'cls', axis=0, tiled=True)  10.7 us
    pallas_call x1, Pallas kernels, arrange_references(): pl.pallas_call(reference_body, grid_spec=pltpu.PrefetchScalarGridSpec(num...  7.64 us
    unnamed x49, local copies, waits for them, and re-layouts  5.64 us
    pallas_call x2, Pallas kernels, arrange_particles(): pl.pallas_call(functools.partial(particle_body, distances=distances, n_pr...  5.34 us
  transfers between devices with their start and end apart: 37, of which 13 were waited for; matrix products, arithmetic and copies ran while one was open for 0% of the time, Pallas kernels for 19%

profile of v12, /device:TPU:0, one launch (start us, length us, event | category | flops | bytes accessed | tf_op | source)
XLA Modules:
  0.0 184.7 jit_solution(4438770899499128)
XLA Ops:
  4.0 2.7 %arrange_particles.2 = (bf16[129,16,128]{2,1,0:T(8,128)(2,1)S(1)}, bf16[129,16,128]{2,1,0:T(8,128)(2,1)S(1)}) custom-call(s32[1]{0:T(128)} %bitcast.at_ref, bf16[16,128,512]{2,1,0:T(8,128)(2,1)S(1)} %copy-done, s32[16,20]{1,0:T(8,128)S(1)} %pad_add_fusion.meta_ref), custom_call_target="tpu_custom_call" | custom-call | flops 134217728 | bytes 2097152 | tf_op jit(solution)/shard_map/arrange_particles/pallas_call | solution.py:281
  6.7 4.1 %collective-permute-start = (bf16[129,16,128]{2,1,0:T(8,128)(2,1)S(1)}, bf16[129,16,128]{2,1,0:T(8,128)(2,1)S(1)}, u32[]{:S(2)}, u32[]{:S(2)}) collective-permute-start(bf16[129,16,128]{2,1,0:T(8,128)(2,1)S(1)} %get-tuple-element.45), channel_id=1, source_target_pairs={{0,2},{1,3},{2,0},{3,1},{4,6},{5,7},{6,4},{7,5},{8,10},{9,11},{10,... | collective-permute-start | bytes 1585160 | tf_op jit(solution)/shard_map/ppermute | solution.py:712
  13.8 2.7 %arrange_particles.3 = (bf16[129,16,128]{2,1,0:T(8,128)(2,1)S(1)}, bf16[129,16,128]{2,1,0:T(8,128)(2,1)S(1)}) custom-call(s32[1]{0:T(128)} %bitcast.at_ref, bf16[16,128,512]{2,1,0:T(8,128)(2,1)S(1)} %copy-done, s32[16,20]{1,0:T(8,128)S(1)} %pad_add_fusion.meta_ref), custom_call_target="tpu_custom_call" | custom-call | flops 134217728 | bytes 2097152 | tf_op jit(solution)/shard_map/arrange_particles/pallas_call | solution.py:281
  16.5 17.7 %collective-permute-done.refs_0_.refs_16_ = bf16[129,16,128]{2,1,0:T(8,128)(2,1)S(1)} collective-permute-done((bf16[129,16,128]{2,1,0:T(8,128)(2,1)S(1)}, bf16[129,16,128]{2,1,0:T(8,128)(2,1)S(1)}, u32[]{:S(2)}, u32[]{:S(2)}) %collective-permute-start) | collective-permute-done | bytes 528416 | tf_op jit(solution)/shard_map/ppermute | solution.py:712
  38.4 7.6 %arrange_references.1 = (bf16[128,64,128]{2,1,0:T(8,128)(2,1)}, f32[64,128]{1,0:T(8,128)}) custom-call(s32[1]{0:T(128)} %bitcast.at_ref, bf16[64,128,512]{2,1,0:T(8,128)(2,1)} %x_ref.4), custom_call_target="tpu_custom_call" | custom-call | flops 268435456 | bytes 4194304 | tf_op jit(solution)/shard_map/arrange_references/pallas_call | solution.py:322
  46.0 3.1 %collective-permute-done.3.refs_4_.refs_20_ = bf16[129,16,128]{2,1,0:T(8,128)(2,1)S(1)} collective-permute-done((bf16[129,16,128]{2,1,0:T(8,128)(2,1)S(1)}, bf16[129,16,128]{2,1,0:T(8,128)(2,1)S(1)}, u32[]{:S(2)}, u32[]{:S(2)}) %collective-permute-start.3) | collective-permute-done | bytes 528416 | tf_op jit(solution)/shard_map/ppermute | solution.py:712
  49.1 9.7 %collective-permute-done.7.refs_6_ = bf16[129,16,128]{2,1,0:T(8,128)(2,1)} collective-permute-done((bf16[129,16,128]{2,1,0:T(8,128)(2,1)S(1)}, bf16[129,16,128]{2,1,0:T(8,128)(2,1)}, u32[]{:S(2)}, u32[]{:S(2)}) %collective-permute-start.7) | collective-permute-done | bytes 528416 | tf_op jit(solution)/shard_map/ppermute | solution.py:712
  61.7 4.3 %collective-permute-start.22 = (bf16[129,16,128]{2,1,0:T(8,128)(2,1)S(1)}, bf16[129,16,128]{2,1,0:T(8,128)(2,1)S(1)}, u32[]{:S(2)}, u32[]{:S(2)}) collective-permute-start(bf16[129,16,128]{2,1,0:T(8,128)(2,1)S(1)} %get-tuple-element.67), channel_id=1, source_target_pairs={{0,3},{1,2},{2,1},{3,0},{4,7},{5,6},{6,5},{7,4},{8,11},{9,10},{10,... | collective-permute-start | bytes 1585160 | tf_op jit(solution)/shard_map/ppermute | solution.py:712
  69.0 6.1 %cross_coefficients.4 = (f32[144,128]{1,0:T(8,128)}, f32[8,128]{1,0:T(8,128)}) custom-call(s32[1]{0:T(128)} %bitcast.2.at_ref, bf16[129,16,128]{2,1,0:T(8,128)(2,1)} %copy-done.1, bf16[129,16,128]{2,1,0:T(8,128)(2,1)} %collective-permute-done.4.refs_1_, bf16[129,16,128]{2,1,0:T(8,128)(2,1)} %copy-done.3, ...), custom_call_target="tpu_custom_call" | custom-call | flops 541065216 | bytes 4227072 | tf_op jit(solution)/shard_map/cross_coefficients/pallas_call | solution.py:467
  75.6 2.8 %collective-permute-done.22.refs_0_.refs_24_ = bf16[129,16,128]{2,1,0:T(8,128)(2,1)S(1)} collective-permute-done((bf16[129,16,128]{2,1,0:T(8,128)(2,1)S(1)}, bf16[129,16,128]{2,1,0:T(8,128)(2,1)S(1)}, u32[]{:S(2)}, u32[]{:S(2)}) %collective-permute-start.22) | collective-permute-done | bytes 528416 | tf_op jit(solution)/shard_map/ppermute | solution.py:712
  78.4 6.7 %collective-permute-done.12.refs_2_.refs_10_ = bf16[129,16,128]{2,1,0:T(8,128)(2,1)S(1)} collective-permute-done((bf16[129,16,128]{2,1,0:T(8,128)(2,1)}, bf16[129,16,128]{2,1,0:T(8,128)(2,1)S(1)}, u32[]{:S(2)}, u32[]{:S(2)}) %collective-permute-start.12) | collective-permute-done | bytes 528416 | tf_op jit(solution)/shard_map/ppermute | solution.py:712
  89.3 6.1 %cross_coefficients.5 = (f32[144,128]{1,0:T(8,128)}, f32[8,128]{1,0:T(8,128)}) custom-call(s32[1]{0:T(128)} %bitcast.2.at_ref, bf16[129,16,128]{2,1,0:T(8,128)(2,1)} %copy-done.2, bf16[129,16,128]{2,1,0:T(8,128)(2,1)} %copy-done.9, bf16[129,16,128]{2,1,0:T(8,128)(2,1)} %collective-permute-done.10.refs_2_.refs_18_, bf16[129,16,128]{2,1,0:T(8,128)(2,1)} %copy-done.10, ...), custom_call_target="tpu_custom_call" | custom-call | flops 541065216 | bytes 4227072 | tf_op jit(solution)/shard_map/cross_coefficients/pallas_call | solution.py:467
  95.3 4.8 %collective-permute-done.16.refs_6_.refs_14_ = bf16[129,16,128]{2,1,0:T(8,128)(2,1)} collective-permute-done((bf16[129,16,128]{2,1,0:T(8,128)(2,1)S(1)}, bf16[129,16,128]{2,1,0:T(8,128)(2,1)}, u32[]{:S(2)}, u32[]{:S(2)}) %collective-permute-start.16) | collective-permute-done | bytes 528416 | tf_op jit(solution)/shard_map/ppermute | solution.py:712
  100.1 10.8 %collective-permute-done.27.refs_4_.refs_28_ = bf16[129,16,128]{2,1,0:T(8,128)(2,1)S(1)} collective-permute-done((bf16[129,16,128]{2,1,0:T(8,128)(2,1)S(1)}, bf16[129,16,128]{2,1,0:T(8,128)(2,1)S(1)}, u32[]{:S(2)}, u32[]{:S(2)}) %collective-permute-start.27) | collective-permute-done | bytes 528416 | tf_op jit(solution)/shard_map/ppermute | solution.py:712
  114.0 6.0 %cross_coefficients.6 = (f32[144,128]{1,0:T(8,128)}, f32[8,128]{1,0:T(8,128)}) custom-call(s32[1]{0:T(128)} %bitcast.2.at_ref, bf16[129,16,128]{2,1,0:T(8,128)(2,1)} %collective-permute-done.9.refs_0_.refs_8_, bf16[129,16,128]{2,1,0:T(8,128)(2,1)} %collective-permute-done.11.refs_1_.refs_9_, bf16[129,16,128]{2,1,0:T(8,128)(2,1)} %copy-done.7, ...), custom_call_target="tpu_custom_call" | custom-call | flops 541065216 | bytes 4227072 | tf_op jit(solution)/shard_map/cross_coefficients/pallas_call | solution.py:467
  120.0 5.3 %collective-permute-done.29.refs_6_.refs_30_ = bf16[129,16,128]{2,1,0:T(8,128)(2,1)S(1)} collective-permute-done((bf16[129,16,128]{2,1,0:T(8,128)(2,1)S(1)}, bf16[129,16,128]{2,1,0:T(8,128)(2,1)S(1)}, u32[]{:S(2)}, u32[]{:S(2)}) %collective-permute-start.29) | collective-permute-done | bytes 528416 | tf_op jit(solution)/shard_map/ppermute | solution.py:712
  125.3 3.3 %collective-permute-start.32 = (f32[144,128]{1,0:T(8,128)S(1)}, f32[144,128]{1,0:T(8,128)S(1)}, u32[]{:S(2)}, u32[]{:S(2)}) collective-permute-start(f32[144,128]{1,0:T(8,128)S(1)} %copy-done.23), channel_id=1, source_target_pairs={{0,2},{1,3},{2,0},{3,1},{4,6},{5,7},{6,4},{7,5},{8,10},{9,11},{10,... | collective-permute-start | bytes 221192 | tf_op jit(solution)/shard_map/ppermute | solution.py:712
  131.1 6.0 %cross_coefficients.7 = (f32[144,128]{1,0:T(8,128)}, f32[8,128]{1,0:T(8,128)}) custom-call(s32[1]{0:T(128)} %bitcast.2.at_ref, bf16[129,16,128]{2,1,0:T(8,128)(2,1)} %copy-done.6, bf16[129,16,128]{2,1,0:T(8,128)(2,1)} %collective-permute-done.24.refs_1_.refs_25_, bf16[129,16,128]{2,1,0:T(8,128)(2,1)} %collective-permute-done.25.refs_2_.refs_26_, ...), custom_call_target="tpu_custom_call" | custom-call | flops 541065216 | bytes 4227072 | tf_op jit(solution)/shard_map/cross_coefficients/pallas_call | solution.py:467
  138.5 5.1 %collective-permute-done.33.refs_3_ = f32[144,128]{1,0:T(8,128)S(1)} collective-permute-done((f32[144,128]{1,0:T(8,128)}, f32[144,128]{1,0:T(8,128)S(1)}, u32[]{:S(2)}, u32[]{:S(2)}) %collective-permute-start.33) | collective-permute-done | bytes 73760 | tf_op jit(solution)/shard_map/ppermute | solution.py:712
  146.2 10.7 %all-gather.1.stat_ref = f32[8,2,128]{2,1,0:T(2,128)} all-gather(f32[1,2,128]{2,1,0:T(2,128)} %bitcast.9), channel_id=2, replica_groups=mesh['cls'=8,'prt'=4] {'cls'}, dimensions={0}, use_global_device_ids=true | all-gather | bytes 9216 | tf_op jit(solution)/shard_map/all_gather | solution.py:801
  160.4 3.1 %collective-permute-start.34 = (f32[144,128]{1,0:T(8,128)}, f32[144,128]{1,0:T(8,128)S(1)}, u32[]{:S(2)}, u32[]{:S(2)}) collective-permute-start(f32[144,128]{1,0:T(8,128)} %get-tuple-element.78.refs_32_), channel_id=1, source_target_pairs={{0,1},{1,0},{2,3},{3,2},{4,5},{5,4},{6,7},{7,6},{8,9},{9,8},{10,11... | collective-permute-start | bytes 221192 | tf_op jit(solution)/shard_map/ppermute | solution.py:712
  163.4 2.8 %collective-permute-done.36.refs_35_ = f32[144,128]{1,0:T(8,128)S(1)} collective-permute-done((f32[144,128]{1,0:T(8,128)}, f32[144,128]{1,0:T(8,128)S(1)}, u32[]{:S(2)}, u32[]{:S(2)}) %collective-permute-start.36) | collective-permute-done | bytes 73760 | tf_op jit(solution)/shard_map/ppermute | solution.py:712
  166.2 2.5 %collective-permute-done.35.refs_34_ = f32[144,128]{1,0:T(8,128)S(1)} collective-permute-done((f32[144,128]{1,0:T(8,128)}, f32[144,128]{1,0:T(8,128)S(1)}, u32[]{:S(2)}, u32[]{:S(2)}) %collective-permute-start.35) | collective-permute-done | bytes 73760 | tf_op jit(solution)/shard_map/ppermute | solution.py:712
  169.4 15.2 %sums.1 = (f32[64,32,512]{2,1,0:T(8,128)}, f32[1,64]{1,0:T(1,128)}) custom-call(bf16[129,16,128]{2,1,0:T(8,128)(2,1)} %copy-done.1, bf16[129,16,128]{2,1,0:T(8,128)(2,1)} %collective-permute-done.4.refs_1_, bf16[129,16,128]{2,1,0:T(8,128)(2,1)} %copy-done.3, bf16[129,16,128]{2,1,0:T(8,128)(2,1)} %collective-permute-done.5.refs_3_, ...), custom_call_target="tpu_custom_call" | custom-call | flops 2164260864 | bytes 21102592 | tf_op jit(solution)/shard_map/sums/pallas_call | solution.py:678
  (113 shorter events, 34.8 us)
Async XLA Ops:
  6.7 27.4 %collective-permute-start = (bf16[129,16,128]{2,1,0:T(8,128)(2,1)S(1)}, bf16[129,16,128]{2,1,0:T(8,128)(2,1)S(1)}, u32[]{:S(2)}, u32[]{:S(2)}) collective-permute-start(bf16[129,16,128]{2,1,0:T(8,128)(2,1)S(1)} %get-tuple-element.45), channel_id=1, source_target_pairs={{0,2},{1,3},{2,0},{3,1},{4,6},{5,7},{6,4},{7,5},{8,10},{9,11},{10,... | collective-permute-start | bytes 1585160 | tf_op jit(solution)/shard_map/ppermute | solution.py:712
  10.8 24.9 %collective-permute-start.1 = (bf16[129,16,128]{2,1,0:T(8,128)(2,1)S(1)}, bf16[129,16,128]{2,1,0:T(8,128)(2,1)S(1)}, u32[]{:S(2)}, u32[]{:S(2)}) collective-permute-start(bf16[129,16,128]{2,1,0:T(8,128)(2,1)S(1)} %get-tuple-element.51.refs_0_), channel_id=1, source_target_pairs={{0,8},{4,12},{8,0},{12,4},{16,24},{20,28},{24,16},{28,20},{1,9},{5... | collective-permute-start | bytes 1585160 | tf_op jit(solution)/shard_map/ppermute | solution.py:712
  12.3 26.1 %collective-permute-start.2 = (bf16[129,16,128]{2,1,0:T(8,128)(2,1)S(1)}, bf16[129,16,128]{2,1,0:T(8,128)(2,1)S(1)}, u32[]{:S(2)}, u32[]{:S(2)}) collective-permute-start(bf16[129,16,128]{2,1,0:T(8,128)(2,1)S(1)} %get-tuple-element.51.refs_0_), channel_id=1, source_target_pairs={{0,16},{4,20},{8,24},{12,28},{16,0},{20,4},{24,8},{28,12},{1,17},{... | collective-permute-start | bytes 1585160 | tf_op jit(solution)/shard_map/ppermute | solution.py:712
  34.1 14.9 %collective-permute-start.3 = (bf16[129,16,128]{2,1,0:T(8,128)(2,1)S(1)}, bf16[129,16,128]{2,1,0:T(8,128)(2,1)S(1)}, u32[]{:S(2)}, u32[]{:S(2)}) collective-permute-start(bf16[129,16,128]{2,1,0:T(8,128)(2,1)S(1)} %collective-permute-done.refs_0_.refs_16_), channel_id=1, source_target_pairs={{0,16},{4,20},{8,24},{12,28},{16,0},{20,4},{24,8},{28,12},{1,17},{... | collective-permute-start | bytes 1585160 | tf_op jit(solution)/shard_map/ppermute | solution.py:712
  35.7 23.1 %collective-permute-start.7 = (bf16[129,16,128]{2,1,0:T(8,128)(2,1)S(1)}, bf16[129,16,128]{2,1,0:T(8,128)(2,1)}, u32[]{:S(2)}, u32[]{:S(2)}) collective-permute-start(bf16[129,16,128]{2,1,0:T(8,128)(2,1)S(1)} %collective-permute-done.1.refs_2_), channel_id=1, source_target_pairs={{0,16},{4,20},{8,24},{12,28},{16,0},{20,4},{24,8},{28,12},{1,17},{... | collective-permute-start | bytes 1585160 | tf_op jit(solution)/shard_map/ppermute | solution.py:712
  36.2 23.2 %collective-permute-start.9 = (bf16[129,16,128]{2,1,0:T(8,128)(2,1)S(1)}, bf16[129,16,128]{2,1,0:T(8,128)(2,1)}, u32[]{:S(2)}, u32[]{:S(2)}) collective-permute-start(bf16[129,16,128]{2,1,0:T(8,128)(2,1)S(1)} %get-tuple-element.55), channel_id=1, source_target_pairs={{0,1},{1,0},{2,3},{3,2},{4,5},{5,4},{6,7},{7,6},{8,9},{9,8},{10,11... | collective-permute-start | bytes 1585160 | tf_op jit(solution)/shard_map/ppermute | solution.py:712
  36.9 22.9 %collective-permute-start.10 = (bf16[129,16,128]{2,1,0:T(8,128)(2,1)S(1)}, bf16[129,16,128]{2,1,0:T(8,128)(2,1)}, u32[]{:S(2)}, u32[]{:S(2)}) collective-permute-start(bf16[129,16,128]{2,1,0:T(8,128)(2,1)S(1)} %collective-permute-done.refs_0_.refs_16_), channel_id=1, source_target_pairs={{0,8},{4,12},{8,0},{12,4},{16,24},{20,28},{24,16},{28,20},{1,9},{5... | collective-permute-start | bytes 1585160 | tf_op jit(solution)/shard_map/ppermute | solution.py:712
  59.8 15.3 %collective-permute-start.20 = (bf16[129,16,128]{2,1,0:T(8,128)(2,1)S(1)}, bf16[129,16,128]{2,1,0:T(8,128)(2,1)}, u32[]{:S(2)}, u32[]{:S(2)}) collective-permute-start(bf16[129,16,128]{2,1,0:T(8,128)(2,1)S(1)} %collective-permute-done.3.refs_4_.refs_20_), channel_id=1, source_target_pairs={{0,8},{4,12},{8,0},{12,4},{16,24},{20,28},{24,16},{28,20},{1,9},{5... | collective-permute-start | bytes 1585160 | tf_op jit(solution)/shard_map/ppermute | solution.py:712
  61.7 16.7 %collective-permute-start.22 = (bf16[129,16,128]{2,1,0:T(8,128)(2,1)S(1)}, bf16[129,16,128]{2,1,0:T(8,128)(2,1)S(1)}, u32[]{:S(2)}, u32[]{:S(2)}) collective-permute-start(bf16[129,16,128]{2,1,0:T(8,128)(2,1)S(1)} %get-tuple-element.67), channel_id=1, source_target_pairs={{0,3},{1,2},{2,1},{3,0},{4,7},{5,6},{6,5},{7,4},{8,11},{9,10},{10,... | collective-permute-start | bytes 1585160 | tf_op jit(solution)/shard_map/ppermute | solution.py:712
  66.0 19.1 %collective-permute-start.12 = (bf16[129,16,128]{2,1,0:T(8,128)(2,1)}, bf16[129,16,128]{2,1,0:T(8,128)(2,1)S(1)}, u32[]{:S(2)}, u32[]{:S(2)}) collective-permute-start(bf16[129,16,128]{2,1,0:T(8,128)(2,1)} %collective-permute-done.9.refs_0_.refs_8_), channel_id=1, source_target_pairs={{0,8},{4,12},{8,0},{12,4},{16,24},{20,28},{24,16},{28,20},{1,9},{5... | collective-permute-start | bytes 1585160 | tf_op jit(solution)/shard_map/ppermute | solution.py:712
  67.5 17.6 %collective-permute-start.14 = (bf16[129,16,128]{2,1,0:T(8,128)(2,1)}, bf16[129,16,128]{2,1,0:T(8,128)(2,1)S(1)}, u32[]{:S(2)}, u32[]{:S(2)}) collective-permute-start(bf16[129,16,128]{2,1,0:T(8,128)(2,1)} %collective-permute-done.9.refs_0_.refs_8_), channel_id=1, source_target_pairs={{0,16},{4,20},{8,24},{12,28},{16,0},{20,4},{24,8},{28,12},{1,17},{... | collective-permute-start | bytes 1585160 | tf_op jit(solution)/shard_map/ppermute | solution.py:712
  75.1 11.4 %collective-permute-start.17 = (bf16[129,16,128]{2,1,0:T(8,128)(2,1)S(1)}, bf16[129,16,128]{2,1,0:T(8,128)(2,1)S(1)}, u32[]{:S(2)}, u32[]{:S(2)}) collective-permute-start(bf16[129,16,128]{2,1,0:T(8,128)(2,1)S(1)} %collective-permute-done.refs_0_.refs_16_), channel_id=1, source_target_pairs={{0,4},{4,0},{8,12},{12,8},{16,20},{20,16},{24,28},{28,24},{1,5},{5... | collective-permute-start | bytes 1585160 | tf_op jit(solution)/shard_map/ppermute | solution.py:712
  75.1 12.1 %collective-permute-start.18 = (bf16[129,16,128]{2,1,0:T(8,128)(2,1)}, bf16[129,16,128]{2,1,0:T(8,128)(2,1)S(1)}, u32[]{:S(2)}, u32[]{:S(2)}) collective-permute-start(bf16[129,16,128]{2,1,0:T(8,128)(2,1)} %collective-permute-done.10.refs_2_.refs_18_), channel_id=1, source_target_pairs={{0,4},{4,0},{8,12},{12,8},{16,20},{20,16},{24,28},{28,24},{1,5},{5... | collective-permute-start | bytes 1585160 | tf_op jit(solution)/shard_map/ppermute | solution.py:712
  85.1 15.0 %collective-permute-start.16 = (bf16[129,16,128]{2,1,0:T(8,128)(2,1)S(1)}, bf16[129,16,128]{2,1,0:T(8,128)(2,1)}, u32[]{:S(2)}, u32[]{:S(2)}) collective-permute-start(bf16[129,16,128]{2,1,0:T(8,128)(2,1)S(1)} %collective-permute-done.12.refs_2_.refs_10_), channel_id=1, source_target_pairs={{0,16},{4,20},{8,24},{12,28},{16,0},{20,4},{24,8},{28,12},{1,17},{... | collective-permute-start | bytes 1585160 | tf_op jit(solution)/shard_map/ppermute | solution.py:712
  86.4 24.4 %collective-permute-start.27 = (bf16[129,16,128]{2,1,0:T(8,128)(2,1)S(1)}, bf16[129,16,128]{2,1,0:T(8,128)(2,1)S(1)}, u32[]{:S(2)}, u32[]{:S(2)}) collective-permute-start(bf16[129,16,128]{2,1,0:T(8,128)(2,1)S(1)} %collective-permute-done.22.refs_0_.refs_24_), channel_id=1, source_target_pairs={{0,16},{4,20},{8,24},{12,28},{16,0},{20,4},{24,8},{28,12},{1,17},{... | collective-permute-start | bytes 1585160 | tf_op jit(solution)/shard_map/ppermute | solution.py:712
  87.2 23.7 %collective-permute-start.25 = (bf16[129,16,128]{2,1,0:T(8,128)(2,1)S(1)}, bf16[129,16,128]{2,1,0:T(8,128)(2,1)}, u32[]{:S(2)}, u32[]{:S(2)}) collective-permute-start(bf16[129,16,128]{2,1,0:T(8,128)(2,1)S(1)} %collective-permute-done.22.refs_0_.refs_24_), channel_id=1, source_target_pairs={{0,8},{4,12},{8,0},{12,4},{16,24},{20,28},{24,16},{28,20},{1,9},{5... | collective-permute-start | bytes 1585160 | tf_op jit(solution)/shard_map/ppermute | solution.py:712
  88.5 24.2 %collective-permute-start.13 = (bf16[129,16,128]{2,1,0:T(8,128)(2,1)S(1)}, bf16[129,16,128]{2,1,0:T(8,128)(2,1)}, u32[]{:S(2)}, u32[]{:S(2)}) collective-permute-start(bf16[129,16,128]{2,1,0:T(8,128)(2,1)S(1)} %collective-permute-done.12.refs_2_.refs_10_), channel_id=1, source_target_pairs={{0,4},{4,0},{8,12},{12,8},{16,20},{20,16},{24,28},{28,24},{1,5},{5... | collective-permute-start | bytes 1585160 | tf_op jit(solution)/shard_map/ppermute | solution.py:712
  88.6 23.6 %collective-permute-start.11 = (bf16[129,16,128]{2,1,0:T(8,128)(2,1)}, bf16[129,16,128]{2,1,0:T(8,128)(2,1)}, u32[]{:S(2)}, u32[]{:S(2)}) collective-permute-start(bf16[129,16,128]{2,1,0:T(8,128)(2,1)} %collective-permute-done.9.refs_0_.refs_8_), channel_id=1, source_target_pairs={{0,4},{4,0},{8,12},{12,8},{16,20},{20,16},{24,28},{28,24},{1,5},{5... | collective-permute-start | bytes 1585160 | tf_op jit(solution)/shard_map/ppermute | solution.py:712
  100.1 12.3 %collective-permute-start.15 = (bf16[129,16,128]{2,1,0:T(8,128)(2,1)S(1)}, bf16[129,16,128]{2,1,0:T(8,128)(2,1)S(1)}, u32[]{:S(2)}, u32[]{:S(2)}) collective-permute-start(bf16[129,16,128]{2,1,0:T(8,128)(2,1)S(1)} %collective-permute-done.14.refs_4_.refs_12_), channel_id=1, source_target_pairs={{0,4},{4,0},{8,12},{12,8},{16,20},{20,16},{24,28},{28,24},{1,5},{5... | collective-permute-start | bytes 1585160 | tf_op jit(solution)/shard_map/ppermute | solution.py:712
  110.9 14.4 %collective-permute-start.29 = (bf16[129,16,128]{2,1,0:T(8,128)(2,1)S(1)}, bf16[129,16,128]{2,1,0:T(8,128)(2,1)S(1)}, u32[]{:S(2)}, u32[]{:S(2)}) collective-permute-start(bf16[129,16,128]{2,1,0:T(8,128)(2,1)S(1)} %collective-permute-done.27.refs_4_.refs_28_), channel_id=1, source_target_pairs={{0,8},{4,12},{8,0},{12,4},{16,24},{20,28},{24,16},{28,20},{1,9},{5... | collective-permute-start | bytes 1585160 | tf_op jit(solution)/shard_map/ppermute | solution.py:712
  112.2 16.4 %collective-permute-start.24 = (bf16[129,16,128]{2,1,0:T(8,128)(2,1)S(1)}, bf16[129,16,128]{2,1,0:T(8,128)(2,1)}, u32[]{:S(2)}, u32[]{:S(2)}) collective-permute-start(bf16[129,16,128]{2,1,0:T(8,128)(2,1)S(1)} %collective-permute-done.22.refs_0_.refs_24_), channel_id=1, source_target_pairs={{0,4},{4,0},{8,12},{12,8},{16,20},{20,16},{24,28},{28,24},{1,5},{5... | collective-permute-start | bytes 1585160 | tf_op jit(solution)/shard_map/ppermute | solution.py:712
  112.4 17.9 %collective-permute-start.28 = (bf16[129,16,128]{2,1,0:T(8,128)(2,1)S(1)}, bf16[129,16,128]{2,1,0:T(8,128)(2,1)}, u32[]{:S(2)}, u32[]{:S(2)}) collective-permute-start(bf16[129,16,128]{2,1,0:T(8,128)(2,1)S(1)} %collective-permute-done.27.refs_4_.refs_28_), channel_id=1, source_target_pairs={{0,4},{4,0},{8,12},{12,8},{16,20},{20,16},{24,28},{28,24},{1,5},{5... | collective-permute-start | bytes 1585160 | tf_op jit(solution)/shard_map/ppermute | solution.py:712
  112.7 17.5 %collective-permute-start.26 = (bf16[129,16,128]{2,1,0:T(8,128)(2,1)}, bf16[129,16,128]{2,1,0:T(8,128)(2,1)}, u32[]{:S(2)}, u32[]{:S(2)}) collective-permute-start(bf16[129,16,128]{2,1,0:T(8,128)(2,1)} %collective-permute-done.25.refs_2_.refs_26_), channel_id=1, source_target_pairs={{0,4},{4,0},{8,12},{12,8},{16,20},{20,16},{24,28},{28,24},{1,5},{5... | collective-permute-start | bytes 1585160 | tf_op jit(solution)/shard_map/ppermute | solution.py:712
  125.3 13.1 %collective-permute-start.32 = (f32[144,128]{1,0:T(8,128)S(1)}, f32[144,128]{1,0:T(8,128)S(1)}, u32[]{:S(2)}, u32[]{:S(2)}) collective-permute-start(f32[144,128]{1,0:T(8,128)S(1)} %copy-done.23), channel_id=1, source_target_pairs={{0,2},{1,3},{2,0},{3,1},{4,6},{5,7},{6,4},{7,5},{8,10},{9,11},{10,... | collective-permute-start | bytes 221192 | tf_op jit(solution)/shard_map/ppermute | solution.py:712
  (37 other events, 441.3 us)

commit v13 on v11

--- a/solution.py
+++ b/solution.py
@@ -383,16 +383,16 @@
     return [rows == cand[q : q + 1] for q in range(CAND_OWN)]
 
 
-def residue_weights(q_ref, g, special):
+def residue_weights(q_ref, g):
     imag, odd = lane_signs()
     sign = jnp.where(imag == odd, -1.0, 1.0)
     first, second = [], []
     for i in range(TURNS):
         q = q_ref[g * TURNS + i].astype(jnp.float32)
         turned = pltpu.roll(q, LANES // 2, 1) * sign
-        if special:
-            first.append(jnp.where((g == 0) & odd, 0.0, q))
-            second.append(jnp.where(g == 0, jnp.where(odd, q, 0.0), turned))
+        if g == 0:
+            first.append(jnp.where(odd, 0.0, q))
+            second.append(jnp.where(odd, q, 0.0))
         else:
             first.append(q)
             second.append(turned)
@@ -413,8 +413,8 @@
 
 
 def cross_body(at_ref, *refs):
-    blocks = refs[:-7]
-    q_ref, norm_ref, coef_ref, cand_ref, held, acc, sems = refs[-7:]
+    blocks = refs[:-6]
+    q_ref, norm_ref, coef_ref, cand_ref, held, sems = refs[-6:]
     groups = q_ref.shape[1]
     imag, odd = lane_signs()
     copies = fetch(blocks, held, sems)
@@ -440,27 +440,21 @@
         if i == 0:
             b = jnp.zeros_like(b)
         w = jnp.concatenate([a, b], 0).astype(jnp.bfloat16)
-        acc[...] += nt_dot(w, lanes_of(held, BODY + i // 2, 1))
-        if i == 0:
-            acc[:groups, :] -= 0.5 * jnp.sum(norm_ref[...], axis=1, keepdims=True)
+        return nt_dot(w, lanes_of(held, BODY + i // 2, 1))
 
     for r in range(1, len(RANGES)):
         for copy in copies[r]:
             copy.wait()
 
-        def one(u, carry):
-            g = (r - 1) * RANGE + u
-            acc[...] = nt_dot(residue_weights(q_ref, g, r == 1), lanes_of(held, g * TURNS, TURNS))
-            if r == 1:
-                for i in range(TAIL):
-                    pl.when(g == i)(functools.partial(tail, i))
+        for g in range((r - 1) * RANGE, r * RANGE):
+            acc = nt_dot(residue_weights(q_ref, g), lanes_of(held, g * TURNS, TURNS))
+            if g < TAIL:
+                acc += tail(g)
+            if g == 0:
+                half_norm = 0.5 * jnp.sum(norm_ref[...], axis=1, keepdims=True)
+                acc = jnp.concatenate([acc[:groups] - half_norm, acc[groups:]], 0)
             block = 2 * CAND_OWN
-            coef_ref[pl.ds(pl.multiple_of(g * block, block), block), :] = chosen_rows(
-                acc[...], cand_ref[...]
-            )
-            return carry
-
-        lax.fori_loop(0, RANGE, one, 0)
+            coef_ref[g * block : (g + 1) * block, :] = chosen_rows(acc, cand_ref[...])
 
 
 def cross_coefficients(blocks, arranged, norms, cls):
@@ -481,7 +475,6 @@
         ],
         scratch_shapes=[
             pltpu.VMEM((number, *blocks[0].shape), jnp.bfloat16),
-            pltpu.VMEM((2 * groups, total), jnp.float32),
             pltpu.SemaphoreType.DMA((len(RANGES), number)),
         ],
         compiler_params=pltpu.CompilerParams(vmem_limit_bytes=60 << 20),
@@ -621,11 +614,10 @@
             for copy in copies[r]:
                 copy.wait()
 
-            def one(u, carry):
-                g = (r - 1) * RANGE + u
-                hot = hot_masks(cand[...], groups)
-                block = 2 * CAND_OWN
-                mine = mix[pl.ds(pl.multiple_of(g * block, block), block), :]
+            hot = hot_masks(cand[...], groups)
+            block = 2 * CAND_OWN
+            for g in range((r - 1) * RANGE, r * RANGE):
+                mine = mix[g * block : (g + 1) * block, :]
                 halves = []
                 for ab in range(2):
                     dense = jnp.zeros((groups, total), jnp.float32)
@@ -640,17 +632,14 @@
                 for t in range(TURNS):
                     g1 = made[:groups, t * LANES : (t + 1) * LANES]
                     g2 = made[groups:, t * LANES : (t + 1) * LANES]
-                    value = g1 + sign * pltpu.roll(g2, LANES // 2, 1)
-                    if r == 1:
-                        value = jnp.where(g == 0, jnp.where(odd, g2, g1), value)
-                    start = pl.multiple_of((g * TURNS + t) * groups, groups)
-                    planes[pl.ds(start, groups), :] = value
-                if r == 1:
-                    for t in range(TAIL):
-                        pl.when(g == t)(functools.partial(tail, t, weights))
-                return carry
-
-            lax.fori_loop(0, RANGE, one, 0)
+                    if g == 0:
+                        value = jnp.where(odd, g2, g1)
+                    else:
+                        value = g1 + sign * pltpu.roll(g2, LANES // 2, 1)
+                    start = (g * TURNS + t) * groups
+                    planes[start : start + groups, :] = value
+                if g < TAIL:
+                    tail(g, weights)
 
     @pl.when(step > 0)
     def _():
@@ -817,7 +806,7 @@
     groups = references.shape[0]
     cap = max(2, 2 * count * OWN_TOP // n_cls)
     powers = n_cls & (n_cls - 1) == 0 and n_prt & (n_prt - 1) == 0
-    fits = 4 * cycles == LANES * n_prt and n_cls * CAND_OWN <= LANES and groups % 16 == 0 and n_cls >= 4
+    fits = 4 * cycles == LANES * n_prt and n_cls * CAND_OWN <= LANES and groups % 16 == 0 and n_cls >= 4 and n_prt >= 4
     fits = fits and powers and n_cls * count == LANES
     plan = gather_device if cap >= count and fits else dispatch_device
     return plan(particles, references, owner_groups, class_order)

time: 182 us -> 174 us (0.956)
  Pallas kernels: 76.8 us -> 56.5 us
  waiting for transfers between devices: 46.9 us -> 59.8 us
    pallas_call x4, Pallas kernels: 40 us -> 24.2 us  [cross_coefficients(): pl.pallas_call(cross_body, in_specs=[pl.BlockSpec(memory_space=pltpu.SMEM...]
    ppermute x37, waiting for transfers between devices: 46.9 us -> 59.8 us  [hop(): return lax.ppermute(value, axis, [(i, i ^ distance) for i in range(size)])]
    pallas_call x1, Pallas kernels: 19.7 us -> 15.2 us  [sums(): pl.pallas_call(functools.partial(sums_body, number=number, pieces=len(mix...]
  transfers between devices with their start and end apart: 37 -> 37, of which waited for: 10 -> 12; matrix products, arithmetic and copies ran while one was open for 0% -> 0% of each run, Pallas kernels for 28% -> 20%
where the time goes in v13:
time: 174 us; the launch traced here: 173 us
  waiting for transfers between devices  59.8 us (34%)
  Pallas kernels  56.5 us (32%)
  starting transfers between devices  37.8 us (22%)
  blocking collectives  9.93 us (6%)
  local copies, waits for them, and re-layouts  8.38 us (5%)
    ppermute x37, waiting for transfers between devices, hop(): return lax.ppermute(value, axis, [(i, i ^ distance) for i in range(size)])  59.8 us
    ppermute x37, starting transfers between devices, hop(): return lax.ppermute(value, axis, [(i, i ^ distance) for i in range(size)])  37.8 us
    pallas_call x4, Pallas kernels, cross_coefficients(): pl.pallas_call(cross_body, in_specs=[pl.BlockSpec(memory_space=pltpu.SMEM...  24.2 us
    pallas_call x1, Pallas kernels, sums(): pl.pallas_call(functools.partial(sums_body, number=number, pieces=len(mix...  15.2 us
    all_gather x1, blocking collectives, gather_device(): lax.all_gather(stat.reshape(1, *stat.shape), 'cls', axis=0, tiled=True)  9.93 us
    pallas_call x1, Pallas kernels, arrange_references(): pl.pallas_call(reference_body, grid_spec=pltpu.PrefetchScalarGridSpec(num...  7.66 us
    unnamed x51, local copies, waits for them, and re-layouts  7.45 us
    pallas_call x2, Pallas kernels, arrange_particles(): pl.pallas_call(functools.partial(particle_body, distances=distances, n_pr...  5.35 us
  transfers between devices with their start and end apart: 37, of which 12 were waited for; matrix products, arithmetic and copies ran while one was open for 0% of the time, Pallas kernels for 20%

profile of v13, /device:TPU:0, one launch (start us, length us, event | category | flops | bytes accessed | tf_op | source)
XLA Modules:
  0.0 173.5 jit_solution(16336514431221226192)
XLA Ops:
  4.0 2.7 %arrange_particles.2 = (bf16[129,16,128]{2,1,0:T(8,128)(2,1)S(1)}, bf16[129,16,128]{2,1,0:T(8,128)(2,1)S(1)}) custom-call(s32[1]{0:T(128)} %bitcast.at_ref, bf16[16,128,512]{2,1,0:T(8,128)(2,1)S(1)} %copy-done, s32[16,20]{1,0:T(8,128)S(1)} %pad_add_fusion.meta_ref), custom_call_target="tpu_custom_call" | custom-call | flops 134217728 | bytes 2097152 | tf_op jit(solution)/shard_map/arrange_particles/pallas_call | solution.py:281
  6.7 3.1 %collective-permute-start = (bf16[129,16,128]{2,1,0:T(8,128)(2,1)S(1)}, bf16[129,16,128]{2,1,0:T(8,128)(2,1)S(1)}, u32[]{:S(2)}, u32[]{:S(2)}) collective-permute-start(bf16[129,16,128]{2,1,0:T(8,128)(2,1)S(1)} %get-tuple-element.45), channel_id=1, source_target_pairs={{0,1},{1,0},{2,3},{3,2},{4,5},{5,4},{6,7},{7,6},{8,9},{9,8},{10,11... | collective-permute-start | bytes 1585160 | tf_op jit(solution)/shard_map/ppermute | solution.py:712
  12.8 2.7 %arrange_particles.3 = (bf16[129,16,128]{2,1,0:T(8,128)(2,1)S(1)}, bf16[129,16,128]{2,1,0:T(8,128)(2,1)S(1)}) custom-call(s32[1]{0:T(128)} %bitcast.at_ref, bf16[16,128,512]{2,1,0:T(8,128)(2,1)S(1)} %copy-done, s32[16,20]{1,0:T(8,128)S(1)} %pad_add_fusion.meta_ref), custom_call_target="tpu_custom_call" | custom-call | flops 134217728 | bytes 2097152 | tf_op jit(solution)/shard_map/arrange_particles/pallas_call | solution.py:281
  15.5 6.3 %collective-permute-done.refs_0_.refs_8_ = bf16[129,16,128]{2,1,0:T(8,128)(2,1)S(1)} collective-permute-done((bf16[129,16,128]{2,1,0:T(8,128)(2,1)S(1)}, bf16[129,16,128]{2,1,0:T(8,128)(2,1)S(1)}, u32[]{:S(2)}, u32[]{:S(2)}) %collective-permute-start) | collective-permute-done | bytes 528416 | tf_op jit(solution)/shard_map/ppermute | solution.py:712
  25.5 2.6 %collective-permute-start.15 = (bf16[129,16,128]{2,1,0:T(8,128)(2,1)S(1)}, bf16[129,16,128]{2,1,0:T(8,128)(2,1)}, u32[]{:S(2)}, u32[]{:S(2)}) collective-permute-start(bf16[129,16,128]{2,1,0:T(8,128)(2,1)S(1)} %get-tuple-element.62), channel_id=1, source_target_pairs={{0,2},{1,3},{2,0},{3,1},{4,6},{5,7},{6,4},{7,5},{8,10},{9,11},{10,... | collective-permute-start | bytes 1585160 | tf_op jit(solution)/shard_map/ppermute | solution.py:712
  28.1 7.7 %arrange_references.1 = (bf16[128,64,128]{2,1,0:T(8,128)(2,1)}, f32[64,128]{1,0:T(8,128)}) custom-call(s32[1]{0:T(128)} %bitcast.at_ref, bf16[64,128,512]{2,1,0:T(8,128)(2,1)} %x_ref.4), custom_call_target="tpu_custom_call" | custom-call | flops 268435456 | bytes 4194304 | tf_op jit(solution)/shard_map/arrange_references/pallas_call | solution.py:322
  35.8 2.8 %collective-permute-done.7.refs_6_ = bf16[129,16,128]{2,1,0:T(8,128)(2,1)} collective-permute-done((bf16[129,16,128]{2,1,0:T(8,128)(2,1)S(1)}, bf16[129,16,128]{2,1,0:T(8,128)(2,1)}, u32[]{:S(2)}, u32[]{:S(2)}) %collective-permute-start.7) | collective-permute-done | bytes 528416 | tf_op jit(solution)/shard_map/ppermute | solution.py:712
  39.1 8.4 %collective-permute-done.9.refs_2_.refs_10_ = bf16[129,16,128]{2,1,0:T(8,128)(2,1)} collective-permute-done((bf16[129,16,128]{2,1,0:T(8,128)(2,1)S(1)}, bf16[129,16,128]{2,1,0:T(8,128)(2,1)}, u32[]{:S(2)}, u32[]{:S(2)}) %collective-permute-start.9) | collective-permute-done | bytes 528416 | tf_op jit(solution)/shard_map/ppermute | solution.py:712
  53.4 3.5 %collective-permute-start.22 = (bf16[129,16,128]{2,1,0:T(8,128)(2,1)S(1)}, bf16[129,16,128]{2,1,0:T(8,128)(2,1)S(1)}, u32[]{:S(2)}, u32[]{:S(2)}) collective-permute-start(bf16[129,16,128]{2,1,0:T(8,128)(2,1)S(1)} %get-tuple-element.67), channel_id=1, source_target_pairs={{0,3},{1,2},{2,1},{3,0},{4,7},{5,6},{6,5},{7,4},{8,11},{9,10},{10,... | collective-permute-start | bytes 1585160 | tf_op jit(solution)/shard_map/ppermute | solution.py:712
  56.9 6.0 %cross_coefficients.4 = (f32[144,128]{1,0:T(8,128)}, f32[8,128]{1,0:T(8,128)}) custom-call(s32[1]{0:T(128)} %bitcast.2.at_ref, bf16[129,16,128]{2,1,0:T(8,128)(2,1)} %copy-done.1, bf16[129,16,128]{2,1,0:T(8,128)(2,1)} %collective-permute-done.4.refs_1_, bf16[129,16,128]{2,1,0:T(8,128)(2,1)} %copy-done.4, ...), custom_call_target="tpu_custom_call" | custom-call | flops 541065216 | bytes 4227072 | tf_op jit(solution)/shard_map/cross_coefficients/pallas_call | solution.py:467
  65.1 9.4 %collective-permute-done.19.refs_4_.refs_20_ = bf16[129,16,128]{2,1,0:T(8,128)(2,1)S(1)} collective-permute-done((bf16[129,16,128]{2,1,0:T(8,128)(2,1)}, bf16[129,16,128]{2,1,0:T(8,128)(2,1)S(1)}, u32[]{:S(2)}, u32[]{:S(2)}) %collective-permute-start.19) | collective-permute-done | bytes 528416 | tf_op jit(solution)/shard_map/ppermute | solution.py:712
  80.5 6.1 %cross_coefficients.5 = (f32[144,128]{1,0:T(8,128)}, f32[8,128]{1,0:T(8,128)}) custom-call(s32[1]{0:T(128)} %bitcast.2.at_ref, bf16[129,16,128]{2,1,0:T(8,128)(2,1)} %copy-done.2, bf16[129,16,128]{2,1,0:T(8,128)(2,1)} %copy-done.9, bf16[129,16,128]{2,1,0:T(8,128)(2,1)} %collective-permute-done.9.refs_2_.refs_10_, bf16[129,16,128]{2,1,0:T(8,128)(2,1)} %copy-done.10, ...), custom_call_target="tpu_custom_call" | custom-call | flops 541065216 | bytes 4227072 | tf_op jit(solution)/shard_map/cross_coefficients/pallas_call | solution.py:467
  86.5 3.4 %collective-permute-done.21.refs_6_.refs_22_ = bf16[129,16,128]{2,1,0:T(8,128)(2,1)S(1)} collective-permute-done((bf16[129,16,128]{2,1,0:T(8,128)(2,1)S(1)}, bf16[129,16,128]{2,1,0:T(8,128)(2,1)S(1)}, u32[]{:S(2)}, u32[]{:S(2)}) %collective-permute-start.21) | collective-permute-done | bytes 528416 | tf_op jit(solution)/shard_map/ppermute | solution.py:712
  89.9 10.5 %collective-permute-done.25.refs_2_.refs_26_ = bf16[129,16,128]{2,1,0:T(8,128)(2,1)S(1)} collective-permute-done((bf16[129,16,128]{2,1,0:T(8,128)(2,1)S(1)}, bf16[129,16,128]{2,1,0:T(8,128)(2,1)S(1)}, u32[]{:S(2)}, u32[]{:S(2)}) %collective-permute-start.25) | collective-permute-done | bytes 528416 | tf_op jit(solution)/shard_map/ppermute | solution.py:712
  104.3 6.0 %cross_coefficients.6 = (f32[144,128]{1,0:T(8,128)}, f32[8,128]{1,0:T(8,128)}) custom-call(s32[1]{0:T(128)} %bitcast.2.at_ref, bf16[129,16,128]{2,1,0:T(8,128)(2,1)} %collective-permute-done.15.refs_0_.refs_16_, bf16[129,16,128]{2,1,0:T(8,128)(2,1)} %collective-permute-done.16.refs_1_.refs_17_, bf16[129,16,128]{2,1,0:T(8,128)(2,1)} %copy-done.7, ...), custom_call_target="tpu_custom_call" | custom-call | flops 541065216 | bytes 4227072 | tf_op jit(solution)/shard_map/cross_coefficients/pallas_call | solution.py:467
  110.4 4.5 %collective-permute-done.29.refs_6_.refs_30_ = bf16[129,16,128]{2,1,0:T(8,128)(2,1)} collective-permute-done((bf16[129,16,128]{2,1,0:T(8,128)(2,1)S(1)}, bf16[129,16,128]{2,1,0:T(8,128)(2,1)}, u32[]{:S(2)}, u32[]{:S(2)}) %collective-permute-start.29) | collective-permute-done | bytes 528416 | tf_op jit(solution)/shard_map/ppermute | solution.py:712
  116.4 3.4 %collective-permute-start.32 = (f32[144,128]{1,0:T(8,128)}, f32[144,128]{1,0:T(8,128)S(1)}, u32[]{:S(2)}, u32[]{:S(2)}) collective-permute-start(f32[144,128]{1,0:T(8,128)} %get-tuple-element.72), channel_id=1, source_target_pairs={{0,2},{1,3},{2,0},{3,1},{4,6},{5,7},{6,4},{7,5},{8,10},{9,11},{10,... | collective-permute-start | bytes 221192 | tf_op jit(solution)/shard_map/ppermute | solution.py:712
  120.6 6.0 %cross_coefficients.7 = (f32[144,128]{1,0:T(8,128)}, f32[8,128]{1,0:T(8,128)}) custom-call(s32[1]{0:T(128)} %bitcast.2.at_ref, bf16[129,16,128]{2,1,0:T(8,128)(2,1)} %copy-done.8, bf16[129,16,128]{2,1,0:T(8,128)(2,1)} %collective-permute-done.24.refs_1_.refs_25_, bf16[129,16,128]{2,1,0:T(8,128)(2,1)} %copy-done.14, ...), custom_call_target="tpu_custom_call" | custom-call | flops 541065216 | bytes 4227072 | tf_op jit(solution)/shard_map/cross_coefficients/pallas_call | solution.py:467
  128.3 4.8 %collective-permute-done.33.refs_3_ = f32[144,128]{1,0:T(8,128)S(1)} collective-permute-done((f32[144,128]{1,0:T(8,128)}, f32[144,128]{1,0:T(8,128)S(1)}, u32[]{:S(2)}, u32[]{:S(2)}) %collective-permute-start.33) | collective-permute-done | bytes 73760 | tf_op jit(solution)/shard_map/ppermute | solution.py:712
  135.8 9.9 %all-gather.1.stat_ref = f32[8,2,128]{2,1,0:T(2,128)} all-gather(f32[1,2,128]{2,1,0:T(2,128)} %bitcast.9), channel_id=2, replica_groups=mesh['cls'=8,'prt'=4] {'cls'}, dimensions={0}, use_global_device_ids=true | all-gather | bytes 9216 | tf_op jit(solution)/shard_map/all_gather | solution.py:793
  149.3 2.8 %collective-permute-start.34 = (f32[144,128]{1,0:T(8,128)}, f32[144,128]{1,0:T(8,128)S(1)}, u32[]{:S(2)}, u32[]{:S(2)}) collective-permute-start(f32[144,128]{1,0:T(8,128)} %get-tuple-element.78.refs_32_), channel_id=1, source_target_pairs={{0,1},{1,0},{2,3},{3,2},{4,5},{5,4},{6,7},{7,6},{8,9},{9,8},{10,11... | collective-permute-start | bytes 221192 | tf_op jit(solution)/shard_map/ppermute | solution.py:712
  152.2 2.8 %collective-permute-done.36.refs_35_ = f32[144,128]{1,0:T(8,128)S(1)} collective-permute-done((f32[144,128]{1,0:T(8,128)}, f32[144,128]{1,0:T(8,128)S(1)}, u32[]{:S(2)}, u32[]{:S(2)}) %collective-permute-start.36) | collective-permute-done | bytes 73760 | tf_op jit(solution)/shard_map/ppermute | solution.py:712
  155.0 2.5 %collective-permute-done.35.refs_34_ = f32[144,128]{1,0:T(8,128)S(1)} collective-permute-done((f32[144,128]{1,0:T(8,128)}, f32[144,128]{1,0:T(8,128)S(1)}, u32[]{:S(2)}, u32[]{:S(2)}) %collective-permute-start.35) | collective-permute-done | bytes 73760 | tf_op jit(solution)/shard_map/ppermute | solution.py:712
  158.1 15.2 %sums.1 = (f32[64,32,512]{2,1,0:T(8,128)}, f32[1,64]{1,0:T(1,128)}) custom-call(bf16[129,16,128]{2,1,0:T(8,128)(2,1)} %copy-done.1, bf16[129,16,128]{2,1,0:T(8,128)(2,1)} %collective-permute-done.4.refs_1_, bf16[129,16,128]{2,1,0:T(8,128)(2,1)} %copy-done.4, bf16[129,16,128]{2,1,0:T(8,128)(2,1)} %collective-permute-done.5.refs_3_, ...), custom_call_target="tpu_custom_call" | custom-call | flops 2164260864 | bytes 21102592 | tf_op jit(solution)/shard_map/sums/pallas_call | solution.py:678
  (115 shorter events, 39.5 us)
Async XLA Ops:
  6.7 15.1 %collective-permute-start = (bf16[129,16,128]{2,1,0:T(8,128)(2,1)S(1)}, bf16[129,16,128]{2,1,0:T(8,128)(2,1)S(1)}, u32[]{:S(2)}, u32[]{:S(2)}) collective-permute-start(bf16[129,16,128]{2,1,0:T(8,128)(2,1)S(1)} %get-tuple-element.45), channel_id=1, source_target_pairs={{0,1},{1,0},{2,3},{3,2},{4,5},{5,4},{6,7},{7,6},{8,9},{9,8},{10,11... | collective-permute-start | bytes 1585160 | tf_op jit(solution)/shard_map/ppermute | solution.py:712
  9.8 13.7 %collective-permute-start.2 = (bf16[129,16,128]{2,1,0:T(8,128)(2,1)S(1)}, bf16[129,16,128]{2,1,0:T(8,128)(2,1)S(1)}, u32[]{:S(2)}, u32[]{:S(2)}) collective-permute-start(bf16[129,16,128]{2,1,0:T(8,128)(2,1)S(1)} %get-tuple-element.51.refs_0_), channel_id=1, source_target_pairs={{0,16},{4,20},{8,24},{12,28},{16,0},{20,4},{24,8},{28,12},{1,17},{... | collective-permute-start | bytes 1585160 | tf_op jit(solution)/shard_map/ppermute | solution.py:712
  11.3 16.8 %collective-permute-start.1 = (bf16[129,16,128]{2,1,0:T(8,128)(2,1)S(1)}, bf16[129,16,128]{2,1,0:T(8,128)(2,1)S(1)}, u32[]{:S(2)}, u32[]{:S(2)}) collective-permute-start(bf16[129,16,128]{2,1,0:T(8,128)(2,1)S(1)} %get-tuple-element.51.refs_0_), channel_id=1, source_target_pairs={{0,8},{4,12},{8,0},{12,4},{16,24},{20,28},{24,16},{28,20},{1,9},{5... | collective-permute-start | bytes 1585160 | tf_op jit(solution)/shard_map/ppermute | solution.py:712
  21.8 14.0 %collective-permute-start.3 = (bf16[129,16,128]{2,1,0:T(8,128)(2,1)S(1)}, bf16[129,16,128]{2,1,0:T(8,128)(2,1)S(1)}, u32[]{:S(2)}, u32[]{:S(2)}) collective-permute-start(bf16[129,16,128]{2,1,0:T(8,128)(2,1)S(1)} %collective-permute-done.refs_0_.refs_8_), channel_id=1, source_target_pairs={{0,16},{4,20},{8,24},{12,28},{16,0},{20,4},{24,8},{28,12},{1,17},{... | collective-permute-start | bytes 1585160 | tf_op jit(solution)/shard_map/ppermute | solution.py:712
  23.5 15.1 %collective-permute-start.7 = (bf16[129,16,128]{2,1,0:T(8,128)(2,1)S(1)}, bf16[129,16,128]{2,1,0:T(8,128)(2,1)}, u32[]{:S(2)}, u32[]{:S(2)}) collective-permute-start(bf16[129,16,128]{2,1,0:T(8,128)(2,1)S(1)} %collective-permute-done.2.refs_4_), channel_id=1, source_target_pairs={{0,8},{4,12},{8,0},{12,4},{16,24},{20,28},{24,16},{28,20},{1,9},{5... | collective-permute-start | bytes 1585160 | tf_op jit(solution)/shard_map/ppermute | solution.py:712
  25.0 22.5 %collective-permute-start.9 = (bf16[129,16,128]{2,1,0:T(8,128)(2,1)S(1)}, bf16[129,16,128]{2,1,0:T(8,128)(2,1)}, u32[]{:S(2)}, u32[]{:S(2)}) collective-permute-start(bf16[129,16,128]{2,1,0:T(8,128)(2,1)S(1)} %collective-permute-done.refs_0_.refs_8_), channel_id=1, source_target_pairs={{0,8},{4,12},{8,0},{12,4},{16,24},{20,28},{24,16},{28,20},{1,9},{5... | collective-permute-start | bytes 1585160 | tf_op jit(solution)/shard_map/ppermute | solution.py:712
  25.5 24.4 %collective-permute-start.15 = (bf16[129,16,128]{2,1,0:T(8,128)(2,1)S(1)}, bf16[129,16,128]{2,1,0:T(8,128)(2,1)}, u32[]{:S(2)}, u32[]{:S(2)}) collective-permute-start(bf16[129,16,128]{2,1,0:T(8,128)(2,1)S(1)} %get-tuple-element.62), channel_id=1, source_target_pairs={{0,2},{1,3},{2,0},{3,1},{4,6},{5,7},{6,4},{7,5},{8,10},{9,11},{10,... | collective-permute-start | bytes 1585160 | tf_op jit(solution)/shard_map/ppermute | solution.py:712
  38.5 13.4 %collective-permute-start.4 = (bf16[129,16,128]{2,1,0:T(8,128)(2,1)S(1)}, bf16[129,16,128]{2,1,0:T(8,128)(2,1)}, u32[]{:S(2)}, u32[]{:S(2)}) collective-permute-start(bf16[129,16,128]{2,1,0:T(8,128)(2,1)S(1)} %get-tuple-element.51.refs_0_), channel_id=1, source_target_pairs={{0,4},{4,0},{8,12},{12,8},{16,20},{20,16},{24,28},{28,24},{1,5},{5... | collective-permute-start | bytes 1585160 | tf_op jit(solution)/shard_map/ppermute | solution.py:712
  39.0 14.4 %collective-permute-start.5 = (bf16[129,16,128]{2,1,0:T(8,128)(2,1)S(1)}, bf16[129,16,128]{2,1,0:T(8,128)(2,1)}, u32[]{:S(2)}, u32[]{:S(2)}) collective-permute-start(bf16[129,16,128]{2,1,0:T(8,128)(2,1)S(1)} %collective-permute-done.1.refs_2_), channel_id=1, source_target_pairs={{0,4},{4,0},{8,12},{12,8},{16,20},{20,16},{24,28},{28,24},{1,5},{5... | collective-permute-start | bytes 1585160 | tf_op jit(solution)/shard_map/ppermute | solution.py:712
  49.9 15.3 %collective-permute-start.13 = (bf16[129,16,128]{2,1,0:T(8,128)(2,1)}, bf16[129,16,128]{2,1,0:T(8,128)(2,1)}, u32[]{:S(2)}, u32[]{:S(2)}) collective-permute-start(bf16[129,16,128]{2,1,0:T(8,128)(2,1)} %collective-permute-done.9.refs_2_.refs_10_), channel_id=1, source_target_pairs={{0,16},{4,20},{8,24},{12,28},{16,0},{20,4},{24,8},{28,12},{1,17},{... | collective-permute-start | bytes 1585160 | tf_op jit(solution)/shard_map/ppermute | solution.py:712
  51.1 23.4 %collective-permute-start.19 = (bf16[129,16,128]{2,1,0:T(8,128)(2,1)}, bf16[129,16,128]{2,1,0:T(8,128)(2,1)S(1)}, u32[]{:S(2)}, u32[]{:S(2)}) collective-permute-start(bf16[129,16,128]{2,1,0:T(8,128)(2,1)} %collective-permute-done.15.refs_0_.refs_16_), channel_id=1, source_target_pairs={{0,16},{4,20},{8,24},{12,28},{16,0},{20,4},{24,8},{28,12},{1,17},{... | collective-permute-start | bytes 1585160 | tf_op jit(solution)/shard_map/ppermute | solution.py:712
  51.9 22.6 %collective-permute-start.17 = (bf16[129,16,128]{2,1,0:T(8,128)(2,1)}, bf16[129,16,128]{2,1,0:T(8,128)(2,1)S(1)}, u32[]{:S(2)}, u32[]{:S(2)}) collective-permute-start(bf16[129,16,128]{2,1,0:T(8,128)(2,1)} %collective-permute-done.15.refs_0_.refs_16_), channel_id=1, source_target_pairs={{0,8},{4,12},{8,0},{12,4},{16,24},{20,28},{24,16},{28,20},{1,9},{5... | collective-permute-start | bytes 1585160 | tf_op jit(solution)/shard_map/ppermute | solution.py:712
  53.4 21.6 %collective-permute-start.22 = (bf16[129,16,128]{2,1,0:T(8,128)(2,1)S(1)}, bf16[129,16,128]{2,1,0:T(8,128)(2,1)S(1)}, u32[]{:S(2)}, u32[]{:S(2)}) collective-permute-start(bf16[129,16,128]{2,1,0:T(8,128)(2,1)S(1)} %get-tuple-element.67), channel_id=1, source_target_pairs={{0,3},{1,2},{2,1},{3,0},{4,7},{5,6},{6,5},{7,4},{8,11},{9,10},{10,... | collective-permute-start | bytes 1585160 | tf_op jit(solution)/shard_map/ppermute | solution.py:712
  62.9 13.6 %collective-permute-start.10 = (bf16[129,16,128]{2,1,0:T(8,128)(2,1)S(1)}, bf16[129,16,128]{2,1,0:T(8,128)(2,1)S(1)}, u32[]{:S(2)}, u32[]{:S(2)}) collective-permute-start(bf16[129,16,128]{2,1,0:T(8,128)(2,1)S(1)} %collective-permute-done.refs_0_.refs_8_), channel_id=1, source_target_pairs={{0,4},{4,0},{8,12},{12,8},{16,20},{20,16},{24,28},{28,24},{1,5},{5... | collective-permute-start | bytes 1585160 | tf_op jit(solution)/shard_map/ppermute | solution.py:712
  75.0 14.9 %collective-permute-start.21 = (bf16[129,16,128]{2,1,0:T(8,128)(2,1)S(1)}, bf16[129,16,128]{2,1,0:T(8,128)(2,1)S(1)}, u32[]{:S(2)}, u32[]{:S(2)}) collective-permute-start(bf16[129,16,128]{2,1,0:T(8,128)(2,1)S(1)} %collective-permute-done.19.refs_4_.refs_20_), channel_id=1, source_target_pairs={{0,8},{4,12},{8,0},{12,4},{16,24},{20,28},{24,16},{28,20},{1,9},{5... | collective-permute-start | bytes 1585160 | tf_op jit(solution)/shard_map/ppermute | solution.py:712
  76.5 23.8 %collective-permute-start.25 = (bf16[129,16,128]{2,1,0:T(8,128)(2,1)S(1)}, bf16[129,16,128]{2,1,0:T(8,128)(2,1)S(1)}, u32[]{:S(2)}, u32[]{:S(2)}) collective-permute-start(bf16[129,16,128]{2,1,0:T(8,128)(2,1)S(1)} %collective-permute-done.22.refs_0_.refs_24_), channel_id=1, source_target_pairs={{0,8},{4,12},{8,0},{12,4},{16,24},{20,28},{24,16},{28,20},{1,9},{5... | collective-permute-start | bytes 1585160 | tf_op jit(solution)/shard_map/ppermute | solution.py:712
  77.1 23.3 %collective-permute-start.27 = (bf16[129,16,128]{2,1,0:T(8,128)(2,1)S(1)}, bf16[129,16,128]{2,1,0:T(8,128)(2,1)}, u32[]{:S(2)}, u32[]{:S(2)}) collective-permute-start(bf16[129,16,128]{2,1,0:T(8,128)(2,1)S(1)} %collective-permute-done.22.refs_0_.refs_24_), channel_id=1, source_target_pairs={{0,16},{4,20},{8,24},{12,28},{16,0},{20,4},{24,8},{28,12},{1,17},{... | collective-permute-start | bytes 1585160 | tf_op jit(solution)/shard_map/ppermute | solution.py:712
  78.8 23.5 %collective-permute-start.20 = (bf16[129,16,128]{2,1,0:T(8,128)(2,1)S(1)}, bf16[129,16,128]{2,1,0:T(8,128)(2,1)}, u32[]{:S(2)}, u32[]{:S(2)}) collective-permute-start(bf16[129,16,128]{2,1,0:T(8,128)(2,1)S(1)} %collective-permute-done.19.refs_4_.refs_20_), channel_id=1, source_target_pairs={{0,4},{4,0},{8,12},{12,8},{16,20},{20,16},{24,28},{28,24},{1,5},{5... | collective-permute-start | bytes 1585160 | tf_op jit(solution)/shard_map/ppermute | solution.py:712
  80.4 21.8 %collective-permute-start.16 = (bf16[129,16,128]{2,1,0:T(8,128)(2,1)}, bf16[129,16,128]{2,1,0:T(8,128)(2,1)}, u32[]{:S(2)}, u32[]{:S(2)}) collective-permute-start(bf16[129,16,128]{2,1,0:T(8,128)(2,1)} %collective-permute-done.15.refs_0_.refs_16_), channel_id=1, source_target_pairs={{0,4},{4,0},{8,12},{12,8},{16,20},{20,16},{24,28},{28,24},{1,5},{5... | collective-permute-start | bytes 1585160 | tf_op jit(solution)/shard_map/ppermute | solution.py:712
  100.4 14.5 %collective-permute-start.29 = (bf16[129,16,128]{2,1,0:T(8,128)(2,1)S(1)}, bf16[129,16,128]{2,1,0:T(8,128)(2,1)}, u32[]{:S(2)}, u32[]{:S(2)}) collective-permute-start(bf16[129,16,128]{2,1,0:T(8,128)(2,1)S(1)} %collective-permute-done.25.refs_2_.refs_26_), channel_id=1, source_target_pairs={{0,16},{4,20},{8,24},{12,28},{16,0},{20,4},{24,8},{28,12},{1,17},{... | collective-permute-start | bytes 1585160 | tf_op jit(solution)/shard_map/ppermute | solution.py:712
  102.2 14.2 %collective-permute-start.24 = (bf16[129,16,128]{2,1,0:T(8,128)(2,1)S(1)}, bf16[129,16,128]{2,1,0:T(8,128)(2,1)}, u32[]{:S(2)}, u32[]{:S(2)}) collective-permute-start(bf16[129,16,128]{2,1,0:T(8,128)(2,1)S(1)} %collective-permute-done.22.refs_0_.refs_24_), channel_id=1, source_target_pairs={{0,4},{4,0},{8,12},{12,8},{16,20},{20,16},{24,28},{28,24},{1,5},{5... | collective-permute-start | bytes 1585160 | tf_op jit(solution)/shard_map/ppermute | solution.py:712
  102.4 17.4 %collective-permute-start.26 = (bf16[129,16,128]{2,1,0:T(8,128)(2,1)S(1)}, bf16[129,16,128]{2,1,0:T(8,128)(2,1)}, u32[]{:S(2)}, u32[]{:S(2)}) collective-permute-start(bf16[129,16,128]{2,1,0:T(8,128)(2,1)S(1)} %collective-permute-done.25.refs_2_.refs_26_), channel_id=1, source_target_pairs={{0,4},{4,0},{8,12},{12,8},{16,20},{20,16},{24,28},{28,24},{1,5},{5... | collective-permute-start | bytes 1585160 | tf_op jit(solution)/shard_map/ppermute | solution.py:712
  102.7 17.1 %collective-permute-start.28 = (bf16[129,16,128]{2,1,0:T(8,128)(2,1)}, bf16[129,16,128]{2,1,0:T(8,128)(2,1)}, u32[]{:S(2)}, u32[]{:S(2)}) collective-permute-start(bf16[129,16,128]{2,1,0:T(8,128)(2,1)} %collective-permute-done.27.refs_4_.refs_28_), channel_id=1, source_target_pairs={{0,4},{4,0},{8,12},{12,8},{16,20},{20,16},{24,28},{28,24},{1,5},{5... | collective-permute-start | bytes 1585160 | tf_op jit(solution)/shard_map/ppermute | solution.py:712
  114.9 13.4 %collective-permute-start.31 = (f32[144,128]{1,0:T(8,128)S(1)}, f32[144,128]{1,0:T(8,128)S(1)}, u32[]{:S(2)}, u32[]{:S(2)}) collective-permute-start(f32[144,128]{1,0:T(8,128)S(1)} %copy-done.24), channel_id=1, source_target_pairs={{0,1},{1,0},{2,3},{3,2},{4,5},{5,4},{6,7},{7,6},{8,9},{9,8},{10,11... | collective-permute-start | bytes 221192 | tf_op jit(solution)/shard_map/ppermute | solution.py:712
  (38 other events, 436.1 us)

commit v14 on v13

--- a/solution.py
+++ b/solution.py
@@ -752,8 +752,7 @@
     meta = jnp.concatenate([owner_groups, picks], 1)
     cls, prt = (index.reshape(1).astype(jnp.int32) for index in (cls, prt))
     outgoing = []
-    for first in range(0, n_prt, 2):
-        distances = tuple(range(first, min(first + 2, n_prt)))
+    for distances in (tuple(range(min(n_prt, 3))), tuple(range(3, n_prt))):
         place = after(prt, outgoing[0]) if outgoing else prt
         outgoing += arrange_particles(
             place, particles, meta, n_prt, distances
@@ -764,12 +763,12 @@
         arrived.append(hop(outgoing[d], "prt", d))
     early = after(arrived[1], outgoing[-1])
     known.append({0: early, **direct(early)})
-    relayed(known[0], 0, outgoing[-1])
+    relayed(known[0], 0, outgoing[-1], arrived[2])
     place = after(prt, *arrived[1:2], *[known[0][1 << b] for b in range(1, n_cls.bit_length() - 1)])
     arranged, norms = arrange_references(references, place, n_prt)
     for d in range(2, n_prt):
         if d > 2:
-            arrived.append(hop(after(outgoing[d], arrived[d - 1], arranged), "prt", d))
+            arrived.append(hop(after(outgoing[d], arrived[d - 1]), "prt", d))
         own = after(arrived[d], arranged) if d == 2 else arrived[d]
         known.append({0: own, **direct(own)})
     for d in range(1, n_prt, 2):

time: 174 us -> 181 us (1.040)
  waiting for transfers between devices: 59.8 us -> 71.1 us
  starting transfers between devices: 37.8 us -> 33.7 us
    ppermute x37, waiting for transfers between devices: 59.8 us -> 71.1 us  [hop(): return lax.ppermute(value, axis, [(i, i ^ distance) for i in range(size)])]
    ppermute x37, starting transfers between devices: 37.8 us -> 33.7 us  [hop(): return lax.ppermute(value, axis, [(i, i ^ distance) for i in range(size)])]
    unnamed x51 -> x55, local copies, waits for them, and re-layouts: 7.45 us -> 6.65 us
  transfers between devices with their start and end apart: 37 -> 37, of which waited for: 12 -> 14; matrix products, arithmetic and copies ran while one was open for 0% -> 0% of each run, Pallas kernels for 20% -> 19%
where the time goes in v14:
time: 181 us; the launch traced here: 180 us
  waiting for transfers between devices  71.1 us (39%)
  Pallas kernels  56.5 us (31%)
  starting transfers between devices  33.7 us (19%)
  blocking collectives  10.3 us (6%)
  local copies, waits for them, and re-layouts  7.57 us (4%)
    ppermute x37, waiting for transfers between devices, hop(): return lax.ppermute(value, axis, [(i, i ^ distance) for i in range(size)])  71.1 us
    ppermute x37, starting transfers between devices, hop(): return lax.ppermute(value, axis, [(i, i ^ distance) for i in range(size)])  33.7 us
    pallas_call x4, Pallas kernels, cross_coefficients(): pl.pallas_call(cross_body, in_specs=[pl.BlockSpec(memory_space=pltpu.SMEM...  24.2 us
    pallas_call x1, Pallas kernels, sums(): pl.pallas_call(functools.partial(sums_body, number=number, pieces=len(mix...  15.2 us
    all_gather x1, blocking collectives, gather_device(): lax.all_gather(stat.reshape(1, *stat.shape), 'cls', axis=0, tiled=True)  10.3 us
    pallas_call x1, Pallas kernels, arrange_references(): pl.pallas_call(reference_body, grid_spec=pltpu.PrefetchScalarGridSpec(num...  7.65 us
    unnamed x55, local copies, waits for them, and re-layouts  6.65 us
    pallas_call x2, Pallas kernels, arrange_particles(): pl.pallas_call(functools.partial(particle_body, distances=distances, n_pr...  5.33 us
  transfers between devices with their start and end apart: 37, of which 14 were waited for; matrix products, arithmetic and copies ran while one was open for 0% of the time, Pallas kernels for 19%

profile of v14, /device:TPU:0, one launch (start us, length us, event | category | flops | bytes accessed | tf_op | source)
XLA Modules:
  0.0 180.4 jit_solution(13310545615593034977)
XLA Ops:
  4.0 3.5 %arrange_particles.2 = (bf16[129,16,128]{2,1,0:T(8,128)(2,1)S(1)}, bf16[129,16,128]{2,1,0:T(8,128)(2,1)S(1)}, bf16[129,16,128]{2,1,0:T(8,128)(2,1)S(1)}) custom-call(s32[1]{0:T(128)} %bitcast.at_ref, bf16[16,128,512]{2,1,0:T(8,128)(2,1)S(1)} %copy-done, s32[16,20]{1,0:T(8,128)S(1)} %pad_add_fusion.meta_ref), custom_call_target="tpu_custom_call" | custom-call | flops 201326592 | bytes 3145728 | tf_op jit(solution)/shard_map/arrange_particles/pallas_call | solution.py:281
  7.6 3.1 %collective-permute-start = (bf16[129,16,128]{2,1,0:T(8,128)(2,1)S(1)}, bf16[129,16,128]{2,1,0:T(8,128)(2,1)S(1)}, u32[]{:S(2)}, u32[]{:S(2)}) collective-permute-start(bf16[129,16,128]{2,1,0:T(8,128)(2,1)S(1)} %get-tuple-element.44), channel_id=1, source_target_pairs={{0,1},{1,0},{2,3},{3,2},{4,5},{5,4},{6,7},{7,6},{8,9},{9,8},{10,11... | collective-permute-start | bytes 1585160 | tf_op jit(solution)/shard_map/ppermute | solution.py:712
  10.7 2.6 %collective-permute-start.7 = (bf16[129,16,128]{2,1,0:T(8,128)(2,1)S(1)}, bf16[129,16,128]{2,1,0:T(8,128)(2,1)S(1)}, u32[]{:S(2)}, u32[]{:S(2)}) collective-permute-start(bf16[129,16,128]{2,1,0:T(8,128)(2,1)S(1)} %get-tuple-element.52), channel_id=1, source_target_pairs={{0,2},{1,3},{2,0},{3,1},{4,6},{5,7},{6,4},{7,5},{8,10},{9,11},{10,... | collective-permute-start | bytes 1585160 | tf_op jit(solution)/shard_map/ppermute | solution.py:712
  18.0 15.8 %collective-permute-done.refs_0_.refs_8_ = bf16[129,16,128]{2,1,0:T(8,128)(2,1)S(1)} collective-permute-done((bf16[129,16,128]{2,1,0:T(8,128)(2,1)S(1)}, bf16[129,16,128]{2,1,0:T(8,128)(2,1)S(1)}, u32[]{:S(2)}, u32[]{:S(2)}) %collective-permute-start) | collective-permute-done | bytes 528416 | tf_op jit(solution)/shard_map/ppermute | solution.py:712
  38.5 7.7 %arrange_references.1 = (bf16[128,64,128]{2,1,0:T(8,128)(2,1)}, f32[64,128]{1,0:T(8,128)}) custom-call(s32[1]{0:T(128)} %bitcast.at_ref, bf16[64,128,512]{2,1,0:T(8,128)(2,1)} %x_ref.4), custom_call_target="tpu_custom_call" | custom-call | flops 268435456 | bytes 4194304 | tf_op jit(solution)/shard_map/arrange_references/pallas_call | solution.py:322
  47.1 4.4 %collective-permute-done.8.refs_6_ = bf16[129,16,128]{2,1,0:T(8,128)(2,1)} collective-permute-done((bf16[129,16,128]{2,1,0:T(8,128)(2,1)S(1)}, bf16[129,16,128]{2,1,0:T(8,128)(2,1)}, u32[]{:S(2)}, u32[]{:S(2)}) %collective-permute-start.8) | collective-permute-done | bytes 528416 | tf_op jit(solution)/shard_map/ppermute | solution.py:712
  52.6 7.1 %collective-permute-done.10.refs_2_.refs_10_ = bf16[129,16,128]{2,1,0:T(8,128)(2,1)} collective-permute-done((bf16[129,16,128]{2,1,0:T(8,128)(2,1)S(1)}, bf16[129,16,128]{2,1,0:T(8,128)(2,1)}, u32[]{:S(2)}, u32[]{:S(2)}) %collective-permute-start.10) | collective-permute-done | bytes 528416 | tf_op jit(solution)/shard_map/ppermute | solution.py:712
  60.3 2.3 %collective-permute-start.22 = (bf16[129,16,128]{2,1,0:T(8,128)(2,1)S(1)}, bf16[129,16,128]{2,1,0:T(8,128)(2,1)}, u32[]{:S(2)}, u32[]{:S(2)}) collective-permute-start(bf16[129,16,128]{2,1,0:T(8,128)(2,1)S(1)} %arrange_particles.3), channel_id=1, source_target_pairs={{0,3},{1,2},{2,1},{3,0},{4,7},{5,6},{6,5},{7,4},{8,11},{9,10},{10,... | collective-permute-start | bytes 1585160 | tf_op jit(solution)/shard_map/ppermute | solution.py:712
  65.7 6.1 %cross_coefficients.4 = (f32[144,128]{1,0:T(8,128)}, f32[8,128]{1,0:T(8,128)}) custom-call(s32[1]{0:T(128)} %bitcast.2.at_ref, bf16[129,16,128]{2,1,0:T(8,128)(2,1)} %copy-done.1, bf16[129,16,128]{2,1,0:T(8,128)(2,1)} %collective-permute-done.4.refs_1_, bf16[129,16,128]{2,1,0:T(8,128)(2,1)} %copy-done.5, ...), custom_call_target="tpu_custom_call" | custom-call | flops 541065216 | bytes 4227072 | tf_op jit(solution)/shard_map/cross_coefficients/pallas_call | solution.py:467
  71.8 3.1 %collective-permute-done.14.refs_6_.refs_14_ = bf16[129,16,128]{2,1,0:T(8,128)(2,1)} collective-permute-done((bf16[129,16,128]{2,1,0:T(8,128)(2,1)}, bf16[129,16,128]{2,1,0:T(8,128)(2,1)}, u32[]{:S(2)}, u32[]{:S(2)}) %collective-permute-start.14) | collective-permute-done | bytes 528416 | tf_op jit(solution)/shard_map/ppermute | solution.py:712
  75.5 6.6 %collective-permute-done.19.refs_4_.refs_20_ = bf16[129,16,128]{2,1,0:T(8,128)(2,1)S(1)} collective-permute-done((bf16[129,16,128]{2,1,0:T(8,128)(2,1)S(1)}, bf16[129,16,128]{2,1,0:T(8,128)(2,1)S(1)}, u32[]{:S(2)}, u32[]{:S(2)}) %collective-permute-start.19) | collective-permute-done | bytes 528416 | tf_op jit(solution)/shard_map/ppermute | solution.py:712
  85.8 6.0 %cross_coefficients.5 = (f32[144,128]{1,0:T(8,128)}, f32[8,128]{1,0:T(8,128)}) custom-call(s32[1]{0:T(128)} %bitcast.2.at_ref, bf16[129,16,128]{2,1,0:T(8,128)(2,1)} %copy-done.2, bf16[129,16,128]{2,1,0:T(8,128)(2,1)} %copy-done.10, bf16[129,16,128]{2,1,0:T(8,128)(2,1)} %collective-permute-done.10.refs_2_.refs_10_, bf16[129,16,128]{2,1,0:T(8,128)(2,1)} %copy-done.11, ...), custom_call_target="tpu_custom_call" | custom-call | flops 541065216 | bytes 4227072 | tf_op jit(solution)/shard_map/cross_coefficients/pallas_call | solution.py:467
  91.9 5.2 %collective-permute-done.21.refs_6_.refs_22_ = bf16[129,16,128]{2,1,0:T(8,128)(2,1)} collective-permute-done((bf16[129,16,128]{2,1,0:T(8,128)(2,1)S(1)}, bf16[129,16,128]{2,1,0:T(8,128)(2,1)}, u32[]{:S(2)}, u32[]{:S(2)}) %collective-permute-start.21) | collective-permute-done | bytes 528416 | tf_op jit(solution)/shard_map/ppermute | solution.py:712
  97.1 10.8 %collective-permute-done.25.refs_2_.refs_26_ = bf16[129,16,128]{2,1,0:T(8,128)(2,1)S(1)} collective-permute-done((bf16[129,16,128]{2,1,0:T(8,128)(2,1)}, bf16[129,16,128]{2,1,0:T(8,128)(2,1)S(1)}, u32[]{:S(2)}, u32[]{:S(2)}) %collective-permute-start.25) | collective-permute-done | bytes 528416 | tf_op jit(solution)/shard_map/ppermute | solution.py:712
  110.8 6.0 %cross_coefficients.6 = (f32[144,128]{1,0:T(8,128)}, f32[8,128]{1,0:T(8,128)}) custom-call(s32[1]{0:T(128)} %bitcast.2.at_ref, bf16[129,16,128]{2,1,0:T(8,128)(2,1)} %copy-done.3, bf16[129,16,128]{2,1,0:T(8,128)(2,1)} %collective-permute-done.16.refs_1_.refs_17_, bf16[129,16,128]{2,1,0:T(8,128)(2,1)} %copy-done.9, bf16[129,16,128]{2,1,0:T(8,128)(2,1)} %copy-done.16, ...), custom_call_target="tpu_custom_call" | custom-call | flops 541065216 | bytes 4227072 | tf_op jit(solution)/shard_map/cross_coefficients/pallas_call | solution.py:467
  116.9 5.5 %collective-permute-done.29.refs_6_.refs_30_ = bf16[129,16,128]{2,1,0:T(8,128)(2,1)} collective-permute-done((bf16[129,16,128]{2,1,0:T(8,128)(2,1)S(1)}, bf16[129,16,128]{2,1,0:T(8,128)(2,1)}, u32[]{:S(2)}, u32[]{:S(2)}) %collective-permute-start.29) | collective-permute-done | bytes 528416 | tf_op jit(solution)/shard_map/ppermute | solution.py:712
  122.4 2.5 %collective-permute-start.31 = (f32[144,128]{1,0:T(8,128)S(1)}, f32[144,128]{1,0:T(8,128)S(1)}, u32[]{:S(2)}, u32[]{:S(2)}) collective-permute-start(f32[144,128]{1,0:T(8,128)S(1)} %copy-done.26), channel_id=1, source_target_pairs={{0,1},{1,0},{2,3},{3,2},{4,5},{5,4},{6,7},{7,6},{8,9},{9,8},{10,11... | collective-permute-start | bytes 221192 | tf_op jit(solution)/shard_map/ppermute | solution.py:712
  126.8 6.0 %cross_coefficients.7 = (f32[144,128]{1,0:T(8,128)}, f32[8,128]{1,0:T(8,128)}) custom-call(s32[1]{0:T(128)} %bitcast.2.at_ref, bf16[129,16,128]{2,1,0:T(8,128)(2,1)} %collective-permute-done.22.refs_0_.refs_24_, bf16[129,16,128]{2,1,0:T(8,128)(2,1)} %copy-done.18, bf16[129,16,128]{2,1,0:T(8,128)(2,1)} %copy-done.14, ...), custom_call_target="tpu_custom_call" | custom-call | flops 541065216 | bytes 4227072 | tf_op jit(solution)/shard_map/cross_coefficients/pallas_call | solution.py:467
  132.8 2.2 %collective-permute-start.33 = (f32[144,128]{1,0:T(8,128)}, f32[144,128]{1,0:T(8,128)S(1)}, u32[]{:S(2)}, u32[]{:S(2)}) collective-permute-start(f32[144,128]{1,0:T(8,128)} %get-tuple-element.72), channel_id=1, source_target_pairs={{0,3},{1,2},{2,1},{3,0},{4,7},{5,6},{6,5},{7,4},{8,11},{9,10},{10,... | collective-permute-start | bytes 221192 | tf_op jit(solution)/shard_map/ppermute | solution.py:712
  135.1 4.3 %collective-permute-done.33.refs_3_ = f32[144,128]{1,0:T(8,128)S(1)} collective-permute-done((f32[144,128]{1,0:T(8,128)}, f32[144,128]{1,0:T(8,128)S(1)}, u32[]{:S(2)}, u32[]{:S(2)}) %collective-permute-start.33) | collective-permute-done | bytes 73760 | tf_op jit(solution)/shard_map/ppermute | solution.py:712
  142.1 10.3 %all-gather.1.stat_ref = f32[8,2,128]{2,1,0:T(2,128)} all-gather(f32[1,2,128]{2,1,0:T(2,128)} %bitcast.9), channel_id=2, replica_groups=mesh['cls'=8,'prt'=4] {'cls'}, dimensions={0}, use_global_device_ids=true | all-gather | bytes 9216 | tf_op jit(solution)/shard_map/all_gather | solution.py:792
  158.9 2.8 %collective-permute-done.36.refs_35_ = f32[144,128]{1,0:T(8,128)S(1)} collective-permute-done((f32[144,128]{1,0:T(8,128)}, f32[144,128]{1,0:T(8,128)S(1)}, u32[]{:S(2)}, u32[]{:S(2)}) %collective-permute-start.36) | collective-permute-done | bytes 73760 | tf_op jit(solution)/shard_map/ppermute | solution.py:712
  161.7 2.6 %collective-permute-done.35.refs_34_ = f32[144,128]{1,0:T(8,128)S(1)} collective-permute-done((f32[144,128]{1,0:T(8,128)}, f32[144,128]{1,0:T(8,128)S(1)}, u32[]{:S(2)}, u32[]{:S(2)}) %collective-permute-start.35) | collective-permute-done | bytes 73760 | tf_op jit(solution)/shard_map/ppermute | solution.py:712
  165.0 15.2 %sums.1 = (f32[64,32,512]{2,1,0:T(8,128)}, f32[1,64]{1,0:T(1,128)}) custom-call(bf16[129,16,128]{2,1,0:T(8,128)(2,1)} %copy-done.1, bf16[129,16,128]{2,1,0:T(8,128)(2,1)} %collective-permute-done.4.refs_1_, bf16[129,16,128]{2,1,0:T(8,128)(2,1)} %copy-done.5, bf16[129,16,128]{2,1,0:T(8,128)(2,1)} %collective-permute-done.5.refs_3_, ...), custom_call_target="tpu_custom_call" | custom-call | flops 2164260864 | bytes 21102592 | tf_op jit(solution)/shard_map/sums/pallas_call | solution.py:678
  (119 shorter events, 37.4 us)
Async XLA Ops:
  7.6 26.3 %collective-permute-start = (bf16[129,16,128]{2,1,0:T(8,128)(2,1)S(1)}, bf16[129,16,128]{2,1,0:T(8,128)(2,1)S(1)}, u32[]{:S(2)}, u32[]{:S(2)}) collective-permute-start(bf16[129,16,128]{2,1,0:T(8,128)(2,1)S(1)} %get-tuple-element.44), channel_id=1, source_target_pairs={{0,1},{1,0},{2,3},{3,2},{4,5},{5,4},{6,7},{7,6},{8,9},{9,8},{10,11... | collective-permute-start | bytes 1585160 | tf_op jit(solution)/shard_map/ppermute | solution.py:712
  10.7 25.7 %collective-permute-start.7 = (bf16[129,16,128]{2,1,0:T(8,128)(2,1)S(1)}, bf16[129,16,128]{2,1,0:T(8,128)(2,1)S(1)}, u32[]{:S(2)}, u32[]{:S(2)}) collective-permute-start(bf16[129,16,128]{2,1,0:T(8,128)(2,1)S(1)} %get-tuple-element.52), channel_id=1, source_target_pairs={{0,2},{1,3},{2,0},{3,1},{4,6},{5,7},{6,4},{7,5},{8,10},{9,11},{10,... | collective-permute-start | bytes 1585160 | tf_op jit(solution)/shard_map/ppermute | solution.py:712
  13.2 23.2 %collective-permute-start.2 = (bf16[129,16,128]{2,1,0:T(8,128)(2,1)S(1)}, bf16[129,16,128]{2,1,0:T(8,128)(2,1)S(1)}, u32[]{:S(2)}, u32[]{:S(2)}) collective-permute-start(bf16[129,16,128]{2,1,0:T(8,128)(2,1)S(1)} %get-tuple-element.49.refs_0_), channel_id=1, source_target_pairs={{0,16},{4,20},{8,24},{12,28},{16,0},{20,4},{24,8},{28,12},{1,17},{... | collective-permute-start | bytes 1585160 | tf_op jit(solution)/shard_map/ppermute | solution.py:712
  14.8 23.7 %collective-permute-start.1 = (bf16[129,16,128]{2,1,0:T(8,128)(2,1)S(1)}, bf16[129,16,128]{2,1,0:T(8,128)(2,1)S(1)}, u32[]{:S(2)}, u32[]{:S(2)}) collective-permute-start(bf16[129,16,128]{2,1,0:T(8,128)(2,1)S(1)} %get-tuple-element.49.refs_0_), channel_id=1, source_target_pairs={{0,8},{4,12},{8,0},{12,4},{16,24},{20,28},{24,16},{28,20},{1,9},{5... | collective-permute-start | bytes 1585160 | tf_op jit(solution)/shard_map/ppermute | solution.py:712
  33.9 13.2 %collective-permute-start.3 = (bf16[129,16,128]{2,1,0:T(8,128)(2,1)S(1)}, bf16[129,16,128]{2,1,0:T(8,128)(2,1)S(1)}, u32[]{:S(2)}, u32[]{:S(2)}) collective-permute-start(bf16[129,16,128]{2,1,0:T(8,128)(2,1)S(1)} %collective-permute-done.refs_0_.refs_8_), channel_id=1, source_target_pairs={{0,16},{4,20},{8,24},{12,28},{16,0},{20,4},{24,8},{28,12},{1,17},{... | collective-permute-start | bytes 1585160 | tf_op jit(solution)/shard_map/ppermute | solution.py:712
  36.4 15.1 %collective-permute-start.8 = (bf16[129,16,128]{2,1,0:T(8,128)(2,1)S(1)}, bf16[129,16,128]{2,1,0:T(8,128)(2,1)}, u32[]{:S(2)}, u32[]{:S(2)}) collective-permute-start(bf16[129,16,128]{2,1,0:T(8,128)(2,1)S(1)} %collective-permute-done.2.refs_4_), channel_id=1, source_target_pairs={{0,8},{4,12},{8,0},{12,4},{16,24},{20,28},{24,16},{28,20},{1,9},{5... | collective-permute-start | bytes 1585160 | tf_op jit(solution)/shard_map/ppermute | solution.py:712
  38.0 21.7 %collective-permute-start.10 = (bf16[129,16,128]{2,1,0:T(8,128)(2,1)S(1)}, bf16[129,16,128]{2,1,0:T(8,128)(2,1)}, u32[]{:S(2)}, u32[]{:S(2)}) collective-permute-start(bf16[129,16,128]{2,1,0:T(8,128)(2,1)S(1)} %collective-permute-done.refs_0_.refs_8_), channel_id=1, source_target_pairs={{0,8},{4,12},{8,0},{12,4},{16,24},{20,28},{24,16},{28,20},{1,9},{5... | collective-permute-start | bytes 1585160 | tf_op jit(solution)/shard_map/ppermute | solution.py:712
  52.0 12.2 %collective-permute-start.5 = (bf16[129,16,128]{2,1,0:T(8,128)(2,1)S(1)}, bf16[129,16,128]{2,1,0:T(8,128)(2,1)}, u32[]{:S(2)}, u32[]{:S(2)}) collective-permute-start(bf16[129,16,128]{2,1,0:T(8,128)(2,1)S(1)} %collective-permute-done.1.refs_2_), channel_id=1, source_target_pairs={{0,4},{4,0},{8,12},{12,8},{16,20},{20,16},{24,28},{28,24},{1,5},{5... | collective-permute-start | bytes 1585160 | tf_op jit(solution)/shard_map/ppermute | solution.py:712
  52.1 13.6 %collective-permute-start.6 = (bf16[129,16,128]{2,1,0:T(8,128)(2,1)S(1)}, bf16[129,16,128]{2,1,0:T(8,128)(2,1)}, u32[]{:S(2)}, u32[]{:S(2)}) collective-permute-start(bf16[129,16,128]{2,1,0:T(8,128)(2,1)S(1)} %collective-permute-done.2.refs_4_), channel_id=1, source_target_pairs={{0,4},{4,0},{8,12},{12,8},{16,20},{20,16},{24,28},{28,24},{1,5},{5... | collective-permute-start | bytes 1585160 | tf_op jit(solution)/shard_map/ppermute | solution.py:712
  59.7 15.3 %collective-permute-start.14 = (bf16[129,16,128]{2,1,0:T(8,128)(2,1)}, bf16[129,16,128]{2,1,0:T(8,128)(2,1)}, u32[]{:S(2)}, u32[]{:S(2)}) collective-permute-start(bf16[129,16,128]{2,1,0:T(8,128)(2,1)} %collective-permute-done.10.refs_2_.refs_10_), channel_id=1, source_target_pairs={{0,16},{4,20},{8,24},{12,28},{16,0},{20,4},{24,8},{28,12},{1,17},{... | collective-permute-start | bytes 1585160 | tf_op jit(solution)/shard_map/ppermute | solution.py:712
  60.3 14.6 %collective-permute-start.22 = (bf16[129,16,128]{2,1,0:T(8,128)(2,1)S(1)}, bf16[129,16,128]{2,1,0:T(8,128)(2,1)}, u32[]{:S(2)}, u32[]{:S(2)}) collective-permute-start(bf16[129,16,128]{2,1,0:T(8,128)(2,1)S(1)} %arrange_particles.3), channel_id=1, source_target_pairs={{0,3},{1,2},{2,1},{3,0},{4,7},{5,6},{6,5},{7,4},{8,11},{9,10},{10,... | collective-permute-start | bytes 1585160 | tf_op jit(solution)/shard_map/ppermute | solution.py:712
  62.7 19.4 %collective-permute-start.19 = (bf16[129,16,128]{2,1,0:T(8,128)(2,1)S(1)}, bf16[129,16,128]{2,1,0:T(8,128)(2,1)S(1)}, u32[]{:S(2)}, u32[]{:S(2)}) collective-permute-start(bf16[129,16,128]{2,1,0:T(8,128)(2,1)S(1)} %collective-permute-done.7.refs_0_.refs_16_), channel_id=1, source_target_pairs={{0,16},{4,20},{8,24},{12,28},{16,0},{20,4},{24,8},{28,12},{1,17},{... | collective-permute-start | bytes 1585160 | tf_op jit(solution)/shard_map/ppermute | solution.py:712
  64.2 17.9 %collective-permute-start.17 = (bf16[129,16,128]{2,1,0:T(8,128)(2,1)S(1)}, bf16[129,16,128]{2,1,0:T(8,128)(2,1)S(1)}, u32[]{:S(2)}, u32[]{:S(2)}) collective-permute-start(bf16[129,16,128]{2,1,0:T(8,128)(2,1)S(1)} %collective-permute-done.7.refs_0_.refs_16_), channel_id=1, source_target_pairs={{0,8},{4,12},{8,0},{12,4},{16,24},{20,28},{24,16},{28,20},{1,9},{5... | collective-permute-start | bytes 1585160 | tf_op jit(solution)/shard_map/ppermute | solution.py:712
  71.8 11.9 %collective-permute-start.11 = (bf16[129,16,128]{2,1,0:T(8,128)(2,1)S(1)}, bf16[129,16,128]{2,1,0:T(8,128)(2,1)S(1)}, u32[]{:S(2)}, u32[]{:S(2)}) collective-permute-start(bf16[129,16,128]{2,1,0:T(8,128)(2,1)S(1)} %collective-permute-done.refs_0_.refs_8_), channel_id=1, source_target_pairs={{0,4},{4,0},{8,12},{12,8},{16,20},{20,16},{24,28},{28,24},{1,5},{5... | collective-permute-start | bytes 1585160 | tf_op jit(solution)/shard_map/ppermute | solution.py:712
  82.1 15.0 %collective-permute-start.21 = (bf16[129,16,128]{2,1,0:T(8,128)(2,1)S(1)}, bf16[129,16,128]{2,1,0:T(8,128)(2,1)}, u32[]{:S(2)}, u32[]{:S(2)}) collective-permute-start(bf16[129,16,128]{2,1,0:T(8,128)(2,1)S(1)} %collective-permute-done.19.refs_4_.refs_20_), channel_id=1, source_target_pairs={{0,8},{4,12},{8,0},{12,4},{16,24},{20,28},{24,16},{28,20},{1,9},{5... | collective-permute-start | bytes 1585160 | tf_op jit(solution)/shard_map/ppermute | solution.py:712
  83.7 24.2 %collective-permute-start.25 = (bf16[129,16,128]{2,1,0:T(8,128)(2,1)}, bf16[129,16,128]{2,1,0:T(8,128)(2,1)S(1)}, u32[]{:S(2)}, u32[]{:S(2)}) collective-permute-start(bf16[129,16,128]{2,1,0:T(8,128)(2,1)} %collective-permute-done.22.refs_0_.refs_24_), channel_id=1, source_target_pairs={{0,8},{4,12},{8,0},{12,4},{16,24},{20,28},{24,16},{28,20},{1,9},{5... | collective-permute-start | bytes 1585160 | tf_op jit(solution)/shard_map/ppermute | solution.py:712
  84.2 23.7 %collective-permute-start.27 = (bf16[129,16,128]{2,1,0:T(8,128)(2,1)}, bf16[129,16,128]{2,1,0:T(8,128)(2,1)}, u32[]{:S(2)}, u32[]{:S(2)}) collective-permute-start(bf16[129,16,128]{2,1,0:T(8,128)(2,1)} %collective-permute-done.22.refs_0_.refs_24_), channel_id=1, source_target_pairs={{0,16},{4,20},{8,24},{12,28},{16,0},{20,4},{24,8},{28,12},{1,17},{... | collective-permute-start | bytes 1585160 | tf_op jit(solution)/shard_map/ppermute | solution.py:712
  84.5 24.0 %collective-permute-start.20 = (bf16[129,16,128]{2,1,0:T(8,128)(2,1)S(1)}, bf16[129,16,128]{2,1,0:T(8,128)(2,1)S(1)}, u32[]{:S(2)}, u32[]{:S(2)}) collective-permute-start(bf16[129,16,128]{2,1,0:T(8,128)(2,1)S(1)} %collective-permute-done.19.refs_4_.refs_20_), channel_id=1, source_target_pairs={{0,4},{4,0},{8,12},{12,8},{16,20},{20,16},{24,28},{28,24},{1,5},{5... | collective-permute-start | bytes 1585160 | tf_op jit(solution)/shard_map/ppermute | solution.py:712
  85.8 22.4 %collective-permute-start.16 = (bf16[129,16,128]{2,1,0:T(8,128)(2,1)S(1)}, bf16[129,16,128]{2,1,0:T(8,128)(2,1)}, u32[]{:S(2)}, u32[]{:S(2)}) collective-permute-start(bf16[129,16,128]{2,1,0:T(8,128)(2,1)S(1)} %collective-permute-done.7.refs_0_.refs_16_), channel_id=1, source_target_pairs={{0,4},{4,0},{8,12},{12,8},{16,20},{20,16},{24,28},{28,24},{1,5},{5... | collective-permute-start | bytes 1585160 | tf_op jit(solution)/shard_map/ppermute | solution.py:712
  107.8 14.5 %collective-permute-start.29 = (bf16[129,16,128]{2,1,0:T(8,128)(2,1)S(1)}, bf16[129,16,128]{2,1,0:T(8,128)(2,1)}, u32[]{:S(2)}, u32[]{:S(2)}) collective-permute-start(bf16[129,16,128]{2,1,0:T(8,128)(2,1)S(1)} %collective-permute-done.25.refs_2_.refs_26_), channel_id=1, source_target_pairs={{0,16},{4,20},{8,24},{12,28},{16,0},{20,4},{24,8},{28,12},{1,17},{... | collective-permute-start | bytes 1585160 | tf_op jit(solution)/shard_map/ppermute | solution.py:712
  108.2 16.7 %collective-permute-start.24 = (bf16[129,16,128]{2,1,0:T(8,128)(2,1)}, bf16[129,16,128]{2,1,0:T(8,128)(2,1)S(1)}, u32[]{:S(2)}, u32[]{:S(2)}) collective-permute-start(bf16[129,16,128]{2,1,0:T(8,128)(2,1)} %collective-permute-done.22.refs_0_.refs_24_), channel_id=1, source_target_pairs={{0,4},{4,0},{8,12},{12,8},{16,20},{20,16},{24,28},{28,24},{1,5},{5... | collective-permute-start | bytes 1585160 | tf_op jit(solution)/shard_map/ppermute | solution.py:712
  108.4 17.5 %collective-permute-start.26 = (bf16[129,16,128]{2,1,0:T(8,128)(2,1)S(1)}, bf16[129,16,128]{2,1,0:T(8,128)(2,1)}, u32[]{:S(2)}, u32[]{:S(2)}) collective-permute-start(bf16[129,16,128]{2,1,0:T(8,128)(2,1)S(1)} %collective-permute-done.25.refs_2_.refs_26_), channel_id=1, source_target_pairs={{0,4},{4,0},{8,12},{12,8},{16,20},{20,16},{24,28},{28,24},{1,5},{5... | collective-permute-start | bytes 1585160 | tf_op jit(solution)/shard_map/ppermute | solution.py:712
  108.7 17.2 %collective-permute-start.28 = (bf16[129,16,128]{2,1,0:T(8,128)(2,1)}, bf16[129,16,128]{2,1,0:T(8,128)(2,1)}, u32[]{:S(2)}, u32[]{:S(2)}) collective-permute-start(bf16[129,16,128]{2,1,0:T(8,128)(2,1)} %collective-permute-done.27.refs_4_.refs_28_), channel_id=1, source_target_pairs={{0,4},{4,0},{8,12},{12,8},{16,20},{20,16},{24,28},{28,24},{1,5},{5... | collective-permute-start | bytes 1585160 | tf_op jit(solution)/shard_map/ppermute | solution.py:712
  122.4 12.7 %collective-permute-start.31 = (f32[144,128]{1,0:T(8,128)S(1)}, f32[144,128]{1,0:T(8,128)S(1)}, u32[]{:S(2)}, u32[]{:S(2)}) collective-permute-start(f32[144,128]{1,0:T(8,128)S(1)} %copy-done.26), channel_id=1, source_target_pairs={{0,1},{1,0},{2,3},{3,2},{4,5},{5,4},{6,7},{7,6},{8,9},{9,8},{10,11... | collective-permute-start | bytes 221192 | tf_op jit(solution)/shard_map/ppermute | solution.py:712
  (40 other events, 415.4 us)

commit v15 on v13

--- a/solution.py
+++ b/solution.py
@@ -783,7 +783,8 @@
         if d and d % 2 == 0:
             relayed(known[d], d, coefs[0])
         each = [arranged, known[1][n_cls // 2]] if d == 0 else coefs[:1] if d < 3 else []
-        blocks.append(paired(known[d], each, coefs[-1:]))
+        last = coefs[-1:] + (sent[1:] if d == n_prt - 1 else [])
+        blocks.append(paired(known[d], each, last))
         ready = after(arranged, *waits) if waits else arranged
         coef, cand = cross_coefficients(blocks[d], ready, norms, cls)
         coefs.append(coef)

time: 174 us -> 183 us (1.052)
  waiting for transfers between devices: 59.8 us -> 68.9 us
    ppermute x37, waiting for transfers between devices: 59.8 us -> 68.9 us  [hop(): return lax.ppermute(value, axis, [(i, i ^ distance) for i in range(size)])]
    unnamed x51 -> x57, local copies, waits for them, and re-layouts: 7.45 us -> 5.7 us
  transfers between devices with their start and end apart: 37 -> 37, of which waited for: 12 -> 17; matrix products, arithmetic and copies ran while one was open for 0% -> 0% of each run, Pallas kernels for 20% -> 16%
where the time goes in v15:
time: 183 us
  waiting for transfers between devices  68.9 us (38%)
  Pallas kernels  56.5 us (31%)
  starting transfers between devices  38.9 us (21%)
  blocking collectives  10.5 us (6%)
  local copies, waits for them, and re-layouts  6.62 us (4%)
    ppermute x37, waiting for transfers between devices, hop(): return lax.ppermute(value, axis, [(i, i ^ distance) for i in range(size)])  68.9 us
    ppermute x37, starting transfers between devices, hop(): return lax.ppermute(value, axis, [(i, i ^ distance) for i in range(size)])  38.9 us
    pallas_call x4, Pallas kernels, cross_coefficients(): pl.pallas_call(cross_body, in_specs=[pl.BlockSpec(memory_space=pltpu.SMEM...  24.2 us
    pallas_call x1, Pallas kernels, sums(): pl.pallas_call(functools.partial(sums_body, number=number, pieces=len(mix...  15.2 us
    all_gather x1, blocking collectives, gather_device(): lax.all_gather(stat.reshape(1, *stat.shape), 'cls', axis=0, tiled=True)  10.5 us
    pallas_call x1, Pallas kernels, arrange_references(): pl.pallas_call(reference_body, grid_spec=pltpu.PrefetchScalarGridSpec(num...  7.66 us
    unnamed x57, local copies, waits for them, and re-layouts  5.7 us
    pallas_call x2, Pallas kernels, arrange_particles(): pl.pallas_call(functools.partial(particle_body, distances=distances, n_pr...  5.35 us
  transfers between devices with their start and end apart: 37, of which 17 were waited for; matrix products, arithmetic and copies ran while one was open for 0% of the time, Pallas kernels for 16%

profile of v15, /device:TPU:0, one launch (start us, length us, event | category | flops | bytes accessed | tf_op | source)
XLA Modules:
  0.0 182.5 jit_solution(1150950405908964021)
XLA Ops:
  4.0 2.7 %arrange_particles.2 = (bf16[129,16,128]{2,1,0:T(8,128)(2,1)S(1)}, bf16[129,16,128]{2,1,0:T(8,128)(2,1)S(1)}) custom-call(s32[1]{0:T(128)} %bitcast.at_ref, bf16[16,128,512]{2,1,0:T(8,128)(2,1)S(1)} %copy-done, s32[16,20]{1,0:T(8,128)S(1)} %pad_add_fusion.meta_ref), custom_call_target="tpu_custom_call" | custom-call | flops 134217728 | bytes 2097152 | tf_op jit(solution)/shard_map/arrange_particles/pallas_call | solution.py:281
  6.7 3.0 %collective-permute-start.2 = (bf16[129,16,128]{2,1,0:T(8,128)(2,1)S(1)}, bf16[129,16,128]{2,1,0:T(8,128)(2,1)S(1)}, u32[]{:S(2)}, u32[]{:S(2)}) collective-permute-start(bf16[129,16,128]{2,1,0:T(8,128)(2,1)S(1)} %get-tuple-element.51.refs_0_), channel_id=1, source_target_pairs={{0,16},{4,20},{8,24},{12,28},{16,0},{20,4},{24,8},{28,12},{1,17},{... | collective-permute-start | bytes 1585160 | tf_op jit(solution)/shard_map/ppermute | solution.py:712
  12.8 2.7 %arrange_particles.3 = (bf16[129,16,128]{2,1,0:T(8,128)(2,1)S(1)}, bf16[129,16,128]{2,1,0:T(8,128)(2,1)S(1)}) custom-call(s32[1]{0:T(128)} %bitcast.at_ref, bf16[16,128,512]{2,1,0:T(8,128)(2,1)S(1)} %copy-done, s32[16,20]{1,0:T(8,128)S(1)} %pad_add_fusion.meta_ref), custom_call_target="tpu_custom_call" | custom-call | flops 134217728 | bytes 2097152 | tf_op jit(solution)/shard_map/arrange_particles/pallas_call | solution.py:281
  15.5 6.2 %collective-permute-done.2.refs_4_ = bf16[129,16,128]{2,1,0:T(8,128)(2,1)S(1)} collective-permute-done((bf16[129,16,128]{2,1,0:T(8,128)(2,1)S(1)}, bf16[129,16,128]{2,1,0:T(8,128)(2,1)S(1)}, u32[]{:S(2)}, u32[]{:S(2)}) %collective-permute-start.2) | collective-permute-done | bytes 528416 | tf_op jit(solution)/shard_map/ppermute | solution.py:712
  25.6 2.8 %collective-permute-start.15 = (bf16[129,16,128]{2,1,0:T(8,128)(2,1)S(1)}, bf16[129,16,128]{2,1,0:T(8,128)(2,1)}, u32[]{:S(2)}, u32[]{:S(2)}) collective-permute-start(bf16[129,16,128]{2,1,0:T(8,128)(2,1)S(1)} %get-tuple-element.62), channel_id=1, source_target_pairs={{0,2},{1,3},{2,0},{3,1},{4,6},{5,7},{6,4},{7,5},{8,10},{9,11},{10,... | collective-permute-start | bytes 1585160 | tf_op jit(solution)/shard_map/ppermute | solution.py:712
  28.3 7.7 %arrange_references.1 = (bf16[128,64,128]{2,1,0:T(8,128)(2,1)}, f32[64,128]{1,0:T(8,128)}) custom-call(s32[1]{0:T(128)} %bitcast.at_ref, bf16[64,128,512]{2,1,0:T(8,128)(2,1)} %x_ref.4), custom_call_target="tpu_custom_call" | custom-call | flops 268435456 | bytes 4194304 | tf_op jit(solution)/shard_map/arrange_references/pallas_call | solution.py:322
  38.7 8.5 %collective-permute-done.9.refs_2_.refs_10_ = bf16[129,16,128]{2,1,0:T(8,128)(2,1)} collective-permute-done((bf16[129,16,128]{2,1,0:T(8,128)(2,1)S(1)}, bf16[129,16,128]{2,1,0:T(8,128)(2,1)}, u32[]{:S(2)}, u32[]{:S(2)}) %collective-permute-start.9) | collective-permute-done | bytes 528416 | tf_op jit(solution)/shard_map/ppermute | solution.py:712
  47.2 2.7 %collective-permute-done.15.refs_0_.refs_16_ = bf16[129,16,128]{2,1,0:T(8,128)(2,1)} collective-permute-done((bf16[129,16,128]{2,1,0:T(8,128)(2,1)S(1)}, bf16[129,16,128]{2,1,0:T(8,128)(2,1)}, u32[]{:S(2)}, u32[]{:S(2)}) %collective-permute-start.15) | collective-permute-done | bytes 528416 | tf_op jit(solution)/shard_map/ppermute | solution.py:712
  54.3 3.5 %collective-permute-start.22 = (bf16[129,16,128]{2,1,0:T(8,128)(2,1)S(1)}, bf16[129,16,128]{2,1,0:T(8,128)(2,1)S(1)}, u32[]{:S(2)}, u32[]{:S(2)}) collective-permute-start(bf16[129,16,128]{2,1,0:T(8,128)(2,1)S(1)} %get-tuple-element.67), channel_id=1, source_target_pairs={{0,3},{1,2},{2,1},{3,0},{4,7},{5,6},{6,5},{7,4},{8,11},{9,10},{10,... | collective-permute-start | bytes 1585160 | tf_op jit(solution)/shard_map/ppermute | solution.py:712
  57.8 6.0 %cross_coefficients.4 = (f32[144,128]{1,0:T(8,128)}, f32[8,128]{1,0:T(8,128)}) custom-call(s32[1]{0:T(128)} %bitcast.2.at_ref, bf16[129,16,128]{2,1,0:T(8,128)(2,1)} %copy-done.1, bf16[129,16,128]{2,1,0:T(8,128)(2,1)} %copy-done.7, bf16[129,16,128]{2,1,0:T(8,128)(2,1)} %copy-done.4, bf16[129,16,128]{2,1,0:T(8,128)(2,1)} %copy-done.8, ...), custom_call_target="tpu_custom_call" | custom-call | flops 541065216 | bytes 4227072 | tf_op jit(solution)/shard_map/cross_coefficients/pallas_call | solution.py:467
  65.2 9.2 %collective-permute-done.19.refs_4_.refs_20_ = bf16[129,16,128]{2,1,0:T(8,128)(2,1)} collective-permute-done((bf16[129,16,128]{2,1,0:T(8,128)(2,1)}, bf16[129,16,128]{2,1,0:T(8,128)(2,1)}, u32[]{:S(2)}, u32[]{:S(2)}) %collective-permute-start.19) | collective-permute-done | bytes 528416 | tf_op jit(solution)/shard_map/ppermute | solution.py:712
  77.9 6.1 %cross_coefficients.5 = (f32[144,128]{1,0:T(8,128)}, f32[8,128]{1,0:T(8,128)}) custom-call(s32[1]{0:T(128)} %bitcast.2.at_ref, bf16[129,16,128]{2,1,0:T(8,128)(2,1)} %copy-done.3, bf16[129,16,128]{2,1,0:T(8,128)(2,1)} %copy-done.11, bf16[129,16,128]{2,1,0:T(8,128)(2,1)} %collective-permute-done.9.refs_2_.refs_10_, bf16[129,16,128]{2,1,0:T(8,128)(2,1)} %copy-done.12, ...), custom_call_target="tpu_custom_call" | custom-call | flops 541065216 | bytes 4227072 | tf_op jit(solution)/shard_map/cross_coefficients/pallas_call | solution.py:467
  84.0 6.0 %collective-permute-done.21.refs_6_.refs_22_ = bf16[129,16,128]{2,1,0:T(8,128)(2,1)S(1)} collective-permute-done((bf16[129,16,128]{2,1,0:T(8,128)(2,1)}, bf16[129,16,128]{2,1,0:T(8,128)(2,1)S(1)}, u32[]{:S(2)}, u32[]{:S(2)}) %collective-permute-start.21) | collective-permute-done | bytes 528416 | tf_op jit(solution)/shard_map/ppermute | solution.py:712
  90.0 10.5 %collective-permute-done.25.refs_2_.refs_26_ = bf16[129,16,128]{2,1,0:T(8,128)(2,1)S(1)} collective-permute-done((bf16[129,16,128]{2,1,0:T(8,128)(2,1)S(1)}, bf16[129,16,128]{2,1,0:T(8,128)(2,1)S(1)}, u32[]{:S(2)}, u32[]{:S(2)}) %collective-permute-start.25) | collective-permute-done | bytes 528416 | tf_op jit(solution)/shard_map/ppermute | solution.py:712
  105.9 6.0 %cross_coefficients.6 = (f32[144,128]{1,0:T(8,128)}, f32[8,128]{1,0:T(8,128)}) custom-call(s32[1]{0:T(128)} %bitcast.2.at_ref, bf16[129,16,128]{2,1,0:T(8,128)(2,1)} %collective-permute-done.15.refs_0_.refs_16_, bf16[129,16,128]{2,1,0:T(8,128)(2,1)} %collective-permute-done.16.refs_1_.refs_17_, bf16[129,16,128]{2,1,0:T(8,128)(2,1)} %copy-done.9, ...), custom_call_target="tpu_custom_call" | custom-call | flops 541065216 | bytes 4227072 | tf_op jit(solution)/shard_map/cross_coefficients/pallas_call | solution.py:467
  115.4 9.5 %collective-permute-done.29.refs_6_.refs_30_ = bf16[129,16,128]{2,1,0:T(8,128)(2,1)S(1)} collective-permute-done((bf16[129,16,128]{2,1,0:T(8,128)(2,1)S(1)}, bf16[129,16,128]{2,1,0:T(8,128)(2,1)S(1)}, u32[]{:S(2)}, u32[]{:S(2)}) %collective-permute-start.29) | collective-permute-done | bytes 528416 | tf_op jit(solution)/shard_map/ppermute | solution.py:712
  127.8 6.1 %cross_coefficients.7 = (f32[144,128]{1,0:T(8,128)}, f32[8,128]{1,0:T(8,128)}) custom-call(s32[1]{0:T(128)} %bitcast.2.at_ref, bf16[129,16,128]{2,1,0:T(8,128)(2,1)} %copy-done.10, bf16[129,16,128]{2,1,0:T(8,128)(2,1)} %copy-done.19, bf16[129,16,128]{2,1,0:T(8,128)(2,1)} %copy-done.15, bf16[129,16,128]{2,1,0:T(8,128)(2,1)} %copy-done.20, ...), custom_call_target="tpu_custom_call" | custom-call | flops 541065216 | bytes 4227072 | tf_op jit(solution)/shard_map/cross_coefficients/pallas_call | solution.py:467
  133.9 4.7 %collective-permute-start.33 = (f32[144,128]{1,0:T(8,128)}, f32[144,128]{1,0:T(8,128)S(1)}, u32[]{:S(2)}, u32[]{:S(2)}) collective-permute-start(f32[144,128]{1,0:T(8,128)} %get-tuple-element.74), channel_id=1, source_target_pairs={{0,3},{1,2},{2,1},{3,0},{4,7},{5,6},{6,5},{7,4},{8,11},{9,10},{10,... | collective-permute-start | bytes 221192 | tf_op jit(solution)/shard_map/ppermute | solution.py:712
  138.6 2.8 %collective-permute-done.33.refs_3_ = f32[144,128]{1,0:T(8,128)S(1)} collective-permute-done((f32[144,128]{1,0:T(8,128)}, f32[144,128]{1,0:T(8,128)S(1)}, u32[]{:S(2)}, u32[]{:S(2)}) %collective-permute-start.33) | collective-permute-done | bytes 73760 | tf_op jit(solution)/shard_map/ppermute | solution.py:712
  144.0 10.5 %all-gather.1.stat_ref = f32[8,2,128]{2,1,0:T(2,128)} all-gather(f32[1,2,128]{2,1,0:T(2,128)} %bitcast.9), channel_id=2, replica_groups=mesh['cls'=8,'prt'=4] {'cls'}, dimensions={0}, use_global_device_ids=true | all-gather | bytes 9216 | tf_op jit(solution)/shard_map/all_gather | solution.py:794
  156.6 3.6 %collective-permute-start.36 = (f32[144,128]{1,0:T(8,128)}, f32[144,128]{1,0:T(8,128)S(1)}, u32[]{:S(2)}, u32[]{:S(2)}) collective-permute-start(f32[144,128]{1,0:T(8,128)} %get-tuple-element.78.refs_32_), channel_id=1, source_target_pairs={{0,3},{1,2},{2,1},{3,0},{4,7},{5,6},{6,5},{7,4},{8,11},{9,10},{10,... | collective-permute-start | bytes 221192 | tf_op jit(solution)/shard_map/ppermute | solution.py:712
  161.0 2.7 %collective-permute-done.36.refs_35_ = f32[144,128]{1,0:T(8,128)S(1)} collective-permute-done((f32[144,128]{1,0:T(8,128)}, f32[144,128]{1,0:T(8,128)S(1)}, u32[]{:S(2)}, u32[]{:S(2)}) %collective-permute-start.36) | collective-permute-done | bytes 73760 | tf_op jit(solution)/shard_map/ppermute | solution.py:712
  163.7 2.7 %collective-permute-done.35.refs_34_ = f32[144,128]{1,0:T(8,128)S(1)} collective-permute-done((f32[144,128]{1,0:T(8,128)}, f32[144,128]{1,0:T(8,128)S(1)}, u32[]{:S(2)}, u32[]{:S(2)}) %collective-permute-start.35) | collective-permute-done | bytes 73760 | tf_op jit(solution)/shard_map/ppermute | solution.py:712
  167.2 15.2 %sums.1 = (f32[64,32,512]{2,1,0:T(8,128)}, f32[1,64]{1,0:T(1,128)}) custom-call(bf16[129,16,128]{2,1,0:T(8,128)(2,1)} %copy-done.1, bf16[129,16,128]{2,1,0:T(8,128)(2,1)} %copy-done.7, bf16[129,16,128]{2,1,0:T(8,128)(2,1)} %copy-done.4, bf16[129,16,128]{2,1,0:T(8,128)(2,1)} %copy-done.8, bf16[129,16,128]{2,1,0:T(8,128)(2,1)} %copy-done.2, ...), custom_call_target="tpu_custom_call" | custom-call | flops 2164260864 | bytes 21102592 | tf_op jit(solution)/shard_map/sums/pallas_call | solution.py:678
  (121 shorter events, 40.3 us)
Async XLA Ops:
  6.7 15.0 %collective-permute-start.2 = (bf16[129,16,128]{2,1,0:T(8,128)(2,1)S(1)}, bf16[129,16,128]{2,1,0:T(8,128)(2,1)S(1)}, u32[]{:S(2)}, u32[]{:S(2)}) collective-permute-start(bf16[129,16,128]{2,1,0:T(8,128)(2,1)S(1)} %get-tuple-element.51.refs_0_), channel_id=1, source_target_pairs={{0,16},{4,20},{8,24},{12,28},{16,0},{20,4},{24,8},{28,12},{1,17},{... | collective-permute-start | bytes 1585160 | tf_op jit(solution)/shard_map/ppermute | solution.py:712
  9.7 13.5 %collective-permute-start = (bf16[129,16,128]{2,1,0:T(8,128)(2,1)S(1)}, bf16[129,16,128]{2,1,0:T(8,128)(2,1)S(1)}, u32[]{:S(2)}, u32[]{:S(2)}) collective-permute-start(bf16[129,16,128]{2,1,0:T(8,128)(2,1)S(1)} %get-tuple-element.45), channel_id=1, source_target_pairs={{0,1},{1,0},{2,3},{3,2},{4,5},{5,4},{6,7},{7,6},{8,9},{9,8},{10,11... | collective-permute-start | bytes 1585160 | tf_op jit(solution)/shard_map/ppermute | solution.py:712
  11.3 17.0 %collective-permute-start.1 = (bf16[129,16,128]{2,1,0:T(8,128)(2,1)S(1)}, bf16[129,16,128]{2,1,0:T(8,128)(2,1)S(1)}, u32[]{:S(2)}, u32[]{:S(2)}) collective-permute-start(bf16[129,16,128]{2,1,0:T(8,128)(2,1)S(1)} %get-tuple-element.51.refs_0_), channel_id=1, source_target_pairs={{0,8},{4,12},{8,0},{12,4},{16,24},{20,28},{24,16},{28,20},{1,9},{5... | collective-permute-start | bytes 1585160 | tf_op jit(solution)/shard_map/ppermute | solution.py:712
  23.2 14.9 %collective-permute-start.7 = (bf16[129,16,128]{2,1,0:T(8,128)(2,1)S(1)}, bf16[129,16,128]{2,1,0:T(8,128)(2,1)S(1)}, u32[]{:S(2)}, u32[]{:S(2)}) collective-permute-start(bf16[129,16,128]{2,1,0:T(8,128)(2,1)S(1)} %collective-permute-done.2.refs_4_), channel_id=1, source_target_pairs={{0,8},{4,12},{8,0},{12,4},{16,24},{20,28},{24,16},{28,20},{1,9},{5... | collective-permute-start | bytes 1585160 | tf_op jit(solution)/shard_map/ppermute | solution.py:712
  24.7 13.5 %collective-permute-start.3 = (bf16[129,16,128]{2,1,0:T(8,128)(2,1)S(1)}, bf16[129,16,128]{2,1,0:T(8,128)(2,1)}, u32[]{:S(2)}, u32[]{:S(2)}) collective-permute-start(bf16[129,16,128]{2,1,0:T(8,128)(2,1)S(1)} %collective-permute-done.refs_0_.refs_8_), channel_id=1, source_target_pairs={{0,16},{4,20},{8,24},{12,28},{16,0},{20,4},{24,8},{28,12},{1,17},{... | collective-permute-start | bytes 1585160 | tf_op jit(solution)/shard_map/ppermute | solution.py:712
  25.2 22.1 %collective-permute-start.9 = (bf16[129,16,128]{2,1,0:T(8,128)(2,1)S(1)}, bf16[129,16,128]{2,1,0:T(8,128)(2,1)}, u32[]{:S(2)}, u32[]{:S(2)}) collective-permute-start(bf16[129,16,128]{2,1,0:T(8,128)(2,1)S(1)} %collective-permute-done.refs_0_.refs_8_), channel_id=1, source_target_pairs={{0,8},{4,12},{8,0},{12,4},{16,24},{20,28},{24,16},{28,20},{1,9},{5... | collective-permute-start | bytes 1585160 | tf_op jit(solution)/shard_map/ppermute | solution.py:712
  25.6 24.4 %collective-permute-start.15 = (bf16[129,16,128]{2,1,0:T(8,128)(2,1)S(1)}, bf16[129,16,128]{2,1,0:T(8,128)(2,1)}, u32[]{:S(2)}, u32[]{:S(2)}) collective-permute-start(bf16[129,16,128]{2,1,0:T(8,128)(2,1)S(1)} %get-tuple-element.62), channel_id=1, source_target_pairs={{0,2},{1,3},{2,0},{3,1},{4,6},{5,7},{6,4},{7,5},{8,10},{9,11},{10,... | collective-permute-start | bytes 1585160 | tf_op jit(solution)/shard_map/ppermute | solution.py:712
  38.1 13.1 %collective-permute-start.8 = (bf16[129,16,128]{2,1,0:T(8,128)(2,1)S(1)}, bf16[129,16,128]{2,1,0:T(8,128)(2,1)S(1)}, u32[]{:S(2)}, u32[]{:S(2)}) collective-permute-start(bf16[129,16,128]{2,1,0:T(8,128)(2,1)S(1)} %collective-permute-done.7.refs_6_), channel_id=1, source_target_pairs={{0,4},{4,0},{8,12},{12,8},{16,20},{20,16},{24,28},{28,24},{1,5},{5... | collective-permute-start | bytes 1585160 | tf_op jit(solution)/shard_map/ppermute | solution.py:712
  38.2 13.8 %collective-permute-start.4 = (bf16[129,16,128]{2,1,0:T(8,128)(2,1)S(1)}, bf16[129,16,128]{2,1,0:T(8,128)(2,1)S(1)}, u32[]{:S(2)}, u32[]{:S(2)}) collective-permute-start(bf16[129,16,128]{2,1,0:T(8,128)(2,1)S(1)} %get-tuple-element.51.refs_0_), channel_id=1, source_target_pairs={{0,4},{4,0},{8,12},{12,8},{16,20},{20,16},{24,28},{28,24},{1,5},{5... | collective-permute-start | bytes 1585160 | tf_op jit(solution)/shard_map/ppermute | solution.py:712
  38.7 14.8 %collective-permute-start.5 = (bf16[129,16,128]{2,1,0:T(8,128)(2,1)S(1)}, bf16[129,16,128]{2,1,0:T(8,128)(2,1)S(1)}, u32[]{:S(2)}, u32[]{:S(2)}) collective-permute-start(bf16[129,16,128]{2,1,0:T(8,128)(2,1)S(1)} %collective-permute-done.1.refs_2_), channel_id=1, source_target_pairs={{0,4},{4,0},{8,12},{12,8},{16,20},{20,16},{24,28},{28,24},{1,5},{5... | collective-permute-start | bytes 1585160 | tf_op jit(solution)/shard_map/ppermute | solution.py:712
  49.9 15.3 %collective-permute-start.13 = (bf16[129,16,128]{2,1,0:T(8,128)(2,1)}, bf16[129,16,128]{2,1,0:T(8,128)(2,1)}, u32[]{:S(2)}, u32[]{:S(2)}) collective-permute-start(bf16[129,16,128]{2,1,0:T(8,128)(2,1)} %collective-permute-done.9.refs_2_.refs_10_), channel_id=1, source_target_pairs={{0,16},{4,20},{8,24},{12,28},{16,0},{20,4},{24,8},{28,12},{1,17},{... | collective-permute-start | bytes 1585160 | tf_op jit(solution)/shard_map/ppermute | solution.py:712
  51.3 23.1 %collective-permute-start.19 = (bf16[129,16,128]{2,1,0:T(8,128)(2,1)}, bf16[129,16,128]{2,1,0:T(8,128)(2,1)}, u32[]{:S(2)}, u32[]{:S(2)}) collective-permute-start(bf16[129,16,128]{2,1,0:T(8,128)(2,1)} %collective-permute-done.15.refs_0_.refs_16_), channel_id=1, source_target_pairs={{0,16},{4,20},{8,24},{12,28},{16,0},{20,4},{24,8},{28,12},{1,17},{... | collective-permute-start | bytes 1585160 | tf_op jit(solution)/shard_map/ppermute | solution.py:712
  52.0 22.4 %collective-permute-start.17 = (bf16[129,16,128]{2,1,0:T(8,128)(2,1)}, bf16[129,16,128]{2,1,0:T(8,128)(2,1)S(1)}, u32[]{:S(2)}, u32[]{:S(2)}) collective-permute-start(bf16[129,16,128]{2,1,0:T(8,128)(2,1)} %collective-permute-done.15.refs_0_.refs_16_), channel_id=1, source_target_pairs={{0,8},{4,12},{8,0},{12,4},{16,24},{20,28},{24,16},{28,20},{1,9},{5... | collective-permute-start | bytes 1585160 | tf_op jit(solution)/shard_map/ppermute | solution.py:712
  54.3 20.6 %collective-permute-start.22 = (bf16[129,16,128]{2,1,0:T(8,128)(2,1)S(1)}, bf16[129,16,128]{2,1,0:T(8,128)(2,1)S(1)}, u32[]{:S(2)}, u32[]{:S(2)}) collective-permute-start(bf16[129,16,128]{2,1,0:T(8,128)(2,1)S(1)} %get-tuple-element.67), channel_id=1, source_target_pairs={{0,3},{1,2},{2,1},{3,0},{4,7},{5,6},{6,5},{7,4},{8,11},{9,10},{10,... | collective-permute-start | bytes 1585160 | tf_op jit(solution)/shard_map/ppermute | solution.py:712
  74.9 15.1 %collective-permute-start.21 = (bf16[129,16,128]{2,1,0:T(8,128)(2,1)}, bf16[129,16,128]{2,1,0:T(8,128)(2,1)S(1)}, u32[]{:S(2)}, u32[]{:S(2)}) collective-permute-start(bf16[129,16,128]{2,1,0:T(8,128)(2,1)} %collective-permute-done.19.refs_4_.refs_20_), channel_id=1, source_target_pairs={{0,8},{4,12},{8,0},{12,4},{16,24},{20,28},{24,16},{28,20},{1,9},{5... | collective-permute-start | bytes 1585160 | tf_op jit(solution)/shard_map/ppermute | solution.py:712
  76.5 24.0 %collective-permute-start.25 = (bf16[129,16,128]{2,1,0:T(8,128)(2,1)S(1)}, bf16[129,16,128]{2,1,0:T(8,128)(2,1)S(1)}, u32[]{:S(2)}, u32[]{:S(2)}) collective-permute-start(bf16[129,16,128]{2,1,0:T(8,128)(2,1)S(1)} %collective-permute-done.22.refs_0_.refs_24_), channel_id=1, source_target_pairs={{0,8},{4,12},{8,0},{12,4},{16,24},{20,28},{24,16},{28,20},{1,9},{5... | collective-permute-start | bytes 1585160 | tf_op jit(solution)/shard_map/ppermute | solution.py:712
  77.0 24.8 %collective-permute-start.16 = (bf16[129,16,128]{2,1,0:T(8,128)(2,1)}, bf16[129,16,128]{2,1,0:T(8,128)(2,1)}, u32[]{:S(2)}, u32[]{:S(2)}) collective-permute-start(bf16[129,16,128]{2,1,0:T(8,128)(2,1)} %collective-permute-done.15.refs_0_.refs_16_), channel_id=1, source_target_pairs={{0,4},{4,0},{8,12},{12,8},{16,20},{20,16},{24,28},{28,24},{1,5},{5... | collective-permute-start | bytes 1585160 | tf_op jit(solution)/shard_map/ppermute | solution.py:712
  77.0 25.5 %collective-permute-start.20 = (bf16[129,16,128]{2,1,0:T(8,128)(2,1)}, bf16[129,16,128]{2,1,0:T(8,128)(2,1)}, u32[]{:S(2)}, u32[]{:S(2)}) collective-permute-start(bf16[129,16,128]{2,1,0:T(8,128)(2,1)} %collective-permute-done.19.refs_4_.refs_20_), channel_id=1, source_target_pairs={{0,4},{4,0},{8,12},{12,8},{16,20},{20,16},{24,28},{28,24},{1,5},{5... | collective-permute-start | bytes 1585160 | tf_op jit(solution)/shard_map/ppermute | solution.py:712
  77.5 27.6 %collective-permute-start.18 = (bf16[129,16,128]{2,1,0:T(8,128)(2,1)S(1)}, bf16[129,16,128]{2,1,0:T(8,128)(2,1)}, u32[]{:S(2)}, u32[]{:S(2)}) collective-permute-start(bf16[129,16,128]{2,1,0:T(8,128)(2,1)S(1)} %collective-permute-done.17.refs_2_.refs_18_), channel_id=1, source_target_pairs={{0,4},{4,0},{8,12},{12,8},{16,20},{20,16},{24,28},{28,24},{1,5},{5... | collective-permute-start | bytes 1585160 | tf_op jit(solution)/shard_map/ppermute | solution.py:712
  90.0 15.1 %collective-permute-start.23 = (bf16[129,16,128]{2,1,0:T(8,128)(2,1)S(1)}, bf16[129,16,128]{2,1,0:T(8,128)(2,1)S(1)}, u32[]{:S(2)}, u32[]{:S(2)}) collective-permute-start(bf16[129,16,128]{2,1,0:T(8,128)(2,1)S(1)} %collective-permute-done.21.refs_6_.refs_22_), channel_id=1, source_target_pairs={{0,4},{4,0},{8,12},{12,8},{16,20},{20,16},{24,28},{28,24},{1,5},{5... | collective-permute-start | bytes 1585160 | tf_op jit(solution)/shard_map/ppermute | solution.py:712
  100.5 14.9 %collective-permute-start.27 = (bf16[129,16,128]{2,1,0:T(8,128)(2,1)S(1)}, bf16[129,16,128]{2,1,0:T(8,128)(2,1)S(1)}, u32[]{:S(2)}, u32[]{:S(2)}) collective-permute-start(bf16[129,16,128]{2,1,0:T(8,128)(2,1)S(1)} %collective-permute-done.22.refs_0_.refs_24_), channel_id=1, source_target_pairs={{0,16},{4,20},{8,24},{12,28},{16,0},{20,4},{24,8},{28,12},{1,17},{... | collective-permute-start | bytes 1585160 | tf_op jit(solution)/shard_map/ppermute | solution.py:712
  101.8 23.1 %collective-permute-start.29 = (bf16[129,16,128]{2,1,0:T(8,128)(2,1)S(1)}, bf16[129,16,128]{2,1,0:T(8,128)(2,1)S(1)}, u32[]{:S(2)}, u32[]{:S(2)}) collective-permute-start(bf16[129,16,128]{2,1,0:T(8,128)(2,1)S(1)} %collective-permute-done.25.refs_2_.refs_26_), channel_id=1, source_target_pairs={{0,16},{4,20},{8,24},{12,28},{16,0},{20,4},{24,8},{28,12},{1,17},{... | collective-permute-start | bytes 1585160 | tf_op jit(solution)/shard_map/ppermute | solution.py:712
  102.5 22.5 %collective-permute-start.30 = (f32[144,128]{1,0:T(8,128)}, f32[144,128]{1,0:T(8,128)S(1)}, u32[]{:S(2)}, u32[]{:S(2)}) collective-permute-start(f32[144,128]{1,0:T(8,128)} %get-tuple-element.69), channel_id=1, source_target_pairs={{0,1},{1,0},{2,3},{3,2},{4,5},{5,4},{6,7},{7,6},{8,9},{9,8},{10,11... | collective-permute-start | bytes 221192 | tf_op jit(solution)/shard_map/ppermute | solution.py:712
  111.9 13.0 %collective-permute-start.31 = (f32[144,128]{1,0:T(8,128)}, f32[144,128]{1,0:T(8,128)S(1)}, u32[]{:S(2)}, u32[]{:S(2)}) collective-permute-start(f32[144,128]{1,0:T(8,128)} %get-tuple-element.72), channel_id=1, source_target_pairs={{0,2},{1,3},{2,0},{3,1},{4,6},{5,7},{6,4},{7,5},{8,10},{9,11},{10,... | collective-permute-start | bytes 221192 | tf_op jit(solution)/shard_map/ppermute | solution.py:712
  (41 other events, 401.6 us)

commit v16 on v13

--- a/solution.py
+++ b/solution.py
@@ -673,7 +673,7 @@
     count = blocks[0].shape[1]
     total = number * count
     size = blocks[0].size * number
-    block = 8
+    block = 16
     whole = lambda i: (0, 0)
     return pl.pallas_call(
         functools.partial(sums_body, number=number, pieces=len(mixes)),

time: 174 us -> 173 us (level)
  no operation moved by 1% of the time
where the time goes in v16:
time: 173 us; the launch traced here: 172 us
  waiting for transfers between devices  59.8 us (35%)
  Pallas kernels  55.2 us (32%)
  starting transfers between devices  37.8 us (22%)
  blocking collectives  9.93 us (6%)
  local copies, waits for them, and re-layouts  8.38 us (5%)
    ppermute x37, waiting for transfers between devices, hop(): return lax.ppermute(value, axis, [(i, i ^ distance) for i in range(size)])  59.8 us
    ppermute x37, starting transfers between devices, hop(): return lax.ppermute(value, axis, [(i, i ^ distance) for i in range(size)])  37.8 us
    pallas_call x4, Pallas kernels, cross_coefficients(): pl.pallas_call(cross_body, in_specs=[pl.BlockSpec(memory_space=pltpu.SMEM...  24.2 us
    pallas_call x1, Pallas kernels, sums(): pl.pallas_call(functools.partial(sums_body, number=number, pieces=len(mix...  13.9 us
    all_gather x1, blocking collectives, gather_device(): lax.all_gather(stat.reshape(1, *stat.shape), 'cls', axis=0, tiled=True)  9.93 us
    pallas_call x1, Pallas kernels, arrange_references(): pl.pallas_call(reference_body, grid_spec=pltpu.PrefetchScalarGridSpec(num...  7.66 us
    unnamed x51, local copies, waits for them, and re-layouts  7.45 us
    pallas_call x2, Pallas kernels, arrange_particles(): pl.pallas_call(functools.partial(particle_body, distances=distances, n_pr...  5.35 us
  transfers between devices with their start and end apart: 37, of which 12 were waited for; matrix products, arithmetic and copies ran while one was open for 0% of the time, Pallas kernels for 20%

profile of v16, /device:TPU:0, one launch (start us, length us, event | category | flops | bytes accessed | tf_op | source)
XLA Modules:
  0.0 172.2 jit_solution(561375877814778682)
XLA Ops:
  4.0 2.7 %arrange_particles.2 = (bf16[129,16,128]{2,1,0:T(8,128)(2,1)S(1)}, bf16[129,16,128]{2,1,0:T(8,128)(2,1)S(1)}) custom-call(s32[1]{0:T(128)} %bitcast.at_ref, bf16[16,128,512]{2,1,0:T(8,128)(2,1)S(1)} %copy-done, s32[16,20]{1,0:T(8,128)S(1)} %pad_add_fusion.meta_ref), custom_call_target="tpu_custom_call" | custom-call | flops 134217728 | bytes 2097152 | tf_op jit(solution)/shard_map/arrange_particles/pallas_call | solution.py:281
  6.7 3.1 %collective-permute-start = (bf16[129,16,128]{2,1,0:T(8,128)(2,1)S(1)}, bf16[129,16,128]{2,1,0:T(8,128)(2,1)S(1)}, u32[]{:S(2)}, u32[]{:S(2)}) collective-permute-start(bf16[129,16,128]{2,1,0:T(8,128)(2,1)S(1)} %get-tuple-element.45), channel_id=1, source_target_pairs={{0,1},{1,0},{2,3},{3,2},{4,5},{5,4},{6,7},{7,6},{8,9},{9,8},{10,11... | collective-permute-start | bytes 1585160 | tf_op jit(solution)/shard_map/ppermute | solution.py:712
  12.8 2.7 %arrange_particles.3 = (bf16[129,16,128]{2,1,0:T(8,128)(2,1)S(1)}, bf16[129,16,128]{2,1,0:T(8,128)(2,1)S(1)}) custom-call(s32[1]{0:T(128)} %bitcast.at_ref, bf16[16,128,512]{2,1,0:T(8,128)(2,1)S(1)} %copy-done, s32[16,20]{1,0:T(8,128)S(1)} %pad_add_fusion.meta_ref), custom_call_target="tpu_custom_call" | custom-call | flops 134217728 | bytes 2097152 | tf_op jit(solution)/shard_map/arrange_particles/pallas_call | solution.py:281
  15.5 6.3 %collective-permute-done.refs_0_.refs_8_ = bf16[129,16,128]{2,1,0:T(8,128)(2,1)S(1)} collective-permute-done((bf16[129,16,128]{2,1,0:T(8,128)(2,1)S(1)}, bf16[129,16,128]{2,1,0:T(8,128)(2,1)S(1)}, u32[]{:S(2)}, u32[]{:S(2)}) %collective-permute-start) | collective-permute-done | bytes 528416 | tf_op jit(solution)/shard_map/ppermute | solution.py:712
  25.5 2.6 %collective-permute-start.15 = (bf16[129,16,128]{2,1,0:T(8,128)(2,1)S(1)}, bf16[129,16,128]{2,1,0:T(8,128)(2,1)}, u32[]{:S(2)}, u32[]{:S(2)}) collective-permute-start(bf16[129,16,128]{2,1,0:T(8,128)(2,1)S(1)} %get-tuple-element.62), channel_id=1, source_target_pairs={{0,2},{1,3},{2,0},{3,1},{4,6},{5,7},{6,4},{7,5},{8,10},{9,11},{10,... | collective-permute-start | bytes 1585160 | tf_op jit(solution)/shard_map/ppermute | solution.py:712
  28.1 7.7 %arrange_references.1 = (bf16[128,64,128]{2,1,0:T(8,128)(2,1)}, f32[64,128]{1,0:T(8,128)}) custom-call(s32[1]{0:T(128)} %bitcast.at_ref, bf16[64,128,512]{2,1,0:T(8,128)(2,1)} %x_ref.4), custom_call_target="tpu_custom_call" | custom-call | flops 268435456 | bytes 4194304 | tf_op jit(solution)/shard_map/arrange_references/pallas_call | solution.py:322
  35.8 2.8 %collective-permute-done.7.refs_6_ = bf16[129,16,128]{2,1,0:T(8,128)(2,1)} collective-permute-done((bf16[129,16,128]{2,1,0:T(8,128)(2,1)S(1)}, bf16[129,16,128]{2,1,0:T(8,128)(2,1)}, u32[]{:S(2)}, u32[]{:S(2)}) %collective-permute-start.7) | collective-permute-done | bytes 528416 | tf_op jit(solution)/shard_map/ppermute | solution.py:712
  39.1 8.4 %collective-permute-done.9.refs_2_.refs_10_ = bf16[129,16,128]{2,1,0:T(8,128)(2,1)} collective-permute-done((bf16[129,16,128]{2,1,0:T(8,128)(2,1)S(1)}, bf16[129,16,128]{2,1,0:T(8,128)(2,1)}, u32[]{:S(2)}, u32[]{:S(2)}) %collective-permute-start.9) | collective-permute-done | bytes 528416 | tf_op jit(solution)/shard_map/ppermute | solution.py:712
  53.4 3.5 %collective-permute-start.22 = (bf16[129,16,128]{2,1,0:T(8,128)(2,1)S(1)}, bf16[129,16,128]{2,1,0:T(8,128)(2,1)S(1)}, u32[]{:S(2)}, u32[]{:S(2)}) collective-permute-start(bf16[129,16,128]{2,1,0:T(8,128)(2,1)S(1)} %get-tuple-element.67), channel_id=1, source_target_pairs={{0,3},{1,2},{2,1},{3,0},{4,7},{5,6},{6,5},{7,4},{8,11},{9,10},{10,... | collective-permute-start | bytes 1585160 | tf_op jit(solution)/shard_map/ppermute | solution.py:712
  56.9 6.0 %cross_coefficients.4 = (f32[144,128]{1,0:T(8,128)}, f32[8,128]{1,0:T(8,128)}) custom-call(s32[1]{0:T(128)} %bitcast.2.at_ref, bf16[129,16,128]{2,1,0:T(8,128)(2,1)} %copy-done.1, bf16[129,16,128]{2,1,0:T(8,128)(2,1)} %collective-permute-done.4.refs_1_, bf16[129,16,128]{2,1,0:T(8,128)(2,1)} %copy-done.4, ...), custom_call_target="tpu_custom_call" | custom-call | flops 541065216 | bytes 4227072 | tf_op jit(solution)/shard_map/cross_coefficients/pallas_call | solution.py:467
  65.1 9.4 %collective-permute-done.19.refs_4_.refs_20_ = bf16[129,16,128]{2,1,0:T(8,128)(2,1)S(1)} collective-permute-done((bf16[129,16,128]{2,1,0:T(8,128)(2,1)}, bf16[129,16,128]{2,1,0:T(8,128)(2,1)S(1)}, u32[]{:S(2)}, u32[]{:S(2)}) %collective-permute-start.19) | collective-permute-done | bytes 528416 | tf_op jit(solution)/shard_map/ppermute | solution.py:712
  80.5 6.1 %cross_coefficients.5 = (f32[144,128]{1,0:T(8,128)}, f32[8,128]{1,0:T(8,128)}) custom-call(s32[1]{0:T(128)} %bitcast.2.at_ref, bf16[129,16,128]{2,1,0:T(8,128)(2,1)} %copy-done.2, bf16[129,16,128]{2,1,0:T(8,128)(2,1)} %copy-done.9, bf16[129,16,128]{2,1,0:T(8,128)(2,1)} %collective-permute-done.9.refs_2_.refs_10_, bf16[129,16,128]{2,1,0:T(8,128)(2,1)} %copy-done.10, ...), custom_call_target="tpu_custom_call" | custom-call | flops 541065216 | bytes 4227072 | tf_op jit(solution)/shard_map/cross_coefficients/pallas_call | solution.py:467
  86.5 3.4 %collective-permute-done.21.refs_6_.refs_22_ = bf16[129,16,128]{2,1,0:T(8,128)(2,1)S(1)} collective-permute-done((bf16[129,16,128]{2,1,0:T(8,128)(2,1)S(1)}, bf16[129,16,128]{2,1,0:T(8,128)(2,1)S(1)}, u32[]{:S(2)}, u32[]{:S(2)}) %collective-permute-start.21) | collective-permute-done | bytes 528416 | tf_op jit(solution)/shard_map/ppermute | solution.py:712
  89.9 10.5 %collective-permute-done.25.refs_2_.refs_26_ = bf16[129,16,128]{2,1,0:T(8,128)(2,1)S(1)} collective-permute-done((bf16[129,16,128]{2,1,0:T(8,128)(2,1)S(1)}, bf16[129,16,128]{2,1,0:T(8,128)(2,1)S(1)}, u32[]{:S(2)}, u32[]{:S(2)}) %collective-permute-start.25) | collective-permute-done | bytes 528416 | tf_op jit(solution)/shard_map/ppermute | solution.py:712
  104.3 6.0 %cross_coefficients.6 = (f32[144,128]{1,0:T(8,128)}, f32[8,128]{1,0:T(8,128)}) custom-call(s32[1]{0:T(128)} %bitcast.2.at_ref, bf16[129,16,128]{2,1,0:T(8,128)(2,1)} %collective-permute-done.15.refs_0_.refs_16_, bf16[129,16,128]{2,1,0:T(8,128)(2,1)} %collective-permute-done.16.refs_1_.refs_17_, bf16[129,16,128]{2,1,0:T(8,128)(2,1)} %copy-done.7, ...), custom_call_target="tpu_custom_call" | custom-call | flops 541065216 | bytes 4227072 | tf_op jit(solution)/shard_map/cross_coefficients/pallas_call | solution.py:467
  110.4 4.5 %collective-permute-done.29.refs_6_.refs_30_ = bf16[129,16,128]{2,1,0:T(8,128)(2,1)} collective-permute-done((bf16[129,16,128]{2,1,0:T(8,128)(2,1)S(1)}, bf16[129,16,128]{2,1,0:T(8,128)(2,1)}, u32[]{:S(2)}, u32[]{:S(2)}) %collective-permute-start.29) | collective-permute-done | bytes 528416 | tf_op jit(solution)/shard_map/ppermute | solution.py:712
  116.4 3.4 %collective-permute-start.32 = (f32[144,128]{1,0:T(8,128)}, f32[144,128]{1,0:T(8,128)S(1)}, u32[]{:S(2)}, u32[]{:S(2)}) collective-permute-start(f32[144,128]{1,0:T(8,128)} %get-tuple-element.72), channel_id=1, source_target_pairs={{0,2},{1,3},{2,0},{3,1},{4,6},{5,7},{6,4},{7,5},{8,10},{9,11},{10,... | collective-permute-start | bytes 221192 | tf_op jit(solution)/shard_map/ppermute | solution.py:712
  120.6 6.0 %cross_coefficients.7 = (f32[144,128]{1,0:T(8,128)}, f32[8,128]{1,0:T(8,128)}) custom-call(s32[1]{0:T(128)} %bitcast.2.at_ref, bf16[129,16,128]{2,1,0:T(8,128)(2,1)} %copy-done.8, bf16[129,16,128]{2,1,0:T(8,128)(2,1)} %collective-permute-done.24.refs_1_.refs_25_, bf16[129,16,128]{2,1,0:T(8,128)(2,1)} %copy-done.14, ...), custom_call_target="tpu_custom_call" | custom-call | flops 541065216 | bytes 4227072 | tf_op jit(solution)/shard_map/cross_coefficients/pallas_call | solution.py:467
  128.3 4.8 %collective-permute-done.33.refs_3_ = f32[144,128]{1,0:T(8,128)S(1)} collective-permute-done((f32[144,128]{1,0:T(8,128)}, f32[144,128]{1,0:T(8,128)S(1)}, u32[]{:S(2)}, u32[]{:S(2)}) %collective-permute-start.33) | collective-permute-done | bytes 73760 | tf_op jit(solution)/shard_map/ppermute | solution.py:712
  135.8 9.9 %all-gather.1.stat_ref = f32[8,2,128]{2,1,0:T(2,128)} all-gather(f32[1,2,128]{2,1,0:T(2,128)} %bitcast.9), channel_id=2, replica_groups=mesh['cls'=8,'prt'=4] {'cls'}, dimensions={0}, use_global_device_ids=true | all-gather | bytes 9216 | tf_op jit(solution)/shard_map/all_gather | solution.py:793
  149.3 2.8 %collective-permute-start.34 = (f32[144,128]{1,0:T(8,128)}, f32[144,128]{1,0:T(8,128)S(1)}, u32[]{:S(2)}, u32[]{:S(2)}) collective-permute-start(f32[144,128]{1,0:T(8,128)} %get-tuple-element.78.refs_32_), channel_id=1, source_target_pairs={{0,1},{1,0},{2,3},{3,2},{4,5},{5,4},{6,7},{7,6},{8,9},{9,8},{10,11... | collective-permute-start | bytes 221192 | tf_op jit(solution)/shard_map/ppermute | solution.py:712
  152.2 2.8 %collective-permute-done.36.refs_35_ = f32[144,128]{1,0:T(8,128)S(1)} collective-permute-done((f32[144,128]{1,0:T(8,128)}, f32[144,128]{1,0:T(8,128)S(1)}, u32[]{:S(2)}, u32[]{:S(2)}) %collective-permute-start.36) | collective-permute-done | bytes 73760 | tf_op jit(solution)/shard_map/ppermute | solution.py:712
  155.0 2.5 %collective-permute-done.35.refs_34_ = f32[144,128]{1,0:T(8,128)S(1)} collective-permute-done((f32[144,128]{1,0:T(8,128)}, f32[144,128]{1,0:T(8,128)S(1)}, u32[]{:S(2)}, u32[]{:S(2)}) %collective-permute-start.35) | collective-permute-done | bytes 73760 | tf_op jit(solution)/shard_map/ppermute | solution.py:712
  158.1 13.9 %sums.1 = (f32[64,32,512]{2,1,0:T(8,128)}, f32[1,64]{1,0:T(1,128)}) custom-call(bf16[129,16,128]{2,1,0:T(8,128)(2,1)} %copy-done.1, bf16[129,16,128]{2,1,0:T(8,128)(2,1)} %collective-permute-done.4.refs_1_, bf16[129,16,128]{2,1,0:T(8,128)(2,1)} %copy-done.4, bf16[129,16,128]{2,1,0:T(8,128)(2,1)} %collective-permute-done.5.refs_3_, ...), custom_call_target="tpu_custom_call" | custom-call | flops 2164260864 | bytes 21102592 | tf_op jit(solution)/shard_map/sums/pallas_call | solution.py:678
  (115 shorter events, 39.5 us)
Async XLA Ops:
  6.7 15.1 %collective-permute-start = (bf16[129,16,128]{2,1,0:T(8,128)(2,1)S(1)}, bf16[129,16,128]{2,1,0:T(8,128)(2,1)S(1)}, u32[]{:S(2)}, u32[]{:S(2)}) collective-permute-start(bf16[129,16,128]{2,1,0:T(8,128)(2,1)S(1)} %get-tuple-element.45), channel_id=1, source_target_pairs={{0,1},{1,0},{2,3},{3,2},{4,5},{5,4},{6,7},{7,6},{8,9},{9,8},{10,11... | collective-permute-start | bytes 1585160 | tf_op jit(solution)/shard_map/ppermute | solution.py:712
  9.8 13.7 %collective-permute-start.2 = (bf16[129,16,128]{2,1,0:T(8,128)(2,1)S(1)}, bf16[129,16,128]{2,1,0:T(8,128)(2,1)S(1)}, u32[]{:S(2)}, u32[]{:S(2)}) collective-permute-start(bf16[129,16,128]{2,1,0:T(8,128)(2,1)S(1)} %get-tuple-element.51.refs_0_), channel_id=1, source_target_pairs={{0,16},{4,20},{8,24},{12,28},{16,0},{20,4},{24,8},{28,12},{1,17},{... | collective-permute-start | bytes 1585160 | tf_op jit(solution)/shard_map/ppermute | solution.py:712
  11.3 16.8 %collective-permute-start.1 = (bf16[129,16,128]{2,1,0:T(8,128)(2,1)S(1)}, bf16[129,16,128]{2,1,0:T(8,128)(2,1)S(1)}, u32[]{:S(2)}, u32[]{:S(2)}) collective-permute-start(bf16[129,16,128]{2,1,0:T(8,128)(2,1)S(1)} %get-tuple-element.51.refs_0_), channel_id=1, source_target_pairs={{0,8},{4,12},{8,0},{12,4},{16,24},{20,28},{24,16},{28,20},{1,9},{5... | collective-permute-start | bytes 1585160 | tf_op jit(solution)/shard_map/ppermute | solution.py:712
  21.8 14.0 %collective-permute-start.3 = (bf16[129,16,128]{2,1,0:T(8,128)(2,1)S(1)}, bf16[129,16,128]{2,1,0:T(8,128)(2,1)S(1)}, u32[]{:S(2)}, u32[]{:S(2)}) collective-permute-start(bf16[129,16,128]{2,1,0:T(8,128)(2,1)S(1)} %collective-permute-done.refs_0_.refs_8_), channel_id=1, source_target_pairs={{0,16},{4,20},{8,24},{12,28},{16,0},{20,4},{24,8},{28,12},{1,17},{... | collective-permute-start | bytes 1585160 | tf_op jit(solution)/shard_map/ppermute | solution.py:712
  23.5 15.1 %collective-permute-start.7 = (bf16[129,16,128]{2,1,0:T(8,128)(2,1)S(1)}, bf16[129,16,128]{2,1,0:T(8,128)(2,1)}, u32[]{:S(2)}, u32[]{:S(2)}) collective-permute-start(bf16[129,16,128]{2,1,0:T(8,128)(2,1)S(1)} %collective-permute-done.2.refs_4_), channel_id=1, source_target_pairs={{0,8},{4,12},{8,0},{12,4},{16,24},{20,28},{24,16},{28,20},{1,9},{5... | collective-permute-start | bytes 1585160 | tf_op jit(solution)/shard_map/ppermute | solution.py:712
  25.0 22.5 %collective-permute-start.9 = (bf16[129,16,128]{2,1,0:T(8,128)(2,1)S(1)}, bf16[129,16,128]{2,1,0:T(8,128)(2,1)}, u32[]{:S(2)}, u32[]{:S(2)}) collective-permute-start(bf16[129,16,128]{2,1,0:T(8,128)(2,1)S(1)} %collective-permute-done.refs_0_.refs_8_), channel_id=1, source_target_pairs={{0,8},{4,12},{8,0},{12,4},{16,24},{20,28},{24,16},{28,20},{1,9},{5... | collective-permute-start | bytes 1585160 | tf_op jit(solution)/shard_map/ppermute | solution.py:712
  25.5 24.4 %collective-permute-start.15 = (bf16[129,16,128]{2,1,0:T(8,128)(2,1)S(1)}, bf16[129,16,128]{2,1,0:T(8,128)(2,1)}, u32[]{:S(2)}, u32[]{:S(2)}) collective-permute-start(bf16[129,16,128]{2,1,0:T(8,128)(2,1)S(1)} %get-tuple-element.62), channel_id=1, source_target_pairs={{0,2},{1,3},{2,0},{3,1},{4,6},{5,7},{6,4},{7,5},{8,10},{9,11},{10,... | collective-permute-start | bytes 1585160 | tf_op jit(solution)/shard_map/ppermute | solution.py:712
  38.5 13.4 %collective-permute-start.4 = (bf16[129,16,128]{2,1,0:T(8,128)(2,1)S(1)}, bf16[129,16,128]{2,1,0:T(8,128)(2,1)}, u32[]{:S(2)}, u32[]{:S(2)}) collective-permute-start(bf16[129,16,128]{2,1,0:T(8,128)(2,1)S(1)} %get-tuple-element.51.refs_0_), channel_id=1, source_target_pairs={{0,4},{4,0},{8,12},{12,8},{16,20},{20,16},{24,28},{28,24},{1,5},{5... | collective-permute-start | bytes 1585160 | tf_op jit(solution)/shard_map/ppermute | solution.py:712
  39.0 14.4 %collective-permute-start.5 = (bf16[129,16,128]{2,1,0:T(8,128)(2,1)S(1)}, bf16[129,16,128]{2,1,0:T(8,128)(2,1)}, u32[]{:S(2)}, u32[]{:S(2)}) collective-permute-start(bf16[129,16,128]{2,1,0:T(8,128)(2,1)S(1)} %collective-permute-done.1.refs_2_), channel_id=1, source_target_pairs={{0,4},{4,0},{8,12},{12,8},{16,20},{20,16},{24,28},{28,24},{1,5},{5... | collective-permute-start | bytes 1585160 | tf_op jit(solution)/shard_map/ppermute | solution.py:712
  49.9 15.3 %collective-permute-start.13 = (bf16[129,16,128]{2,1,0:T(8,128)(2,1)}, bf16[129,16,128]{2,1,0:T(8,128)(2,1)}, u32[]{:S(2)}, u32[]{:S(2)}) collective-permute-start(bf16[129,16,128]{2,1,0:T(8,128)(2,1)} %collective-permute-done.9.refs_2_.refs_10_), channel_id=1, source_target_pairs={{0,16},{4,20},{8,24},{12,28},{16,0},{20,4},{24,8},{28,12},{1,17},{... | collective-permute-start | bytes 1585160 | tf_op jit(solution)/shard_map/ppermute | solution.py:712
  51.1 23.4 %collective-permute-start.19 = (bf16[129,16,128]{2,1,0:T(8,128)(2,1)}, bf16[129,16,128]{2,1,0:T(8,128)(2,1)S(1)}, u32[]{:S(2)}, u32[]{:S(2)}) collective-permute-start(bf16[129,16,128]{2,1,0:T(8,128)(2,1)} %collective-permute-done.15.refs_0_.refs_16_), channel_id=1, source_target_pairs={{0,16},{4,20},{8,24},{12,28},{16,0},{20,4},{24,8},{28,12},{1,17},{... | collective-permute-start | bytes 1585160 | tf_op jit(solution)/shard_map/ppermute | solution.py:712
  51.9 22.6 %collective-permute-start.17 = (bf16[129,16,128]{2,1,0:T(8,128)(2,1)}, bf16[129,16,128]{2,1,0:T(8,128)(2,1)S(1)}, u32[]{:S(2)}, u32[]{:S(2)}) collective-permute-start(bf16[129,16,128]{2,1,0:T(8,128)(2,1)} %collective-permute-done.15.refs_0_.refs_16_), channel_id=1, source_target_pairs={{0,8},{4,12},{8,0},{12,4},{16,24},{20,28},{24,16},{28,20},{1,9},{5... | collective-permute-start | bytes 1585160 | tf_op jit(solution)/shard_map/ppermute | solution.py:712
  53.4 21.6 %collective-permute-start.22 = (bf16[129,16,128]{2,1,0:T(8,128)(2,1)S(1)}, bf16[129,16,128]{2,1,0:T(8,128)(2,1)S(1)}, u32[]{:S(2)}, u32[]{:S(2)}) collective-permute-start(bf16[129,16,128]{2,1,0:T(8,128)(2,1)S(1)} %get-tuple-element.67), channel_id=1, source_target_pairs={{0,3},{1,2},{2,1},{3,0},{4,7},{5,6},{6,5},{7,4},{8,11},{9,10},{10,... | collective-permute-start | bytes 1585160 | tf_op jit(solution)/shard_map/ppermute | solution.py:712
  62.9 13.6 %collective-permute-start.10 = (bf16[129,16,128]{2,1,0:T(8,128)(2,1)S(1)}, bf16[129,16,128]{2,1,0:T(8,128)(2,1)S(1)}, u32[]{:S(2)}, u32[]{:S(2)}) collective-permute-start(bf16[129,16,128]{2,1,0:T(8,128)(2,1)S(1)} %collective-permute-done.refs_0_.refs_8_), channel_id=1, source_target_pairs={{0,4},{4,0},{8,12},{12,8},{16,20},{20,16},{24,28},{28,24},{1,5},{5... | collective-permute-start | bytes 1585160 | tf_op jit(solution)/shard_map/ppermute | solution.py:712
  75.0 14.9 %collective-permute-start.21 = (bf16[129,16,128]{2,1,0:T(8,128)(2,1)S(1)}, bf16[129,16,128]{2,1,0:T(8,128)(2,1)S(1)}, u32[]{:S(2)}, u32[]{:S(2)}) collective-permute-start(bf16[129,16,128]{2,1,0:T(8,128)(2,1)S(1)} %collective-permute-done.19.refs_4_.refs_20_), channel_id=1, source_target_pairs={{0,8},{4,12},{8,0},{12,4},{16,24},{20,28},{24,16},{28,20},{1,9},{5... | collective-permute-start | bytes 1585160 | tf_op jit(solution)/shard_map/ppermute | solution.py:712
  76.5 23.8 %collective-permute-start.25 = (bf16[129,16,128]{2,1,0:T(8,128)(2,1)S(1)}, bf16[129,16,128]{2,1,0:T(8,128)(2,1)S(1)}, u32[]{:S(2)}, u32[]{:S(2)}) collective-permute-start(bf16[129,16,128]{2,1,0:T(8,128)(2,1)S(1)} %collective-permute-done.22.refs_0_.refs_24_), channel_id=1, source_target_pairs={{0,8},{4,12},{8,0},{12,4},{16,24},{20,28},{24,16},{28,20},{1,9},{5... | collective-permute-start | bytes 1585160 | tf_op jit(solution)/shard_map/ppermute | solution.py:712
  77.1 23.3 %collective-permute-start.27 = (bf16[129,16,128]{2,1,0:T(8,128)(2,1)S(1)}, bf16[129,16,128]{2,1,0:T(8,128)(2,1)}, u32[]{:S(2)}, u32[]{:S(2)}) collective-permute-start(bf16[129,16,128]{2,1,0:T(8,128)(2,1)S(1)} %collective-permute-done.22.refs_0_.refs_24_), channel_id=1, source_target_pairs={{0,16},{4,20},{8,24},{12,28},{16,0},{20,4},{24,8},{28,12},{1,17},{... | collective-permute-start | bytes 1585160 | tf_op jit(solution)/shard_map/ppermute | solution.py:712
  78.8 23.5 %collective-permute-start.20 = (bf16[129,16,128]{2,1,0:T(8,128)(2,1)S(1)}, bf16[129,16,128]{2,1,0:T(8,128)(2,1)}, u32[]{:S(2)}, u32[]{:S(2)}) collective-permute-start(bf16[129,16,128]{2,1,0:T(8,128)(2,1)S(1)} %collective-permute-done.19.refs_4_.refs_20_), channel_id=1, source_target_pairs={{0,4},{4,0},{8,12},{12,8},{16,20},{20,16},{24,28},{28,24},{1,5},{5... | collective-permute-start | bytes 1585160 | tf_op jit(solution)/shard_map/ppermute | solution.py:712
  80.4 21.8 %collective-permute-start.16 = (bf16[129,16,128]{2,1,0:T(8,128)(2,1)}, bf16[129,16,128]{2,1,0:T(8,128)(2,1)}, u32[]{:S(2)}, u32[]{:S(2)}) collective-permute-start(bf16[129,16,128]{2,1,0:T(8,128)(2,1)} %collective-permute-done.15.refs_0_.refs_16_), channel_id=1, source_target_pairs={{0,4},{4,0},{8,12},{12,8},{16,20},{20,16},{24,28},{28,24},{1,5},{5... | collective-permute-start | bytes 1585160 | tf_op jit(solution)/shard_map/ppermute | solution.py:712
  100.4 14.5 %collective-permute-start.29 = (bf16[129,16,128]{2,1,0:T(8,128)(2,1)S(1)}, bf16[129,16,128]{2,1,0:T(8,128)(2,1)}, u32[]{:S(2)}, u32[]{:S(2)}) collective-permute-start(bf16[129,16,128]{2,1,0:T(8,128)(2,1)S(1)} %collective-permute-done.25.refs_2_.refs_26_), channel_id=1, source_target_pairs={{0,16},{4,20},{8,24},{12,28},{16,0},{20,4},{24,8},{28,12},{1,17},{... | collective-permute-start | bytes 1585160 | tf_op jit(solution)/shard_map/ppermute | solution.py:712
  102.2 14.2 %collective-permute-start.24 = (bf16[129,16,128]{2,1,0:T(8,128)(2,1)S(1)}, bf16[129,16,128]{2,1,0:T(8,128)(2,1)}, u32[]{:S(2)}, u32[]{:S(2)}) collective-permute-start(bf16[129,16,128]{2,1,0:T(8,128)(2,1)S(1)} %collective-permute-done.22.refs_0_.refs_24_), channel_id=1, source_target_pairs={{0,4},{4,0},{8,12},{12,8},{16,20},{20,16},{24,28},{28,24},{1,5},{5... | collective-permute-start | bytes 1585160 | tf_op jit(solution)/shard_map/ppermute | solution.py:712
  102.4 17.4 %collective-permute-start.26 = (bf16[129,16,128]{2,1,0:T(8,128)(2,1)S(1)}, bf16[129,16,128]{2,1,0:T(8,128)(2,1)}, u32[]{:S(2)}, u32[]{:S(2)}) collective-permute-start(bf16[129,16,128]{2,1,0:T(8,128)(2,1)S(1)} %collective-permute-done.25.refs_2_.refs_26_), channel_id=1, source_target_pairs={{0,4},{4,0},{8,12},{12,8},{16,20},{20,16},{24,28},{28,24},{1,5},{5... | collective-permute-start | bytes 1585160 | tf_op jit(solution)/shard_map/ppermute | solution.py:712
  102.7 17.1 %collective-permute-start.28 = (bf16[129,16,128]{2,1,0:T(8,128)(2,1)}, bf16[129,16,128]{2,1,0:T(8,128)(2,1)}, u32[]{:S(2)}, u32[]{:S(2)}) collective-permute-start(bf16[129,16,128]{2,1,0:T(8,128)(2,1)} %collective-permute-done.27.refs_4_.refs_28_), channel_id=1, source_target_pairs={{0,4},{4,0},{8,12},{12,8},{16,20},{20,16},{24,28},{28,24},{1,5},{5... | collective-permute-start | bytes 1585160 | tf_op jit(solution)/shard_map/ppermute | solution.py:712
  114.9 13.4 %collective-permute-start.31 = (f32[144,128]{1,0:T(8,128)S(1)}, f32[144,128]{1,0:T(8,128)S(1)}, u32[]{:S(2)}, u32[]{:S(2)}) collective-permute-start(f32[144,128]{1,0:T(8,128)S(1)} %copy-done.24), channel_id=1, source_target_pairs={{0,1},{1,0},{2,3},{3,2},{4,5},{5,4},{6,7},{7,6},{8,9},{9,8},{10,11... | collective-permute-start | bytes 221192 | tf_op jit(solution)/shard_map/ppermute | solution.py:712
  (38 other events, 436.1 us)
